TPU v7x, 32 devices: a whole 2x2x4 slice. The times are simulated.
32 devices in a mesh: dp: 8 (over y, x, core), fsdp: 4 (over z).
Axes of the slice: x: 2, y: 2, z: 4, core: 2. Of those that a mesh axis runs over, the one named last changes fastest.
Arguments:
- tokens: bfloat16 [2, 8192, 1024], P(None, ('dp', 'fsdp')), may hold values from -6 to 6
- cotangent: bfloat16 [2, 8192, 1024], P(None, ('dp', 'fsdp')), may hold values from -6 to 6
- doc_lengths: int32 [2, 8], replicated, may hold values from 0 to 8192, as said below
- partner: int32 [2, 8], replicated, may hold values from 0 to 7, as said below
- memory_picks: int32 [2, 8, 8, 128], P(None, 'dp'), may hold values from 0 to 1023, as said below
- attention_in: bfloat16 [2, 1024, 3072], P(None, ('dp', 'fsdp')), may hold values from -0.1875 to 0.1875
- attention_out: bfloat16 [2, 1024, 1024], P(None, ('dp', 'fsdp')), may hold values from -1.5 to 1.5
- feed_in: bfloat16 [2, 1024, 5632], P(None, ('dp', 'fsdp')), may hold values from -0.1875 to 0.1875
- feed_out: bfloat16 [2, 2816, 1024], P(None, ('dp', 'fsdp')), may hold values from -0.109375 to 0.109375
- norm_gains: bfloat16 [2, 2, 1024], P(None, None, ('dp', 'fsdp')), may hold values from 0.5 to 1.5
Outputs:
- layer_output: bfloat16 [2, 8192, 1024], P(None, ('dp', 'fsdp'))
- input_grad: float32 [2, 8192, 1024], P(None, ('dp', 'fsdp'))
- grad_attention_in: float32 [2, 1024, 3072], P(None, ('dp', 'fsdp'))
- grad_attention_out: float32 [2, 1024, 1024], P(None, ('dp', 'fsdp'))
- grad_feed_in: float32 [2, 1024, 5632], P(None, ('dp', 'fsdp'))
- grad_feed_out: float32 [2, 2816, 1024], P(None, ('dp', 'fsdp'))
- grad_norm_gains: float32 [2, 2, 1024], P(None, None, ('dp', 'fsdp'))
Inputs may be any that keep to these rules, and one draw needn't show every extreme that they name: `doc_lengths`: the documents of a row fill its slots exactly, each one's last slot at least half full. A slot's partner is another slot of the same micro-batch. `memory_picks`: for each micro-batch, slot and head, 128 distinct places, all among the slot's non-padding tokens.
All inputs are finite; a program needn't handle non-finite values.
Results may differ from a plain program's by a relative error of at most 0.02.
Values may be sent and summed in bfloat16 or wider, within the bound.
A program may use at most 576 MiB of HBM per device.

v0:
```python
from functools import reduce
import math

import jax
import jax.numpy as jnp
from jax import lax
from jax.sharding import PartitionSpec as P

D = 1024
HEADS = 8
HEAD_DIM = 128
SEG = 1024
TOPK = 128
LAYERS = 2


epsilon = 1e-06
masked_score = -1e30


def rms_gain(hidden, gain_row):
    return (
        hidden * lax.rsqrt(jnp.mean(hidden * hidden, axis=-1, keepdims=True) + epsilon) * gain_row
    )


def rotate(values):
    half_dim = values.shape[-1] // 2
    return jnp.concatenate([-values[..., half_dim:], values[..., :half_dim]], axis=-1)


def rotate_back(values):
    half_dim = values.shape[-1] // 2
    return jnp.concatenate([values[..., half_dim:], -values[..., :half_dim]], axis=-1)


def rope_tables(positions):
    half_dim = HEAD_DIM // 2
    frequency = jnp.exp(
        jnp.arange(half_dim, dtype=jnp.float32) * (-2.0 * math.log(10000.0) / HEAD_DIM)
    )
    angles = positions.astype(jnp.float32)[:, None] * frequency[None, :]
    cos_table = jnp.concatenate([jnp.cos(angles), jnp.cos(angles)], axis=-1)[:, None, :]
    sin_table = jnp.concatenate([jnp.sin(angles), jnp.sin(angles)], axis=-1)[:, None, :]
    return (cos_table, sin_table)


def rotary(values, cos_table, sin_table):
    return values * cos_table + rotate(values) * sin_table


def rotary_back(gradient, cos_table, sin_table):
    return gradient * cos_table + rotate_back(gradient * sin_table)


def slot_layout(lengths):
    slot_total = lengths.shape[0]
    slot_counts = ((lengths + SEG - 1) // SEG).astype(jnp.int32)
    slot_starts = (jnp.cumsum(slot_counts) - slot_counts).astype(jnp.int32)
    slot_index = jnp.arange(slot_total, dtype=jnp.int32)
    started = (slot_starts[None, :] <= slot_index[:, None]) & (slot_counts[None, :] > 0)
    owner_doc = (jnp.sum(started.astype(jnp.int32), axis=1) - 1).astype(jnp.int32)
    owner_pick = slot_index[None, :] == owner_doc[:, None]
    first_slot = jnp.sum(jnp.where(owner_pick, slot_starts[None, :], 0), axis=1).astype(jnp.int32)
    doc_total = jnp.sum(jnp.where(owner_pick, lengths[None, :], 0), axis=1).astype(jnp.int32)
    valid_rows = jnp.clip(doc_total - (slot_index - first_slot) * SEG, 0, SEG).astype(jnp.int32)
    return (valid_rows, owner_doc)


def memory_plan(lengths, partner_row):
    valid_rows, owner_doc = slot_layout(lengths)
    block_ids = jnp.arange(lengths.shape[0], dtype=jnp.int32)
    earlier = (block_ids[None, :] < block_ids[:, None]) & (owner_doc[None, :] == owner_doc[:, None])
    visible = earlier | (block_ids[None, :] == partner_row[:, None])
    return (valid_rows, visible)


def pick_memory(values, pick_rows):
    chosen = jnp.take_along_axis(jnp.swapaxes(values, 0, 1), pick_rows[:, :, None], axis=1)
    return jnp.swapaxes(chosen, 0, 1)


def group_scores(query_part, key_part, allowed):
    raw_scores = jnp.einsum(
        "ihd,jhd->hij", query_part, key_part, preferred_element_type=jnp.float32
    ) * HEAD_DIM ** (-0.5)
    return jnp.where(allowed[None], raw_scores, masked_score)


def attention_forward(groups):
    score_list = [group_scores(group[0], group[1], group[3]) for group in groups]
    row_max = reduce(
        jnp.maximum, [jnp.max(score_block, axis=-1, keepdims=True) for score_block in score_list]
    )
    row_total = sum(
        (
            jnp.sum(jnp.exp(score_block - row_max), axis=-1, keepdims=True)
            for score_block in score_list
        )
    )
    logsum = row_max + jnp.log(row_total)
    attended = sum(
        (
            jnp.einsum(
                "hij,jhd->ihd",
                jnp.exp(score_block - logsum).astype(jnp.bfloat16),
                group[2],
                preferred_element_type=jnp.float32,
            )
            for score_block, group in zip(score_list, groups)
        )
    )
    return (attended, logsum)


def attention_backward(groups, logsum, grad_heads):
    score_scale = HEAD_DIM ** (-0.5)
    prob_list = [jnp.exp(group_scores(group[0], group[1], group[3]) - logsum) for group in groups]
    grad_prob_list = [
        jnp.einsum("ihd,jhd->hij", grad_heads, group[2], preferred_element_type=jnp.float32)
        for group in groups
    ]
    inner_sum = sum(
        (
            jnp.sum(prob_block * grad_block, axis=-1, keepdims=True)
            for prob_block, grad_block in zip(prob_list, grad_prob_list)
        )
    )
    results = []
    for group, prob_block, grad_block in zip(groups, prob_list, grad_prob_list):
        grad_score = (prob_block * (grad_block - inner_sum)).astype(jnp.bfloat16)
        grad_query = (
            jnp.einsum("hij,jhd->ihd", grad_score, group[1], preferred_element_type=jnp.float32)
            * score_scale
        )
        grad_keys = (
            jnp.einsum("hij,ihd->jhd", grad_score, group[0], preferred_element_type=jnp.float32)
            * score_scale
        )
        grad_values = jnp.einsum(
            "hij,ihd->jhd",
            prob_block.astype(jnp.bfloat16),
            grad_heads,
            preferred_element_type=jnp.float32,
        )
        results.append((grad_query, grad_keys, grad_values))
    return results


def local(
    tokens,
    cotangent,
    doc_lengths,
    partner,
    memory_picks,
    attention_in,
    attention_out,
    feed_in,
    feed_out,
    norm_gains,
):
    own_slot = lax.axis_index("dp")
    own_piece = lax.axis_index("fsdp")
    row_count = tokens.shape[1]
    positions = own_piece * row_count + jnp.arange(row_count, dtype=jnp.int32)
    cos_table, sin_table = rope_tables(positions)
    valid_all, visible_all = jax.vmap(memory_plan)(doc_lengths, partner)
    valid_mine = jnp.take(valid_all, own_slot, axis=1)
    visible_mine = jnp.take(visible_all, own_slot, axis=1)
    pick_mine = memory_picks[:, 0]
    key_places = jnp.arange(SEG, dtype=jnp.int32)
    causal_mask = key_places[None, :] <= positions[:, None]
    head_ids = jnp.arange(HEADS)[:, None]

    def build_groups(query_rot, segment, query_raw, memory_all, valid_rows, visible_row):
        local_mask = causal_mask & (key_places[None, :] < valid_rows)
        groups = [(query_rot, segment[:, 0], segment[:, -1], local_mask)]
        if memory_all is not None:
            groups.append(
                (
                    query_raw,
                    memory_all[:, 0],
                    memory_all[:, 1],
                    jnp.repeat(visible_row, TOPK)[None, :],
                )
            )
        return groups

    def forward_layer(weights, memory, stream_all):
        weight_qkv, weight_out, weight_gate_up, weight_down, gain_pair = weights

        def forward_advance(carried, entries):
            hidden, valid_rows, visible_row, pick_rows = entries
            normed = rms_gain(hidden, gain_pair[0].astype(jnp.float32)).astype(jnp.bfloat16)
            projected = jnp.dot(normed, weight_qkv, preferred_element_type=jnp.float32)
            query_part, key_part, value_part = [
                block.reshape(row_count, HEADS, HEAD_DIM)
                for block in jnp.split(projected, 3, axis=1)
            ]
            query_rot = rotary(query_part, cos_table, sin_table).astype(jnp.bfloat16)
            key_rot = rotary(key_part, cos_table, sin_table).astype(jnp.bfloat16)
            value_low = value_part.astype(jnp.bfloat16)
            if memory:
                query_raw = query_part.astype(jnp.bfloat16)
                packed = jnp.stack([key_rot, key_part.astype(jnp.bfloat16), value_low], axis=1)
            else:
                query_raw = None
                packed = jnp.stack([key_rot, value_low], axis=1)
            segment = lax.all_gather(packed, "fsdp", axis=0, tiled=True)
            memory_all = None
            if memory:
                chosen = jnp.stack(
                    [pick_memory(segment[:, 1], pick_rows), pick_memory(segment[:, 2], pick_rows)],
                    axis=1,
                )
                memory_all = lax.all_gather(chosen, "dp", axis=0, tiled=True)
            groups = build_groups(
                query_rot, segment, query_raw, memory_all, valid_rows, visible_row
            )
            attended, logsum = attention_forward(groups)
            attended_low = attended.reshape(row_count, D).astype(jnp.bfloat16)
            mid_stream = hidden + jnp.dot(
                attended_low, weight_out, preferred_element_type=jnp.float32
            )
            normed_ffn = rms_gain(mid_stream, gain_pair[1].astype(jnp.float32)).astype(jnp.bfloat16)
            gate_up = jnp.dot(normed_ffn, weight_gate_up, preferred_element_type=jnp.float32)
            gate_half, up_half = jnp.split(gate_up, 2, axis=1)
            ffn_hidden = (jax.nn.silu(gate_half) * up_half).astype(jnp.bfloat16)
            new_hidden = mid_stream + jnp.dot(
                ffn_hidden, weight_down, preferred_element_type=jnp.float32
            )
            saved = {
                "hidden": hidden,
                "mid_stream": mid_stream,
                "normed": normed,
                "normed_ffn": normed_ffn,
                "gate_up": gate_up,
                "ffn_hidden": ffn_hidden,
                "query_rot": query_rot,
                "segment": segment,
                "logsum": logsum,
                "attended_low": attended_low,
            }
            if memory:
                saved["query_raw"] = query_raw
                saved["memory_all"] = memory_all
            return (carried, (new_hidden, saved))

        _, (stream_next, saved_all) = lax.scan(
            forward_advance,
            jnp.zeros((), jnp.float32),
            (stream_all, valid_mine, visible_mine, pick_mine),
        )
        return (stream_next, saved_all)

    stream = tokens.astype(jnp.float32)
    kept_weights = []
    saved_layers = []
    for layer_index in range(LAYERS):
        weights = (
            lax.all_gather(attention_in[layer_index], ("dp", "fsdp"), axis=0, tiled=True),
            lax.all_gather(attention_out[layer_index], ("dp", "fsdp"), axis=0, tiled=True),
            lax.all_gather(feed_in[layer_index], ("dp", "fsdp"), axis=0, tiled=True),
            lax.all_gather(feed_out[layer_index], ("dp", "fsdp"), axis=0, tiled=True),
            lax.all_gather(norm_gains[layer_index], ("dp", "fsdp"), axis=1, tiled=True),
        )
        kept_weights.append(weights)
        stream, saved_all = forward_layer(weights, layer_index == LAYERS - 1, stream)
        saved_layers.append(saved_all)
    layer_output = stream.astype(jnp.bfloat16)
    grad_stream = cotangent.astype(jnp.float32)
    shard_list = [None] * LAYERS
    for layer_index in reversed(range(LAYERS)):
        weights = (
            lax.all_gather(attention_in[layer_index], ("dp", "fsdp"), axis=0, tiled=True),
            lax.all_gather(attention_out[layer_index], ("dp", "fsdp"), axis=0, tiled=True),
            lax.all_gather(feed_in[layer_index], ("dp", "fsdp"), axis=0, tiled=True),
            lax.all_gather(feed_out[layer_index], ("dp", "fsdp"), axis=0, tiled=True),
            lax.all_gather(norm_gains[layer_index], ("dp", "fsdp"), axis=1, tiled=True),
        )
        backward_memory = layer_index == LAYERS - 1
        (
            backward_weight_qkv,
            backward_weight_out,
            backward_weight_gate_up,
            backward_weight_down,
            backward_gain_pair,
        ) = weights

        def backward_advance(grad_sums, entries):
            grad_new, saved, valid_rows, visible_row, pick_rows = entries
            grad_ffn = grad_new.astype(jnp.bfloat16)
            grad_down = jnp.einsum(
                "rf,rd->fd", saved["ffn_hidden"], grad_ffn, preferred_element_type=jnp.float32
            )
            grad_hid = jnp.einsum(
                "rd,fd->rf", grad_ffn, backward_weight_down, preferred_element_type=jnp.float32
            )
            gate_half, up_half = jnp.split(saved["gate_up"], 2, axis=1)
            sigmoid_gate = jax.nn.sigmoid(gate_half)
            grad_gate = grad_hid * up_half * sigmoid_gate * (1.0 + gate_half * (1.0 - sigmoid_gate))
            grad_up = grad_hid * gate_half * sigmoid_gate
            grad_gate_up = jnp.concatenate([grad_gate, grad_up], axis=1).astype(jnp.bfloat16)
            grad_in_ffn = jnp.einsum(
                "rd,rk->dk", saved["normed_ffn"], grad_gate_up, preferred_element_type=jnp.float32
            )
            grad_normed_ffn = jnp.einsum(
                "rk,dk->rd",
                grad_gate_up,
                backward_weight_gate_up,
                preferred_element_type=jnp.float32,
            )
            _, norm_pull_ffn = jax.vjp(
                rms_gain, saved["mid_stream"], backward_gain_pair[1].astype(jnp.float32)
            )
            grad_mid_part, grad_gain_ffn = norm_pull_ffn(grad_normed_ffn)
            grad_mid = grad_new + grad_mid_part
            grad_attended = grad_mid.astype(jnp.bfloat16)
            grad_out_weight = jnp.einsum(
                "rk,rd->kd",
                saved["attended_low"],
                grad_attended,
                preferred_element_type=jnp.float32,
            )
            grad_heads = jnp.einsum(
                "rd,kd->rk", grad_attended, backward_weight_out, preferred_element_type=jnp.float32
            )
            grad_heads = grad_heads.astype(jnp.bfloat16).reshape(row_count, HEADS, HEAD_DIM)
            memory_all = saved["memory_all"] if backward_memory else None
            query_raw = saved["query_raw"] if backward_memory else None
            groups = build_groups(
                saved["query_rot"], saved["segment"], query_raw, memory_all, valid_rows, visible_row
            )
            results = attention_backward(groups, saved["logsum"], grad_heads)
            grad_query_rot, grad_local_keys, grad_local_values = results[0]
            grad_query = rotary_back(grad_query_rot, cos_table, sin_table)
            if backward_memory:
                grad_query_raw, grad_memory_keys, grad_memory_values = results[1]
                own_grads = lax.psum_scatter(
                    jnp.stack([grad_memory_keys, grad_memory_values], axis=1).astype(jnp.bfloat16),
                    "dp",
                    scatter_dimension=0,
                    tiled=True,
                ).astype(jnp.float32)
                spread = (
                    jnp.zeros((2, HEADS, SEG, HEAD_DIM), jnp.float32)
                    .at[:, head_ids, pick_rows]
                    .add(jnp.transpose(own_grads, (1, 2, 0, 3)))
                )
                packed = jnp.stack(
                    [
                        grad_local_keys,
                        jnp.swapaxes(spread[0], 0, 1),
                        grad_local_values + jnp.swapaxes(spread[1], 0, 1),
                    ],
                    axis=1,
                )
                grad_query = grad_query + grad_query_raw
            else:
                packed = jnp.stack([grad_local_keys, grad_local_values], axis=1)
            local_grads = lax.psum_scatter(
                packed.astype(jnp.bfloat16), "fsdp", scatter_dimension=0, tiled=True
            ).astype(jnp.float32)
            grad_key = rotary_back(local_grads[:, 0], cos_table, sin_table)
            if backward_memory:
                grad_key = grad_key + local_grads[:, 1]
            grad_value = local_grads[:, -1]
            grad_projected = jnp.concatenate(
                [
                    grad_query.reshape(row_count, D),
                    grad_key.reshape(row_count, D),
                    grad_value.reshape(row_count, D),
                ],
                axis=1,
            ).astype(jnp.bfloat16)
            grad_in_qkv = jnp.einsum(
                "rd,rk->dk", saved["normed"], grad_projected, preferred_element_type=jnp.float32
            )
            grad_normed_attn = jnp.einsum(
                "rk,dk->rd", grad_projected, backward_weight_qkv, preferred_element_type=jnp.float32
            )
            _, norm_pull_attn = jax.vjp(
                rms_gain, saved["hidden"], backward_gain_pair[0].astype(jnp.float32)
            )
            grad_hidden_part, grad_gain_attn = norm_pull_attn(grad_normed_attn)
            grad_hidden = grad_mid + grad_hidden_part
            updates = (
                grad_in_qkv,
                grad_out_weight,
                grad_in_ffn,
                grad_down,
                jnp.stack([grad_gain_attn, grad_gain_ffn]),
            )
            return (
                tuple((previous + update for previous, update in zip(grad_sums, updates))),
                grad_hidden,
            )

        zero_sums = (
            jnp.zeros(backward_weight_qkv.shape, jnp.float32),
            jnp.zeros(backward_weight_out.shape, jnp.float32),
            jnp.zeros(backward_weight_gate_up.shape, jnp.float32),
            jnp.zeros(backward_weight_down.shape, jnp.float32),
            jnp.zeros(backward_gain_pair.shape, jnp.float32),
        )
        grad_sums, grad_previous = lax.scan(
            backward_advance,
            zero_sums,
            (grad_stream, saved_layers[layer_index], valid_mine, visible_mine, pick_mine),
        )
        grad_stream, grad_sums = (grad_previous, grad_sums)
        shard_list[layer_index] = (
            lax.psum_scatter(grad_sums[0], ("dp", "fsdp"), scatter_dimension=0, tiled=True),
            lax.psum_scatter(grad_sums[1], ("dp", "fsdp"), scatter_dimension=0, tiled=True),
            lax.psum_scatter(grad_sums[2], ("dp", "fsdp"), scatter_dimension=0, tiled=True),
            lax.psum_scatter(grad_sums[3], ("dp", "fsdp"), scatter_dimension=0, tiled=True),
            lax.psum_scatter(grad_sums[4], ("dp", "fsdp"), scatter_dimension=1, tiled=True),
        )
    return (
        layer_output,
        grad_stream,
        jnp.stack([shard_set[0] for shard_set in shard_list]),
        jnp.stack([shard_set[1] for shard_set in shard_list]),
        jnp.stack([shard_set[2] for shard_set in shard_list]),
        jnp.stack([shard_set[3] for shard_set in shard_list]),
        jnp.stack([shard_set[4] for shard_set in shard_list]),
    )


def solution(mesh):
    in_specs = (
        P(None, ("dp", "fsdp"), None),
        P(None, ("dp", "fsdp"), None),
        P(),
        P(),
        P(None, "dp", None, None),
        P(None, ("dp", "fsdp"), None),
        P(None, ("dp", "fsdp"), None),
        P(None, ("dp", "fsdp"), None),
        P(None, ("dp", "fsdp"), None),
        P(None, None, ("dp", "fsdp")),
    )
    out_specs = (
        P(None, ("dp", "fsdp"), None),
        P(None, ("dp", "fsdp"), None),
        P(None, ("dp", "fsdp"), None),
        P(None, ("dp", "fsdp"), None),
        P(None, ("dp", "fsdp"), None),
        P(None, ("dp", "fsdp"), None),
        P(None, None, ("dp", "fsdp")),
    )
    return jax.shard_map(local, mesh=mesh, in_specs=in_specs, out_specs=out_specs, check_vma=False)
```

profile of v0, /device:TPU:0, one launch (start us, length us, event | category | flops | bytes accessed | tf_op | source)
XLA Modules:
  0.0 4838.9 jit_solution(5174664680796852475)
XLA Ops:
  16.8 74.5 %all-gather = bf16[1,2,1024]{1,0,2:T(2,128)(2,1)S(1)} all-gather(bf16[1,2,32]{1,0,2:T(2,128)(2,1)S(1)} %copy.262), channel_id=2, replica_groups=mesh['dp'=8,'fsdp'=4] {'dp','fsdp'}, dimensions={2}, use_global_device_ids=true | all-gather | bytes 4224 | tf_op jit(solution)/shard_map/all_gather | solution.py:265
  140.7 72.0 %all-gather.22.cloned.1.call-done = bf16[1,1024,3072]{2,1,0:T(8,128)(2,1)} async-done(((bf16[1,32,3072]{2,1,0:T(8,128)(2,1)}), bf16[1,1024,3072]{2,1,0:T(8,128)(2,1)}) %all-gather.22.cloned.1.call-update) | async-done | bytes 6291472 | tf_op jit(solution)/shard_map/all_gather | solution.py:261
  212.7 93.1 %all-gather.26.cloned.1.call-done = bf16[1,1024,5632]{2,1,0:T(8,128)(2,1)} async-done(((bf16[1,32,5632]{2,1,0:T(8,128)(2,1)}), bf16[1,1024,5632]{2,1,0:T(8,128)(2,1)}) %all-gather.26.cloned.1.call-update) | async-done | bytes 11534352 | tf_op jit(solution)/shard_map/all_gather | solution.py:263
  325.9 238.6 %while.106 = (s32[]{:T(128)}, f32[2,256,1024]{2,1,0:T(8,128)}, bf16[2,256,1024]{1,2,0:T(8,128)(2,1)}, bf16[2,256,2816]{2,1,0:T(8,128)(2,1)}, f32[2,256,5632]{2,1...) while((s32[]{:T(128)}, f32[2,256,1024]{2,1,0:T(8,128)}, ...), condition=%wide.region_9.10_spmd.clone, body=%wide.region_4.9_spmd.clone.sunk | while | flops 7688029696 | bytes 310355712 | solution.py:249
  693.1 71.4 %all-gather.30.cloned.1.call-done = bf16[1,1024,3072]{2,1,0:T(8,128)(2,1)} async-done(((bf16[1,32,3072]{2,1,0:T(8,128)(2,1)}), bf16[1,1024,3072]{2,1,0:T(8,128)(2,1)}) %all-gather.30.cloned.1.call-update) | async-done | bytes 6291472 | tf_op jit(solution)/shard_map/all_gather | solution.py:261
  764.6 93.0 %all-gather.34.cloned.1.call-done = bf16[1,1024,5632]{2,1,0:T(8,128)(2,1)} async-done(((bf16[1,32,5632]{2,1,0:T(8,128)(2,1)}), bf16[1,1024,5632]{2,1,0:T(8,128)(2,1)}) %all-gather.34.cloned.1.call-update) | async-done | bytes 11534352 | tf_op jit(solution)/shard_map/all_gather | solution.py:263
  877.0 463.7 %while.107 = (s32[]{:T(128)}, bf16[2,256,1024]{2,1,0:T(8,128)(2,1)}, bf16[2,256,1024]{1,2,0:T(8,128)(2,1)}, bf16[2,256,2816]{2,1,0:T(8,128)(2,1)}, f32[2,256,563...) while((s32[]{:T(128)}, bf16[2,256,1024]{2,1,0:T(8,128)(2,1)}, ...), condition=%wide.region_17.19_spmd.clone, body=%wide.region_10.18_spmd.clone.sunk | while | flops 8786952192 | bytes 483668288 | solution.py:249
  888.9 113.2 %all-gather.40.cloned.1.call-done = bf16[1024,3,8,128]{3,0,2,1:T(8,128)(2,1)} async-done(((bf16[256,3,8,128]{3,0,2,1:T(8,128)(2,1)}), bf16[1024,3,8,128]{3,0,2,1:T(8,128)(2,1)}) %all-gather.40.cloned.1.call-update) | async-done | bytes 6291472 | tf_op jit(solution)/shard_map/while/body/eval_jaxpr/all_gather | solution.py:209
  1119.9 114.8 %all-gather.40.cloned.1.call-done = bf16[1024,3,8,128]{3,0,2,1:T(8,128)(2,1)} async-done(((bf16[256,3,8,128]{3,0,2,1:T(8,128)(2,1)}), bf16[1024,3,8,128]{3,0,2,1:T(8,128)(2,1)}) %all-gather.40.cloned.1.call-update) | async-done | bytes 6291472 | tf_op jit(solution)/shard_map/while/body/eval_jaxpr/all_gather | solution.py:209
  1342.3 829.1 %while.108 = (s32[]{:T(128)}, f32[1024,3072]{1,0:T(8,128)}, f32[1024,1024]{1,0:T(8,128)}, f32[1024,5632]{1,0:T(8,128)}, f32[2816,1024]{1,0:T(8,128)}, /*index=5*...) while((s32[]{:T(128)}, f32[1024,3072]{1,0:T(8,128)}, ...), condition=%wide.region_30.32_spmd.clone, body=%wide.region_18.31_spmd.clone.sunk | while | flops 18670446592 | bytes 1016110976 | solution.py:406
  1482.7 97.2 %scatter_fusion = f32[2,8192,128]{2,0,1:T(2,128)} fusion(f32[2,8192,128]{2,0,1:T(2,128)} %broadcast.947, s32[1024]{0:T(1024)S(1)} %select_bitcast_fusion.7, f32[1024,2,128]{2,1,0:T(2,128)S(1)} %copy.379), kind=kCustom, calls=%fused_computation.2.clone.clone.1 | custom fusion | flops 262144 | bytes 3149824 | tf_op jit(solution)/shard_map/while
  1648.7 77.6 %reduce-scatter.44.cloned.1.call-done = bf16[256,3,8,128]{0,3,2,1:T(8,128)(2,1)} async-done(((bf16[1024,3,8,128]{0,3,2,1:T(8,128)(2,1)}), bf16[256,3,8,128]{0,3,2,1:T(8,128)(2,1)}) %reduce-scatter.44.cloned.1.call-update) | async-done | bytes 1572880 | tf_op jit(solution)/shard_map/while/body/eval_jaxpr/reduce_scatter | solution.py:361
  1887.0 97.2 %scatter_fusion = f32[2,8192,128]{2,0,1:T(2,128)} fusion(f32[2,8192,128]{2,0,1:T(2,128)} %broadcast.947, s32[1024]{0:T(1024)S(1)} %select_bitcast_fusion.7, f32[1024,2,128]{2,1,0:T(2,128)S(1)} %copy.379), kind=kCustom, calls=%fused_computation.2.clone.clone.1 | custom fusion | flops 262144 | bytes 3149824 | tf_op jit(solution)/shard_map/while
  2173.0 275.5 %while.109 = (s32[]{:T(128)}, f32[1024,3072]{1,0:T(8,128)}, f32[1024,1024]{1,0:T(8,128)}, f32[1024,5632]{1,0:T(8,128)}, f32[2816,1024]{1,0:T(8,128)}, /*index=5*...) while((s32[]{:T(128)}, f32[1024,3072]{1,0:T(8,128)}, ...), condition=%wide.region_40.42_spmd.clone, body=%wide.region_31.41_spmd.clone.sunk | while | flops 15942557696 | bytes 533104192 | solution.py:406
  2457.3 129.4 %reduce-scatter.38.cloned.1.call-done = f32[32,2]{1,0:T(8,128)} async-done(((f32[1024,2]{1,0:T(8,128)}), f32[32,2]{1,0:T(8,128)}) %reduce-scatter.38.cloned.1.call-update) | async-done | bytes 272
  2587.5 132.5 %reduce-scatter.40.cloned.1.call-done = f32[32,2]{1,0:T(8,128)} async-done(((f32[1024,2]{1,0:T(8,128)}), f32[32,2]{1,0:T(8,128)}) %reduce-scatter.40.cloned.1.call-update) | async-done | bytes 272
  2721.3 145.1 %reduce-scatter.26.cloned.1.call-done = f32[32,1024]{1,0:T(8,128)} async-done(((f32[1024,1024]{1,0:T(8,128)}), f32[32,1024]{1,0:T(8,128)}) %reduce-scatter.26.cloned.1.call-update) | async-done | bytes 131088 | tf_op jit(solution)/shard_map/reduce_scatter | solution.py:414
  2866.5 149.0 %reduce-scatter.28.cloned.1.call-done = f32[32,1024]{1,0:T(8,128)} async-done(((f32[1024,1024]{1,0:T(8,128)}), f32[32,1024]{1,0:T(8,128)}) %reduce-scatter.28.cloned.1.call-update) | async-done | bytes 131088 | tf_op jit(solution)/shard_map/reduce_scatter | solution.py:414
  3017.1 158.2 %reduce-scatter.22.cloned.1.call-done = f32[32,3072]{1,0:T(8,128)} async-done(((f32[1024,3072]{1,0:T(8,128)}), f32[32,3072]{1,0:T(8,128)}) %reduce-scatter.22.cloned.1.call-update) | async-done | bytes 393232 | tf_op jit(solution)/shard_map/reduce_scatter | solution.py:413
  3175.3 161.5 %reduce-scatter.24.cloned.1.call-done = f32[32,3072]{1,0:T(8,128)} async-done(((f32[1024,3072]{1,0:T(8,128)}), f32[32,3072]{1,0:T(8,128)}) %reduce-scatter.24.cloned.1.call-update) | async-done | bytes 393232 | tf_op jit(solution)/shard_map/reduce_scatter | solution.py:413
  3338.9 250.2 %reduce-scatter.34.cloned.1.call-done = f32[88,1024]{1,0:T(8,128)} async-done(((f32[2816,1024]{1,0:T(8,128)}), f32[88,1024]{1,0:T(8,128)}) %reduce-scatter.34.cloned.1.call-update) | async-done | bytes 360464 | tf_op jit(solution)/shard_map/reduce_scatter | solution.py:416
  3589.1 250.8 %reduce-scatter.36.cloned.1.call-done = f32[88,1024]{1,0:T(8,128)} async-done(((f32[2816,1024]{1,0:T(8,128)}), f32[88,1024]{1,0:T(8,128)}) %reduce-scatter.36.cloned.1.call-update) | async-done | bytes 360464 | tf_op jit(solution)/shard_map/reduce_scatter | solution.py:416
  3841.9 492.2 %reduce-scatter.30.cloned.1.call-done = f32[32,5632]{1,0:T(8,128)} async-done(((f32[1024,5632]{1,0:T(8,128)}), f32[32,5632]{1,0:T(8,128)}) %reduce-scatter.30.cloned.1.call-update) | async-done | bytes 720912 | tf_op jit(solution)/shard_map/reduce_scatter | solution.py:415
  4334.1 495.2 %reduce-scatter.32.cloned.1.call-done = f32[32,5632]{1,0:T(8,128)} async-done(((f32[1024,5632]{1,0:T(8,128)}), f32[32,5632]{1,0:T(8,128)}) %reduce-scatter.32.cloned.1.call-update) | async-done | bytes 720912 | tf_op jit(solution)/shard_map/reduce_scatter | solution.py:415
  (1094 shorter events, 1529.9 us)
Async XLA Ops:
  8.9 131.9 %all-gather.28.cloned.1.call-start = ((), (), s32[]{:S(2)}) async-start(), calls=%async_computation.24 | async-start | bytes 5947392 | tf_op jit(solution)/shard_map/all_gather | solution.py:264
  10.7 202.0 %all-gather.22.cloned.1.call-start = ((), (), s32[]{:S(2)}) async-start(), calls=%async_computation.21 | async-start | bytes 6488064 | tf_op jit(solution)/shard_map/all_gather | solution.py:261
  12.6 293.2 %all-gather.26.cloned.1.call-start = ((), (), s32[]{:S(2)}) async-start(), calls=%async_computation.23 | async-start | bytes 11894784 | tf_op jit(solution)/shard_map/all_gather | solution.py:263
  565.4 127.7 %all-gather.36.cloned.1.call-start = ((), (), s32[]{:S(2)}) async-start(), calls=%async_computation.28 | async-start | bytes 5947392 | tf_op jit(solution)/shard_map/all_gather | solution.py:264
  566.1 198.4 %all-gather.30.cloned.1.call-start = ((), (), s32[]{:S(2)}) async-start(), calls=%async_computation.25 | async-start | bytes 6488064 | tf_op jit(solution)/shard_map/all_gather | solution.py:261
  566.9 290.7 %all-gather.34.cloned.1.call-start = ((), (), s32[]{:S(2)}) async-start(), calls=%async_computation.27 | async-start | bytes 11894784 | tf_op jit(solution)/shard_map/all_gather | solution.py:263
  877.1 125.1 %all-gather.40.cloned.1.call-start = ((), (), s32[]{:S(2)}) async-start(), calls=%async_computation.32 | async-start | bytes 7864320 | tf_op jit(solution)/shard_map/while/body/eval_jaxpr/all_gather | solution.py:209
  888.3 182.6 %all-gather.42.cloned.1.call-start = ((), (), s32[]{:S(2)}) async-start(), calls=%async_computation.33 | async-start | bytes 4718592 | tf_op jit(solution)/shard_map/while/body/eval_jaxpr/all_gather | solution.py:216
  1108.1 126.6 %all-gather.40.cloned.1.call-start = ((), (), s32[]{:S(2)}) async-start(), calls=%async_computation.32 | async-start | bytes 7864320 | tf_op jit(solution)/shard_map/while/body/eval_jaxpr/all_gather | solution.py:209
  1119.2 184.2 %all-gather.42.cloned.1.call-start = ((), (), s32[]{:S(2)}) async-start(), calls=%async_computation.33 | async-start | bytes 4718592 | tf_op jit(solution)/shard_map/while/body/eval_jaxpr/all_gather | solution.py:216
  1342.7 132.0 %reduce-scatter.42.cloned.1.call-start = ((), (), s32[]{:S(2)}) async-start(), calls=%async_computation.34 | async-start | bytes 4718592 | tf_op jit(solution)/shard_map/while
  1423.2 303.0 %reduce-scatter.44.cloned.1.call-start = ((), (), s32[]{:S(2)}) async-start(), calls=%async_computation.35 | async-start | bytes 7864320 | tf_op jit(solution)/shard_map/while/body/eval_jaxpr/reduce_scatter | solution.py:361
  1746.3 132.8 %reduce-scatter.42.cloned.1.call-start = ((), (), s32[]{:S(2)}) async-start(), calls=%async_computation.34 | async-start | bytes 4718592 | tf_op jit(solution)/shard_map/while
  1827.0 303.7 %reduce-scatter.44.cloned.1.call-start = ((), (), s32[]{:S(2)}) async-start(), calls=%async_computation.35 | async-start | bytes 7864320 | tf_op jit(solution)/shard_map/while/body/eval_jaxpr/reduce_scatter | solution.py:361
  2448.4 138.2 %reduce-scatter.38.cloned.1.call-start = ((), (), s32[]{:S(2)}) async-start(), calls=%async_computation.29 | async-start | bytes 540672
  2450.2 269.8 %reduce-scatter.40.cloned.1.call-start = ((), (), s32[]{:S(2)}) async-start(), calls=%async_computation.30 | async-start | bytes 540672
  2452.0 414.5 %reduce-scatter.26.cloned.1.call-start = ((), (), s32[]{:S(2)}) async-start(), calls=%async_computation.15 | async-start | bytes 4325376 | tf_op jit(solution)/shard_map/reduce_scatter | solution.py:414
  2452.7 562.7 %reduce-scatter.28.cloned.1.call-start = ((), (), s32[]{:S(2)}) async-start(), calls=%async_computation.16 | async-start | bytes 4325376 | tf_op jit(solution)/shard_map/reduce_scatter | solution.py:414
  2453.3 722.1 %reduce-scatter.22.cloned.1.call-start = ((), (), s32[]{:S(2)}) async-start(), calls=%async_computation.13 | async-start | bytes 12976128 | tf_op jit(solution)/shard_map/reduce_scatter | solution.py:413
  2454.0 882.8 %reduce-scatter.24.cloned.1.call-start = ((), (), s32[]{:S(2)}) async-start(), calls=%async_computation.14 | async-start | bytes 12976128 | tf_op jit(solution)/shard_map/reduce_scatter | solution.py:413
  2454.6 1134.4 %reduce-scatter.34.cloned.1.call-start = ((), (), s32[]{:S(2)}) async-start(), calls=%async_computation.19 | async-start | bytes 11894784 | tf_op jit(solution)/shard_map/reduce_scatter | solution.py:416
  2455.2 1384.6 %reduce-scatter.36.cloned.1.call-start = ((), (), s32[]{:S(2)}) async-start(), calls=%async_computation.20 | async-start | bytes 11894784 | tf_op jit(solution)/shard_map/reduce_scatter | solution.py:416
  2456.0 1878.1 %reduce-scatter.30.cloned.1.call-start = ((), (), s32[]{:S(2)}) async-start(), calls=%async_computation.17 | async-start | bytes 23789568 | tf_op jit(solution)/shard_map/reduce_scatter | solution.py:415
  2456.7 2372.6 %reduce-scatter.32.cloned.1.call-start = ((), (), s32[]{:S(2)}) async-start(), calls=%async_computation.18 | async-start | bytes 23789568 | tf_op jit(solution)/shard_map/reduce_scatter | solution.py:415
  (275 other events, 5188.9 us)
Sparse Core Ops, SparseCore 0:
  74.5 66.1 all-gather.27
  144.2 68.5 all-gather.21
  216.0 89.7 all-gather.25
  335.3 79.1 all-gather.37
  454.2 79.2 all-gather.37
  627.2 65.8 all-gather.35
  696.0 68.5 all-gather.29
  767.8 89.7 all-gather.33
  888.4 113.7 all-gather.39
  1119.4 115.3 all-gather.39
  1615.5 110.7 reduce-scatter.43
  2019.8 110.9 reduce-scatter.43
  2213.8 77.2 reduce-scatter.45
  2351.5 77.2 reduce-scatter.45
  2452.1 134.5 reduce-scatter.37
  2589.6 130.3 reduce-scatter.39
  2722.2 144.1 reduce-scatter.25
  2868.6 146.7 reduce-scatter.27
  3021.4 153.8 reduce-scatter.21
  3182.3 154.5 reduce-scatter.23
  3339.0 250.0 reduce-scatter.33
  3591.4 248.4 reduce-scatter.35
  3842.1 491.8 reduce-scatter.29
  4336.2 493.0 reduce-scatter.31
  (6 shorter events, 288.1 us)
where the time goes:
time: 4850 us; the launch traced here: 4840 us
  waiting for transfers between devices  3510 us (72%)
  matrix products  433 us (9%)
  other arithmetic  359 us (7%)
  local copies, waits for them, and re-layouts  347 us (7%)
  blocking collectives  146 us (3%)
    reduce_scatter x2, waiting for transfers between devices, local(): lax.psum_scatter(grad_sums[2], ('dp', 'fsdp'), scatter_dimension=0, tiled...  987 us
    reduce_scatter x2, waiting for transfers between devices, local(): lax.psum_scatter(grad_sums[3], ('dp', 'fsdp'), scatter_dimension=0, tiled...  501 us
    all_gather x4, waiting for transfers between devices, forward_advance(): segment = lax.all_gather(packed, 'fsdp', axis=0, tiled=True)  364 us
    reduce_scatter x2, waiting for transfers between devices, local(): lax.psum_scatter(grad_sums[0], ('dp', 'fsdp'), scatter_dimension=0, tiled...  320 us
    reduce_scatter x2, waiting for transfers between devices, local(): lax.psum_scatter(grad_sums[1], ('dp', 'fsdp'), scatter_dimension=0, tiled...  294 us
    unnamed x20, waiting for transfers between devices  269 us
    reduce_scatter x4, waiting for transfers between devices, backward_advance(): lax.psum_scatter(packed.astype(jnp.bfloat16), 'fsdp', scatter_dimension=0...  226 us
    while x30, other arithmetic  195 us
  transfers between devices with their start and end apart: 30, of which 28 were waited for; matrix products, arithmetic and copies ran while one was open for 5% of the time, Pallas kernels for 0%

commit v1 on v0

v1 whole, which is shorter than its diff:
```python
import functools
import math

import jax
import jax.numpy as jnp
from jax import lax
from jax.experimental import pallas as pl
from jax.experimental.pallas import tpu as pltpu
from jax.sharding import PartitionSpec as P

HEAD_DIM = 128
SEG = 1024
MICRO = 2
EPSILON = 1e-06
MASKED = -1e30
SCALE = HEAD_DIM ** (-0.5)
LOG2E = 1.0 / math.log(2.0)
BF = jnp.bfloat16
F32 = jnp.float32
VMEM_LIMIT = 48 * 1024 * 1024


def slot_layout(lengths):
    slot_total = lengths.shape[0]
    slot_counts = ((lengths + SEG - 1) // SEG).astype(jnp.int32)
    slot_starts = (jnp.cumsum(slot_counts) - slot_counts).astype(jnp.int32)
    slot_index = jnp.arange(slot_total, dtype=jnp.int32)
    started = (slot_starts[None, :] <= slot_index[:, None]) & (slot_counts[None, :] > 0)
    owner_doc = (jnp.sum(started.astype(jnp.int32), axis=1) - 1).astype(jnp.int32)
    owner_pick = slot_index[None, :] == owner_doc[:, None]
    first_slot = jnp.sum(jnp.where(owner_pick, slot_starts[None, :], 0), axis=1).astype(jnp.int32)
    doc_total = jnp.sum(jnp.where(owner_pick, lengths[None, :], 0), axis=1).astype(jnp.int32)
    valid_rows = jnp.clip(doc_total - (slot_index - first_slot) * SEG, 0, SEG).astype(jnp.int32)
    return (valid_rows, owner_doc)


def memory_plan(lengths, partner_row):
    valid_rows, owner_doc = slot_layout(lengths)
    block_ids = jnp.arange(lengths.shape[0], dtype=jnp.int32)
    earlier = (block_ids[None, :] < block_ids[:, None]) & (owner_doc[None, :] == owner_doc[:, None])
    visible = earlier | (block_ids[None, :] == partner_row[:, None])
    return (valid_rows, visible)


class Grid:
    def __init__(self, n_dp, pieces):
        self.n_dp, self.F = n_dp, pieces
        self.J = n_dp // 2
        self.bits = self.J.bit_length() - 1
        self.Q = pieces // 4
        self.U = 2 * self.Q
        self.R = SEG // pieces
        self.T = 2 * self.R

    def trace(self):
        dp = lax.axis_index("dp")
        self.c, self.j, self.f = dp % 2, dp // 2, lax.axis_index("fsdp")
        self.q, self.g = self.f // self.Q, self.f % self.Q
        self.m, self.r = self.q // 2, self.q % 2
        self.k = self.c * self.Q + self.g
        self.slot = 2 * self.j + self.r

    def permute(self, value, target):
        pairs = []
        for j in range(self.J):
            for c in range(2):
                for f in range(self.F):
                    j2, c2, f2 = target(j, c, f)
                    pairs.append(((j * 2 + c) * self.F + f, (j2 * 2 + c2) * self.F + f2))
        return lax.ppermute(value, ("dp", "fsdp"), pairs)

    def swap(self, value):
        return self.permute(value, lambda j, c, f: (j, 1 - c, f))

    def ring(self, value, t):
        return self.permute(value, lambda j, c, f: (j, c, (f + t) % self.F))

    def bit(self, phase, c):
        return phase if c == 0 else self.bits - 1 - phase

    def flip(self, value, phase):
        return self.permute(value, lambda j, c, f: (j ^ (1 << self.bit(phase, c)), c, f))

    def mask(self, key, c):
        return sum(1 << self.bit(p, c) for p in range(self.bits) if key >> p & 1)

    def place(self, key, c):
        return jnp.where(c == 0, self.j ^ self.mask(key, 0), self.j ^ self.mask(key, 1))

    def member(self, value, t):
        def target(j, c, f):
            q, g = f // self.Q, f % self.Q
            k = (c * self.Q + g + t) % self.U
            return (j, k // self.Q, q * self.Q + k % self.Q)

        return self.permute(value, target)

    def within(self, value, t):
        return self.permute(
            value, lambda j, c, f: (j, c, f // self.Q * self.Q + (f % self.Q + t) % self.Q)
        )

    def slots(self, value, t):
        def target(j, c, f):
            q, g = f // self.Q, f % self.Q
            slot = (2 * j + q % 2 + t) % self.n_dp
            return (slot // 2, c, (2 * (q // 2) + slot % 2) * self.Q + g)

        return self.permute(value, target)

    def _spread(self, second):
        def target(j, c, f):
            m = f // (self.F // 2)
            m = 1 - m if second else m
            k = min(f, self.F - 1 - f)
            return (j, k // self.Q, (2 * m + c) * self.Q + k % self.Q)

        return target

    def _collect(self, second):
        there = self._spread(second)
        back = {
            there(0, c, f): (c, f) for c in range(2) for f in range(self.F)
        }
        return lambda j, c, f: (j,) + back[(0, c, f)]

    def to_units(self, value):
        here = self.f // (self.F // 2)
        first = self.permute(jnp.where(here == 0, value[0], value[1]), self._spread(False))
        second = self.permute(jnp.where(here == 0, value[1], value[0]), self._spread(True))
        return jnp.concatenate(
            [jnp.where(self.m == 0, first, second), jnp.where(self.m == 0, second, first)]
        )

    def from_units(self, value):
        low, high = value[: self.R], value[self.R :]
        first = self.permute(jnp.where(self.m == 0, low, high), self._collect(False))
        second = self.permute(jnp.where(self.m == 0, high, low), self._collect(True))
        here = self.f // (self.F // 2)
        return jnp.stack([jnp.where(here == 0, first, second), jnp.where(here == 0, second, first)])


def any_spec():
    return pl.BlockSpec(memory_space=pl.ANY)


def assemble_body(count, place_ref, *refs):
    blocks, out, sem = refs[: 2 * count], refs[2 * count], refs[2 * count + 1]
    step = pl.program_id(0)
    for i in range(2 * count):

        @pl.when(step == i)
        def _():
            copy = pltpu.make_async_copy(blocks[i], out, sem)
            copy.start()
            copy.wait()


def assemble(grid, own, other):
    count, (rows, half) = len(own), own[0].shape
    places = [grid.place(key, grid.c) for key in range(count)]
    places += [grid.place(key, 1 - grid.c) for key in range(count)]
    places = jnp.stack(places + [grid.c, 1 - grid.c]).astype(jnp.int32)
    size = count * rows * 2 * half
    return pl.pallas_call(
        functools.partial(assemble_body, count),
        grid_spec=pltpu.PrefetchScalarGridSpec(
            num_scalar_prefetch=1,
            grid=(2 * count,),
            in_specs=[any_spec()] * (2 * count),
            out_specs=pl.BlockSpec(
                (rows, half), lambda i, place: (place[i], place[2 * count + i // count])
            ),
            scratch_shapes=[pltpu.SemaphoreType.DMA],
        ),
        out_shape=jax.ShapeDtypeStruct((count * rows, 2 * half), own[0].dtype),
        compiler_params=params(),
        cost_estimate=pl.CostEstimate(flops=0, bytes_accessed=4 * size, transcendentals=0),
    )(places, *own, *other)


def roll_blocks(grid, arrived):
    ordered = [arrived[(grid.F - i) % grid.F] for i in range(grid.F)]
    both = jnp.stack(ordered + ordered[:-1])
    return lax.dynamic_slice_in_dim(both, (grid.F - grid.f) % grid.F, grid.F, axis=0)


def gather_weight(grid, shard):
    rows, width = shard.shape
    half = width // 2
    mine = lax.dynamic_slice_in_dim(shard, grid.c * half, half, axis=1)
    got = grid.swap(lax.dynamic_slice_in_dim(shard, (1 - grid.c) * half, half, axis=1))
    pair = jnp.stack([jnp.where(grid.c == 0, mine, got), jnp.where(grid.c == 0, got, mine)])
    arrived = [pair] + [grid.ring(pair, t) for t in range(1, grid.F)]
    line = jnp.swapaxes(roll_blocks(grid, arrived), 0, 1).reshape(2 * grid.F * rows, half)
    blocks = [line]
    for phase in range(grid.bits):
        blocks = blocks + [grid.flip(block, phase) for block in blocks]
    return assemble(grid, blocks, [grid.swap(block) for block in blocks])


def scatter_gradient(grid, total):
    height, half = total.shape
    rows = height // (grid.J * 2 * grid.F)
    parts = total.reshape(grid.J, height // grid.J, half)
    pieces = {
        key: lax.dynamic_index_in_dim(parts, grid.place(key, grid.c), 0, keepdims=False)
        for key in range(grid.J)
    }
    for phase in range(grid.bits):
        for key in sorted(pieces, reverse=True):
            if key >> phase & 1:
                got = grid.flip(pieces.pop(key), phase)
                here = key ^ (1 << phase)
                pieces[here] = (pieces[here].astype(F32) + got.astype(F32)).astype(BF)
    line = pieces[0].reshape(2, grid.F, rows, half)

    def block(t):
        return lax.dynamic_index_in_dim(line, (grid.f + t) % grid.F, 1, keepdims=False)

    summed = block(0).astype(F32)
    for got in [grid.ring(block(t), t) for t in range(1, grid.F)]:
        summed = summed + got.astype(F32)
    mine = lax.dynamic_index_in_dim(summed, grid.c, 0, keepdims=False)
    give = lax.dynamic_index_in_dim(summed, 1 - grid.c, 0, keepdims=False)
    got = grid.swap(give.astype(BF)).astype(F32)
    return jnp.concatenate(
        [jnp.where(grid.c == 0, mine, got), jnp.where(grid.c == 0, got, mine)], axis=1
    )


def gather_gains(grid, shard):
    value = shard.astype(BF)
    arrived = [value] + [grid.ring(value, t) for t in range(1, grid.F)]
    line = roll_blocks(grid, arrived)
    other = grid.swap(line)
    line = jnp.stack([jnp.where(grid.c == 0, line, other), jnp.where(grid.c == 0, other, line)])
    blocks = [line]
    for phase in range(grid.bits):
        blocks = blocks + [grid.flip(block, phase) for block in blocks]
    whole = jnp.stack(blocks)
    order = jnp.arange(grid.J) ^ grid.j
    if grid.bits > 1:
        turned = sum(((order >> p) & 1) << grid.bit(p, 1) for p in range(grid.bits))
        order = jnp.where(grid.c == 0, order, turned)
    whole = jnp.take(whole, order, axis=0)
    whole = jnp.transpose(whole, (3, 4, 0, 1, 2, 5))
    return whole.reshape(shard.shape[0], shard.shape[1], -1)


def scatter_gains(grid, total):
    layers, kinds, width = total.shape
    rows = width // (grid.n_dp * grid.F)
    total = total + grid.swap(total)
    for phase in range(grid.bits):
        total = total + grid.flip(total, phase)
    parts = total.reshape(layers, kinds, grid.J, 2, grid.F, rows)
    mine = lax.dynamic_index_in_dim(parts, grid.j, 2, keepdims=False)
    mine = lax.dynamic_index_in_dim(mine, grid.c, 2, keepdims=False)

    def block(t):
        return lax.dynamic_index_in_dim(mine, (grid.f + t) % grid.F, 2, keepdims=False)

    return block(0) + sum(grid.ring(block(t), t) for t in range(1, grid.F))


def rope_tables():
    half_dim = HEAD_DIM // 2
    frequency = jnp.exp(
        jnp.arange(half_dim, dtype=F32) * (-2.0 * math.log(10000.0) / HEAD_DIM)
    )
    angles = jnp.arange(SEG, dtype=jnp.int32).astype(F32)[:, None] * frequency[None, :]
    cos, sin = jnp.cos(angles), jnp.sin(angles)
    return (jnp.concatenate([cos, cos], axis=-1), jnp.concatenate([-sin, sin], axis=-1))


def turn(values, cos, sin):
    return values * cos + pltpu.roll(values, HEAD_DIM // 2, 1) * sin


def params():
    return pltpu.CompilerParams(vmem_limit_bytes=VMEM_LIMIT)


def smem():
    return pl.BlockSpec(memory_space=pltpu.SMEM)


def whole_spec(shape):
    return pl.BlockSpec(shape, lambda *_: (0,) * len(shape))


def piece_start(grid, member, part):
    return (member if part == 0 else grid.F - 1 - member) * grid.R


def table_rows(grid, table_ref, member, part):
    start = pl.multiple_of(piece_start(grid, member, part), grid.R)
    return table_ref[pl.ds(start, grid.R), :]


def split_body(grid, memory, info_ref, cos_ref, sin_ref, q_ref, k_ref, v_ref, *outs):
    me = info_ref[0]
    for part in range(2):
        rows = pl.ds(part * grid.R, grid.R)
        cos = table_rows(grid, cos_ref, me, part)
        sin = table_rows(grid, sin_ref, me, part)
        query, key = q_ref[rows, :], k_ref[rows, :]
        outs[0][rows, :] = turn(query, cos, sin).astype(BF)
        outs[1][rows, :] = turn(key, cos, sin).astype(BF)
        outs[2][rows, :] = v_ref[rows, :].astype(BF)
        if memory:
            outs[3][rows, :] = query.astype(BF)
            outs[4][rows, :] = key.astype(BF)


def split_heads(grid, memory, info, tables, projected):
    rows, width = projected.shape
    heads = width // (3 * HEAD_DIM)
    count = 5 if memory else 3
    piece = lambda at: pl.BlockSpec((rows, HEAD_DIM), lambda h: (0, at * heads + h))
    return pl.pallas_call(
        functools.partial(split_body, grid, memory),
        grid=(heads,),
        out_shape=[jax.ShapeDtypeStruct((rows, heads * HEAD_DIM), BF)] * count,
        in_specs=[smem(), whole_spec((SEG, HEAD_DIM)), whole_spec((SEG, HEAD_DIM))]
        + [piece(0), piece(1), piece(2)],
        out_specs=[piece(0)] * count,
        compiler_params=params(),
        cost_estimate=pl.CostEstimate(
            flops=10 * rows * width, bytes_accessed=8 * rows * width, transcendentals=0
        ),
    )(info, *tables, projected, projected, projected)


def dot(left, right, contract):
    return lax.dot_general(
        left, right, (((contract[0],), (contract[1],)), ((), ())), preferred_element_type=F32
    )


def part_scores(grid, info_ref, part, query, keys):
    me, valid = info_ref[0], info_ref[1]
    shape = (grid.R, grid.R)
    apart = lax.broadcasted_iota(jnp.int32, shape, 0) - lax.broadcasted_iota(jnp.int32, shape, 1)
    found = []
    for t in range(grid.U):
        member = lax.rem(me - t + grid.U, grid.U)
        for side in range(part + 1):
            score = dot(keys[t][side * grid.R : (side + 1) * grid.R], query, (1, 1))
            if side == part:
                start = piece_start(grid, member, side)
                allowed = apart <= piece_start(grid, me, part) - start
                if side == 1:
                    down = lax.broadcasted_iota(jnp.int32, shape, 0)
                    allowed = allowed & (down < valid - start)
                score = jnp.where(allowed, score, MASKED)
            found.append((t, side, score))
    return found


def head_halves(own_ref, other_ref, step, per_half):
    return jnp.where(step < per_half, own_ref[...], other_ref[...])


def softmax_parts(scores):
    top = functools.reduce(jnp.maximum, [jnp.max(s, axis=0, keepdims=True) for s in scores])
    powers = [jnp.exp2((s - top) * (SCALE * LOG2E)) for s in scores]
    inverse = 1.0 / sum(jnp.sum(p, axis=0, keepdims=True) for p in powers)
    return [p * inverse for p in powers]


def attend_body(grid, memory, heads, info_ref, *refs):
    U, R = grid.U, grid.R
    q_ref, k_refs, v_refs = refs[0], refs[1 : 1 + U], refs[1 + U : 1 + 2 * U]
    refs = refs[1 + 2 * U :]
    keys, values = [r[...] for r in k_refs], [r[...] for r in v_refs]
    if memory:
        step = pl.program_id(0)
        memory_keys = head_halves(refs[1], refs[2], step, heads // 2)
        memory_values = head_halves(refs[3], refs[4], step, heads // 2)
        bias = refs[5][...]
    out_ref = refs[-1]
    for part in range(2):
        rows = pl.ds(part * R, R)
        found = part_scores(grid, info_ref, part, q_ref[rows, :], keys)
        scores = [s for _, _, s in found]
        mixed = [values[t][side * R : (side + 1) * R] for t, side, _ in found]
        if memory:
            scores.append(dot(memory_keys, refs[0][rows, :], (1, 1)) + bias)
            mixed.append(memory_values)
        total = sum(
            dot(value, p.astype(BF), (0, 0)) for value, p in zip(mixed, softmax_parts(scores))
        )
        out_ref[rows, :] = total.T.astype(BF)


def head_specs(grid, heads, memory_rows):
    per = heads // 2

    def head(h, info):
        return lax.rem(info[2] + h // per, 2) * per + h % per

    piece = pl.BlockSpec((grid.T, HEAD_DIM), lambda h, info: (0, head(h, info)))
    own = pl.BlockSpec((memory_rows, HEAD_DIM), lambda h, info: (0, jnp.minimum(h, per - 1)))
    other = pl.BlockSpec((memory_rows, HEAD_DIM), lambda h, info: (0, jnp.maximum(h - per, 0)))
    return piece, own, other


def attention_cost(grid, heads, memory_rows, products):
    pairs = grid.T * (SEG * 3 // 4 + memory_rows) * heads
    return pl.CostEstimate(
        flops=2 * products * HEAD_DIM * pairs,
        bytes_accessed=2 * HEAD_DIM * heads * 4 * (SEG + memory_rows),
        transcendentals=pairs,
    )


def attend(grid, info, query, keys, values, extra):
    heads = query.shape[1] // HEAD_DIM
    memory = extra is not None
    memory_rows = grid.n_dp * extra["topk"] if memory else 8
    piece, own, other = head_specs(grid, heads, memory_rows)
    operands, specs = [query, *keys, *values], [piece] * (1 + 2 * grid.U)
    if memory:
        operands += [extra["query"], *extra["keys"], *extra["values"], extra["bias"]]
        specs += [piece, own, other, own, other, pl.BlockSpec((memory_rows, 1), lambda h, info: (0, 0))]
    return pl.pallas_call(
        functools.partial(attend_body, grid, memory, heads),
        grid_spec=pltpu.PrefetchScalarGridSpec(
            num_scalar_prefetch=1, grid=(heads,), in_specs=specs, out_specs=piece
        ),
        out_shape=jax.ShapeDtypeStruct(query.shape, BF),
        compiler_params=params(),
        cost_estimate=attention_cost(grid, heads, memory_rows if memory else 0, 2),
    )(info, *operands)


def attend_back_body(grid, memory, heads, info_ref, *refs):
    U, R = grid.U, grid.R
    cos_ref, sin_ref, q_ref, g_ref = refs[:4]
    k_refs, v_refs = refs[4 : 4 + U], refs[4 + U : 4 + 2 * U]
    refs = refs[4 + 2 * U :]
    keys, values = [r[...] for r in k_refs], [r[...] for r in v_refs]
    step = pl.program_id(0)
    if memory:
        query_raw_ref = refs[0]
        memory_keys = head_halves(refs[1], refs[2], step, heads // 2)
        memory_values = head_halves(refs[3], refs[4], step, heads // 2)
        bias = refs[5][...]
        refs = refs[6:]
    dq_ref, dk_refs, dv_refs, refs = refs[0], refs[1 : 1 + U], refs[1 + U : 1 + 2 * U], refs[1 + 2 * U :]
    me = info_ref[0]
    grad_keys, grad_values = {}, {}

    def add(store, at, value):
        store[at] = store[at] + value if at in store else value

    for part in range(2):
        rows = pl.ds(part * R, R)
        query, grad = q_ref[rows, :], g_ref[rows, :]
        found = part_scores(grid, info_ref, part, query, keys)
        places = [(t, side) for t, side, _ in found]
        scores = [s for _, _, s in found]
        part_keys = [keys[t][side * R : (side + 1) * R] for t, side in places]
        part_values = [values[t][side * R : (side + 1) * R] for t, side in places]
        queries = [query] * len(places)
        if memory:
            places.append("memory")
            queries.append(query_raw_ref[rows, :])
            scores.append(dot(memory_keys, queries[-1], (1, 1)) + bias)
            part_keys.append(memory_keys)
            part_values.append(memory_values)
        probs = softmax_parts(scores)
        grads = [dot(value, grad, (1, 1)) for value in part_values]
        inner = sum(jnp.sum(p * d, axis=0, keepdims=True) for p, d in zip(probs, grads))
        local_query, raw_query = None, None
        for at, p, d, key, asked in zip(places, probs, grads, part_keys, queries):
            moved = (p * (d - inner)).astype(BF)
            add(grad_keys, at, dot(moved, asked, (1, 0)))
            add(grad_values, at, dot(p.astype(BF), grad, (1, 0)))
            back = dot(key, moved, (0, 0))
            if at == "memory":
                raw_query = back
            else:
                local_query = back if local_query is None else local_query + back
        cos = table_rows(grid, cos_ref, me, part)
        sin = table_rows(grid, sin_ref, me, part)
        result = turn(local_query.T, cos, -sin)
        if memory:
            result = result + raw_query.T
        dq_ref[rows, :] = (result * SCALE).astype(BF)
    for t in range(U):
        member = lax.rem(me - t + U, U)
        for side in range(2):
            rows = pl.ds(side * R, R)
            cos = table_rows(grid, cos_ref, member, side)
            sin = table_rows(grid, sin_ref, member, side)
            key = turn(grad_keys[(t, side)], cos, -sin) * SCALE
            dk_refs[t][rows, :] = key.astype(dk_refs[t].dtype)
            dv_refs[t][rows, :] = grad_values[(t, side)].astype(dv_refs[t].dtype)
    if memory:
        key = (grad_keys["memory"] * SCALE).astype(BF)
        value = grad_values["memory"].astype(BF)

        @pl.when(step < heads // 2)
        def _():
            refs[0][...] = key
            refs[1][...] = value

        @pl.when(step >= heads // 2)
        def _():
            refs[2][...] = key
            refs[3][...] = value


def attend_back(grid, info, tables, query, grad, keys, values, extra):
    rows, width = query.shape
    heads = width // HEAD_DIM
    memory = extra is not None
    memory_rows = grid.n_dp * extra["topk"] if memory else 8
    piece, own, other = head_specs(grid, heads, memory_rows)
    table = pl.BlockSpec((SEG, HEAD_DIM), lambda h, info: (0, 0))
    operands = [*tables, query, grad, *keys, *values]
    specs = [table, table] + [piece] * (2 + 2 * grid.U)
    own_kind = jax.ShapeDtypeStruct((rows, width), F32)
    sent_kind = jax.ShapeDtypeStruct((rows, width), BF)
    kinds = [own_kind] + [sent_kind] * (grid.U - 1)
    out_shape = [sent_kind] + kinds + kinds
    out_specs = [piece] * len(out_shape)
    if memory:
        operands += [extra["query"], *extra["keys"], *extra["values"], extra["bias"]]
        specs += [piece, own, other, own, other, pl.BlockSpec((memory_rows, 1), lambda h, info: (0, 0))]
        out_shape += [jax.ShapeDtypeStruct((memory_rows, width // 2), BF)] * 4
        out_specs += [own, own, other, other]
    outs = pl.pallas_call(
        functools.partial(attend_back_body, grid, memory, heads),
        grid_spec=pltpu.PrefetchScalarGridSpec(
            num_scalar_prefetch=1, grid=(heads,), in_specs=specs, out_specs=out_specs
        ),
        out_shape=out_shape,
        compiler_params=params(),
        cost_estimate=attention_cost(grid, heads, memory_rows if memory else 0, 5),
    )(info, *operands)
    U = grid.U
    return outs[0], outs[1 : 1 + U], outs[1 + U : 1 + 2 * U], outs[1 + 2 * U :]


def pick_body(grid, info_ref, picks_ref, *refs):
    U, R = grid.U, grid.R
    out_ref = refs[-1]
    picks = picks_ref[0]
    key, value = 0.0, 0.0
    for t in range(U):
        member = lax.rem(info_ref[0] - t + U, U)
        for side in range(2):
            across = lax.broadcasted_iota(jnp.int32, (picks.shape[0], R), 1)
            chosen = (picks == across + piece_start(grid, member, side)).astype(BF)
            rows = pl.ds(side * R, R)
            key = key + dot(chosen, refs[t][rows, :], (1, 0))
            value = value + dot(chosen, refs[U + t][rows, :], (1, 0))
    out_ref[0] = key.astype(BF)
    out_ref[1] = value.astype(BF)


def pick_memory(grid, info, picks, keys, values):
    heads, topk = picks.shape
    per = heads // 2
    at = lambda h, info: info[2] * per + h
    piece = pl.BlockSpec((grid.T, HEAD_DIM), lambda h, info: (0, at(h, info)))
    return pl.pallas_call(
        functools.partial(pick_body, grid),
        grid_spec=pltpu.PrefetchScalarGridSpec(
            num_scalar_prefetch=1,
            grid=(per,),
            in_specs=[pl.BlockSpec((1, topk, 1), lambda h, info: (at(h, info), 0, 0))]
            + [piece] * (2 * grid.U),
            out_specs=pl.BlockSpec((2, topk, HEAD_DIM), lambda h, info: (0, 0, h)),
        ),
        out_shape=jax.ShapeDtypeStruct((2, topk, per * HEAD_DIM), BF),
        compiler_params=params(),
        cost_estimate=pl.CostEstimate(
            flops=4 * topk * SEG * HEAD_DIM * per, bytes_accessed=4 * SEG * HEAD_DIM * per, transcendentals=0
        ),
    )(info, picks[:, :, None], *keys, *values)


def finish_body(grid, memory, heads, info_ref, *refs):
    U, R = grid.U, grid.R
    dk_refs, dv_refs = refs[:U], refs[U : 2 * U]
    refs = refs[2 * U :]
    key = sum(r[...].astype(F32) for r in dk_refs)
    value = sum(r[...].astype(F32) for r in dv_refs)
    key_ref, value_ref = refs[-2:]
    if not memory:
        key_ref[...] = key.astype(BF)
        value_ref[...] = value.astype(BF)
        return
    picks = refs[0][0]
    step = pl.program_id(0)
    back = head_halves(refs[1], refs[2], step, heads // 2)
    for side in range(2):
        down = lax.broadcasted_iota(jnp.int32, (R, picks.shape[1]), 0)
        chosen = (down + piece_start(grid, info_ref[0], side) == picks).astype(BF)
        rows = slice(side * R, (side + 1) * R)
        key_ref[rows, :] = (key[rows] + dot(chosen, back[0], (1, 0))).astype(BF)
        value_ref[rows, :] = (value[rows] + dot(chosen, back[1], (1, 0))).astype(BF)


def finish_keys(grid, info, grad_keys, grad_values, picks, halves):
    rows, width = grad_keys[0].shape
    heads = width // HEAD_DIM
    memory = halves is not None
    per = heads // 2
    piece, _, _ = head_specs(grid, heads, 8)
    operands, specs = [*grad_keys, *grad_values], [piece] * (2 * grid.U)
    if memory:
        topk = picks.shape[1]
        operands += [picks[:, None, :], *halves]
        specs += [
            pl.BlockSpec((1, 1, topk), lambda h, info: (lax.rem(info[2] + h // per, 2) * per + h % per, 0, 0)),
            pl.BlockSpec((2, topk, HEAD_DIM), lambda h, info: (0, 0, jnp.minimum(h, per - 1))),
            pl.BlockSpec((2, topk, HEAD_DIM), lambda h, info: (0, 0, jnp.maximum(h - per, 0))),
        ]
    return pl.pallas_call(
        functools.partial(finish_body, grid, memory, heads),
        grid_spec=pltpu.PrefetchScalarGridSpec(
            num_scalar_prefetch=1, grid=(heads,), in_specs=specs, out_specs=[piece, piece]
        ),
        out_shape=[jax.ShapeDtypeStruct((rows, width), BF)] * 2,
        compiler_params=params(),
        cost_estimate=pl.CostEstimate(
            flops=2 * rows * width, bytes_accessed=16 * rows * width, transcendentals=0
        ),
    )(info, *operands)


def norm(value, gain):
    return value * lax.rsqrt(jnp.mean(value * value, axis=-1, keepdims=True) + EPSILON) * gain


def norm_back(value, gain, grad):
    inverse = lax.rsqrt(jnp.mean(value * value, axis=-1, keepdims=True) + EPSILON)
    unit = value * inverse
    grad_gain = jnp.sum(grad * unit, axis=0)
    scaled = grad * gain
    pulled = inverse * (scaled - unit * jnp.mean(scaled * unit, axis=-1, keepdims=True))
    return pulled, grad_gain


def mm(left, right, contract=(1, 0)):
    return dot(left, right, contract)


def local(
    n_dp,
    pieces,
    tokens,
    cotangent,
    doc_lengths,
    partner,
    memory_picks,
    attention_in,
    attention_out,
    feed_in,
    feed_out,
    norm_gains,
):
    grid = Grid(n_dp, pieces)
    grid.trace()
    layers = attention_in.shape[0]
    width = tokens.shape[2]
    heads = width // HEAD_DIM
    topk = memory_picks.shape[3]
    valid_all, visible_all = jax.vmap(memory_plan)(doc_lengths, partner)
    valid = valid_all[grid.m, grid.slot]
    visible = visible_all[grid.m, grid.slot]
    relative = (grid.slot - jnp.arange(n_dp)) % n_dp
    bias = jnp.repeat(jnp.where(visible[relative], 0.0, MASKED), topk)[:, None].astype(F32)
    info = jnp.stack([grid.k, valid, grid.c]).astype(jnp.int32)
    tables = rope_tables()

    hidden = grid.to_units(tokens).astype(F32)
    gains = gather_gains(grid, norm_gains).astype(F32)
    picks_there = grid.swap(memory_picks)
    picks = jnp.where(
        grid.r == grid.c, memory_picks[grid.m, 0], picks_there[grid.m, 0]
    )

    weights = []
    for l in range(layers):
        weights.append(
            [gather_weight(grid, w[l]) for w in (attention_in, attention_out, feed_in, feed_out)]
        )
    grad_stream = grid.to_units(cotangent).astype(F32)

    def exchange(value):
        return [value] + [grid.member(value, t) for t in range(1, grid.U)]

    saved = []
    for l in range(layers):
        w_qkv, w_out, w_up, w_down = weights[l]
        memory = l == layers - 1
        normed = norm(hidden, gains[l, 0]).astype(BF)
        projected = mm(normed, w_qkv)
        split = split_heads(grid, memory, info, tables, projected)
        query = split[0]
        keys, values = exchange(split[1]), exchange(split[2])
        extra = None
        if memory:
            raw_keys = exchange(split[4])
            chosen = pick_memory(grid, info, picks, raw_keys, values)
            slots = [chosen] + [grid.slots(chosen, t) for t in range(1, n_dp)]
            half = [jnp.concatenate([s[i] for s in slots]) for i in range(2)]
            there = [grid.swap(h) for h in half]
            extra = {
                "topk": topk,
                "query": split[3],
                "keys": (half[0], there[0]),
                "values": (half[1], there[1]),
                "bias": bias,
            }
        attended = attend(grid, info, query, keys, values, extra)
        middle = hidden + mm(attended, w_out)
        normed_feed = norm(middle, gains[l, 1]).astype(BF)
        gate_up = mm(normed_feed, w_up)
        gate, up = jnp.split(gate_up, 2, axis=1)
        inner = (jax.nn.silu(gate) * up).astype(BF)
        saved.append((hidden, middle, normed, normed_feed, gate_up, inner, query, keys, values, extra, attended))
        hidden = middle + mm(inner, w_down)
    layer_output = grid.from_units(hidden.astype(BF))

    def gradient(left, right):
        half = right.shape[1] // 2
        mine = lax.dynamic_slice_in_dim(right, grid.c * half, half, axis=1)
        give = lax.dynamic_slice_in_dim(right, (1 - grid.c) * half, half, axis=1)
        left = jnp.concatenate([left, grid.swap(left)])
        right = jnp.concatenate([mine, grid.swap(give)])
        return scatter_gradient(grid, mm(left, right, (0, 0)).astype(BF))

    grads = [None] * layers
    grad_gains = [None] * layers
    for l in reversed(range(layers)):
        w_qkv, w_out, w_up, w_down = weights[l]
        hidden, middle, normed, normed_feed, gate_up, inner, query, keys, values, extra, attended = saved[l]
        grad_low = grad_stream.astype(BF)
        grad_inner = mm(grad_low, w_down, (1, 1))
        grad_w_down = gradient(inner, grad_low)
        gate, up = jnp.split(gate_up, 2, axis=1)
        sigmoid = jax.nn.sigmoid(gate)
        grad_gate = grad_inner * up * sigmoid * (1.0 + gate * (1.0 - sigmoid))
        grad_up = grad_inner * gate * sigmoid
        grad_gate_up = jnp.concatenate([grad_gate, grad_up], axis=1).astype(BF)
        grad_w_up = gradient(normed_feed, grad_gate_up)
        pulled, gain_feed = norm_back(middle, gains[l, 1], mm(grad_gate_up, w_up, (1, 1)))
        grad_middle = grad_stream + pulled
        grad_attended = grad_middle.astype(BF)
        grad_w_out = gradient(attended, grad_attended)
        grad_heads = mm(grad_attended, w_out, (1, 1)).astype(BF)
        grad_query, grad_keys, grad_values, memory_grads = attend_back(
            grid, info, tables, query, grad_heads, keys, values, extra
        )
        grad_keys = [grad_keys[0]] + [
            grid.member(grad_keys[t], grid.U - t) for t in range(1, grid.U)
        ]
        grad_values = [grad_values[0]] + [
            grid.member(grad_values[t], grid.U - t) for t in range(1, grid.U)
        ]
        halves = None
        if extra is not None:
            own = [memory_grads[0], memory_grads[1]]
            there = [grid.swap(memory_grads[2]), grid.swap(memory_grads[3])]
            joined = jnp.stack([a.astype(F32) + b.astype(F32) for a, b in zip(own, there)])
            joined = joined.astype(BF).reshape(2, n_dp, topk, -1)
            total = joined[:, 0].astype(F32)
            for t in range(1, n_dp):
                total = total + grid.slots(joined[:, t], n_dp - t).astype(F32)
            low = total.astype(BF)
            for t in range(1, grid.Q):
                total = total + grid.within(low, t).astype(F32)
            total = total.astype(BF)
            halves = (total, grid.swap(total))
        grad_key, grad_value = finish_keys(grid, info, grad_keys, grad_values, picks, halves)
        grad_projected = jnp.concatenate([grad_query, grad_key, grad_value], axis=1)
        grad_w_qkv = gradient(normed, grad_projected)
        pulled, gain_attention = norm_back(hidden, gains[l, 0], mm(grad_projected, w_qkv, (1, 1)))
        grad_stream = grad_middle + pulled
        grads[l] = (grad_w_qkv, grad_w_out, grad_w_up, grad_w_down)
        grad_gains[l] = jnp.stack([gain_attention, gain_feed])
    input_grad = grid.from_units(grad_stream.astype(BF)).astype(F32)
    return (
        layer_output,
        input_grad,
        *(jnp.stack([grads[l][i] for l in range(layers)]) for i in range(4)),
        scatter_gains(grid, jnp.stack(grad_gains)),
    )


def solution(mesh):
    rows = P(None, ("dp", "fsdp"), None)
    in_specs = (rows, rows, P(), P(), P(None, "dp", None, None), rows, rows, rows, rows, P(None, None, ("dp", "fsdp")))
    out_specs = (rows, rows, rows, rows, rows, rows, P(None, None, ("dp", "fsdp")))
    body = functools.partial(local, mesh.shape["dp"], mesh.shape["fsdp"])
    return jax.shard_map(body, mesh=mesh, in_specs=in_specs, out_specs=out_specs, check_vma=False)
```

time: 4850 us -> 1240 us (0.26)
  waiting for transfers between devices: 3510 us -> 497 us
  other arithmetic: 359 us -> 56.4 us
  matrix products: 433 us -> 162 us
  local copies, waits for them, and re-layouts: 347 us -> 93.9 us
  starting transfers between devices: 1.05 us -> 217 us
  Pallas kernels: 0 us -> 194 us
  blocking collectives: 146 us -> 0 us
    reduce_scatter x12 -> x0, waiting for transfers between devices: 2330 us -> none  [the longest x2 987 us: local(): lax.psum_scatter(grad_sums[2], ('dp', 'fsdp'), scatter_dimension=0, tiled...]
    all_gather x14 -> x0, waiting for transfers between devices: 822 us -> none  [the longest x4 364 us: forward_advance(): segment = lax.all_gather(packed, 'fsdp', axis=0, tiled=True)]
    ppermute x0 -> x210, waiting for transfers between devices: none -> 497 us  [permute(): return lax.ppermute(value, ('dp', 'fsdp'), pairs)]
    dot_general x90 -> x24, matrix products: 433 us -> 162 us  [dot(): lax.dot_general(left, right, (((contract[0],), (contract[1],)), ((), ()))...]
    unnamed x20 -> x0, waiting for transfers between devices: 269 us -> none
    ppermute x0 -> x210, starting transfers between devices: none -> 217 us  [permute(): return lax.ppermute(value, ('dp', 'fsdp'), pairs)]
    while x30 -> x0, other arithmetic: 195 us -> none
    pallas_call x0 -> x17, Pallas kernels: none -> 194 us  [the longest x8 65.4 us: assemble(): pl.pallas_call(functools.partial(assemble_body, count), grid_spec=pltpu.P...]
  transfers between devices with their start and end apart: 30 -> 210, of which waited for: 28 -> 83; matrix products, arithmetic and copies ran while one was open for 5% -> 18% of each run, Pallas kernels for 0% -> 14%
where the time goes in v1:
time: 1240 us; the launch traced here: 1220 us
  waiting for transfers between devices  497 us (40%)
  starting transfers between devices  217 us (18%)
  Pallas kernels  194 us (16%)
  matrix products  162 us (13%)
  local copies, waits for them, and re-layouts  93.9 us (8%)
  other arithmetic  56.4 us (5%)
    ppermute x210, waiting for transfers between devices, permute(): return lax.ppermute(value, ('dp', 'fsdp'), pairs)  497 us
    ppermute x210, starting transfers between devices, permute(): return lax.ppermute(value, ('dp', 'fsdp'), pairs)  217 us
    dot_general x24, matrix products, dot(): lax.dot_general(left, right, (((contract[0],), (contract[1],)), ((), ()))...  162 us
    pallas_call x8, Pallas kernels, assemble(): pl.pallas_call(functools.partial(assemble_body, count), grid_spec=pltpu.P...  65.4 us
    pallas_call x2, Pallas kernels, attend_back(): pl.pallas_call(functools.partial(attend_back_body, grid, memory, heads),...  60.6 us
    unnamed x429, local copies, waits for them, and re-layouts  58.6 us
    pallas_call x2, Pallas kernels, attend(): pl.pallas_call(functools.partial(attend_body, grid, memory, heads), grid_...  37.6 us
  transfers between devices with their start and end apart: 210, of which 83 were waited for; matrix products, arithmetic and copies ran while one was open for 18% of the time, Pallas kernels for 14%

profile of v1, /device:TPU:0, one launch (start us, length us, event | category | flops | bytes accessed | tf_op | source)
XLA Modules:
  0.0 1224.8 jit_solution(13734329338288862687)
XLA Ops:
  159.7 11.5 collective-permute-done.92
  193.1 12.9 %collective-permute-done.35 = bf16[2,32,2816]{2,1,0:T(8,128)(2,1)S(1)} collective-permute-done((bf16[2,32,2816]{2,1,0:T(8,128)(2,1)S(1)}, bf16[2,32,2816]{2,1,0:T(8,128)(2,1)S(1)}, u32[]{:S(2)}, u32[]{:S(2)}) %collective-permute-start.35) | collective-permute-done | bytes 360480 | tf_op jit(solution)/shard_map/ppermute | solution.py:70
  229.1 11.0 collective-permute-start.51
  249.0 13.1 %collective-permute-done.59.refs_1_ = bf16[256,1536]{1,0:T(8,128)(2,1)S(1)} collective-permute-done((bf16[256,1536]{1,0:T(8,128)(2,1)S(1)}, bf16[256,1536]{1,0:T(8,128)(2,1)S(1)}, u32[]{:S(2)}, u32[]{:S(2)}) %collective-permute-start.59) | collective-permute-done | bytes 786464 | tf_op jit(solution)/shard_map/ppermute | solution.py:70
  262.1 17.0 %collective-permute-done.13.refs_1_ = bf16[256,1536]{1,0:T(8,128)(2,1)} collective-permute-done((bf16[256,1536]{1,0:T(8,128)(2,1)}, bf16[256,1536]{1,0:T(8,128)(2,1)}, u32[]{:S(2)}, u32[]{:S(2)}) %collective-permute-start.13) | collective-permute-done | bytes 786464 | tf_op jit(solution)/shard_map/ppermute | solution.py:70
  304.2 12.5 %shard_map.153 = bf16[1024,3072]{1,0:T(8,128)(2,1)} custom-call(s32[10]{0:T(128)S(1)} %stack.481.place_ref, bf16[256,1536]{1,0:T(8,128)(2,1)} %bitcast.33.refs_0_, bf16[256,1536]{1,0:T(8,128)(2,1)} %collective-permute-done.13.refs_1_, bf16[256,1536]{1,0:T(8,128)(2,1)} %collective-permute-done.14.refs_2_, bf16[256,1536]{1,0:T(8,128)(2,1)} %collective-permute-done.15.refs_3_, ...), custom_call_target="tpu_custom_call" | custom-call | bytes 12582912 | tf_op jit(solution)/shard_map/pallas_call | solution.py:165
  389.8 13.4 %shard_map.155 = bf16[512,1024]{1,0:T(8,128)(2,1)S(1)} custom-call(s32[3]{0:T(128)S(1)} %pad_add_fusion.info_ref, bf16[512,1024]{1,0:T(8,128)(2,1)S(1)} %copy-done.11, bf16[512,1024]{1,0:T(8,128)(2,1)S(1)} %copy-done.14, bf16[512,1024]{1,0:T(8,128)(2,1)S(1)} %copy-done.16, bf16[512,1024]{1,0:T(8,128)(2,1)} %get-tuple-element.35.refs_3_.refs_6_, ...), custom_call_target="tpu_custom_call" | custom-call | flops 1610612736 | bytes 8388608 | tf_op jit(solution)/shard_map/pallas_call | solution.py:428
  412.0 12.8 %shard_map.157 = bf16[1024,5632]{1,0:T(8,128)(2,1)} custom-call(s32[10]{0:T(128)S(1)} %stack.481.place_ref, bf16[256,2816]{1,0:T(8,128)(2,1)S(1)} %bitcast.637, bf16[256,2816]{1,0:T(8,128)(2,1)} %collective-permute-done.37.refs_1_, bf16[256,2816]{1,0:T(8,128)(2,1)S(1)} %collective-permute-done.38.refs_2_, ...), custom_call_target="tpu_custom_call" | custom-call | bytes 23068672 | tf_op jit(solution)/shard_map/pallas_call | solution.py:165
  477.2 14.0 %collective-permute-done.94.refs_1_ = bf16[256,2816]{1,0:T(8,128)(2,1)} collective-permute-done((bf16[256,2816]{1,0:T(8,128)(2,1)S(1)}, bf16[256,2816]{1,0:T(8,128)(2,1)}, u32[]{:S(2)}, u32[]{:S(2)}) %collective-permute-start.94) | collective-permute-done | bytes 1441824 | tf_op jit(solution)/shard_map/ppermute | solution.py:70
  575.9 15.2 %shard_map.164 = bf16[1024,5632]{1,0:T(8,128)(2,1)} custom-call(s32[10]{0:T(128)S(1)} %stack.481.place_ref, bf16[256,2816]{1,0:T(8,128)(2,1)S(1)} %bitcast.633, bf16[256,2816]{1,0:T(8,128)(2,1)} %collective-permute-done.94.refs_1_, bf16[256,2816]{1,0:T(8,128)(2,1)} %collective-permute-done.95.refs_2_, bf16[256,2816]{1,0:T(8,128)(2,1)} %collective-permute-done.96.refs_3_, ...), custom_call_target="tpu_custom_call" | custom-call | bytes 23068672 | tf_op jit(solution)/shard_map/pallas_call | solution.py:165
  591.2 24.2 %shard_map.162 = bf16[512,1024]{1,0:T(8,128)(2,1)} custom-call(s32[3]{0:T(128)S(1)} %pad_add_fusion.info_ref, bf16[512,1024]{1,0:T(8,128)(2,1)S(1)} %copy-done.93, bf16[512,1024]{1,0:T(8,128)(2,1)} %get-tuple-element.37.refs_1_.refs_4_, bf16[512,1024]{1,0:T(8,128)(2,1)} %collective-permute-done.66.refs_2_.refs_5_, bf16[512,1024]{1,0:T(8,128)(2,1)S(1)} %copy-done.21, ...), custom_call_target="tpu_custom_call" | custom-call | flops 3758096384 | bytes 16777216 | tf_op jit(solution)/shard_map/pallas_call | solution.py:428
  618.3 14.3 %fusion.201 = f32[512,5632]{1,0:T(8,128)} fusion(bf16[512,1024]{1,0:T(8,128)(2,1)S(1)} %multiply_convert_fusion.6, bf16[1024,5632]{1,0:T(8,128)(2,1)} %shard_map.164), kind=kOutput, calls=%fused_computation.597 | convolution fusion | flops 5905580032 | bytes 24117248 | tf_op jit(solution)/shard_map/dot_general | solution.py:337
  632.7 10.8 multiply_convert_fusion.3
  643.5 12.9 %multiply_reduce_fusion = (f32[1024]{0:T(1024)S(1)}, f32[512]{0:T(512)S(1)}, f32[512,1024]{1,0:T(8,128)}) fusion(f32[512,1024]{1,0:T(8,128)S(1)} %get-tuple-element.235, f32[512]{0:T(512)S(1)} %add_rsqrt_fusion, f32[1024]{0:T(1024)S(1)} %bitcast.713, bf16[1024,5632]{1,0:T(8,128)(2,1)} %shard_map.164, bf16[512,2816]{1,0:T(8,128)(2,1)} %get-tuple-element.80, ...), kind=kOutput, calls=%fused_computation.113 | convolution fusion | flops 5920258560 | bytes 21508096 | tf_op jit(solution)/shard_map/dot_general | solution.py:337
  662.1 38.9 %shard_map.166 = (bf16[512,1024]{1,0:T(8,128)(2,1)S(1)}, f32[512,1024]{1,0:T(8,128)}, bf16[512,1024]{1,0:T(8,128)(2,1)S(1)}, f32[512,1024]{1,0:T(8,128)}, bf16[5...) custom-call(s32[3]{0:T(128)S(1)} %pad_add_fusion.info_ref, ...), custom_call_target="tpu_custom_call" | custom-call | flops 9395240960 | bytes 16777216 | tf_op jit(solution)/shard_map/pallas_call | solution.py:536
  727.2 11.4 collective-permute-done.113
  751.0 13.9 %collective-permute-start.126 = (bf16[2,128,512]{2,1,0:T(8,128)(2,1)S(1)}, bf16[2,128,512]{2,1,0:T(8,128)(2,1)S(1)}, u32[]{:S(2)}, u32[]{:S(2)}) collective-permute-start(bf16[2,128,512]{2,1,0:T(8,128)(2,1)S(1)} %get-tuple-element.107), channel_id=1, source_target_pairs={{0,1},{1,8},{2,3},{3,10},{4,5},{5,12},{6,7},{7,14},{8,9},{9,16},{1... | collective-permute-start | bytes 786440 | tf_op jit(solution)/shard_map/ppermute | solution.py:70
  804.6 12.7 %multiply_reduce_fusion.2 = (f32[1024]{0:T(1024)S(1)}, f32[512]{0:T(512)S(1)}, f32[512,1024]{1,0:T(8,128)}) fusion(f32[512,1024]{1,0:T(8,128)S(1)} %copy-done.106, f32[512]{0:T(512)S(1)} %copy-done.175, f32[1024]{0:T(1024)S(1)} %bitcast.719, bf16[1024,5632]{1,0:T(8,128)(2,1)} %shard_map.157, bf16[512,2816]{1,0:T(8,128)(2,1)} %get-tuple-element.78, ...), kind=kOutput, calls=%fused_computation.115 | convolution fusion | flops 5920258560 | bytes 21508096 | tf_op jit(solution)/shard_map/dot_general | solution.py:337
  833.7 21.6 %shard_map.168 = (bf16[512,1024]{1,0:T(8,128)(2,1)S(1)}, f32[512,1024]{1,0:T(8,128)}, bf16[512,1024]{1,0:T(8,128)(2,1)S(1)}, f32[512,1024]{1,0:T(8,128)}, bf16[512,1024]{1,0:T(8,128)(2,1)S(1)}) custom-call(s32[3]{0:T(128)S(1)} %pad_add_fusion.info_ref, f32[1024,128]{1,0:T(8,128)S(1)} %get-tuple-element.240.cos_ref.refs_0_, f32[1024,128]{1,0:T(8,128)S(1)} %copy-done.1, ...), custom_call_target="tpu_custom_call" | custom-call | flops 4026531840 | bytes 8388608 | tf_op jit(solution)/shard_map/pallas_call | solution.py:536
  974.2 11.1 collective-permute-done.131
  1020.1 13.7 %collective-permute-done.197 = bf16[704,512]{1,0:T(8,128)(2,1)S(1)} collective-permute-done((bf16[704,512]{1,0:T(8,128)(2,1)}, bf16[704,512]{1,0:T(8,128)(2,1)S(1)}, u32[]{:S(2)}, u32[]{:S(2)}) %collective-permute-start.197) | collective-permute-done | bytes 720928 | tf_op jit(solution)/shard_map/ppermute | solution.py:70
  1103.2 36.8 %collective-permute-done.136 = bf16[256,1536]{1,0:T(8,128)(2,1)S(1)} collective-permute-done((bf16[256,1536]{1,0:T(8,128)(2,1)S(1)}, bf16[256,1536]{1,0:T(8,128)(2,1)S(1)}, u32[]{:S(2)}, u32[]{:S(2)}) %collective-permute-start.136) | collective-permute-done | bytes 786464 | tf_op jit(solution)/shard_map/ppermute | solution.py:70
  1172.0 11.4 collective-permute-done.183
  1207.4 14.0 %collective-permute-done.174 = bf16[2,32,2816]{2,1,0:T(8,128)(2,1)S(1)} collective-permute-done((bf16[2,32,2816]{2,1,0:T(8,128)(2,1)S(1)}, bf16[2,32,2816]{2,1,0:T(8,128)(2,1)S(1)}, u32[]{:S(2)}, u32[]{:S(2)}) %collective-permute-start.174) | collective-permute-done | bytes 360480 | tf_op jit(solution)/shard_map/ppermute | solution.py:70
  (1096 shorter events, 839.3 us)
Async XLA Ops:
  19.2 49.3 %collective-permute-start.90 = (bf16[32,2816]{1,0:T(8,128)(2,1)}, bf16[32,2816]{1,0:T(8,128)(2,1)}, u32[]{:S(2)}, u32[]{:S(2)}) collective-permute-start(bf16[32,2816]{1,0:T(8,128)(2,1)} %dynamic-slice_bitcast_fusion.42), channel_id=1, source_target_pairs={{0,4},{1,5},{2,6},{3,7},{4,0},{5,1},{6,2},{7,3},{8,12},{9,13},{10,... | collective-permute-start | bytes 540680 | tf_op jit(solution)/shard_map/ppermute | solution.py:70
  19.3 51.0 %collective-permute-start.33 = (bf16[32,2816]{1,0:T(8,128)(2,1)}, bf16[32,2816]{1,0:T(8,128)(2,1)S(1)}, u32[]{:S(2)}, u32[]{:S(2)}) collective-permute-start(bf16[32,2816]{1,0:T(8,128)(2,1)} %dynamic-slice_bitcast_fusion.43), channel_id=1, source_target_pairs={{0,4},{1,5},{2,6},{3,7},{4,0},{5,1},{6,2},{7,3},{8,12},{9,13},{10,... | collective-permute-start | bytes 540680 | tf_op jit(solution)/shard_map/ppermute | solution.py:70
  60.0 153.4 %collective-permute-start = (bf16[256,1024]{1,0:T(8,128)(2,1)}, bf16[256,1024]{1,0:T(8,128)(2,1)S(1)}, u32[]{:S(2)}, u32[]{:S(2)}) collective-permute-start(bf16[256,1024]{1,0:T(8,128)(2,1)} %get-tuple-element.141), channel_id=1, source_target_pairs={{0,0},{1,4},{2,6},{3,2},{4,1},{5,5},{6,7},{7,3},{8,8},{9,12},{10,1... | collective-permute-start | bytes 1572872 | tf_op jit(solution)/shard_map/ppermute | solution.py:70
  66.3 125.9 %collective-permute-start.7 = (bf16[2,4,2,2,32]{4,3,2,1,0:T(2,128)(2,1)S(1)}, bf16[2,4,2,2,32]{4,3,2,1,0:T(2,128)(2,1)S(1)}, u32[]{:S(2)}, u32[]{:S(2)}) collective-permute-start(bf16[2,4,2,2,32]{4,3,2,1,0:T(2,128)(2,1)S(1)} %pad_maximum_fusion.25), channel_id=1, source_target_pairs={{0,16},{1,17},{2,18},{3,19},{4,12},{5,13},{6,14},{7,15},{8,24},{9,... | collective-permute-start | bytes 6152 | tf_op jit(solution)/shard_map/ppermute | solution.py:70
  67.8 125.3 %collective-permute-start.8 = (bf16[2,4,2,2,32]{4,3,2,1,0:T(2,128)(2,1)S(1)}, bf16[2,4,2,2,32]{4,3,2,1,0:T(2,128)(2,1)S(1)}, u32[]{:S(2)}, u32[]{:S(2)}) collective-permute-start(bf16[2,4,2,2,32]{4,3,2,1,0:T(2,128)(2,1)S(1)} %collective-permute-done.6), channel_id=1, source_target_pairs={{0,16},{1,17},{2,18},{3,19},{4,12},{5,13},{6,14},{7,15},{8,24},{9,... | collective-permute-start | bytes 6152 | tf_op jit(solution)/shard_map/ppermute | solution.py:70
  99.4 107.0 %collective-permute-start.26 = (bf16[256,512]{1,0:T(8,128)(2,1)S(1)}, bf16[256,512]{1,0:T(8,128)(2,1)S(1)}, u32[]{:S(2)}, u32[]{:S(2)}) collective-permute-start(bf16[256,512]{1,0:T(8,128)(2,1)S(1)} %bitcast.650), channel_id=1, source_target_pairs={{0,8},{1,9},{2,10},{3,11},{4,20},{5,21},{6,22},{7,23},{8,0},{9,1},... | collective-permute-start | bytes 786440 | tf_op jit(solution)/shard_map/ppermute | solution.py:70
  345.5 59.5 %collective-permute-start.40 = (bf16[256,2816]{1,0:T(8,128)(2,1)S(1)}, bf16[256,2816]{1,0:T(8,128)(2,1)}, u32[]{:S(2)}, u32[]{:S(2)}) collective-permute-start(bf16[256,2816]{1,0:T(8,128)(2,1)S(1)} %bitcast.636), channel_id=1, source_target_pairs={{0,4},{1,5},{2,6},{3,7},{4,0},{5,1},{6,2},{7,3},{8,12},{9,13},{10,... | collective-permute-start | bytes 4325384 | tf_op jit(solution)/shard_map/ppermute | solution.py:70
  345.6 61.1 %collective-permute-start.41 = (bf16[256,2816]{1,0:T(8,128)(2,1)}, bf16[256,2816]{1,0:T(8,128)(2,1)}, u32[]{:S(2)}, u32[]{:S(2)}) collective-permute-start(bf16[256,2816]{1,0:T(8,128)(2,1)} %collective-permute-done.37.refs_1_), channel_id=1, source_target_pairs={{0,4},{1,5},{2,6},{3,7},{4,0},{5,1},{6,2},{7,3},{8,12},{9,13},{10,... | collective-permute-start | bytes 4325384 | tf_op jit(solution)/shard_map/ppermute | solution.py:70
  354.6 54.1 %collective-permute-start.42 = (bf16[256,2816]{1,0:T(8,128)(2,1)S(1)}, bf16[256,2816]{1,0:T(8,128)(2,1)}, u32[]{:S(2)}, u32[]{:S(2)}) collective-permute-start(bf16[256,2816]{1,0:T(8,128)(2,1)S(1)} %collective-permute-done.38.refs_2_), channel_id=1, source_target_pairs={{0,4},{1,5},{2,6},{3,7},{4,0},{5,1},{6,2},{7,3},{8,12},{9,13},{10,... | collective-permute-start | bytes 4325384 | tf_op jit(solution)/shard_map/ppermute | solution.py:70
  354.6 55.8 %collective-permute-start.43 = (bf16[256,2816]{1,0:T(8,128)(2,1)S(1)}, bf16[256,2816]{1,0:T(8,128)(2,1)}, u32[]{:S(2)}, u32[]{:S(2)}) collective-permute-start(bf16[256,2816]{1,0:T(8,128)(2,1)S(1)} %collective-permute-done.39.refs_3_), channel_id=1, source_target_pairs={{0,4},{1,5},{2,6},{3,7},{4,0},{5,1},{6,2},{7,3},{8,12},{9,13},{10,... | collective-permute-start | bytes 4325384 | tf_op jit(solution)/shard_map/ppermute | solution.py:70
  385.7 60.7 %collective-permute-start.68 = (s32[2,1,8,128]{3,2,1,0:T(8,128)S(1)}, s32[2,1,8,128]{3,2,1,0:T(8,128)S(1)}, u32[]{:S(2)}, u32[]{:S(2)}) collective-permute-start(s32[2,1,8,128]{3,2,1,0:T(8,128)S(1)} %copy-done.178), channel_id=1, source_target_pairs={{0,4},{1,5},{2,6},{3,7},{4,0},{5,1},{6,2},{7,3},{8,12},{9,13},{10,... | collective-permute-start | bytes 24584 | tf_op jit(solution)/shard_map/ppermute | solution.py:70
  662.0 78.2 %collective-permute-start.159 = (bf16[512,1024]{1,0:T(8,128)(2,1)}, bf16[512,1024]{1,0:T(8,128)(2,1)}, u32[]{:S(2)}, u32[]{:S(2)}) collective-permute-start(bf16[512,1024]{1,0:T(8,128)(2,1)} %shard_map.162), channel_id=1, source_target_pairs={{0,4},{1,5},{2,6},{3,7},{4,0},{5,1},{6,2},{7,3},{8,12},{9,13},{10,... | collective-permute-start | bytes 3145736 | tf_op jit(solution)/shard_map/ppermute | solution.py:70
  725.8 48.6 %collective-permute-start.116 = (bf16[512,1024]{1,0:T(8,128)(2,1)S(1)}, bf16[512,1024]{1,0:T(8,128)(2,1)S(1)}, u32[]{:S(2)}, u32[]{:S(2)}) collective-permute-start(bf16[512,1024]{1,0:T(8,128)(2,1)S(1)} %get-tuple-element.43), channel_id=1, source_target_pairs={{0,4},{1,5},{2,6},{3,7},{4,0},{5,1},{6,2},{7,3},{8,12},{9,13},{10,... | collective-permute-start | bytes 3145736 | tf_op jit(solution)/shard_map/ppermute | solution.py:70
  726.2 48.3 %collective-permute-start.117 = (bf16[512,1024]{1,0:T(8,128)(2,1)S(1)}, bf16[512,1024]{1,0:T(8,128)(2,1)S(1)}, u32[]{:S(2)}, u32[]{:S(2)}) collective-permute-start(bf16[512,1024]{1,0:T(8,128)(2,1)S(1)} %get-tuple-element.45), channel_id=1, source_target_pairs={{0,4},{1,5},{2,6},{3,7},{4,0},{5,1},{6,2},{7,3},{8,12},{9,13},{10,... | collective-permute-start | bytes 3145736 | tf_op jit(solution)/shard_map/ppermute | solution.py:70
  767.9 100.2 %collective-permute-start.150 = (bf16[512,1024]{1,0:T(8,128)(2,1)S(1)}, bf16[512,1024]{1,0:T(8,128)(2,1)}, u32[]{:S(2)}, u32[]{:S(2)}) collective-permute-start(bf16[512,1024]{1,0:T(8,128)(2,1)S(1)} %copy-done.18), channel_id=1, source_target_pairs={{0,4},{1,5},{2,6},{3,7},{4,0},{5,1},{6,2},{7,3},{8,12},{9,13},{10,... | collective-permute-start | bytes 3145736 | tf_op jit(solution)/shard_map/ppermute | solution.py:70
  774.4 97.8 %collective-permute-start.186 = (bf16[512,2816]{1,0:T(8,128)(2,1)}, bf16[512,2816]{1,0:T(8,128)(2,1)}, u32[]{:S(2)}, u32[]{:S(2)}) collective-permute-start(bf16[512,2816]{1,0:T(8,128)(2,1)} %multiply_convert_fusion.5), channel_id=1, source_target_pairs={{0,4},{1,5},{2,6},{3,7},{4,0},{5,1},{6,2},{7,3},{8,12},{9,13},{10,... | collective-permute-start | bytes 8650760 | tf_op jit(solution)/shard_map/ppermute | solution.py:70
  861.9 80.8 %collective-permute-start.195 = (bf16[512,2816]{1,0:T(8,128)(2,1)}, bf16[512,2816]{1,0:T(8,128)(2,1)}, u32[]{:S(2)}, u32[]{:S(2)}) collective-permute-start(bf16[512,2816]{1,0:T(8,128)(2,1)} %get-tuple-element.81), channel_id=1, source_target_pairs={{0,4},{1,5},{2,6},{3,7},{4,0},{5,1},{6,2},{7,3},{8,12},{9,13},{10,... | collective-permute-start | bytes 8650760 | tf_op jit(solution)/shard_map/ppermute | solution.py:70
  872.1 61.6 %collective-permute-start.178 = (bf16[512,2816]{1,0:T(8,128)(2,1)}, bf16[512,2816]{1,0:T(8,128)(2,1)}, u32[]{:S(2)}, u32[]{:S(2)}) collective-permute-start(bf16[512,2816]{1,0:T(8,128)(2,1)} %get-tuple-element.89), channel_id=1, source_target_pairs={{0,4},{1,5},{2,6},{3,7},{4,0},{5,1},{6,2},{7,3},{8,12},{9,13},{10,... | collective-permute-start | bytes 8650760 | tf_op jit(solution)/shard_map/ppermute | solution.py:70
  942.7 62.6 %collective-permute-start.133 = (bf16[512,1536]{1,0:T(8,128)(2,1)S(1)}, bf16[512,1536]{1,0:T(8,128)(2,1)}, u32[]{:S(2)}, u32[]{:S(2)}) collective-permute-start(bf16[512,1536]{1,0:T(8,128)(2,1)S(1)} %copy-done.125), channel_id=1, source_target_pairs={{0,4},{1,5},{2,6},{3,7},{4,0},{5,1},{6,2},{7,3},{8,12},{9,13},{10,... | collective-permute-start | bytes 4718600 | tf_op jit(solution)/shard_map/ppermute | solution.py:70
  989.2 53.2 %collective-permute-start.169 = (bf16[512,2816]{1,0:T(8,128)(2,1)S(1)}, bf16[512,2816]{1,0:T(8,128)(2,1)}, u32[]{:S(2)}, u32[]{:S(2)}) collective-permute-start(bf16[512,2816]{1,0:T(8,128)(2,1)S(1)} %copy-done.118), channel_id=1, source_target_pairs={{0,4},{1,5},{2,6},{3,7},{4,0},{5,1},{6,2},{7,3},{8,12},{9,13},{10,... | collective-permute-start | bytes 8650760 | tf_op jit(solution)/shard_map/ppermute | solution.py:70
  1005.2 135.6 %collective-permute-start.179 = (bf16[256,2816]{1,0:T(8,128)(2,1)}, bf16[256,2816]{1,0:T(8,128)(2,1)S(1)}, u32[]{:S(2)}, u32[]{:S(2)}) collective-permute-start(bf16[256,2816]{1,0:T(8,128)(2,1)} %get-tuple-element.86), channel_id=1, source_target_pairs={{0,8},{1,9},{2,10},{3,11},{4,20},{5,21},{6,22},{7,23},{8,0},{9,1},... | collective-permute-start | bytes 4325384 | tf_op jit(solution)/shard_map/ppermute | solution.py:70
  1088.8 56.9 %collective-permute-start.181 = (bf16[256,2816]{1,0:T(8,128)(2,1)S(1)}, bf16[256,2816]{1,0:T(8,128)(2,1)S(1)}, u32[]{:S(2)}, u32[]{:S(2)}) collective-permute-start(bf16[256,2816]{1,0:T(8,128)(2,1)S(1)} %fusion.44), channel_id=1, source_target_pairs={{0,16},{1,17},{2,18},{3,19},{4,12},{5,13},{6,14},{7,15},{8,24},{9,... | collective-permute-start | bytes 4325384 | tf_op jit(solution)/shard_map/ppermute | solution.py:70
  1089.8 78.2 %collective-permute-start.171 = (bf16[256,2816]{1,0:T(8,128)(2,1)S(1)}, bf16[256,2816]{1,0:T(8,128)(2,1)S(1)}, u32[]{:S(2)}, u32[]{:S(2)}) collective-permute-start(bf16[256,2816]{1,0:T(8,128)(2,1)S(1)} %get-tuple-element.83), channel_id=1, source_target_pairs={{0,8},{1,9},{2,10},{3,11},{4,20},{5,21},{6,22},{7,23},{8,0},{9,1},... | collective-permute-start | bytes 4325384 | tf_op jit(solution)/shard_map/ppermute | solution.py:70
  1101.4 89.2 %collective-permute-start.170 = (bf16[256,2816]{1,0:T(8,128)(2,1)S(1)}, bf16[256,2816]{1,0:T(8,128)(2,1)S(1)}, u32[]{:S(2)}, u32[]{:S(2)}) collective-permute-start(bf16[256,2816]{1,0:T(8,128)(2,1)S(1)} %get-tuple-element.82), channel_id=1, source_target_pairs={{0,8},{1,9},{2,10},{3,11},{4,20},{5,21},{6,22},{7,23},{8,0},{9,1},... | collective-permute-start | bytes 4325384 | tf_op jit(solution)/shard_map/ppermute | solution.py:70
  (376 other events, 6093.5 us)

commit v2 on v1

--- a/solution.py
+++ b/solution.py
@@ -144,124 +144,344 @@
     return pl.BlockSpec(memory_space=pl.ANY)
 
 
-def assemble_body(count, place_ref, *refs):
-    blocks, out, sem = refs[: 2 * count], refs[2 * count], refs[2 * count + 1]
-    step = pl.program_id(0)
-    for i in range(2 * count):
-
-        @pl.when(step == i)
-        def _():
-            copy = pltpu.make_async_copy(blocks[i], out, sem)
+MESH = pl.DeviceIdType.MESH
+
+
+class Here:
+    def __init__(self, grid):
+        self.grid = grid
+        dp = lax.axis_index("dp")
+        self.j, self.c, self.f = dp // 2, dp % 2, lax.axis_index("fsdp")
+        self.q, self.g = self.f // grid.Q, self.f % grid.Q
+        self.m, self.r = self.q // 2, self.q % 2
+        self.k = self.c * grid.Q + self.g
+        self.swap = self.device(self.j, 1 - self.c, self.f)
+
+    def device(self, j, c, f):
+        return {"dp": 2 * j + c, "fsdp": f}
+
+    def ring(self, t):
+        return self.device(self.j, self.c, (self.f + t) % self.grid.F)
+
+    def step(self, phase):
+        first, second = (1 << self.grid.bit(phase, c) for c in (0, 1))
+        return first + self.c * (second - first)
+
+    def moved(self, j, phase):
+        step = self.step(phase)
+        return j + step * (1 - 2 * ((j // step) % 2))
+
+    def flip(self, phase):
+        return self.device(self.moved(self.j, phase), self.c, self.f)
+
+    def place(self, key):
+        j = self.j
+        for phase in range(self.grid.bits):
+            if key >> phase & 1:
+                j = self.moved(j, phase)
+        return j
+
+    def greet(self):
+        grid = self.grid
+        barrier = pltpu.get_barrier_semaphore()
+        peers = [self.ring(t) for t in range(1, grid.F)]
+        peers += [self.device(self.j, 1 - self.c, (self.f + t) % grid.F) for t in range(grid.F)]
+        for bit in range(grid.bits):
+            step = 1 << bit
+            peers.append(self.device(self.j + step * (1 - 2 * ((self.j // step) % 2)), self.c, self.f))
+        for peer in peers:
+            pl.semaphore_signal(barrier, inc=1, device_id=peer, device_id_type=MESH)
+        pl.semaphore_wait(barrier, len(peers))
+
+
+def remote(source, target, sems, index, device):
+    return pltpu.make_async_remote_copy(
+        src_ref=source,
+        dst_ref=target,
+        send_sem=sems.at[0, index],
+        recv_sem=sems.at[1, index],
+        device_id=device,
+        device_id_type=MESH,
+    )
+
+
+class Spread:
+    def __init__(self, here, shard, whole, sems, own_sem, split):
+        grid = here.grid
+        self.here, self.split = here, split
+        rows, width = shard.shape
+        half = width // 2 if split else width
+
+        def part(ref, c):
+            if not split:
+                return ref
+            return ref.at[(slice(None),) * (len(ref.shape) - 1) + (pl.ds(pl.multiple_of(c * half, 128), half),)]
+
+        j, c, f = here.j, here.c, here.f
+        mine = part(whole, c)
+        self.own = pltpu.make_async_copy(part(shard, c), part(whole.at[j, c, f], c), own_sem)
+        other = 1 - c if split else c
+        self.pre = remote(part(shard, other), part(whole.at[j, c, f], other), sems, 0, here.swap)
+        at = 1
+        self.line = []
+        for t in range(1, grid.F):
+            block = mine.at[j, :, f]
+            self.line.append(remote(block, block, sems, at, here.ring(t)))
+            at += 1
+        self.flips = []
+        for phase in range(grid.bits):
+            sent = []
+            for key in range(1 << phase):
+                block = mine.at[here.place(key)]
+                sent.append(remote(block, block, sems, at, here.flip(phase)))
+                at += 1
+            self.flips.append(sent)
+        self.swaps = []
+        for key in range(grid.J if split else 0):
+            block = mine.at[here.place(key)]
+            self.swaps.append(remote(block, block, sems, at, here.swap))
+            at += 1
+
+    @staticmethod
+    def count(grid):
+        return 1 + (grid.F - 1) + (grid.J - 1) + grid.J
+
+    def begin(self):
+        self.own.start()
+        self.pre.start()
+
+    def to_line(self):
+        self.own.wait()
+        self.pre.wait()
+        for copy in self.line:
             copy.start()
-            copy.wait()
-
-
-def assemble(grid, own, other):
-    count, (rows, half) = len(own), own[0].shape
-    places = [grid.place(key, grid.c) for key in range(count)]
-    places += [grid.place(key, 1 - grid.c) for key in range(count)]
-    places = jnp.stack(places + [grid.c, 1 - grid.c]).astype(jnp.int32)
-    size = count * rows * 2 * half
-    return pl.pallas_call(
-        functools.partial(assemble_body, count),
-        grid_spec=pltpu.PrefetchScalarGridSpec(
-            num_scalar_prefetch=1,
-            grid=(2 * count,),
-            in_specs=[any_spec()] * (2 * count),
-            out_specs=pl.BlockSpec(
-                (rows, half), lambda i, place: (place[i], place[2 * count + i // count])
-            ),
-            scratch_shapes=[pltpu.SemaphoreType.DMA],
+
+    def _send(self, keys):
+        for key in keys:
+            if self.swaps:
+                self.swaps[key].start()
+        for phase, sent in enumerate(self.flips):
+            for key in keys:
+                if key < 1 << phase:
+                    sent[key].start()
+
+    def steps(self):
+        def first():
+            for copy in self.line:
+                copy.wait()
+            self._send([0])
+
+        def later(phase):
+            for copy in self.flips[phase]:
+                copy.wait()
+            self._send([key + (1 << phase) for key in range(1 << phase)])
+
+        def last():
+            for copy in self.swaps:
+                copy.wait()
+
+        return [first] + [functools.partial(later, p) for p in range(len(self.flips))] + [last]
+
+
+class Regroup:
+    def __init__(self, here, source, target, sems, own_sem):
+        grid = here.grid
+        half = grid.F // 2
+        k = jnp.minimum(here.f, grid.F - 1 - here.f)
+        side = here.f // half
+        self.sends = []
+        for m in range(2):
+            c2, f2 = k // grid.Q, (2 * m + here.c) * grid.Q + k % grid.Q
+            same = (c2 == here.c) & (f2 == here.f)
+            own = pltpu.make_async_copy(source.at[m], target.at[side], own_sem)
+            away = pltpu.make_async_remote_copy(
+                src_ref=source.at[m],
+                dst_ref=target.at[side],
+                send_sem=sems.at[0, m],
+                recv_sem=sems.at[1, side],
+                device_id=here.device(here.j, c2, f2),
+                device_id_type=MESH,
+            )
+            self.sends.append((same, own, away))
+        self.arrivals = []
+        for side in range(2):
+            from_f = here.k if side == 0 else grid.F - 1 - here.k
+            same = (here.r == here.c) & (from_f == here.f)
+            came = pltpu.make_async_remote_copy(
+                src_ref=source.at[0],
+                dst_ref=target.at[side],
+                send_sem=sems.at[0, 0],
+                recv_sem=sems.at[1, side],
+                device_id=here.swap,
+                device_id_type=MESH,
+            )
+            self.arrivals.append((same, came))
+
+    def start(self):
+        for same, own, away in self.sends:
+            pl.when(same)(own.start)
+            pl.when(jnp.logical_not(same))(away.start)
+
+    def wait(self):
+        for same, own, away in self.sends:
+            pl.when(same)(own.wait)
+            pl.when(jnp.logical_not(same))(away.wait_send)
+        for same, came in self.arrivals:
+            pl.when(jnp.logical_not(same))(came.wait_recv)
+
+
+def gather_body(grid, layers, kinds, *refs):
+    tokens, cotangent, gains = refs[:3]
+    shards = refs[3 : 3 + kinds]
+    outs = refs[3 + kinds :]
+    tokens_out, cotangent_out, gains_out = outs[:3]
+    wholes = outs[3 : 3 + layers * kinds]
+    sems, own_sems, regroup_sems = outs[3 + layers * kinds :]
+    here = Here(grid)
+    here.greet()
+    rows = Regroup(here, tokens, tokens_out, regroup_sems.at[0], own_sems.at[0])
+    rows_back = Regroup(here, cotangent, cotangent_out, regroup_sems.at[1], own_sems.at[1])
+    moves = [Spread(here, gains, gains_out, sems.at[0], own_sems.at[2], False)]
+    for l in range(layers):
+        for i in range(kinds):
+            n = l * kinds + i
+            moves.append(
+                Spread(here, shards[i].at[l], wholes[n], sems.at[n + 1], own_sems.at[n + 3], True)
+            )
+    for move in moves:
+        move.begin()
+    rows.start()
+    steps = [move.steps() for move in moves]
+    count = len(steps[0])
+    moves[0].to_line()
+    moves[1].to_line()
+    for at in range(len(moves) + count - 1):
+        if at + 2 < len(moves):
+            moves[at + 2].to_line()
+        if at == len(moves) - 3:
+            rows_back.start()
+        for back in range(count):
+            if 0 <= at - back < len(moves):
+                steps[at - back][back]()
+    rows.wait()
+    rows_back.wait()
+
+
+def gather_all(grid, tokens, cotangent, gains, shards):
+    layers, kinds = shards[0].shape[0], len(shards)
+    packed = jnp.zeros((8, 128), F32).at[: layers * 2, : gains.shape[2]].set(
+        gains.astype(F32).reshape(layers * 2, -1)
+    )
+    whole = lambda shard: jax.ShapeDtypeStruct((grid.J, 2, grid.F) + shard.shape[-2:], shard.dtype)
+    out_shape = [jax.ShapeDtypeStruct(tokens.shape, BF), jax.ShapeDtypeStruct(tokens.shape, BF), whole(packed)]
+    out_shape += [whole(shard) for _ in range(layers) for shard in shards]
+    moves = 1 + layers * kinds
+    outs = pl.pallas_call(
+        functools.partial(gather_body, grid, layers, kinds),
+        in_specs=[any_spec()] * (3 + kinds),
+        out_specs=[any_spec()] * len(out_shape),
+        out_shape=out_shape,
+        scratch_shapes=[
+            pltpu.SemaphoreType.DMA((moves, 2, Spread.count(grid))),
+            pltpu.SemaphoreType.DMA((moves + 2,)),
+            pltpu.SemaphoreType.DMA((2, 2, 2)),
+        ],
+        compiler_params=pltpu.CompilerParams(
+            collective_id=0, has_side_effects=True, vmem_limit_bytes=VMEM_LIMIT
         ),
-        out_shape=jax.ShapeDtypeStruct((count * rows, 2 * half), own[0].dtype),
-        compiler_params=params(),
-        cost_estimate=pl.CostEstimate(flops=0, bytes_accessed=4 * size, transcendentals=0),
-    )(places, *own, *other)
-
-
-def roll_blocks(grid, arrived):
-    ordered = [arrived[(grid.F - i) % grid.F] for i in range(grid.F)]
-    both = jnp.stack(ordered + ordered[:-1])
-    return lax.dynamic_slice_in_dim(both, (grid.F - grid.f) % grid.F, grid.F, axis=0)
-
-
-def gather_weight(grid, shard):
-    rows, width = shard.shape
-    half = width // 2
-    mine = lax.dynamic_slice_in_dim(shard, grid.c * half, half, axis=1)
-    got = grid.swap(lax.dynamic_slice_in_dim(shard, (1 - grid.c) * half, half, axis=1))
-    pair = jnp.stack([jnp.where(grid.c == 0, mine, got), jnp.where(grid.c == 0, got, mine)])
-    arrived = [pair] + [grid.ring(pair, t) for t in range(1, grid.F)]
-    line = jnp.swapaxes(roll_blocks(grid, arrived), 0, 1).reshape(2 * grid.F * rows, half)
-    blocks = [line]
-    for phase in range(grid.bits):
-        blocks = blocks + [grid.flip(block, phase) for block in blocks]
-    return assemble(grid, blocks, [grid.swap(block) for block in blocks])
-
-
-def scatter_gradient(grid, total):
-    height, half = total.shape
-    rows = height // (grid.J * 2 * grid.F)
-    parts = total.reshape(grid.J, height // grid.J, half)
-    pieces = {
-        key: lax.dynamic_index_in_dim(parts, grid.place(key, grid.c), 0, keepdims=False)
-        for key in range(grid.J)
-    }
-    for phase in range(grid.bits):
-        for key in sorted(pieces, reverse=True):
-            if key >> phase & 1:
-                got = grid.flip(pieces.pop(key), phase)
-                here = key ^ (1 << phase)
-                pieces[here] = (pieces[here].astype(F32) + got.astype(F32)).astype(BF)
-    line = pieces[0].reshape(2, grid.F, rows, half)
-
-    def block(t):
-        return lax.dynamic_index_in_dim(line, (grid.f + t) % grid.F, 1, keepdims=False)
-
-    summed = block(0).astype(F32)
-    for got in [grid.ring(block(t), t) for t in range(1, grid.F)]:
-        summed = summed + got.astype(F32)
-    mine = lax.dynamic_index_in_dim(summed, grid.c, 0, keepdims=False)
-    give = lax.dynamic_index_in_dim(summed, 1 - grid.c, 0, keepdims=False)
-    got = grid.swap(give.astype(BF)).astype(F32)
+    )(tokens, cotangent, packed, *shards)
+    width = tokens.shape[2]
+    gains_all = outs[2][..., : layers * 2, : gains.shape[2]]
+    gains_all = jnp.moveaxis(gains_all, 3, 0).reshape(layers, 2, -1)
+    weights = [
+        [outs[3 + l * kinds + i].reshape(-1, shards[i].shape[2]) for i in range(kinds)]
+        for l in range(layers)
+    ]
+    return outs[0].reshape(-1, width), outs[1].reshape(-1, width), gains_all, weights
+
+
+def tie(*values):
+    return lax.optimization_barrier(values)
+
+
+def in_key_order(grid, value, keys, axis):
+    size = value.shape[axis] // grid.J
     return jnp.concatenate(
-        [jnp.where(grid.c == 0, mine, got), jnp.where(grid.c == 0, got, mine)], axis=1
+        [
+            lax.dynamic_slice_in_dim(value, grid.place(key, grid.c) * size, size, axis=axis)
+            for key in keys
+        ],
+        axis=axis,
     )
 
 
-def gather_gains(grid, shard):
-    value = shard.astype(BF)
-    arrived = [value] + [grid.ring(value, t) for t in range(1, grid.F)]
-    line = roll_blocks(grid, arrived)
-    other = grid.swap(line)
-    line = jnp.stack([jnp.where(grid.c == 0, line, other), jnp.where(grid.c == 0, other, line)])
-    blocks = [line]
-    for phase in range(grid.bits):
-        blocks = blocks + [grid.flip(block, phase) for block in blocks]
-    whole = jnp.stack(blocks)
-    order = jnp.arange(grid.J) ^ grid.j
-    if grid.bits > 1:
-        turned = sum(((order >> p) & 1) << grid.bit(p, 1) for p in range(grid.bits))
-        order = jnp.where(grid.c == 0, order, turned)
-    whole = jnp.take(whole, order, axis=0)
-    whole = jnp.transpose(whole, (3, 4, 0, 1, 2, 5))
-    return whole.reshape(shard.shape[0], shard.shape[1], -1)
+class Scatter:
+    def __init__(self, grid, pairs):
+        self.grid = grid
+        self.halves = [right.shape[1] // 2 for _, right in pairs]
+        joined = []
+        for (left, right), half in zip(pairs, self.halves):
+            mine = lax.dynamic_slice_in_dim(right, grid.c * half, half, axis=1)
+            give = lax.dynamic_slice_in_dim(right, (1 - grid.c) * half, half, axis=1)
+            joined.append(
+                (jnp.concatenate([left, grid.swap(left)]), jnp.concatenate([mine, grid.swap(give)]))
+            )
+        self.height = joined[0][0].shape[1]
+        if self.height // grid.J % 128:
+            whole = [mm(left, right, (0, 0)).astype(BF) for left, right in joined]
+            whole = jnp.concatenate(whole, axis=1)
+            part = lambda keys: in_key_order(grid, whole, keys, 0)
+        else:
+            part = lambda keys: jnp.concatenate(
+                [mm(in_key_order(grid, left, keys, 1), right, (0, 0)).astype(BF) for left, right in joined],
+                axis=1,
+            )
+        self.parts = [
+            part([key for key in range(grid.J) if key & 1 == side]) for side in (1, 0)
+        ]
+
+    def across(self):
+        grid, (give, held) = self.grid, self.parts
+        for phase in range(grid.bits):
+            if phase > 0:
+                held = held.reshape(-1, 2, self.height // grid.J, held.shape[1])
+                give, held = (held[:, side].reshape(-1, held.shape[3]) for side in (1, 0))
+            got = grid.flip(give, phase)
+            held = (held.astype(F32) + got.astype(F32)).astype(BF)
+        self.line = held
+
+    def along_line(self):
+        grid = self.grid
+        line = self.line.reshape(2, grid.F, -1, self.line.shape[1])
+
+        def block(t):
+            return lax.dynamic_index_in_dim(line, (grid.f + t) % grid.F, 1, keepdims=False)
+
+        summed = block(0).astype(F32)
+        for got in [grid.ring(block(t), t) for t in range(1, grid.F)]:
+            summed = summed + got.astype(F32)
+        mine = lax.dynamic_index_in_dim(summed, grid.c, 0, keepdims=False)
+        give = lax.dynamic_index_in_dim(summed, 1 - grid.c, 0, keepdims=False)
+        got = grid.swap(give.astype(BF)).astype(F32)
+        self.found, start = [], 0
+        for half in self.halves:
+            a, b = mine[:, start : start + half], got[:, start : start + half]
+            start += half
+            self.found.append(
+                jnp.concatenate([jnp.where(grid.c == 0, a, b), jnp.where(grid.c == 0, b, a)], axis=1)
+            )
 
 
 def scatter_gains(grid, total):
     layers, kinds, width = total.shape
-    rows = width // (grid.n_dp * grid.F)
+    devices = grid.n_dp * grid.F
     total = total + grid.swap(total)
-    for phase in range(grid.bits):
-        total = total + grid.flip(total, phase)
-    parts = total.reshape(layers, kinds, grid.J, 2, grid.F, rows)
-    mine = lax.dynamic_index_in_dim(parts, grid.j, 2, keepdims=False)
-    mine = lax.dynamic_index_in_dim(mine, grid.c, 2, keepdims=False)
-
-    def block(t):
-        return lax.dynamic_index_in_dim(mine, (grid.f + t) % grid.F, 2, keepdims=False)
-
-    return block(0) + sum(grid.ring(block(t), t) for t in range(1, grid.F))
+    for p in range(grid.bits):
+        total = total + grid.permute(total, lambda j, c, f: (j ^ (1 << p), c, f))
+    for step in [1 << p for p in range(grid.F.bit_length() - 1)]:
+        total = total + grid.permute(total, lambda j, c, f: (j, c, f ^ step))
+    here = (grid.j * 2 + grid.c) * grid.F + grid.f
+    return lax.dynamic_slice_in_dim(total, here * (width // devices), width // devices, axis=2)
 
 
 def rope_tables():
@@ -307,25 +527,28 @@
         sin = table_rows(grid, sin_ref, me, part)
         query, key = q_ref[rows, :], k_ref[rows, :]
         outs[0][rows, :] = turn(query, cos, sin).astype(BF)
-        outs[1][rows, :] = turn(key, cos, sin).astype(BF)
-        outs[2][rows, :] = v_ref[rows, :].astype(BF)
+        outs[1][0, rows, :] = turn(key, cos, sin).astype(BF)
+        outs[1][1, rows, :] = v_ref[rows, :].astype(BF)
         if memory:
-            outs[3][rows, :] = query.astype(BF)
-            outs[4][rows, :] = key.astype(BF)
+            outs[1][2, rows, :] = key.astype(BF)
+            outs[2][rows, :] = query.astype(BF)
 
 
 def split_heads(grid, memory, info, tables, projected):
     rows, width = projected.shape
     heads = width // (3 * HEAD_DIM)
-    count = 5 if memory else 3
+    count = 3 if memory else 2
     piece = lambda at: pl.BlockSpec((rows, HEAD_DIM), lambda h: (0, at * heads + h))
+    flat = jax.ShapeDtypeStruct((rows, heads * HEAD_DIM), BF)
+    stacked = jax.ShapeDtypeStruct((count, rows, heads * HEAD_DIM), BF)
     return pl.pallas_call(
         functools.partial(split_body, grid, memory),
         grid=(heads,),
-        out_shape=[jax.ShapeDtypeStruct((rows, heads * HEAD_DIM), BF)] * count,
+        out_shape=[flat, stacked] + [flat] * memory,
         in_specs=[smem(), whole_spec((SEG, HEAD_DIM)), whole_spec((SEG, HEAD_DIM))]
         + [piece(0), piece(1), piece(2)],
-        out_specs=[piece(0)] * count,
+        out_specs=[piece(0), pl.BlockSpec((count, rows, HEAD_DIM), lambda h: (0, 0, h))]
+        + [piece(0)] * memory,
         compiler_params=params(),
         cost_estimate=pl.CostEstimate(
             flops=10 * rows * width, bytes_accessed=8 * rows * width, transcendentals=0
@@ -372,9 +595,9 @@
 
 def attend_body(grid, memory, heads, info_ref, *refs):
     U, R = grid.U, grid.R
-    q_ref, k_refs, v_refs = refs[0], refs[1 : 1 + U], refs[1 + U : 1 + 2 * U]
-    refs = refs[1 + 2 * U :]
-    keys, values = [r[...] for r in k_refs], [r[...] for r in v_refs]
+    q_ref, kv_refs = refs[0], refs[1 : 1 + U]
+    refs = refs[1 + U :]
+    keys, values = [r[0] for r in kv_refs], [r[1] for r in kv_refs]
     if memory:
         step = pl.program_id(0)
         memory_keys = head_halves(refs[1], refs[2], step, heads // 2)
@@ -404,7 +627,8 @@
     piece = pl.BlockSpec((grid.T, HEAD_DIM), lambda h, info: (0, head(h, info)))
     own = pl.BlockSpec((memory_rows, HEAD_DIM), lambda h, info: (0, jnp.minimum(h, per - 1)))
     other = pl.BlockSpec((memory_rows, HEAD_DIM), lambda h, info: (0, jnp.maximum(h - per, 0)))
-    return piece, own, other
+    pair = pl.BlockSpec((2, grid.T, HEAD_DIM), lambda h, info: (0, 0, head(h, info)))
+    return piece, pair, own, other
 
 
 def attention_cost(grid, heads, memory_rows, products):
@@ -416,12 +640,12 @@
     )
 
 
-def attend(grid, info, query, keys, values, extra):
+def attend(grid, info, query, pairs, extra):
     heads = query.shape[1] // HEAD_DIM
     memory = extra is not None
     memory_rows = grid.n_dp * extra["topk"] if memory else 8
-    piece, own, other = head_specs(grid, heads, memory_rows)
-    operands, specs = [query, *keys, *values], [piece] * (1 + 2 * grid.U)
+    piece, pair, own, other = head_specs(grid, heads, memory_rows)
+    operands, specs = [query, *pairs], [piece] + [pair] * grid.U
     if memory:
         operands += [extra["query"], *extra["keys"], *extra["values"], extra["bias"]]
         specs += [piece, own, other, own, other, pl.BlockSpec((memory_rows, 1), lambda h, info: (0, 0))]
@@ -439,9 +663,9 @@
 def attend_back_body(grid, memory, heads, info_ref, *refs):
     U, R = grid.U, grid.R
     cos_ref, sin_ref, q_ref, g_ref = refs[:4]
-    k_refs, v_refs = refs[4 : 4 + U], refs[4 + U : 4 + 2 * U]
-    refs = refs[4 + 2 * U :]
-    keys, values = [r[...] for r in k_refs], [r[...] for r in v_refs]
+    kv_refs = refs[4 : 4 + U]
+    refs = refs[4 + U :]
+    keys, values = [r[0] for r in kv_refs], [r[1] for r in kv_refs]
     step = pl.program_id(0)
     if memory:
         query_raw_ref = refs[0]
@@ -449,7 +673,7 @@
         memory_values = head_halves(refs[3], refs[4], step, heads // 2)
         bias = refs[5][...]
         refs = refs[6:]
-    dq_ref, dk_refs, dv_refs, refs = refs[0], refs[1 : 1 + U], refs[1 + U : 1 + 2 * U], refs[1 + 2 * U :]
+    dq_ref, dkv_refs, refs = refs[0], refs[1 : 1 + U], refs[1 + U :]
     me = info_ref[0]
     grad_keys, grad_values = {}, {}
 
@@ -497,8 +721,8 @@
             cos = table_rows(grid, cos_ref, member, side)
             sin = table_rows(grid, sin_ref, member, side)
             key = turn(grad_keys[(t, side)], cos, -sin) * SCALE
-            dk_refs[t][rows, :] = key.astype(dk_refs[t].dtype)
-            dv_refs[t][rows, :] = grad_values[(t, side)].astype(dv_refs[t].dtype)
+            dkv_refs[t][0, rows, :] = key.astype(dkv_refs[t].dtype)
+            dkv_refs[t][1, rows, :] = grad_values[(t, side)].astype(dkv_refs[t].dtype)
     if memory:
         key = (grad_keys["memory"] * SCALE).astype(BF)
         value = grad_values["memory"].astype(BF)
@@ -514,20 +738,18 @@
             refs[3][...] = value
 
 
-def attend_back(grid, info, tables, query, grad, keys, values, extra):
+def attend_back(grid, info, tables, query, grad, pairs, extra):
     rows, width = query.shape
     heads = width // HEAD_DIM
     memory = extra is not None
     memory_rows = grid.n_dp * extra["topk"] if memory else 8
-    piece, own, other = head_specs(grid, heads, memory_rows)
+    piece, pair, own, other = head_specs(grid, heads, memory_rows)
     table = pl.BlockSpec((SEG, HEAD_DIM), lambda h, info: (0, 0))
-    operands = [*tables, query, grad, *keys, *values]
-    specs = [table, table] + [piece] * (2 + 2 * grid.U)
-    own_kind = jax.ShapeDtypeStruct((rows, width), F32)
-    sent_kind = jax.ShapeDtypeStruct((rows, width), BF)
-    kinds = [own_kind] + [sent_kind] * (grid.U - 1)
-    out_shape = [sent_kind] + kinds + kinds
-    out_specs = [piece] * len(out_shape)
+    operands = [*tables, query, grad, *pairs]
+    specs = [table, table, piece, piece] + [pair] * grid.U
+    out_shape = [jax.ShapeDtypeStruct((rows, width), BF), jax.ShapeDtypeStruct((2, rows, width), F32)]
+    out_shape += [jax.ShapeDtypeStruct((2, rows, width), BF)] * (grid.U - 1)
+    out_specs = [piece] + [pair] * grid.U
     if memory:
         operands += [extra["query"], *extra["keys"], *extra["values"], extra["bias"]]
         specs += [piece, own, other, own, other, pl.BlockSpec((memory_rows, 1), lambda h, info: (0, 0))]
@@ -542,8 +764,7 @@
         compiler_params=params(),
         cost_estimate=attention_cost(grid, heads, memory_rows if memory else 0, 5),
     )(info, *operands)
-    U = grid.U
-    return outs[0], outs[1 : 1 + U], outs[1 + U : 1 + 2 * U], outs[1 + 2 * U :]
+    return outs[0], outs[1 : 1 + grid.U], outs[1 + grid.U :]
 
 
 def pick_body(grid, info_ref, picks_ref, *refs):
@@ -557,24 +778,24 @@
             across = lax.broadcasted_iota(jnp.int32, (picks.shape[0], R), 1)
             chosen = (picks == across + piece_start(grid, member, side)).astype(BF)
             rows = pl.ds(side * R, R)
-            key = key + dot(chosen, refs[t][rows, :], (1, 0))
-            value = value + dot(chosen, refs[U + t][rows, :], (1, 0))
+            key = key + dot(chosen, refs[t][2, rows, :], (1, 0))
+            value = value + dot(chosen, refs[t][1, rows, :], (1, 0))
     out_ref[0] = key.astype(BF)
     out_ref[1] = value.astype(BF)
 
 
-def pick_memory(grid, info, picks, keys, values):
+def pick_memory(grid, info, picks, stacked):
     heads, topk = picks.shape
     per = heads // 2
     at = lambda h, info: info[2] * per + h
-    piece = pl.BlockSpec((grid.T, HEAD_DIM), lambda h, info: (0, at(h, info)))
+    piece = pl.BlockSpec((3, grid.T, HEAD_DIM), lambda h, info: (0, 0, at(h, info)))
     return pl.pallas_call(
         functools.partial(pick_body, grid),
         grid_spec=pltpu.PrefetchScalarGridSpec(
             num_scalar_prefetch=1,
             grid=(per,),
             in_specs=[pl.BlockSpec((1, topk, 1), lambda h, info: (at(h, info), 0, 0))]
-            + [piece] * (2 * grid.U),
+            + [piece] * grid.U,
             out_specs=pl.BlockSpec((2, topk, HEAD_DIM), lambda h, info: (0, 0, h)),
         ),
         out_shape=jax.ShapeDtypeStruct((2, topk, per * HEAD_DIM), BF),
@@ -582,52 +803,64 @@
         cost_estimate=pl.CostEstimate(
             flops=4 * topk * SEG * HEAD_DIM * per, bytes_accessed=4 * SEG * HEAD_DIM * per, transcendentals=0
         ),
-    )(info, picks[:, :, None], *keys, *values)
+    )(info, picks[:, :, None], *stacked)
 
 
 def finish_body(grid, memory, heads, info_ref, *refs):
     U, R = grid.U, grid.R
-    dk_refs, dv_refs = refs[:U], refs[U : 2 * U]
-    refs = refs[2 * U :]
-    key = sum(r[...].astype(F32) for r in dk_refs)
-    value = sum(r[...].astype(F32) for r in dv_refs)
-    key_ref, value_ref = refs[-2:]
-    if not memory:
-        key_ref[...] = key.astype(BF)
-        value_ref[...] = value.astype(BF)
-        return
-    picks = refs[0][0]
-    step = pl.program_id(0)
-    back = head_halves(refs[1], refs[2], step, heads // 2)
-    for side in range(2):
-        down = lax.broadcasted_iota(jnp.int32, (R, picks.shape[1]), 0)
-        chosen = (down + piece_start(grid, info_ref[0], side) == picks).astype(BF)
-        rows = slice(side * R, (side + 1) * R)
-        key_ref[rows, :] = (key[rows] + dot(chosen, back[0], (1, 0))).astype(BF)
-        value_ref[rows, :] = (value[rows] + dot(chosen, back[1], (1, 0))).astype(BF)
-
-
-def finish_keys(grid, info, grad_keys, grad_values, picks, halves):
-    rows, width = grad_keys[0].shape
+    dq_ref, dkv_refs, out_ref = refs[0], refs[1 : 1 + U], refs[-1]
+    refs = refs[1 + U :]
+    kind, head = pl.program_id(0) // heads, pl.program_id(0) % heads
+
+    @pl.when(kind == 0)
+    def _():
+        out_ref[...] = dq_ref[...]
+
+    @pl.when(kind > 0)
+    def _():
+        total = sum(r[0].astype(F32) for r in dkv_refs)
+        if memory:
+            picks = refs[0][0]
+            own = head // (heads // 2) == info_ref[2]
+            back = jnp.where(own, refs[1][0], refs[2][0])
+        for side in range(2):
+            rows = slice(side * R, (side + 1) * R)
+            value = total[rows]
+            if memory:
+                down = lax.broadcasted_iota(jnp.int32, (R, picks.shape[1]), 0)
+                chosen = (down + piece_start(grid, info_ref[0], side) == picks).astype(BF)
+                value = value + dot(chosen, back, (1, 0))
+            out_ref[rows, :] = value.astype(BF)
+
+
+def finish_gradient(grid, info, grad_query, grad_pairs, picks, halves):
+    rows, width = grad_query.shape
     heads = width // HEAD_DIM
     memory = halves is not None
     per = heads // 2
-    piece, _, _ = head_specs(grid, heads, 8)
-    operands, specs = [*grad_keys, *grad_values], [piece] * (2 * grid.U)
+    which = lambda b: jnp.maximum(b // heads - 1, 0)
+    pair = pl.BlockSpec((1, rows, HEAD_DIM), lambda b, info: (which(b), 0, jnp.where(b < heads, 0, b % heads)))
+    operands = [grad_query, *grad_pairs]
+    specs = [pl.BlockSpec((rows, HEAD_DIM), lambda b, info: (0, jnp.minimum(b, heads - 1)))] + [pair] * grid.U
     if memory:
         topk = picks.shape[1]
+        own = lambda b, info: jnp.clip(b % heads - info[2] * per, 0, per - 1)
+        other = lambda b, info: jnp.clip(b % heads - (1 - info[2]) * per, 0, per - 1)
         operands += [picks[:, None, :], *halves]
         specs += [
-            pl.BlockSpec((1, 1, topk), lambda h, info: (lax.rem(info[2] + h // per, 2) * per + h % per, 0, 0)),
-            pl.BlockSpec((2, topk, HEAD_DIM), lambda h, info: (0, 0, jnp.minimum(h, per - 1))),
-            pl.BlockSpec((2, topk, HEAD_DIM), lambda h, info: (0, 0, jnp.maximum(h - per, 0))),
+            pl.BlockSpec((1, 1, topk), lambda b, info: (b % heads, 0, 0)),
+            pl.BlockSpec((1, topk, HEAD_DIM), lambda b, info: (which(b), 0, own(b, info))),
+            pl.BlockSpec((1, topk, HEAD_DIM), lambda b, info: (which(b), 0, other(b, info))),
         ]
     return pl.pallas_call(
         functools.partial(finish_body, grid, memory, heads),
         grid_spec=pltpu.PrefetchScalarGridSpec(
-            num_scalar_prefetch=1, grid=(heads,), in_specs=specs, out_specs=[piece, piece]
+            num_scalar_prefetch=1,
+            grid=(3 * heads,),
+            in_specs=specs,
+            out_specs=pl.BlockSpec((rows, HEAD_DIM), lambda b, info: (0, b)),
         ),
-        out_shape=[jax.ShapeDtypeStruct((rows, width), BF)] * 2,
+        out_shape=jax.ShapeDtypeStruct((rows, 3 * width), BF),
         compiler_params=params(),
         cost_estimate=pl.CostEstimate(
             flops=2 * rows * width, bytes_accessed=16 * rows * width, transcendentals=0
@@ -680,97 +913,72 @@
     info = jnp.stack([grid.k, valid, grid.c]).astype(jnp.int32)
     tables = rope_tables()
 
-    hidden = grid.to_units(tokens).astype(F32)
-    gains = gather_gains(grid, norm_gains).astype(F32)
     picks_there = grid.swap(memory_picks)
     picks = jnp.where(
         grid.r == grid.c, memory_picks[grid.m, 0], picks_there[grid.m, 0]
     )
 
-    weights = []
-    for l in range(layers):
-        weights.append(
-            [gather_weight(grid, w[l]) for w in (attention_in, attention_out, feed_in, feed_out)]
-        )
-    grad_stream = grid.to_units(cotangent).astype(F32)
-
     def exchange(value):
         return [value] + [grid.member(value, t) for t in range(1, grid.U)]
 
-    saved = []
-    for l in range(layers):
-        w_qkv, w_out, w_up, w_down = weights[l]
+    def attention(l, hidden, w_qkv, w_out):
         memory = l == layers - 1
         normed = norm(hidden, gains[l, 0]).astype(BF)
-        projected = mm(normed, w_qkv)
-        split = split_heads(grid, memory, info, tables, projected)
-        query = split[0]
-        keys, values = exchange(split[1]), exchange(split[2])
+        split = split_heads(grid, memory, info, tables, mm(normed, w_qkv))
+        query, pairs = split[0], exchange(split[1])
         extra = None
         if memory:
-            raw_keys = exchange(split[4])
-            chosen = pick_memory(grid, info, picks, raw_keys, values)
+            chosen = pick_memory(grid, info, picks, pairs)
             slots = [chosen] + [grid.slots(chosen, t) for t in range(1, n_dp)]
-            half = [jnp.concatenate([s[i] for s in slots]) for i in range(2)]
-            there = [grid.swap(h) for h in half]
+            half = jnp.stack(slots, axis=1).reshape(2, n_dp * topk, -1)
+            there = grid.swap(half)
             extra = {
                 "topk": topk,
-                "query": split[3],
+                "query": split[2],
                 "keys": (half[0], there[0]),
                 "values": (half[1], there[1]),
                 "bias": bias,
             }
-        attended = attend(grid, info, query, keys, values, extra)
+        attended = attend(grid, info, query, pairs, extra)
         middle = hidden + mm(attended, w_out)
-        normed_feed = norm(middle, gains[l, 1]).astype(BF)
-        gate_up = mm(normed_feed, w_up)
+        return middle, (hidden, normed, query, pairs, extra, attended)
+
+    def feed(l, middle, w_up, w_down):
+        normed = norm(middle, gains[l, 1]).astype(BF)
+        gate_up = mm(normed, w_up)
         gate, up = jnp.split(gate_up, 2, axis=1)
         inner = (jax.nn.silu(gate) * up).astype(BF)
-        saved.append((hidden, middle, normed, normed_feed, gate_up, inner, query, keys, values, extra, attended))
-        hidden = middle + mm(inner, w_down)
-    layer_output = grid.from_units(hidden.astype(BF))
-
-    def gradient(left, right):
-        half = right.shape[1] // 2
-        mine = lax.dynamic_slice_in_dim(right, grid.c * half, half, axis=1)
-        give = lax.dynamic_slice_in_dim(right, (1 - grid.c) * half, half, axis=1)
-        left = jnp.concatenate([left, grid.swap(left)])
-        right = jnp.concatenate([mine, grid.swap(give)])
-        return scatter_gradient(grid, mm(left, right, (0, 0)).astype(BF))
-
-    grads = [None] * layers
-    grad_gains = [None] * layers
-    for l in reversed(range(layers)):
-        w_qkv, w_out, w_up, w_down = weights[l]
-        hidden, middle, normed, normed_feed, gate_up, inner, query, keys, values, extra, attended = saved[l]
-        grad_low = grad_stream.astype(BF)
+        return middle + mm(inner, w_down), (middle, normed, gate_up, inner)
+
+    def feed_back(l, grad, kept, w_up, w_down):
+        middle, normed, gate_up, inner = kept
+        grad_low = grad.astype(BF)
         grad_inner = mm(grad_low, w_down, (1, 1))
-        grad_w_down = gradient(inner, grad_low)
+        down = Scatter(grid, [(inner, grad_low)])
         gate, up = jnp.split(gate_up, 2, axis=1)
         sigmoid = jax.nn.sigmoid(gate)
         grad_gate = grad_inner * up * sigmoid * (1.0 + gate * (1.0 - sigmoid))
         grad_up = grad_inner * gate * sigmoid
         grad_gate_up = jnp.concatenate([grad_gate, grad_up], axis=1).astype(BF)
-        grad_w_up = gradient(normed_feed, grad_gate_up)
-        pulled, gain_feed = norm_back(middle, gains[l, 1], mm(grad_gate_up, w_up, (1, 1)))
-        grad_middle = grad_stream + pulled
-        grad_attended = grad_middle.astype(BF)
-        grad_w_out = gradient(attended, grad_attended)
+        up = Scatter(grid, [(normed, grad_gate_up)])
+        pulled, grad_gain = norm_back(middle, gains[l, 1], mm(grad_gate_up, w_up, (1, 1)))
+        return grad + pulled, grad_gain, down, up
+
+    def attention_back(l, grad, kept, w_qkv, w_out):
+        hidden, normed, query, pairs, extra, attended = kept
+        grad_attended = grad.astype(BF)
         grad_heads = mm(grad_attended, w_out, (1, 1)).astype(BF)
-        grad_query, grad_keys, grad_values, memory_grads = attend_back(
-            grid, info, tables, query, grad_heads, keys, values, extra
+        grad_query, grad_pairs, memory_grads = attend_back(
+            grid, info, tables, query, grad_heads, pairs, extra
         )
-        grad_keys = [grad_keys[0]] + [
-            grid.member(grad_keys[t], grid.U - t) for t in range(1, grid.U)
-        ]
-        grad_values = [grad_values[0]] + [
-            grid.member(grad_values[t], grid.U - t) for t in range(1, grid.U)
+        grad_pairs = [grad_pairs[0]] + [
+            grid.member(grad_pairs[t], grid.U - t) for t in range(1, grid.U)
         ]
         halves = None
         if extra is not None:
-            own = [memory_grads[0], memory_grads[1]]
-            there = [grid.swap(memory_grads[2]), grid.swap(memory_grads[3])]
-            joined = jnp.stack([a.astype(F32) + b.astype(F32) for a, b in zip(own, there)])
+            own = jnp.stack(memory_grads[:2])
+            there = grid.swap(jnp.stack(memory_grads[2:]))
+            joined = own.astype(F32) + there.astype(F32)
             joined = joined.astype(BF).reshape(2, n_dp, topk, -1)
             total = joined[:, 0].astype(F32)
             for t in range(1, n_dp):
@@ -780,19 +988,60 @@
                 total = total + grid.within(low, t).astype(F32)
             total = total.astype(BF)
             halves = (total, grid.swap(total))
-        grad_key, grad_value = finish_keys(grid, info, grad_keys, grad_values, picks, halves)
-        grad_projected = jnp.concatenate([grad_query, grad_key, grad_value], axis=1)
-        grad_w_qkv = gradient(normed, grad_projected)
-        pulled, gain_attention = norm_back(hidden, gains[l, 0], mm(grad_projected, w_qkv, (1, 1)))
-        grad_stream = grad_middle + pulled
-        grads[l] = (grad_w_qkv, grad_w_out, grad_w_up, grad_w_down)
-        grad_gains[l] = jnp.stack([gain_attention, gain_feed])
-    input_grad = grid.from_units(grad_stream.astype(BF)).astype(F32)
+        grad_projected = finish_gradient(grid, info, grad_query, grad_pairs, picks, halves)
+        both = Scatter(grid, [(attended, grad_attended), (normed, grad_projected)])
+        pulled, grad_gain = norm_back(hidden, gains[l, 0], mm(grad_projected, w_qkv, (1, 1)))
+        return grad + pulled, grad_gain, both
+
+    hidden, cotangent_rows, gains, weights = gather_all(
+        grid, tokens, cotangent, norm_gains, [attention_in, attention_out, feed_in, feed_out]
+    )
+    hidden = hidden.astype(F32)
+    first = [w[:2] for w in weights]
+    second = [w[2:3] for w in weights]
+    third = [w[3:] for w in weights]
+    kept_attention, kept_feed = [None] * layers, [None] * layers
+    for l in range(layers):
+        middle, kept_attention[l] = attention(l, hidden, *first[l])
+        hidden, kept_feed[l] = feed(l, middle, *second[l], *third[l])
+    layer_output = grid.from_units(hidden.astype(BF))
+
+    grad = cotangent_rows.astype(F32)
+    downs, ups, boths = [None] * layers, [None] * layers, [None] * layers
+    grad_gains = [[None, None] for _ in range(layers)]
+    for l in reversed(range(layers)):
+        grad, grad_gains[l][1], downs[l], ups[l] = feed_back(
+            l, grad, kept_feed[l], *second[l], *third[l]
+        )
+        if l < layers - 1:
+            boths[l + 1].across()
+            downs[l + 1].along_line()
+            ups[l + 1].along_line()
+            boths[l + 1].line, downs[l + 1].found, ups[l + 1].found, grad, downs[l].parts, ups[l].parts = tie(
+                boths[l + 1].line, downs[l + 1].found, ups[l + 1].found, grad, downs[l].parts, ups[l].parts
+            )
+            boths[l + 1].along_line()
+        else:
+            grad, downs[l].parts, ups[l].parts = tie(grad, downs[l].parts, ups[l].parts)
+        downs[l].across()
+        ups[l].across()
+        grad, grad_gains[l][0], boths[l] = attention_back(l, grad, kept_attention[l], *first[l])
+        grad, boths[l].parts, downs[l].line, ups[l].line = tie(
+            grad, boths[l].parts, downs[l].line, ups[l].line
+        )
+    boths[0].across()
+    boths[0].along_line()
+    downs[0].along_line()
+    ups[0].along_line()
+    input_grad = grid.from_units(grad.astype(BF)).astype(F32)
     return (
         layer_output,
         input_grad,
-        *(jnp.stack([grads[l][i] for l in range(layers)]) for i in range(4)),
-        scatter_gains(grid, jnp.stack(grad_gains)),
+        jnp.stack([both.found[1] for both in boths]),
+        jnp.stack([both.found[0] for both in boths]),
+        jnp.stack([up.found[0] for up in ups]),
+        jnp.stack([down.found[0] for down in downs]),
+        scatter_gains(grid, jnp.stack([jnp.stack(pair) for pair in grad_gains])),
     )
 
 

time: 1240 us -> 1070 us (0.86)
  waiting for transfers between devices: 497 us -> 261 us
  Pallas kernels: 194 us -> 420 us
  starting transfers between devices: 217 us -> 82.4 us
  local copies, waits for them, and re-layouts: 93.9 us -> 46.5 us
  other arithmetic: 56.4 us -> 84.8 us
    ppermute x210 -> x83, waiting for transfers between devices: 497 us -> 261 us  [permute(): return lax.ppermute(value, ('dp', 'fsdp'), pairs)]
    pallas_call x10 -> x3, Pallas kernels: 78.3 us -> 304 us  [the longest x1 275 us: gather_all(): pl.pallas_call(functools.partial(gather_body, grid, layers, kinds), in_sp...]
    ppermute x210 -> x83, starting transfers between devices: 217 us -> 82.4 us  [permute(): return lax.ppermute(value, ('dp', 'fsdp'), pairs)]
    unnamed x429 -> x258, local copies, waits for them, and re-layouts: 58.6 us -> 24.6 us
    concatenate x3 -> x18, other arithmetic: 10.3 us -> 32.5 us  [the longest x6 12.3 us: __init__(): jnp.concatenate([left, grid.swap(left)])]
    dot_general x24 -> x30, matrix products: 162 us -> 166 us  [dot(): lax.dot_general(left, right, (((contract[0],), (contract[1],)), ((), ()))...]
  transfers between devices with their start and end apart: 210 -> 83, of which waited for: 83 -> 36; matrix products, arithmetic and copies ran while one was open for 18% -> 18% of each run, Pallas kernels for 14% -> 8%
where the time goes in v2:
time: 1070 us; the launch traced here: 1060 us
  Pallas kernels  420 us (39%)
  waiting for transfers between devices  261 us (24%)
  matrix products  166 us (16%)
  other arithmetic  84.8 us (8%)
  starting transfers between devices  82.4 us (8%)
  local copies, waits for them, and re-layouts  46.5 us (4%)
    pallas_call x1, Pallas kernels, gather_all(): pl.pallas_call(functools.partial(gather_body, grid, layers, kinds), in_sp...  275 us
    ppermute x83, waiting for transfers between devices, permute(): return lax.ppermute(value, ('dp', 'fsdp'), pairs)  261 us
    dot_general x30, matrix products, dot(): lax.dot_general(left, right, (((contract[0],), (contract[1],)), ((), ()))...  166 us
    ppermute x83, starting transfers between devices, permute(): return lax.ppermute(value, ('dp', 'fsdp'), pairs)  82.4 us
    pallas_call x2, Pallas kernels, attend_back(): pl.pallas_call(functools.partial(attend_back_body, grid, memory, heads),...  59.5 us
    pallas_call x2, Pallas kernels, attend(): pl.pallas_call(functools.partial(attend_body, grid, memory, heads), grid_...  37.7 us
    pallas_call x2, Pallas kernels, finish_gradient(): pl.pallas_call(functools.partial(finish_body, grid, memory, heads), grid_...  29.6 us
    unnamed x258, local copies, waits for them, and re-layouts  24.6 us
  transfers between devices with their start and end apart: 83, of which 36 were waited for; matrix products, arithmetic and copies ran while one was open for 18% of the time, Pallas kernels for 8%

profile of v2, /device:TPU:0, one launch (start us, length us, event | category | flops | bytes accessed | tf_op | source)
XLA Modules:
  0.0 1064.2 jit_solution(9130400815381556454)
XLA Ops:
  9.8 274.8 %shard_map.153 = (bf16[2,256,1024]{2,1,0:T(8,128)(2,1)S(1)}, bf16[2,256,1024]{2,1,0:T(8,128)(2,1)S(1)}, f32[4,2,4,8,128]{4,3,2,1,0:T(8,128)S(1)}, bf16[4,2,4,32,...) custom-call(bf16[2,256,1024]{2,1,0:T(8,128)(2,1)S(1)} %copy-done.12,, ...), custom_call_target="tpu_custom_call" | custom-call | tf_op jit(solution)/shard_map/pallas_call | solution.py:379
  310.7 13.2 %shard_map.155 = bf16[512,1024]{1,0:T(8,128)(2,1)S(1)} custom-call(s32[3]{0:T(128)S(1)} %pad_add_fusion.info_ref, bf16[512,1024]{1,0:T(8,128)(2,1)S(1)} %get-tuple-element.71.refs_0_.refs_2_, bf16[2,512,1024]{2,1,0:T(8,128)(2,1)S(1)} %get-tuple-element.72.refs_1_.refs_4_, bf16[2,512,1024]{2,1,0:T(8,128)(2,1)} %copy-done.60), custom_call_target="tpu_custom_call" | custom-call | flops 1610612736 | bytes 8388608 | tf_op jit(solution)/shard_map/pallas_call | solution.py:652
  326.5 10.3 fusion.157
  377.3 10.3 collective-permute-start.3
  396.8 12.7 %collective-permute-done.4 = bf16[2,128,512]{2,1,0:T(8,128)(2,1)S(1)} collective-permute-done((bf16[2,128,512]{2,1,0:T(8,128)(2,1)S(1)}, bf16[2,128,512]{2,1,0:T(8,128)(2,1)S(1)}, u32[]{:S(2)}, u32[]{:S(2)}) %collective-permute-start.4) | collective-permute-done | bytes 262176 | tf_op jit(solution)/shard_map/ppermute | solution.py:70
  430.1 24.6 %shard_map.158 = bf16[512,1024]{1,0:T(8,128)(2,1)S(1)} custom-call(s32[3]{0:T(128)S(1)} %pad_add_fusion.info_ref, bf16[512,1024]{1,0:T(8,128)(2,1)S(1)} %copy-done.21, bf16[3,512,1024]{2,1,0:T(8,128)(2,1)} %get-tuple-element.78.refs_0_.refs_1_.refs_4_, bf16[3,512,1024]{2,1,0:T(8,128)(2,1)} %collective-permute-done.1.refs_1_.refs_2_.refs_5_, ...), custom_call_target="tpu_custom_call" | custom-call | flops 3758096384 | bytes 16777216 | tf_op jit(solution)/shard_map/pallas_call | solution.py:652
  456.4 14.4 %fusion.159 = f32[512,5632]{1,0:T(8,128)} fusion(bf16[512,1024]{1,0:T(8,128)(2,1)S(1)} %multiply_convert_fusion.6, bf16[1024,5632]{1,0:T(8,128)(2,1)} %bitcast.383), kind=kOutput, calls=%fused_computation.453 | convolution fusion | flops 5905580032 | bytes 24117248 | tf_op jit(solution)/shard_map/dot_general | solution.py:560
  470.8 10.3 multiply_convert_fusion.3
  489.5 12.8 %multiply_reduce_fusion = (f32[1024]{0:T(1024)S(1)}, f32[512]{0:T(512)S(1)}, f32[512,1024]{1,0:T(8,128)}) fusion(f32[512,1024]{1,0:T(8,128)S(1)} %copy-done.45, f32[512]{0:T(512)S(1)} %add_rsqrt_fusion, f32[1024]{0:T(1024)S(1)} %bitcast.371, bf16[1024,5632]{1,0:T(8,128)(2,1)} %bitcast.384, bf16[512,2816]{1,0:T(8,128)(2,1)} %get-tuple-element.132, ...), kind=kOutput, calls=%fused_computation.132 | convolution fusion | flops 5920258560 | bytes 21508096 | tf_op jit(solution)/shard_map/dot_general | solution.py:560
  533.8 38.5 %shard_map.159 = (bf16[512,1024]{1,0:T(8,128)(2,1)S(1)}, f32[2,512,1024]{2,1,0:T(8,128)}, bf16[2,512,1024]{2,1,0:T(8,128)(2,1)}, bf16[1024,512]{1,0:T(8,128)(2,1...) custom-call(s32[3]{0:T(128)S(1)} %pad_add_fusion.info_ref, ...), custom_call_target="tpu_custom_call" | custom-call | flops 9395240960 | bytes 16777216 | tf_op jit(solution)/shard_map/pallas_call | solution.py:758
  598.5 13.3 %collective-permute-done.12 = bf16[256,1024]{1,0:T(8,128)(2,1)} collective-permute-done((bf16[256,1024]{1,0:T(8,128)(2,1)}, bf16[256,1024]{1,0:T(8,128)(2,1)}, u32[]{:S(2)}, u32[]{:S(2)}) %collective-permute-start.12) | collective-permute-done | bytes 524320 | tf_op jit(solution)/shard_map/ppermute | solution.py:70
  632.4 41.3 %collective-permute-done.24 = bf16[2,128,512]{2,1,0:T(8,128)(2,1)S(1)} collective-permute-done((bf16[2,128,512]{2,1,0:T(8,128)(2,1)S(1)}, bf16[2,128,512]{2,1,0:T(8,128)(2,1)S(1)}, u32[]{:S(2)}, u32[]{:S(2)}) %collective-permute-start.24) | collective-permute-done | bytes 262176 | tf_op jit(solution)/shard_map/ppermute | solution.py:70
  696.6 15.3 %shard_map.160 = bf16[512,3072]{1,0:T(8,128)(2,1)} custom-call(s32[3]{0:T(128)S(1)} %pad_add_fusion.info_ref, bf16[512,1024]{1,0:T(8,128)(2,1)S(1)} %get-tuple-element.85.refs_0_, f32[2,512,1024]{2,1,0:T(8,128)} %get-tuple-element.86.refs_1_, bf16[2,512,1024]{2,1,0:T(8,128)(2,1)} %collective-permute-done.17.refs_2_, s32[8,1,128]{2,1,0:T(1,128)S(1)} %bitcast.326, ...), custom_call_target="tpu_custom_call" | custom-call | flops 1048576 | bytes 8388608 | tf_op jit(solution)/shard_map/pallas_call | solution.py:855
  752.1 9.8 multiply_convert_fusion.1
  762.0 13.2 %multiply_reduce_fusion.2 = (f32[1024]{0:T(1024)}, f32[512]{0:T(512)S(1)}, f32[512,1024]{1,0:T(8,128)}) fusion(f32[512,1024]{1,0:T(8,128)S(1)} %copy-done.38, f32[512]{0:T(512)S(1)} %copy-done.99, f32[1024]{0:T(1024)S(1)} %bitcast.362, bf16[1024,5632]{1,0:T(8,128)(2,1)} %bitcast.382, bf16[512,2816]{1,0:T(8,128)(2,1)} %get-tuple-element.130, ...), kind=kOutput, calls=%fused_computation.134 | convolution fusion | flops 5920258560 | bytes 21508096 | tf_op jit(solution)/shard_map/dot_general | solution.py:560
  786.7 15.8 %collective-permute-done.42 = bf16[2,32,2816]{2,1,0:T(8,128)(2,1)S(1)} collective-permute-done((bf16[2,32,2816]{2,1,0:T(8,128)(2,1)S(1)}, bf16[2,32,2816]{2,1,0:T(8,128)(2,1)S(1)}, u32[]{:S(2)}, u32[]{:S(2)}) %collective-permute-start.42) | collective-permute-done | bytes 360480 | tf_op jit(solution)/shard_map/ppermute | solution.py:70
  836.9 21.0 %shard_map.161 = (bf16[512,1024]{1,0:T(8,128)(2,1)S(1)}, f32[2,512,1024]{2,1,0:T(8,128)}, bf16[2,512,1024]{2,1,0:T(8,128)(2,1)}) custom-call(s32[3]{0:T(128)S(1)} %pad_add_fusion.info_ref, f32[1024,128]{1,0:T(8,128)S(1)} %get-tuple-element.255.cos_ref.refs_0_, f32[1024,128]{1,0:T(8,128)S(1)} %get-tuple-element.256.sin_ref.refs_1_, ...), custom_call_target="tpu_custom_call" | custom-call | flops 4026531840 | bytes 8388608 | tf_op jit(solution)/shard_map/pallas_call | solution.py:758
  882.0 14.3 %shard_map.162 = bf16[512,3072]{1,0:T(8,128)(2,1)} custom-call(s32[3]{0:T(128)S(1)} %pad_add_fusion.info_ref, bf16[512,1024]{1,0:T(8,128)(2,1)S(1)} %get-tuple-element.102.refs_0_, f32[2,512,1024]{2,1,0:T(8,128)} %get-tuple-element.103.refs_1_, bf16[2,512,1024]{2,1,0:T(8,128)(2,1)S(1)} %collective-permute-done.49.refs_2_), custom_call_target="tpu_custom_call" | custom-call | flops 1048576 | bytes 8388608 | tf_op jit(solution)/shard_map/pallas_call | solution.py:855
  904.4 12.5 %collective-permute-done.79 = f32[2,2,1024]{2,1,0:T(2,128)S(1)} collective-permute-done((f32[2,2,1024]{2,1,0:T(2,128)S(1)}, f32[2,2,1024]{2,1,0:T(2,128)S(1)}, u32[]{:S(2)}, u32[]{:S(2)}) %collective-permute-start.79) | collective-permute-done | bytes 16416 | tf_op jit(solution)/shard_map/ppermute | solution.py:70
  936.4 11.8 %collective-permute-done.57 = bf16[256,2816]{1,0:T(8,128)(2,1)S(1)} collective-permute-done((bf16[256,2816]{1,0:T(8,128)(2,1)S(1)}, bf16[256,2816]{1,0:T(8,128)(2,1)S(1)}, u32[]{:S(2)}, u32[]{:S(2)}) %collective-permute-start.57) | collective-permute-done | bytes 1441824 | tf_op jit(solution)/shard_map/ppermute | solution.py:70
  976.3 30.1 %collective-permute-done.71 = bf16[2,32,2816]{2,1,0:T(8,128)(2,1)S(1)} collective-permute-done((bf16[2,32,2816]{2,1,0:T(8,128)(2,1)S(1)}, bf16[2,32,2816]{2,1,0:T(8,128)(2,1)S(1)}, u32[]{:S(2)}, u32[]{:S(2)}) %collective-permute-start.71) | collective-permute-done | bytes 360480 | tf_op jit(solution)/shard_map/ppermute | solution.py:70
  1006.7 10.5 collective-permute-done.59
  1021.7 12.9 %collective-permute-done.61 = bf16[256,2048]{1,0:T(8,128)(2,1)S(1)} collective-permute-done((bf16[256,2048]{1,0:T(8,128)(2,1)S(1)}, bf16[256,2048]{1,0:T(8,128)(2,1)S(1)}, u32[]{:S(2)}, u32[]{:S(2)}) %collective-permute-start.61) | collective-permute-done | bytes 1048608 | tf_op jit(solution)/shard_map/ppermute | solution.py:70
  1042.3 18.0 %collective-permute-done.63 = bf16[2,32,2048]{2,1,0:T(8,128)(2,1)S(1)} collective-permute-done((bf16[2,32,2048]{2,1,0:T(8,128)(2,1)S(1)}, bf16[2,32,2048]{2,1,0:T(8,128)(2,1)S(1)}, u32[]{:S(2)}, u32[]{:S(2)}) %collective-permute-start.63) | collective-permute-done | bytes 262176 | tf_op jit(solution)/shard_map/ppermute | solution.py:70
  (607 shorter events, 399.1 us)
Async XLA Ops:
  482.7 105.0 %collective-permute-start.29 = (bf16[512,1024]{1,0:T(8,128)(2,1)}, bf16[512,1024]{1,0:T(8,128)(2,1)}, u32[]{:S(2)}, u32[]{:S(2)}) collective-permute-start(bf16[512,1024]{1,0:T(8,128)(2,1)} %multiply_convert_fusion.7), channel_id=1, source_target_pairs={{0,4},{1,5},{2,6},{3,7},{4,0},{5,1},{6,2},{7,3},{8,12},{9,13},{10,... | collective-permute-start | bytes 3145736 | tf_op jit(solution)/shard_map/ppermute | solution.py:70
  504.6 86.7 %collective-permute-start.47 = (bf16[512,1024]{1,0:T(8,128)(2,1)}, bf16[512,1024]{1,0:T(8,128)(2,1)}, u32[]{:S(2)}, u32[]{:S(2)}) collective-permute-start(bf16[512,1024]{1,0:T(8,128)(2,1)} %multiply_convert_fusion.8), channel_id=1, source_target_pairs={{0,4},{1,5},{2,6},{3,7},{4,0},{5,1},{6,2},{7,3},{8,12},{9,13},{10,... | collective-permute-start | bytes 3145736 | tf_op jit(solution)/shard_map/ppermute | solution.py:70
  506.9 88.9 %collective-permute-start.50 = (bf16[512,1024]{1,0:T(8,128)(2,1)S(1)}, bf16[512,1024]{1,0:T(8,128)(2,1)}, u32[]{:S(2)}, u32[]{:S(2)}) collective-permute-start(bf16[512,1024]{1,0:T(8,128)(2,1)S(1)} %shard_map.155), channel_id=1, source_target_pairs={{0,4},{1,5},{2,6},{3,7},{4,0},{5,1},{6,2},{7,3},{8,12},{9,13},{10,... | collective-permute-start | bytes 3145736 | tf_op jit(solution)/shard_map/ppermute | solution.py:70
  575.8 39.1 %collective-permute-start.18 = (bf16[2,1024,512]{2,1,0:T(8,128)(2,1)}, bf16[2,1024,512]{2,1,0:T(8,128)(2,1)}, u32[]{:S(2)}, u32[]{:S(2)}) collective-permute-start(bf16[2,1024,512]{2,1,0:T(8,128)(2,1)} %pad_maximum_fusion.12), channel_id=1, source_target_pairs={{0,4},{1,5},{2,6},{3,7},{4,0},{5,1},{6,2},{7,3},{8,12},{9,13},{10,... | collective-permute-start | bytes 6291464 | tf_op jit(solution)/shard_map/ppermute | solution.py:70
  591.3 28.2 %collective-permute-start.31 = (bf16[1408,512]{1,0:T(8,128)(2,1)S(1)}, bf16[1408,512]{1,0:T(8,128)(2,1)S(1)}, u32[]{:S(2)}, u32[]{:S(2)}) collective-permute-start(bf16[1408,512]{1,0:T(8,128)(2,1)S(1)} %copy-done.65), channel_id=1, source_target_pairs={{0,8},{1,9},{2,10},{3,11},{4,20},{5,21},{6,22},{7,23},{8,0},{9,1},... | collective-permute-start | bytes 4325384 | tf_op jit(solution)/shard_map/ppermute | solution.py:70
  614.2 80.0 %collective-permute-start.17 = (bf16[2,512,1024]{2,1,0:T(8,128)(2,1)}, bf16[2,512,1024]{2,1,0:T(8,128)(2,1)}, u32[]{:S(2)}, u32[]{:S(2)}) collective-permute-start(bf16[2,512,1024]{2,1,0:T(8,128)(2,1)} %get-tuple-element.87), channel_id=1, source_target_pairs={{0,4},{1,5},{2,6},{3,7},{4,0},{5,1},{6,2},{7,3},{8,12},{9,13},{10,... | collective-permute-start | bytes 6291464 | tf_op jit(solution)/shard_map/ppermute | solution.py:70
  614.9 106.4 %collective-permute-start.33 = (bf16[512,2816]{1,0:T(8,128)(2,1)}, bf16[512,2816]{1,0:T(8,128)(2,1)}, u32[]{:S(2)}, u32[]{:S(2)}) collective-permute-start(bf16[512,2816]{1,0:T(8,128)(2,1)} %convolution_convert_fusion.3), channel_id=1, source_target_pairs={{0,8},{1,9},{2,10},{3,11},{4,20},{5,21},{6,22},{7,23},{8,0},{9,1},... | collective-permute-start | bytes 8650760 | tf_op jit(solution)/shard_map/ppermute | solution.py:70
  618.8 54.9 %collective-permute-start.24 = (bf16[2,128,512]{2,1,0:T(8,128)(2,1)S(1)}, bf16[2,128,512]{2,1,0:T(8,128)(2,1)S(1)}, u32[]{:S(2)}, u32[]{:S(2)}) collective-permute-start(bf16[2,128,512]{2,1,0:T(8,128)(2,1)S(1)} %get-tuple-element.171), channel_id=1, source_target_pairs={{0,8},{1,9},{2,10},{3,11},{4,12},{5,13},{6,14},{7,15},{8,16},{9,17... | collective-permute-start | bytes 786440 | tf_op jit(solution)/shard_map/ppermute | solution.py:70
  619.5 54.2 %collective-permute-start.23 = (bf16[2,128,512]{2,1,0:T(8,128)(2,1)S(1)}, bf16[2,128,512]{2,1,0:T(8,128)(2,1)S(1)}, u32[]{:S(2)}, u32[]{:S(2)}) collective-permute-start(bf16[2,128,512]{2,1,0:T(8,128)(2,1)S(1)} %get-tuple-element.172), channel_id=1, source_target_pairs={{0,9},{1,16},{2,11},{3,18},{4,13},{5,20},{6,15},{7,22},{8,17},{9,2... | collective-permute-start | bytes 786440 | tf_op jit(solution)/shard_map/ppermute | solution.py:70
  629.8 49.6 %collective-permute-start.22 = (bf16[2,128,512]{2,1,0:T(8,128)(2,1)S(1)}, bf16[2,128,512]{2,1,0:T(8,128)(2,1)S(1)}, u32[]{:S(2)}, u32[]{:S(2)}) collective-permute-start(bf16[2,128,512]{2,1,0:T(8,128)(2,1)S(1)} %get-tuple-element.173), channel_id=1, source_target_pairs={{0,16},{1,17},{2,18},{3,19},{4,20},{5,21},{6,22},{7,23},{8,24},{9,... | collective-permute-start | bytes 786440 | tf_op jit(solution)/shard_map/ppermute | solution.py:70
  690.9 113.4 %collective-permute-start.45 = (bf16[512,2816]{1,0:T(8,128)(2,1)}, bf16[512,2816]{1,0:T(8,128)(2,1)}, u32[]{:S(2)}, u32[]{:S(2)}) collective-permute-start(bf16[512,2816]{1,0:T(8,128)(2,1)} %multiply_convert_fusion.5), channel_id=1, source_target_pairs={{0,4},{1,5},{2,6},{3,7},{4,0},{5,1},{6,2},{7,3},{8,12},{9,13},{10,... | collective-permute-start | bytes 8650760 | tf_op jit(solution)/shard_map/ppermute | solution.py:70
  744.4 35.6 %collective-permute-start.39 = (bf16[2,88,512]{2,1,0:T(8,128)(2,1)}, bf16[2,88,512]{2,1,0:T(8,128)(2,1)}, u32[]{:S(2)}, u32[]{:S(2)}) collective-permute-start(bf16[2,88,512]{2,1,0:T(8,128)(2,1)} %get-tuple-element.222), channel_id=1, source_target_pairs={{0,3},{1,0},{2,1},{3,2},{4,7},{5,4},{6,5},{7,6},{8,11},{9,8},{10,9... | collective-permute-start | bytes 540680 | tf_op jit(solution)/shard_map/ppermute | solution.py:70
  744.4 36.0 %collective-permute-start.38 = (bf16[2,88,512]{2,1,0:T(8,128)(2,1)}, bf16[2,88,512]{2,1,0:T(8,128)(2,1)}, u32[]{:S(2)}, u32[]{:S(2)}) collective-permute-start(bf16[2,88,512]{2,1,0:T(8,128)(2,1)} %get-tuple-element.223), channel_id=1, source_target_pairs={{0,2},{1,3},{2,0},{3,1},{4,6},{5,7},{6,4},{7,5},{8,10},{9,11},{10,... | collective-permute-start | bytes 540680 | tf_op jit(solution)/shard_map/ppermute | solution.py:70
  746.9 34.2 %collective-permute-start.37 = (bf16[2,88,512]{2,1,0:T(8,128)(2,1)}, bf16[2,88,512]{2,1,0:T(8,128)(2,1)}, u32[]{:S(2)}, u32[]{:S(2)}) collective-permute-start(bf16[2,88,512]{2,1,0:T(8,128)(2,1)} %get-tuple-element.221), channel_id=1, source_target_pairs={{0,1},{1,2},{2,3},{3,0},{4,5},{5,6},{6,7},{7,4},{8,9},{9,10},{10,1... | collective-permute-start | bytes 540680 | tf_op jit(solution)/shard_map/ppermute | solution.py:70
  747.9 38.0 %collective-permute-start.43 = (bf16[2,32,2816]{2,1,0:T(8,128)(2,1)}, bf16[2,32,2816]{2,1,0:T(8,128)(2,1)S(1)}, u32[]{:S(2)}, u32[]{:S(2)}) collective-permute-start(bf16[2,32,2816]{2,1,0:T(8,128)(2,1)} %get-tuple-element.189), channel_id=1, source_target_pairs={{0,3},{1,0},{2,1},{3,2},{4,7},{5,4},{6,5},{7,6},{8,11},{9,8},{10,9... | collective-permute-start | bytes 1081352 | tf_op jit(solution)/shard_map/ppermute | solution.py:70
  784.0 29.8 %collective-permute-start.35 = (bf16[512,2048]{1,0:T(8,128)(2,1)S(1)}, bf16[512,2048]{1,0:T(8,128)(2,1)S(1)}, u32[]{:S(2)}, u32[]{:S(2)}) collective-permute-start(bf16[512,2048]{1,0:T(8,128)(2,1)S(1)} %copy-done.62), channel_id=1, source_target_pairs={{0,8},{1,9},{2,10},{3,11},{4,20},{5,21},{6,22},{7,23},{8,0},{9,1},... | collective-permute-start | bytes 6291464 | tf_op jit(solution)/shard_map/ppermute | solution.py:70
  859.6 66.8 %collective-permute-start.56 = (bf16[512,2816]{1,0:T(8,128)(2,1)}, bf16[512,2816]{1,0:T(8,128)(2,1)}, u32[]{:S(2)}, u32[]{:S(2)}) collective-permute-start(bf16[512,2816]{1,0:T(8,128)(2,1)} %convolution_convert_fusion.1), channel_id=1, source_target_pairs={{0,8},{1,9},{2,10},{3,11},{4,20},{5,21},{6,22},{7,23},{8,0},{9,1},... | collective-permute-start | bytes 8650760 | tf_op jit(solution)/shard_map/ppermute | solution.py:70
  880.0 41.3 %collective-permute-start.55 = (bf16[704,512]{1,0:T(8,128)(2,1)S(1)}, bf16[704,512]{1,0:T(8,128)(2,1)S(1)}, u32[]{:S(2)}, u32[]{:S(2)}) collective-permute-start(bf16[704,512]{1,0:T(8,128)(2,1)S(1)} %slice_bitcast_fusion.10), channel_id=1, source_target_pairs={{0,16},{1,17},{2,18},{3,19},{4,12},{5,13},{6,14},{7,15},{8,24},{9,... | collective-permute-start | bytes 2162696 | tf_op jit(solution)/shard_map/ppermute | solution.py:70
  903.8 28.2 %collective-permute-start.53 = (bf16[512,1536]{1,0:T(8,128)(2,1)S(1)}, bf16[512,1536]{1,0:T(8,128)(2,1)S(1)}, u32[]{:S(2)}, u32[]{:S(2)}) collective-permute-start(bf16[512,1536]{1,0:T(8,128)(2,1)S(1)} %get-tuple-element.139), channel_id=1, source_target_pairs={{0,4},{1,5},{2,6},{3,7},{4,0},{5,1},{6,2},{7,3},{8,12},{9,13},{10,... | collective-permute-start | bytes 4718600 | tf_op jit(solution)/shard_map/ppermute | solution.py:70
  951.9 54.8 %collective-permute-start.58 = (bf16[256,1024]{1,0:T(8,128)(2,1)S(1)}, bf16[256,1024]{1,0:T(8,128)(2,1)S(1)}, u32[]{:S(2)}, u32[]{:S(2)}) collective-permute-start(bf16[256,1024]{1,0:T(8,128)(2,1)S(1)} %get-tuple-element.200), channel_id=1, source_target_pairs={{0,0},{1,4},{2,3},{3,7},{4,1},{5,5},{6,2},{7,6},{8,8},{9,12},{10,1... | collective-permute-start | bytes 1572872 | tf_op jit(solution)/shard_map/ppermute | solution.py:70
  952.6 66.1 %collective-permute-start.60 = (bf16[512,2048]{1,0:T(8,128)(2,1)S(1)}, bf16[512,2048]{1,0:T(8,128)(2,1)S(1)}, u32[]{:S(2)}, u32[]{:S(2)}) collective-permute-start(bf16[512,2048]{1,0:T(8,128)(2,1)S(1)} %pad_maximum_fusion.15), channel_id=1, source_target_pairs={{0,8},{1,9},{2,10},{3,11},{4,20},{5,21},{6,22},{7,23},{8,0},{9,1},... | collective-permute-start | bytes 6291464 | tf_op jit(solution)/shard_map/ppermute | solution.py:70
  962.8 43.6 %collective-permute-start.71 = (bf16[2,32,2816]{2,1,0:T(8,128)(2,1)S(1)}, bf16[2,32,2816]{2,1,0:T(8,128)(2,1)S(1)}, u32[]{:S(2)}, u32[]{:S(2)}) collective-permute-start(bf16[2,32,2816]{2,1,0:T(8,128)(2,1)S(1)} %get-tuple-element.187), channel_id=1, source_target_pairs={{0,2},{1,3},{2,0},{3,1},{4,6},{5,7},{6,4},{7,5},{8,10},{9,11},{10,... | collective-permute-start | bytes 1081352 | tf_op jit(solution)/shard_map/ppermute | solution.py:70
  963.9 42.5 %collective-permute-start.70 = (bf16[2,32,2816]{2,1,0:T(8,128)(2,1)S(1)}, bf16[2,32,2816]{2,1,0:T(8,128)(2,1)S(1)}, u32[]{:S(2)}, u32[]{:S(2)}) collective-permute-start(bf16[2,32,2816]{2,1,0:T(8,128)(2,1)S(1)} %get-tuple-element.185), channel_id=1, source_target_pairs={{0,1},{1,2},{2,3},{3,0},{4,5},{5,6},{6,7},{7,4},{8,9},{9,10},{10,1... | collective-permute-start | bytes 1081352 | tf_op jit(solution)/shard_map/ppermute | solution.py:70
  974.6 42.5 %collective-permute-start.59 = (bf16[256,1024]{1,0:T(8,128)(2,1)S(1)}, bf16[256,1024]{1,0:T(8,128)(2,1)S(1)}, u32[]{:S(2)}, u32[]{:S(2)}) collective-permute-start(bf16[256,1024]{1,0:T(8,128)(2,1)S(1)} %get-tuple-element.201), channel_id=1, source_target_pairs={{0,3},{1,7},{2,0},{3,4},{4,2},{5,6},{6,1},{7,5},{8,11},{9,15},{10,... | collective-permute-start | bytes 1572872 | tf_op jit(solution)/shard_map/ppermute | solution.py:70
  (184 other events, 2122.7 us)

commit v3 on v2

v3 whole, which is shorter than its diff:
```python
import functools
import math

import jax
import jax.numpy as jnp
from jax import lax
from jax.experimental import pallas as pl
from jax.experimental.pallas import tpu as pltpu
from jax.sharding import PartitionSpec as P

HEAD_DIM = 128
SEG = 1024
MICRO = 2
EPSILON = 1e-06
MASKED = -1e30
SCALE = HEAD_DIM ** (-0.5)
LOG2E = 1.0 / math.log(2.0)
BF = jnp.bfloat16
F32 = jnp.float32
VMEM_LIMIT = 48 * 1024 * 1024


def slot_layout(lengths):
    slot_total = lengths.shape[0]
    slot_counts = ((lengths + SEG - 1) // SEG).astype(jnp.int32)
    slot_starts = (jnp.cumsum(slot_counts) - slot_counts).astype(jnp.int32)
    slot_index = jnp.arange(slot_total, dtype=jnp.int32)
    started = (slot_starts[None, :] <= slot_index[:, None]) & (slot_counts[None, :] > 0)
    owner_doc = (jnp.sum(started.astype(jnp.int32), axis=1) - 1).astype(jnp.int32)
    owner_pick = slot_index[None, :] == owner_doc[:, None]
    first_slot = jnp.sum(jnp.where(owner_pick, slot_starts[None, :], 0), axis=1).astype(jnp.int32)
    doc_total = jnp.sum(jnp.where(owner_pick, lengths[None, :], 0), axis=1).astype(jnp.int32)
    valid_rows = jnp.clip(doc_total - (slot_index - first_slot) * SEG, 0, SEG).astype(jnp.int32)
    return (valid_rows, owner_doc)


def memory_plan(lengths, partner_row):
    valid_rows, owner_doc = slot_layout(lengths)
    block_ids = jnp.arange(lengths.shape[0], dtype=jnp.int32)
    earlier = (block_ids[None, :] < block_ids[:, None]) & (owner_doc[None, :] == owner_doc[:, None])
    visible = earlier | (block_ids[None, :] == partner_row[:, None])
    return (valid_rows, visible)


class Grid:
    def __init__(self, n_dp, pieces):
        self.n_dp, self.F = n_dp, pieces
        self.J = n_dp // 2
        self.bits = self.J.bit_length() - 1
        self.Q = pieces // 4
        self.U = 2 * self.Q
        self.R = SEG // pieces
        self.T = 2 * self.R

    def trace(self):
        dp = lax.axis_index("dp")
        self.c, self.j, self.f = dp % 2, dp // 2, lax.axis_index("fsdp")
        self.q, self.g = self.f // self.Q, self.f % self.Q
        self.m, self.r = self.q // 2, self.q % 2
        self.k = self.c * self.Q + self.g
        self.slot = 2 * self.j + self.r

    def permute(self, value, target):
        pairs = []
        for j in range(self.J):
            for c in range(2):
                for f in range(self.F):
                    j2, c2, f2 = target(j, c, f)
                    pairs.append(((j * 2 + c) * self.F + f, (j2 * 2 + c2) * self.F + f2))
        return lax.ppermute(value, ("dp", "fsdp"), pairs)

    def swap(self, value):
        return self.permute(value, lambda j, c, f: (j, 1 - c, f))

    def ring(self, value, t):
        return self.permute(value, lambda j, c, f: (j, c, (f + t) % self.F))

    def bit(self, phase, c):
        return phase if c == 0 else self.bits - 1 - phase

    def flip(self, value, phase):
        return self.permute(value, lambda j, c, f: (j ^ (1 << self.bit(phase, c)), c, f))

    def mask(self, key, c):
        return sum(1 << self.bit(p, c) for p in range(self.bits) if key >> p & 1)

    def place(self, key, c):
        return jnp.where(c == 0, self.j ^ self.mask(key, 0), self.j ^ self.mask(key, 1))

    def member(self, value, t):
        def target(j, c, f):
            q, g = f // self.Q, f % self.Q
            k = (c * self.Q + g + t) % self.U
            return (j, k // self.Q, q * self.Q + k % self.Q)

        return self.permute(value, target)

    def within(self, value, t):
        return self.permute(
            value, lambda j, c, f: (j, c, f // self.Q * self.Q + (f % self.Q + t) % self.Q)
        )

    def slots(self, value, t):
        def target(j, c, f):
            q, g = f // self.Q, f % self.Q
            slot = (2 * j + q % 2 + t) % self.n_dp
            return (slot // 2, c, (2 * (q // 2) + slot % 2) * self.Q + g)

        return self.permute(value, target)

    def _spread(self, second):
        def target(j, c, f):
            m = f // (self.F // 2)
            m = 1 - m if second else m
            k = min(f, self.F - 1 - f)
            return (j, k // self.Q, (2 * m + c) * self.Q + k % self.Q)

        return target

    def _collect(self, second):
        there = self._spread(second)
        back = {
            there(0, c, f): (c, f) for c in range(2) for f in range(self.F)
        }
        return lambda j, c, f: (j,) + back[(0, c, f)]

    def to_units(self, value):
        here = self.f // (self.F // 2)
        first = self.permute(jnp.where(here == 0, value[0], value[1]), self._spread(False))
        second = self.permute(jnp.where(here == 0, value[1], value[0]), self._spread(True))
        return jnp.concatenate(
            [jnp.where(self.m == 0, first, second), jnp.where(self.m == 0, second, first)]
        )

    def from_units(self, value):
        low, high = value[: self.R], value[self.R :]
        first = self.permute(jnp.where(self.m == 0, low, high), self._collect(False))
        second = self.permute(jnp.where(self.m == 0, high, low), self._collect(True))
        here = self.f // (self.F // 2)
        return jnp.stack([jnp.where(here == 0, first, second), jnp.where(here == 0, second, first)])


def any_spec():
    return pl.BlockSpec(memory_space=pl.ANY)


MESH = pl.DeviceIdType.MESH


class Here:
    def __init__(self, grid):
        self.grid = grid
        dp = lax.axis_index("dp")
        self.j, self.c, self.f = dp // 2, dp % 2, lax.axis_index("fsdp")
        self.q, self.g = self.f // grid.Q, self.f % grid.Q
        self.m, self.r = self.q // 2, self.q % 2
        self.k = self.c * grid.Q + self.g
        self.swap = self.device(self.j, 1 - self.c, self.f)

    def device(self, j, c, f):
        return {"dp": 2 * j + c, "fsdp": f}

    def ring(self, t):
        return self.device(self.j, self.c, (self.f + t) % self.grid.F)

    def step(self, phase):
        first, second = (1 << self.grid.bit(phase, c) for c in (0, 1))
        return first + self.c * (second - first)

    def moved(self, j, phase):
        step = self.step(phase)
        return j + step * (1 - 2 * ((j // step) % 2))

    def flip(self, phase):
        return self.device(self.moved(self.j, phase), self.c, self.f)

    def slots(self, t):
        grid = self.grid
        slot = (2 * self.j + self.r + t) % grid.n_dp
        return self.device(slot // 2, self.c, (2 * self.m + slot % 2) * grid.Q + self.g)

    def member(self, t):
        grid = self.grid
        k = (self.k + t) % grid.U
        return self.device(self.j, k // grid.Q, self.q * grid.Q + k % grid.Q)

    def place(self, key):
        j = self.j
        for phase in range(self.grid.bits):
            if key >> phase & 1:
                j = self.moved(j, phase)
        return j

    def greet(self):
        grid = self.grid
        barrier = pltpu.get_barrier_semaphore()
        peers = [self.ring(t) for t in range(1, grid.F)]
        peers += [self.device(self.j, 1 - self.c, (self.f + t) % grid.F) for t in range(grid.F)]
        for bit in range(grid.bits):
            step = 1 << bit
            peers.append(self.device(self.j + step * (1 - 2 * ((self.j // step) % 2)), self.c, self.f))
        for peer in peers:
            pl.semaphore_signal(barrier, inc=1, device_id=peer, device_id_type=MESH)
        pl.semaphore_wait(barrier, len(peers))


def remote(source, target, sems, index, device):
    return pltpu.make_async_remote_copy(
        src_ref=source,
        dst_ref=target,
        send_sem=sems.at[0, index],
        recv_sem=sems.at[1, index],
        device_id=device,
        device_id_type=MESH,
    )


class Spread:
    def __init__(self, here, shard, whole, sems, own_sem, split):
        grid = here.grid
        self.here, self.split = here, split
        rows, width = shard.shape
        half = width // 2 if split else width

        def part(ref, c):
            if not split:
                return ref
            return ref.at[(slice(None),) * (len(ref.shape) - 1) + (pl.ds(pl.multiple_of(c * half, 128), half),)]

        j, c, f = here.j, here.c, here.f
        mine = part(whole, c)
        self.own = pltpu.make_async_copy(part(shard, c), part(whole.at[j, c, f], c), own_sem)
        other = 1 - c if split else c
        self.pre = remote(part(shard, other), part(whole.at[j, c, f], other), sems, 0, here.swap)
        at = 1
        self.line = []
        for t in range(1, grid.F):
            block = mine.at[j, :, f]
            self.line.append(remote(block, block, sems, at, here.ring(t)))
            at += 1
        self.flips = []
        for phase in range(grid.bits):
            sent = []
            for key in range(1 << phase):
                block = mine.at[here.place(key)]
                sent.append(remote(block, block, sems, at, here.flip(phase)))
                at += 1
            self.flips.append(sent)
        self.swaps = []
        for key in range(grid.J if split else 0):
            block = mine.at[here.place(key)]
            self.swaps.append(remote(block, block, sems, at, here.swap))
            at += 1

    @staticmethod
    def count(grid):
        return 1 + (grid.F - 1) + (grid.J - 1) + grid.J

    def begin(self):
        self.own.start()
        self.pre.start()

    def to_line(self):
        self.own.wait()
        self.pre.wait()
        for copy in self.line:
            copy.start()

    def _send(self, keys):
        for key in keys:
            if self.swaps:
                self.swaps[key].start()
        for phase, sent in enumerate(self.flips):
            for key in keys:
                if key < 1 << phase:
                    sent[key].start()

    def steps(self):
        def first():
            for copy in self.line:
                copy.wait()
            self._send([0])

        def later(phase):
            for copy in self.flips[phase]:
                copy.wait()
            self._send([key + (1 << phase) for key in range(1 << phase)])

        def last():
            for copy in self.swaps:
                copy.wait()

        return [first] + [functools.partial(later, p) for p in range(len(self.flips))] + [last]


class Regroup:
    def __init__(self, here, source, target, sems, own_sem):
        grid = here.grid
        half = grid.F // 2
        k = jnp.minimum(here.f, grid.F - 1 - here.f)
        side = here.f // half
        self.sends = []
        for m in range(2):
            c2, f2 = k // grid.Q, (2 * m + here.c) * grid.Q + k % grid.Q
            same = (c2 == here.c) & (f2 == here.f)
            own = pltpu.make_async_copy(source.at[m], target.at[side], own_sem)
            away = pltpu.make_async_remote_copy(
                src_ref=source.at[m],
                dst_ref=target.at[side],
                send_sem=sems.at[0, m],
                recv_sem=sems.at[1, side],
                device_id=here.device(here.j, c2, f2),
                device_id_type=MESH,
            )
            self.sends.append((same, own, away))
        self.arrivals = []
        for side in range(2):
            from_f = here.k if side == 0 else grid.F - 1 - here.k
            same = (here.r == here.c) & (from_f == here.f)
            came = pltpu.make_async_remote_copy(
                src_ref=source.at[0],
                dst_ref=target.at[side],
                send_sem=sems.at[0, 0],
                recv_sem=sems.at[1, side],
                device_id=here.swap,
                device_id_type=MESH,
            )
            self.arrivals.append((same, came))

    def start(self):
        for same, own, away in self.sends:
            pl.when(same)(own.start)
            pl.when(jnp.logical_not(same))(away.start)

    def wait(self):
        for same, own, away in self.sends:
            pl.when(same)(own.wait)
            pl.when(jnp.logical_not(same))(away.wait_send)
        for same, came in self.arrivals:
            pl.when(jnp.logical_not(same))(came.wait_recv)


def gather_body(grid, layers, kinds, *refs):
    tokens, cotangent, gains = refs[:3]
    shards = refs[3 : 3 + kinds]
    outs = refs[3 + kinds :]
    tokens_out, cotangent_out, gains_out = outs[:3]
    wholes = outs[3 : 3 + layers * kinds]
    sems, own_sems, regroup_sems = outs[3 + layers * kinds :]
    here = Here(grid)
    here.greet()
    rows = Regroup(here, tokens, tokens_out, regroup_sems.at[0], own_sems.at[0])
    rows_back = Regroup(here, cotangent, cotangent_out, regroup_sems.at[1], own_sems.at[1])
    moves = [Spread(here, gains, gains_out, sems.at[0], own_sems.at[2], False)]
    for l in range(layers):
        for i in range(kinds):
            n = l * kinds + i
            moves.append(
                Spread(here, shards[i].at[l], wholes[n], sems.at[n + 1], own_sems.at[n + 3], True)
            )
    for move in moves:
        move.begin()
    rows.start()
    steps = [move.steps() for move in moves]
    count = len(steps[0])
    moves[0].to_line()
    moves[1].to_line()
    for at in range(len(moves) + count - 1):
        if at + 2 < len(moves):
            moves[at + 2].to_line()
        if at == len(moves) - 3:
            rows_back.start()
        for back in range(count):
            if 0 <= at - back < len(moves):
                steps[at - back][back]()
    rows.wait()
    rows_back.wait()


def gather_all(grid, tokens, cotangent, gains, shards):
    layers, kinds = shards[0].shape[0], len(shards)
    packed = jnp.zeros((8, 128), F32).at[: layers * 2, : gains.shape[2]].set(
        gains.astype(F32).reshape(layers * 2, -1)
    )
    whole = lambda shard: jax.ShapeDtypeStruct((grid.J, 2, grid.F) + shard.shape[-2:], shard.dtype)
    out_shape = [jax.ShapeDtypeStruct(tokens.shape, BF), jax.ShapeDtypeStruct(tokens.shape, BF), whole(packed)]
    out_shape += [whole(shard) for _ in range(layers) for shard in shards]
    moves = 1 + layers * kinds
    outs = pl.pallas_call(
        functools.partial(gather_body, grid, layers, kinds),
        in_specs=[any_spec()] * (3 + kinds),
        out_specs=[any_spec()] * len(out_shape),
        out_shape=out_shape,
        scratch_shapes=[
            pltpu.SemaphoreType.DMA((moves, 2, Spread.count(grid))),
            pltpu.SemaphoreType.DMA((moves + 2,)),
            pltpu.SemaphoreType.DMA((2, 2, 2)),
        ],
        compiler_params=pltpu.CompilerParams(
            collective_id=0, has_side_effects=True, vmem_limit_bytes=VMEM_LIMIT
        ),
    )(tokens, cotangent, packed, *shards)
    width = tokens.shape[2]
    gains_all = outs[2][..., : layers * 2, : gains.shape[2]]
    gains_all = jnp.moveaxis(gains_all, 3, 0).reshape(layers, 2, -1)
    weights = [
        [outs[3 + l * kinds + i].reshape(-1, shards[i].shape[2]) for i in range(kinds)]
        for l in range(layers)
    ]
    return outs[0].reshape(-1, width), outs[1].reshape(-1, width), gains_all, weights


class Move:
    def __init__(self, array, shape, count, copies):
        self.array, self.shape, self.count, self.copies = array, shape, count, copies


def flip_move(grid, parts, phase):
    count = parts.shape[0] // 2

    def copies(here, source, target):
        found = []
        for i in range(count):
            at = here.place(2 * i + 1) if phase == 0 else 2 * i + 1
            peer = here.flip(phase)
            found.append((source.at[at], target.at[i], peer, peer))
        return found

    return Move(parts, (count,) + parts.shape[1:], count, copies)


def ring_move(grid, line):
    def copies(here, source, target):
        return [
            (source.at[:, (here.f + t) % grid.F], target.at[t - 1], here.ring(t), here.ring(grid.F - t))
            for t in range(1, grid.F)
        ]

    return Move(line, (grid.F - 1, 2) + line.shape[2:], grid.F - 1, copies)


def swap_move(array, give=None):
    def copies(here, source, target):
        return [(source if give is None else source.at[give(here)], target, here.swap, here.swap)]

    return Move(array, array.shape if give is None else array.shape[1:], 1, copies)


def slots_move(grid, array, back):
    def copies(here, source, target):
        found = []
        for t in range(1, grid.n_dp):
            ahead, behind = here.slots(t), here.slots(grid.n_dp - t)
            if back:
                found.append((source.at[:, t], target.at[t - 1], behind, ahead))
            else:
                found.append((source, target.at[t - 1], ahead, behind))
        return found

    shape = array.shape if not back else array.shape[:1] + array.shape[2:]
    return Move(array, (grid.n_dp - 1,) + shape, grid.n_dp - 1, copies)


def member_move(grid, array, back):
    def copies(here, source, target):
        found = []
        for t in range(1, grid.U):
            ahead, behind = here.member(t), here.member(grid.U - t)
            if back:
                found.append((source.at[t - 1], target.at[t - 1], behind, ahead))
            else:
                found.append((source, target.at[t - 1], ahead, behind))
        return found

    shape = array.shape[1:] if back else array.shape
    return Move(array, (grid.U - 1,) + shape, grid.U - 1, copies)


IDS = [1]


def host(grid, body, steps, in_specs, operands, out_specs, out_shape, moves=(), scratch=(), cost=None, first=None):
    counts = [len(operands), len(moves), len(out_shape), len(moves), len(scratch)]

    def kernel(*refs):
        parts, at = [], 0
        for count in counts:
            parts.append(refs[at : at + count])
            at += count
        ins, sources, outs, targets, held = parts
        here = Here(grid)
        step = pl.program_id(0)
        copies = []
        if moves:
            send_sems, recv_sems = refs[at:]
            listed = [c for m, s, t in zip(moves, sources, targets) for c in m.copies(here, s, t)]
            for i, (source, target, peer, _) in enumerate(listed):
                copies.append(
                    pltpu.make_async_remote_copy(
                        src_ref=source,
                        dst_ref=target,
                        send_sem=send_sems.at[i],
                        recv_sem=recv_sems.at[i],
                        device_id=peer,
                        device_id_type=MESH,
                    )
                )

            @pl.when(step == 0)
            def _():
                barrier = pltpu.get_barrier_semaphore()
                for _, _, _, peer in listed:
                    pl.semaphore_signal(barrier, inc=1, device_id=peer, device_id_type=MESH)
                pl.semaphore_wait(barrier, len(listed))
                for copy in copies:
                    copy.start()

        if body is not None:
            body(here, step, ins, outs, held)
        if moves:

            @pl.when(step == steps - 1)
            def _():
                for copy in copies:
                    copy.wait()

    total = sum(move.count for move in moves)
    extra = {}
    sems = []
    if moves:
        extra = {"collective_id": IDS[0], "has_side_effects": True}
        IDS[0] += 1
        sems = [pltpu.SemaphoreType.DMA((total,)), pltpu.SemaphoreType.DMA((total,))]
    outs = pl.pallas_call(
        kernel,
        grid=(steps,),
        in_specs=list(in_specs) + [any_spec()] * len(moves),
        out_specs=list(out_specs) + [any_spec()] * len(moves),
        out_shape=list(out_shape) + [jax.ShapeDtypeStruct(m.shape, m.array.dtype) for m in moves],
        scratch_shapes=list(scratch) + sems,
        compiler_params=pltpu.CompilerParams(vmem_limit_bytes=VMEM_LIMIT, **extra),
        cost_estimate=cost,
    )(*operands, *[move.array for move in moves])
    return outs[: len(out_shape)], outs[len(out_shape) :]


def send(grid, moves):
    return host(grid, None, 1, [], [], [], [], moves)[1]


def scatter_gains(grid, total):
    layers, kinds, width = total.shape
    devices = grid.n_dp * grid.F
    total = total + grid.swap(total)
    for p in range(grid.bits):
        total = total + grid.permute(total, lambda j, c, f: (j ^ (1 << p), c, f))
    for step in [1 << p for p in range(grid.F.bit_length() - 1)]:
        total = total + grid.permute(total, lambda j, c, f: (j, c, f ^ step))
    here = (grid.j * 2 + grid.c) * grid.F + grid.f
    return lax.dynamic_slice_in_dim(total, here * (width // devices), width // devices, axis=2)


def rope_tables():
    half_dim = HEAD_DIM // 2
    frequency = jnp.exp(
        jnp.arange(half_dim, dtype=F32) * (-2.0 * math.log(10000.0) / HEAD_DIM)
    )
    angles = jnp.arange(SEG, dtype=jnp.int32).astype(F32)[:, None] * frequency[None, :]
    cos, sin = jnp.cos(angles), jnp.sin(angles)
    return (jnp.concatenate([cos, cos], axis=-1), jnp.concatenate([-sin, sin], axis=-1))


def turn(values, cos, sin):
    return values * cos + pltpu.roll(values, HEAD_DIM // 2, 1) * sin


def smem():
    return pl.BlockSpec(memory_space=pltpu.SMEM)


def whole_spec(*shape):
    return pl.BlockSpec(shape, lambda i: (0,) * len(shape))


def columns_spec(*shape, first=0):
    return pl.BlockSpec(shape, lambda i: (0,) * (len(shape) - 1) + (i + first,))


def rows_spec(*shape):
    return pl.BlockSpec(shape, lambda i: (i,) + (0,) * (len(shape) - 1))


def kind(*shape, dtype=BF):
    return jax.ShapeDtypeStruct(shape, dtype)


def piece_start(grid, member, part):
    return (member if part == 0 else grid.F - 1 - member) * grid.R


def table_rows(grid, table_ref, member, part):
    start = pl.multiple_of(piece_start(grid, member, part), grid.R)
    return table_ref[pl.ds(start, grid.R), :]


def dot(left, right, contract):
    return lax.dot_general(
        left, right, (((contract[0],), (contract[1],)), ((), ())), preferred_element_type=F32
    )


def mm(left, right, contract=(1, 0)):
    return dot(left, right, contract)


def split_heads(grid, memory, tables, projected, moves=()):
    rows, width = projected.shape
    heads = width // (3 * HEAD_DIM)
    count = 3 if memory else 2

    def body(here, step, ins, outs, held):
        cos_ref, sin_ref, q_ref, k_ref, v_ref = ins
        for part in range(2):
            at = pl.ds(part * grid.R, grid.R)
            cos = table_rows(grid, cos_ref, here.k, part)
            sin = table_rows(grid, sin_ref, here.k, part)
            query, key = q_ref[at, :], k_ref[at, :]
            outs[0][at, :] = turn(query, cos, sin).astype(BF)
            outs[1][0, at, :] = turn(key, cos, sin).astype(BF)
            outs[1][1, at, :] = v_ref[at, :].astype(BF)
            if memory:
                outs[1][2, at, :] = key.astype(BF)
                outs[2][at, :] = query.astype(BF)

    piece = lambda at: columns_spec(rows, HEAD_DIM, first=at * heads)
    flat = kind(rows, heads * HEAD_DIM)
    table = whole_spec(SEG, HEAD_DIM)
    return host(
        grid,
        body,
        heads,
        [table, table, piece(0), piece(1), piece(2)],
        [*tables, projected, projected, projected],
        [piece(0), columns_spec(count, rows, HEAD_DIM)] + [piece(0)] * memory,
        [flat, kind(count, rows, heads * HEAD_DIM)] + [flat] * memory,
        moves,
        cost=pl.CostEstimate(flops=10 * rows * width, bytes_accessed=8 * rows * width, transcendentals=0),
    )


def part_scores(grid, here, valid, part, query, keys):
    shape = (grid.R, grid.R)
    apart = lax.broadcasted_iota(jnp.int32, shape, 0) - lax.broadcasted_iota(jnp.int32, shape, 1)
    found = []
    for t in range(grid.U):
        member = (here.k - t + grid.U) % grid.U
        for side in range(part + 1):
            score = dot(keys[t][side * grid.R : (side + 1) * grid.R], query, (1, 1))
            if side == part:
                start = piece_start(grid, member, side)
                allowed = apart <= piece_start(grid, here.k, part) - start
                if side == 1:
                    down = lax.broadcasted_iota(jnp.int32, shape, 0)
                    allowed = allowed & (down < valid - start)
                score = jnp.where(allowed, score, MASKED)
            found.append((t, side, score))
    return found


def softmax_parts(scores):
    top = functools.reduce(jnp.maximum, [jnp.max(s, axis=0, keepdims=True) for s in scores])
    powers = [jnp.exp2((s - top) * (SCALE * LOG2E)) for s in scores]
    inverse = 1.0 / sum(jnp.sum(p, axis=0, keepdims=True) for p in powers)
    return [p * inverse for p in powers]


def attention_cost(grid, heads, memory_rows, products):
    pairs = grid.T * (SEG * 3 // 4 + memory_rows) * heads
    return pl.CostEstimate(
        flops=2 * products * HEAD_DIM * pairs,
        bytes_accessed=2 * HEAD_DIM * heads * 4 * (SEG + memory_rows),
        transcendentals=pairs,
    )


def memory_operands(grid, extra):
    rows = extra["keys"].shape[0]
    piece = columns_spec(grid.T, HEAD_DIM)
    column = columns_spec(rows, HEAD_DIM)
    return [extra["query"], extra["keys"], extra["values"], extra["bias"]], [
        piece, column, column, whole_spec(rows, 1)
    ], rows


def attend(grid, valid, query, pairs, extra, moves=()):
    rows, width = query.shape
    heads = width // HEAD_DIM
    R, U = grid.R, grid.U

    def body(here, step, ins, outs, held):
        valid_ref, q_ref, kv_refs, refs = ins[0], ins[1], ins[2 : 2 + U], ins[2 + U :]
        keys, values = [r[0] for r in kv_refs], [r[1] for r in kv_refs]
        for part in range(2):
            at = pl.ds(part * R, R)
            found = part_scores(grid, here, valid_ref[0], part, q_ref[at, :], keys)
            scores = [s for _, _, s in found]
            mixed = [values[t][side * R : (side + 1) * R] for t, side, _ in found]
            if extra is not None:
                scores.append(dot(refs[1][...], refs[0][at, :], (1, 1)) + refs[3][...])
                mixed.append(refs[2][...])
            total = sum(
                dot(value, p.astype(BF), (0, 0)) for value, p in zip(mixed, softmax_parts(scores))
            )
            outs[0][at, :] = total.T.astype(BF)

    piece = columns_spec(rows, HEAD_DIM)
    operands = [valid, query, *pairs]
    specs = [smem(), piece] + [columns_spec(2, rows, HEAD_DIM)] * U
    memory_rows = 0
    if extra is not None:
        more, more_specs, memory_rows = memory_operands(grid, extra)
        operands, specs = operands + more, specs + more_specs
    outs, got = host(
        grid, body, heads, specs, operands, [piece], [kind(rows, width)], moves,
        cost=attention_cost(grid, heads, memory_rows, 2),
    )
    return outs[0], got


def attend_back(grid, valid, tables, query, grad, pairs, extra, moves=()):
    rows, width = query.shape
    heads = width // HEAD_DIM
    R, U = grid.R, grid.U

    def body(here, step, ins, outs, held):
        valid_ref, cos_ref, sin_ref, q_ref, g_ref = ins[:5]
        kv_refs, refs = ins[5 : 5 + U], ins[5 + U :]
        keys, values = [r[0] for r in kv_refs], [r[1] for r in kv_refs]
        grad_keys, grad_values = {}, {}

        def add(store, at, value):
            store[at] = store[at] + value if at in store else value

        for part in range(2):
            at_rows = pl.ds(part * R, R)
            asked, grads_in = q_ref[at_rows, :], g_ref[at_rows, :]
            found = part_scores(grid, here, valid_ref[0], part, asked, keys)
            places = [(t, side) for t, side, _ in found]
            scores = [s for _, _, s in found]
            part_keys = [keys[t][side * R : (side + 1) * R] for t, side in places]
            part_values = [values[t][side * R : (side + 1) * R] for t, side in places]
            queries = [asked] * len(places)
            if extra is not None:
                places.append("memory")
                queries.append(refs[0][at_rows, :])
                scores.append(dot(refs[1][...], queries[-1], (1, 1)) + refs[3][...])
                part_keys.append(refs[1][...])
                part_values.append(refs[2][...])
            probs = softmax_parts(scores)
            grads = [dot(value, grads_in, (1, 1)) for value in part_values]
            inner = sum(jnp.sum(p * d, axis=0, keepdims=True) for p, d in zip(probs, grads))
            local_query, raw_query = None, None
            for at, p, d, key, by in zip(places, probs, grads, part_keys, queries):
                moved = (p * (d - inner)).astype(BF)
                add(grad_keys, at, dot(moved, by, (1, 0)))
                add(grad_values, at, dot(p.astype(BF), grads_in, (1, 0)))
                back = dot(key, moved, (0, 0))
                if at == "memory":
                    raw_query = back
                else:
                    local_query = back if local_query is None else local_query + back
            cos = table_rows(grid, cos_ref, here.k, part)
            sin = table_rows(grid, sin_ref, here.k, part)
            result = turn(local_query.T, cos, -sin)
            if extra is not None:
                result = result + raw_query.T
            outs[0][at_rows, :] = (result * SCALE).astype(BF)
        for t in range(U):
            member = (here.k - t + U) % U
            for side in range(2):
                at_rows = pl.ds(side * R, R)
                cos = table_rows(grid, cos_ref, member, side)
                sin = table_rows(grid, sin_ref, member, side)
                key = turn(grad_keys[(t, side)], cos, -sin) * SCALE
                if t == 0:
                    outs[1][0, at_rows, :] = key
                    outs[1][1, at_rows, :] = grad_values[(t, side)]
                else:
                    outs[2][t - 1, 0, at_rows, :] = key.astype(BF)
                    outs[2][t - 1, 1, at_rows, :] = grad_values[(t, side)].astype(BF)
        if extra is not None:
            outs[3][0] = (grad_keys["memory"] * SCALE).astype(BF)
            outs[3][1] = grad_values["memory"].astype(BF)

    piece = columns_spec(rows, HEAD_DIM)
    pair = columns_spec(2, rows, HEAD_DIM)
    table = whole_spec(SEG, HEAD_DIM)
    operands = [valid, *tables, query, grad, *pairs]
    specs = [smem(), table, table, piece, piece] + [pair] * U
    out_shape = [kind(rows, width), kind(2, rows, width, dtype=F32), kind(U - 1, 2, rows, width)]
    out_specs = [piece, pair, columns_spec(U - 1, 2, rows, HEAD_DIM)]
    memory_rows = 0
    if extra is not None:
        more, more_specs, memory_rows = memory_operands(grid, extra)
        operands, specs = operands + more, specs + more_specs
        out_shape.append(kind(2, memory_rows, width))
        out_specs.append(columns_spec(2, memory_rows, HEAD_DIM))
    return host(
        grid, body, heads, specs, operands, out_specs, out_shape, moves,
        cost=attention_cost(grid, heads, memory_rows, 5),
    )


def pick_memory(grid, picks, stacked, c):
    heads, topk = picks.shape
    per = heads // 2
    R, U = grid.R, grid.U

    def body(info_ref, picks_ref, *refs):
        chosen_from, out_ref = refs[:U], refs[U]
        here = Here(grid)
        picked = picks_ref[0]
        key, value = 0.0, 0.0
        for t in range(U):
            member = (here.k - t + U) % U
            for side in range(2):
                across = lax.broadcasted_iota(jnp.int32, (picked.shape[0], R), 1)
                chosen = (picked == across + piece_start(grid, member, side)).astype(BF)
                at = pl.ds(side * R, R)
                key = key + dot(chosen, chosen_from[t][2, at, :], (1, 0))
                value = value + dot(chosen, chosen_from[t][1, at, :], (1, 0))
        out_ref[0] = key.astype(BF)
        out_ref[1] = value.astype(BF)

    at = lambda h, info: info[0] * per + h
    piece = pl.BlockSpec((3, grid.T, HEAD_DIM), lambda h, info: (0, 0, at(h, info)))
    return pl.pallas_call(
        body,
        grid_spec=pltpu.PrefetchScalarGridSpec(
            num_scalar_prefetch=1,
            grid=(per,),
            in_specs=[pl.BlockSpec((1, topk, 1), lambda h, info: (at(h, info), 0, 0))] + [piece] * U,
            out_specs=pl.BlockSpec((2, topk, HEAD_DIM), lambda h, info: (0, 0, h)),
        ),
        out_shape=kind(2, topk, per * HEAD_DIM),
        compiler_params=pltpu.CompilerParams(vmem_limit_bytes=VMEM_LIMIT),
        cost_estimate=pl.CostEstimate(
            flops=4 * topk * SEG * HEAD_DIM * per, bytes_accessed=4 * SEG * HEAD_DIM * per, transcendentals=0
        ),
    )(c.reshape(1).astype(jnp.int32), picks[:, :, None], *stacked)


def finish_gradient(grid, grad_query, own, others, picks, memory, moves=()):
    rows, width = grad_query.shape
    heads = width // HEAD_DIM
    R, U = grid.R, grid.U

    def body(here, step, ins, outs, held):
        dq_ref, own_ref, others_ref = ins[:3]
        out_ref = outs[0]

        @pl.when(step < heads)
        def _():
            out_ref[...] = dq_ref[...]

        @pl.when(step >= heads)
        def _():
            total = own_ref[0] + sum(others_ref[t, 0].astype(F32) for t in range(U - 1))
            for side in range(2):
                at = slice(side * R, (side + 1) * R)
                value = total[at]
                if memory is not None:
                    picked = ins[3][0]
                    down = lax.broadcasted_iota(jnp.int32, (R, picked.shape[1]), 0)
                    chosen = (down + piece_start(grid, here.k, side) == picked).astype(BF)
                    value = value + dot(chosen, ins[4][0], (1, 0))
                out_ref[at, :] = value.astype(BF)

    which = lambda b: jnp.maximum(b // heads - 1, 0)
    head = lambda b: jnp.where(b < heads, 0, b % heads)
    operands = [grad_query, own, others]
    specs = [
        pl.BlockSpec((rows, HEAD_DIM), lambda b: (0, jnp.minimum(b, heads - 1))),
        pl.BlockSpec((1, rows, HEAD_DIM), lambda b: (which(b), 0, head(b))),
        pl.BlockSpec((U - 1, 1, rows, HEAD_DIM), lambda b: (0, which(b), 0, head(b))),
    ]
    if memory is not None:
        topk = picks.shape[1]
        operands += [picks[:, None, :], memory]
        specs += [
            pl.BlockSpec((1, 1, topk), lambda b: (b % heads, 0, 0)),
            pl.BlockSpec((1, topk, HEAD_DIM), lambda b: (which(b), 0, head(b))),
        ]
    outs, got = host(
        grid, body, 3 * heads, specs, operands, [columns_spec(rows, HEAD_DIM)], [kind(rows, 3 * width)], moves,
        cost=pl.CostEstimate(flops=2 * rows * width, bytes_accessed=16 * rows * width, transcendentals=0),
    )
    return outs[0], got


FEED_TILE = 256


def feed(grid, middle, gain, w_up, w_down, moves=()):
    rows, width = middle.shape
    hidden = w_down.shape[0]
    steps = hidden // FEED_TILE

    def body(here, step, ins, outs, held):
        middle_ref, gain_ref, gate_w, up_w, down_w = ins
        out_ref, normed_ref, both_ref, inner_ref = outs

        @pl.when(step == 0)
        def _():
            value = middle_ref[...]
            normed_ref[...] = norm(value, gain_ref[...]).astype(BF)
            held[0][...] = value

        normed = normed_ref[...]
        gate, up = dot(normed, gate_w[...], (1, 0)), dot(normed, up_w[...], (1, 0))
        both_ref[0] = gate.astype(BF)
        both_ref[1] = up.astype(BF)
        inner = (gate / (1.0 + jnp.exp(-gate)) * up).astype(BF)
        inner_ref[...] = inner
        held[0][...] += dot(inner, down_w[...], (1, 0))

        @pl.when(step == steps - 1)
        def _():
            out_ref[...] = held[0][...]

    tile = columns_spec(width, FEED_TILE)
    return host(
        grid, body, steps,
        [whole_spec(rows, width), whole_spec(1, width), tile, columns_spec(width, FEED_TILE, first=steps), rows_spec(FEED_TILE, width)],
        [middle, gain, w_up, w_up, w_down],
        [whole_spec(rows, width), whole_spec(rows, width), columns_spec(2, rows, FEED_TILE), columns_spec(rows, FEED_TILE)],
        [kind(rows, width, dtype=F32), kind(rows, width), kind(2, rows, hidden), kind(rows, hidden)],
        moves,
        scratch=[pltpu.VMEM((rows, width), F32)],
        cost=pl.CostEstimate(flops=6 * rows * width * hidden, bytes_accessed=6 * width * hidden, transcendentals=rows * hidden),
    )


def feed_back(grid, grad, middle, gain, both, w_up, w_down, moves=()):
    rows, width = grad.shape
    hidden = w_down.shape[0]
    steps = hidden // FEED_TILE

    def body(here, step, ins, outs, held):
        grad_ref, middle_ref, gain_ref, both_ref, gate_w, up_w, down_w = ins
        out_ref, low_ref, grads_ref, gain_out = outs
        total = held[0]

        @pl.when(step == 0)
        def _():
            held[1][...] = grad_ref[...].astype(BF)
            total[...] = jnp.zeros_like(total)

        grad_inner = dot(held[1][...], down_w[...], (1, 1))
        gate, up = both_ref[0].astype(F32), both_ref[1].astype(F32)
        sigmoid = 1.0 / (1.0 + jnp.exp(-gate))
        scaled = grad_inner * sigmoid
        grad_gate = (scaled * up * (1.0 + gate * (1.0 - sigmoid))).astype(BF)
        grad_up = (scaled * gate).astype(BF)
        grads_ref[0] = grad_gate
        grads_ref[1] = grad_up
        total[...] += dot(grad_gate, gate_w[...], (1, 1)) + dot(grad_up, up_w[...], (1, 1))

        @pl.when(step == steps - 1)
        def _():
            pulled, grad_gain = norm_back(middle_ref[...], gain_ref[...], total[...])
            result = grad_ref[...] + pulled
            out_ref[...] = result
            low_ref[...] = result.astype(BF)
            gain_out[...] = grad_gain

    tile = columns_spec(width, FEED_TILE)
    whole = whole_spec(rows, width)
    return host(
        grid, body, steps,
        [whole, whole, whole_spec(1, width), columns_spec(2, rows, FEED_TILE), tile,
         columns_spec(width, FEED_TILE, first=steps), rows_spec(FEED_TILE, width)],
        [grad, middle, gain, both, w_up, w_up, w_down],
        [whole, whole, columns_spec(2, rows, FEED_TILE), whole_spec(1, width)],
        [kind(rows, width, dtype=F32), kind(rows, width), kind(2, rows, hidden), kind(1, width, dtype=F32)],
        moves,
        scratch=[pltpu.VMEM((rows, width), F32), pltpu.VMEM((rows, width), BF)],
        cost=pl.CostEstimate(flops=6 * rows * width * hidden, bytes_accessed=6 * width * hidden, transcendentals=rows * hidden),
    )


def norm(value, gain):
    return value * lax.rsqrt(jnp.mean(value * value, axis=-1, keepdims=True) + EPSILON) * gain


def norm_back(value, gain, grad):
    inverse = lax.rsqrt(jnp.mean(value * value, axis=-1, keepdims=True) + EPSILON)
    unit = value * inverse
    grad_gain = jnp.sum(grad * unit, axis=0, keepdims=True)
    scaled = grad * gain
    pulled = inverse * (scaled - unit * jnp.mean(scaled * unit, axis=-1, keepdims=True))
    return pulled, grad_gain


class Reduce:
    def __init__(self, grid, total):
        self.grid = grid
        self.parts = total.reshape(grid.J, total.shape[0] // grid.J, total.shape[1])
        self.phase = 0

    def flip(self):
        return flip_move(self.grid, self.parts, self.phase)

    def flipped(self, got):
        grid = self.grid
        if self.phase == 0:
            kept = jnp.stack(
                [
                    lax.dynamic_index_in_dim(self.parts, grid.place(2 * i, grid.c), 0, keepdims=False)
                    for i in range(grid.J // 2)
                ]
            )
        else:
            kept = self.parts[0::2]
        self.parts = (kept.astype(F32) + got.astype(F32)).astype(BF)
        self.phase += 1
        if self.phase == grid.bits:
            self.line = self.parts.reshape(2, grid.F, -1, self.parts.shape[2])

    def ring(self):
        while self.phase < self.grid.bits:
            self.flipped(send(self.grid, [self.flip()])[0])
        return ring_move(self.grid, self.line)

    def arrived(self, got):
        grid = self.grid
        here = lax.dynamic_index_in_dim(self.line, grid.f, 1, keepdims=False)
        self.summed = here.astype(F32) + sum(got[t].astype(F32) for t in range(grid.F - 1))
        give = lax.dynamic_index_in_dim(self.summed, 1 - grid.c, 0, keepdims=False)
        self.give = give.astype(BF)

    def done(self, got):
        grid = self.grid
        mine = lax.dynamic_index_in_dim(self.summed, grid.c, 0, keepdims=False)
        got = got.astype(F32)
        return jnp.concatenate(
            [jnp.where(grid.c == 0, mine, got), jnp.where(grid.c == 0, got, mine)], axis=1
        )


def local(
    n_dp,
    pieces,
    tokens,
    cotangent,
    doc_lengths,
    partner,
    memory_picks,
    attention_in,
    attention_out,
    feed_in,
    feed_out,
    norm_gains,
):
    IDS[0] = 1
    grid = Grid(n_dp, pieces)
    grid.trace()
    layers = attention_in.shape[0]
    width = tokens.shape[2]
    heads = width // HEAD_DIM
    topk = memory_picks.shape[3]
    valid_all, visible_all = jax.vmap(memory_plan)(doc_lengths, partner)
    valid = valid_all[grid.m, grid.slot].reshape(1)
    visible = visible_all[grid.m, grid.slot]
    relative = (grid.slot - jnp.arange(n_dp)) % n_dp
    bias = jnp.repeat(jnp.where(visible[relative], 0.0, MASKED), topk)[:, None].astype(F32)
    tables = rope_tables()
    picks_there = grid.swap(memory_picks)
    picks = jnp.where(grid.r == grid.c, memory_picks[grid.m, 0], picks_there[grid.m, 0])
    zero = grid.c == 0

    def both_halves(mine, other):
        return jnp.where(
            zero, jnp.concatenate([mine, other], axis=-1), jnp.concatenate([other, mine], axis=-1)
        )

    def half(value, c):
        size = value.shape[-1] // 2
        return lax.dynamic_slice_in_dim(value, c * size, size, axis=value.ndim - 1)

    def chip(value):
        return jnp.concatenate([value, grid.swap(value)])

    hidden, cotangent_rows, gains, weights = gather_all(
        grid, tokens, cotangent, norm_gains, [attention_in, attention_out, feed_in, feed_out]
    )
    hidden = hidden.astype(F32)
    gain = lambda l, i: gains[l, i][None]
    saved = []
    for l in range(layers):
        w_qkv, w_out, w_up, w_down = weights[l]
        memory = l == layers - 1
        normed = norm(hidden, gain(l, 0)).astype(BF)
        split, _ = split_heads(grid, memory, tables, mm(normed, w_qkv))
        (others,) = send(grid, [member_move(grid, split[1], False)])
        pairs = [split[1]] + [others[t] for t in range(grid.U - 1)]
        extra = None
        if memory:
            chosen = pick_memory(grid, picks, pairs, grid.c)
            (came,) = send(grid, [slots_move(grid, chosen, False)])
            slots = jnp.concatenate([chosen[None], came])
            slots = jnp.swapaxes(slots, 0, 1).reshape(2, n_dp * topk, -1)
            slots = both_halves(slots, grid.swap(slots))
            extra = {"query": split[2], "keys": slots[0], "values": slots[1], "bias": bias}
        attended, _ = attend(grid, valid, split[0], pairs, extra)
        middle = hidden + mm(attended, w_out)
        (out, normed_feed, both, inner), _ = feed(grid, middle, gain(l, 1), w_up, w_down)
        saved.append((hidden, normed, split[0], pairs, extra, attended, middle, normed_feed, both, inner))
        hidden = out
    layer_output = grid.from_units(hidden.astype(BF))

    grad = cotangent_rows.astype(F32)
    found = [[None] * 4 for _ in range(layers)]
    grad_gains = [[None, None] for _ in range(layers)]
    before = None
    for l in reversed(range(layers)):
        w_qkv, w_out, w_up, w_down = weights[l]
        hidden, normed, query, pairs, extra, attended, middle, normed_feed, both, inner = saved[l]
        low = grad.astype(BF)
        right = jnp.concatenate([half(low, grid.c), grid.swap(half(low, 1 - grid.c))])
        down = Reduce(grid, mm(chip(inner), right, (0, 0)).astype(BF))

        moves = [down.flip()] + ([up_before.ring(), last_before.flip()] if before else [])
        (grad, grad_low, grads, gain_feed), got = feed_back(
            grid, grad, middle, gain(l, 1), both, w_up, w_down, moves
        )
        down.flipped(got[0])
        if before:
            up_before.arrived(got[1])
            last_before.flipped(got[2])
        grads_mine = lax.dynamic_index_in_dim(grads, grid.c, 0, keepdims=False)
        grads_give = lax.dynamic_index_in_dim(grads, 1 - grid.c, 0, keepdims=False)
        right = jnp.concatenate([grads_mine, grid.swap(grads_give)])
        up = Reduce(grid, mm(chip(normed_feed), right, (0, 0)).astype(BF))
        grad_heads = mm(grad_low, w_out, (1, 1)).astype(BF)

        moves = [up.flip(), down.flip()] + ([last_before.ring()] if before else [])
        outs, got = attend_back(grid, valid, tables, query, grad_heads, pairs, extra, moves)
        up.flipped(got[0])
        down.flipped(got[1])
        if before:
            last_before.arrived(got[2])
        grad_query, own, others = outs[:3]
        memory_grad = None
        moves = [member_move(grid, others, True)]
        if extra is not None:
            moves.append(swap_move(half(outs[3], 1 - grid.c)))
        got = send(grid, moves)
        others = got[0]
        if extra is not None:
            joined = half(outs[3], grid.c).astype(F32) + got[1].astype(F32)
            joined = joined.astype(BF).reshape(2, n_dp, topk, -1)
            (came,) = send(grid, [slots_move(grid, joined, True)])
            total = joined[:, 0].astype(F32) + sum(came[t].astype(F32) for t in range(n_dp - 1))
            for t in range(1, grid.Q):
                total = total + grid.within(total.astype(BF), t).astype(F32)
            total = total.astype(BF)
            memory_grad = both_halves(total, grid.swap(total))
        grad_projected, got = finish_gradient(
            grid, grad_query, own, others, picks, memory_grad, [up.flip(), down.ring()]
        )
        up.flipped(got[0])
        down.arrived(got[1])
        grads_mine, grads_give = half(grad_projected, grid.c), half(grad_projected, 1 - grid.c)
        right = jnp.concatenate([grads_mine, grid.swap(grads_give)])
        w_qkv_sum = mm(chip(normed), right, (0, 0)).astype(BF)
        right = jnp.concatenate([half(grad_low, grid.c), grid.swap(half(grad_low, 1 - grid.c))])
        w_out_sum = mm(chip(attended), right, (0, 0)).astype(BF)
        last = Reduce(grid, jnp.concatenate([w_out_sum, w_qkv_sum], axis=1))
        pulled, gain_attention = norm_back(hidden, gain(l, 0), mm(grad_projected, w_qkv, (1, 1)))
        grad = grad + pulled
        grad_gains[l] = [gain_attention[0], gain_feed[0]]
        found[l][3] = down.done(grid.swap(down.give))
        if before:
            found[l + 1][2] = up_before.done(grid.swap(up_before.give))
            both_last = last_before.done(grid.swap(last_before.give))
            found[l + 1][0], found[l + 1][1] = last_parts(both_last, width)
        if l > 0:
            (came,) = send(grid, [last.flip()])
            last.flipped(came)
        before, up_before, last_before = True, up, last
    came = send(grid, [last.flip(), up.ring()])
    last.flipped(came[0])
    up.arrived(came[1])
    last.arrived(send(grid, [last.ring()])[0])
    found[0][2] = up.done(grid.swap(up.give))
    found[0][0], found[0][1] = last_parts(last.done(grid.swap(last.give)), width)
    input_grad = grid.from_units(grad.astype(BF)).astype(F32)
    return (
        layer_output,
        input_grad,
        *(jnp.stack([found[l][i] for l in range(layers)]) for i in range(4)),
        scatter_gains(grid, jnp.stack([jnp.stack(pair) for pair in grad_gains])),
    )


def last_parts(value, width):
    size = value.shape[1] // 2
    halves = [value[:, :size], value[:, size:]]
    return (
        jnp.concatenate([h[:, width // 2 :] for h in halves], axis=1),
        jnp.concatenate([h[:, : width // 2] for h in halves], axis=1),
    )


def solution(mesh):
    rows = P(None, ("dp", "fsdp"), None)
    in_specs = (rows, rows, P(), P(), P(None, "dp", None, None), rows, rows, rows, rows, P(None, None, ("dp", "fsdp")))
    out_specs = (rows, rows, rows, rows, rows, rows, P(None, None, ("dp", "fsdp")))
    body = functools.partial(local, mesh.shape["dp"], mesh.shape["fsdp"])
    return jax.shard_map(body, mesh=mesh, in_specs=in_specs, out_specs=out_specs, check_vma=False)
```

time: 1070 us -> 1030 us (0.963)
  Pallas kernels: 420 us -> 752 us
  waiting for transfers between devices: 261 us -> 38 us
  matrix products: 166 us -> 80.9 us
  starting transfers between devices: 82.4 us -> 31.2 us
  other arithmetic: 84.8 us -> 52 us
  local copies, waits for them, and re-layouts: 46.5 us -> 67.5 us
    pallas_call x9 -> x23, Pallas kernels: 145 us -> 477 us  [the longest x22 474 us: host(): pl.pallas_call(kernel, grid=(steps,), in_specs=list(in_specs) + [any_spec...]
    ppermute x83 -> x34, waiting for transfers between devices: 261 us -> 38 us  [permute(): return lax.ppermute(value, ('dp', 'fsdp'), pairs)]
    dot_general x30 -> x16, matrix products: 166 us -> 80.9 us  [dot(): lax.dot_general(left, right, (((contract[0],), (contract[1],)), ((), ()))...]
    ppermute x83 -> x34, starting transfers between devices: 82.4 us -> 31.2 us  [permute(): return lax.ppermute(value, ('dp', 'fsdp'), pairs)]
    concatenate x18 -> x2, other arithmetic: 32.5 us -> 3.14 us  [local(): last = Reduce(grid, jnp.concatenate([w_out_sum, w_qkv_sum], axis=1))]
    unnamed x258 -> x177, local copies, waits for them, and re-layouts: 24.6 us -> 34.8 us
    convert_element_type x24 -> x19, other arithmetic: 23.2 us -> 23 us  [the longest x12 13.5 us: flipped(): self.parts = (kept.astype(F32) + got.astype(F32)).astype(BF)]
  transfers between devices with their start and end apart: 83 -> 34, of which waited for: 36 -> 11; matrix products, arithmetic and copies ran while one was open for 18% -> 11% of each run, Pallas kernels for 8% -> 49%
where the time goes in v3:
time: 1030 us; the launch traced here: 1020 us
  Pallas kernels  752 us (73%)
  matrix products  80.9 us (8%)
  local copies, waits for them, and re-layouts  67.5 us (7%)
  other arithmetic  52 us (5%)
  waiting for transfers between devices  38 us (4%)
  starting transfers between devices  31.2 us (3%)
    pallas_call x22, Pallas kernels, host(): pl.pallas_call(kernel, grid=(steps,), in_specs=list(in_specs) + [any_spec...  474 us
    pallas_call x1, Pallas kernels, gather_all(): pl.pallas_call(functools.partial(gather_body, grid, layers, kinds), in_sp...  274 us
    dot_general x16, matrix products, dot(): lax.dot_general(left, right, (((contract[0],), (contract[1],)), ((), ()))...  80.9 us
    ppermute x34, waiting for transfers between devices, permute(): return lax.ppermute(value, ('dp', 'fsdp'), pairs)  38 us
    unnamed x177, local copies, waits for them, and re-layouts  34.8 us
    ppermute x34, starting transfers between devices, permute(): return lax.ppermute(value, ('dp', 'fsdp'), pairs)  31.2 us
  transfers between devices with their start and end apart: 34, of which 11 were waited for; matrix products, arithmetic and copies ran while one was open for 11% of the time, Pallas kernels for 49%

profile of v3, /device:TPU:0, one launch (start us, length us, event | category | flops | bytes accessed | tf_op | source)
XLA Modules:
  0.0 1023.9 jit_solution(3029619024015197844)
XLA Ops:
  10.3 274.3 %shard_map.153 = (bf16[2,256,1024]{2,1,0:T(8,128)(2,1)S(1)}, bf16[2,256,1024]{2,1,0:T(8,128)(2,1)S(1)}, f32[4,2,4,8,128]{4,3,2,1,0:T(8,128)S(1)}, bf16[4,2,4,32,...) custom-call(bf16[2,256,1024]{2,1,0:T(8,128)(2,1)S(1)} %copy-done.30,, ...), custom_call_target="tpu_custom_call" | custom-call | tf_op jit(solution)/shard_map/pallas_call | solution.py:389
  288.9 8.3 fusion.110.refs_2_.refs_3_.refs_4_
  312.6 12.9 %shard_map.156 = bf16[512,1024]{1,0:T(8,128)(2,1)S(1)} custom-call(s32[1]{0:T(128)} %bitcast.2.refs_0_, bf16[512,1024]{1,0:T(8,128)(2,1)S(1)} %copy-done.16, bf16[2,512,1024]{2,1,0:T(8,128)(2,1)S(1)} %get-tuple-element.81.refs_0_.refs_2_.refs_5_, bf16[2,512,1024]{2,1,0:T(8,128)(2,1)} %bitcast.212), custom_call_target="tpu_custom_call" | custom-call | flops 1610612736 | bytes 8388608 | tf_op jit(solution)/shard_map/pallas_call | solution.py:534
  326.8 19.1 %shard_map.157 = (f32[512,1024]{1,0:T(8,128)S(1)}, bf16[512,1024]{1,0:T(8,128)(2,1)}, bf16[2,512,2816]{2,1,0:T(8,128)(2,1)}, bf16[512,2816]{1,0:T(8,128)(2,1)}) custom-call(f32[512,1024]{1,0:T(8,128)S(1)} %bitcast_add_fusion.refs_0_.refs_1_, f32[1,1024]{1,0:T(1,128)S(1)} %get-tuple-element.198.refs_1_.refs_2_, bf16[1024,5632]{1,0:T(8,128)(2,1)} %bitcast.230, ...), custom_call_target="tpu_custom_call" | custom-call | flops 8858370048 | bytes 17301504 | tf_op jit(solution)/shard_map/pallas_call | solution.py:534
  354.3 7.7 shard_map.158
  377.1 38.9 %shard_map.161 = bf16[7,2,128,512]{3,2,1,0:T(8,128)(2,1)S(1)} custom-call(bf16[2,128,512]{2,1,0:T(8,128)(2,1)S(1)} %shard_map.160.refs_0_), custom_call_target="tpu_custom_call" | custom-call | tf_op jit(solution)/shard_map/pallas_call | solution.py:534
  429.5 24.0 %shard_map.162 = bf16[512,1024]{1,0:T(8,128)(2,1)S(1)} custom-call(s32[1]{0:T(128)} %bitcast.2.refs_0_, bf16[512,1024]{1,0:T(8,128)(2,1)S(1)} %copy-done.37, bf16[3,512,1024]{2,1,0:T(8,128)(2,1)} %get-tuple-element.88.refs_0_.refs_2_.refs_5_, bf16[3,512,1024]{2,1,0:T(8,128)(2,1)} %bitcast.210, bf16[512,1024]{1,0:T(8,128)(2,1)S(1)} %copy-done.40, ...), custom_call_target="tpu_custom_call" | custom-call | flops 3758096384 | bytes 16777216 | tf_op jit(solution)/shard_map/pallas_call | solution.py:534
  454.9 18.4 %shard_map.163 = (f32[512,1024]{1,0:T(8,128)S(1)}, bf16[512,1024]{1,0:T(8,128)(2,1)S(1)}, bf16[2,512,2816]{2,1,0:T(8,128)(2,1)}, bf16[512,2816]{1,0:T(8,128)(2,1)}) custom-call(f32[512,1024]{1,0:T(8,128)S(1)} %convolution_add_fusion.refs_0_.refs_1_, f32[1,1024]{1,0:T(1,128)S(1)} %get-tuple-element.196.refs_1_.refs_2_, bf16[1024,5632]{1,0:T(8,128)(2,1)} %bitcast.234, ...), custom_call_target="tpu_custom_call" | custom-call | flops 8858370048 | bytes 17301504 | tf_op jit(solution)/shard_map/pallas_call | solution.py:534
  489.5 24.0 %shard_map.164 = (f32[512,1024]{1,0:T(8,128)S(1)}, bf16[512,1024]{1,0:T(8,128)(2,1)S(1)}, bf16[2,512,2816]{2,1,0:T(8,128)(2,1)}, f32[1,1024]{1,0:T(1,128)S(1)}, bf16[2,704,512]{2,1,0:T(8,128)(2,1)S(1)}) custom-call(f32[512,1024]{1,0:T(8,128)} %bitcast_convert_fusion.refs_0_, f32[512,1024]{1,0:T(8,128)} %copy-done.29, ...), custom_call_target="tpu_custom_call" | custom-call | flops 8858370048 | bytes 17301504 | tf_op jit(solution)/shard_map/pallas_call | solution.py:534
  533.1 8.3 collective-permute-start.6
  541.4 12.8 %collective-permute-done.3 = bf16[256,1024]{1,0:T(8,128)(2,1)} collective-permute-done((bf16[256,1024]{1,0:T(8,128)(2,1)}, bf16[256,1024]{1,0:T(8,128)(2,1)}, u32[]{:S(2)}, u32[]{:S(2)}) %collective-permute-start.3) | collective-permute-done | bytes 524320 | tf_op jit(solution)/shard_map/ppermute | solution.py:70
  566.9 9.4 fusion.19
  580.8 45.3 %shard_map.165 = (bf16[512,1024]{1,0:T(8,128)(2,1)S(1)}, f32[2,512,1024]{2,1,0:T(8,128)}, bf16[1,2,512,1024]{3,2,1,0:T(8,128)(2,1)}, bf16[2,1024,1024]{2,1,0:T(8...) custom-call(s32[1]{0:T(128)} %bitcast.2.refs_0_, f32[1024,128]{1,0:T(8,128)S(1)} %copy-done.10, ...), custom_call_target="tpu_custom_call" | custom-call | flops 9395240960 | bytes 16777216 | tf_op jit(solution)/shard_map/pallas_call | solution.py:534
  640.0 31.8 %shard_map.167 = bf16[7,2,128,512]{3,2,1,0:T(8,128)(2,1)S(1)} custom-call(bf16[2,8,128,512]{3,2,1,0:T(8,128)(2,1)S(1)} %bitcast.214), custom_call_target="tpu_custom_call" | custom-call | tf_op jit(solution)/shard_map/pallas_call | solution.py:534
  674.8 22.9 %shard_map.168 = (bf16[512,3072]{1,0:T(8,128)(2,1)}, bf16[1,256,2816]{2,1,0:T(8,128)(2,1)S(1)}, bf16[3,2,88,512]{3,2,1,0:T(8,128)(2,1)S(1)}) custom-call(bf16[512,1024]{1,0:T(8,128)(2,1)S(1)} %get-tuple-element.102.refs_0_, f32[2,512,1024]{2,1,0:T(8,128)} %get-tuple-element.103.refs_1_, bf16[1,2,512,1024]{3,2,1,0:T(8,128)(2,1)} %copy-done.28, ...), custom_call_target="tpu_custom_call" | custom-call | flops 1048576 | bytes 8388608 | tf_op jit(solution)/shard_map/pallas_call | solution.py:534
  727.4 26.3 %shard_map.169 = bf16[2,256,2048]{2,1,0:T(8,128)(2,1)S(1)} custom-call(bf16[4,256,2048]{2,1,0:T(8,128)(2,1)} %bitcast.240), custom_call_target="tpu_custom_call" | custom-call | tf_op jit(solution)/shard_map/pallas_call | solution.py:534
  756.3 33.9 %shard_map.170 = (f32[512,1024]{1,0:T(8,128)}, bf16[512,1024]{1,0:T(8,128)(2,1)S(1)}, bf16[2,512,2816]{2,1,0:T(8,128)(2,1)}, f32[1,1024]{1,0:T(1,128)S(1)}, bf16...) custom-call(f32[512,1024]{1,0:T(8,128)} %get-tuple-element.142.refs_0_, ...), custom_call_target="tpu_custom_call" | custom-call | flops 8858370048 | bytes 17301504 | tf_op jit(solution)/shard_map/pallas_call | solution.py:534
  806.8 9.5 fusion.16
  818.7 49.8 %shard_map.171 = (bf16[512,1024]{1,0:T(8,128)(2,1)S(1)}, f32[2,512,1024]{2,1,0:T(8,128)}, bf16[1,2,512,1024]{3,2,1,0:T(8,128)(2,1)}, bf16[2,256,2816]{2,1,0:T(8,...) custom-call(s32[1]{0:T(128)} %bitcast.2.refs_0_, f32[1024,128]{1,0:T(8,128)S(1)} %copy-done.10, ...), custom_call_target="tpu_custom_call" | custom-call | flops 4026531840 | bytes 8388608 | tf_op jit(solution)/shard_map/pallas_call | solution.py:534
  876.8 21.4 %shard_map.173 = (bf16[512,3072]{1,0:T(8,128)(2,1)}, bf16[1,256,2816]{2,1,0:T(8,128)(2,1)S(1)}, bf16[3,2,88,512]{3,2,1,0:T(8,128)(2,1)S(1)}) custom-call(bf16[512,1024]{1,0:T(8,128)(2,1)S(1)} %get-tuple-element.120.refs_0_, f32[2,512,1024]{2,1,0:T(8,128)} %get-tuple-element.121.refs_1_, bf16[1,2,512,1024]{3,2,1,0:T(8,128)(2,1)S(1)} %shard_map.172.refs_2_, ...), custom_call_target="tpu_custom_call" | custom-call | flops 1048576 | bytes 8388608 | tf_op jit(solution)/shard_map/pallas_call | solution.py:534
  928.3 9.1 collective-permute-done.33
  948.2 27.7 %shard_map.174 = (bf16[2,256,2048]{2,1,0:T(8,128)(2,1)S(1)}, bf16[3,2,32,2816]{3,2,1,0:T(8,128)(2,1)S(1)}) custom-call(bf16[4,256,2048]{2,1,0:T(8,128)(2,1)} %bitcast.239, bf16[2,4,32,2816]{3,2,1,0:T(8,128)(2,1)S(1)} %bitcast.218), custom_call_target="tpu_custom_call" | custom-call | tf_op jit(solution)/shard_map/pallas_call | solution.py:534
  976.8 14.9 %shard_map.175 = bf16[1,256,2048]{2,1,0:T(8,128)(2,1)S(1)} custom-call(bf16[2,256,2048]{2,1,0:T(8,128)(2,1)S(1)} %add_convert_fusion.2.refs_0_), custom_call_target="tpu_custom_call" | custom-call | tf_op jit(solution)/shard_map/pallas_call | solution.py:534
  992.1 26.5 %shard_map.176 = bf16[3,2,32,2048]{3,2,1,0:T(8,128)(2,1)S(1)} custom-call(bf16[2,4,32,2048]{3,2,1,0:T(8,128)(2,1)S(1)} %bitcast.220), custom_call_target="tpu_custom_call" | custom-call | tf_op jit(solution)/shard_map/pallas_call | solution.py:534
  (395 shorter events, 244.0 us)
Async XLA Ops:
  0.6 370.9 %collective-permute-start = (s32[2,1,8,128]{3,2,1,0:T(8,128)}, s32[2,1,8,128]{3,2,1,0:T(8,128)S(1)}, u32[]{:S(2)}, u32[]{:S(2)}) collective-permute-start(s32[2,1,8,128]{3,2,1,0:T(8,128)} %param.16), channel_id=1, source_target_pairs={{0,4},{1,5},{2,6},{3,7},{4,0},{5,1},{6,2},{7,3},{8,12},{9,13},{10,... | collective-permute-start | bytes 24584 | tf_op jit(solution)/shard_map/ppermute | solution.py:70
  475.6 6.4 collective-permute-start.4
  476.8 5.2 collective-permute-start.5
  520.2 46.7 %collective-permute-start.7 = (bf16[512,2816]{1,0:T(8,128)(2,1)}, bf16[512,2816]{1,0:T(8,128)(2,1)}, u32[]{:S(2)}, u32[]{:S(2)}) collective-permute-start(bf16[512,2816]{1,0:T(8,128)(2,1)} %get-tuple-element.152), channel_id=1, source_target_pairs={{0,4},{1,5},{2,6},{3,7},{4,0},{5,1},{6,2},{7,3},{8,12},{9,13},{10,... | collective-permute-start | bytes 8650760 | tf_op jit(solution)/shard_map/ppermute | solution.py:70
  524.4 8.7 collective-permute-start.2
  529.7 24.5 %collective-permute-start.3 = (bf16[256,1024]{1,0:T(8,128)(2,1)}, bf16[256,1024]{1,0:T(8,128)(2,1)}, u32[]{:S(2)}, u32[]{:S(2)}) collective-permute-start(bf16[256,1024]{1,0:T(8,128)(2,1)} %get-tuple-element.183), channel_id=1, source_target_pairs={{0,3},{1,7},{2,0},{3,4},{4,2},{5,6},{6,1},{7,5},{8,11},{9,15},{10,... | collective-permute-start | bytes 1572872 | tf_op jit(solution)/shard_map/ppermute | solution.py:70
  532.0 187.3 %collective-permute-start.13 = (bf16[512,1024]{1,0:T(8,128)(2,1)}, bf16[512,1024]{1,0:T(8,128)(2,1)}, u32[]{:S(2)}, u32[]{:S(2)}) collective-permute-start(bf16[512,1024]{1,0:T(8,128)(2,1)} %multiply_convert_fusion), channel_id=1, source_target_pairs={{0,4},{1,5},{2,6},{3,7},{4,0},{5,1},{6,2},{7,3},{8,12},{9,13},{10,... | collective-permute-start | bytes 3145736 | tf_op jit(solution)/shard_map/ppermute | solution.py:70
  532.8 29.4 %collective-permute-start.11 = (bf16[512,1024]{1,0:T(8,128)(2,1)}, bf16[512,1024]{1,0:T(8,128)(2,1)S(1)}, u32[]{:S(2)}, u32[]{:S(2)}) collective-permute-start(bf16[512,1024]{1,0:T(8,128)(2,1)} %copy-done.41), channel_id=1, source_target_pairs={{0,4},{1,5},{2,6},{3,7},{4,0},{5,1},{6,2},{7,3},{8,12},{9,13},{10,... | collective-permute-start | bytes 3145736 | tf_op jit(solution)/shard_map/ppermute | solution.py:70
  533.1 33.8 %collective-permute-start.6 = (bf16[512,1024]{1,0:T(8,128)(2,1)}, bf16[512,1024]{1,0:T(8,128)(2,1)}, u32[]{:S(2)}, u32[]{:S(2)}) collective-permute-start(bf16[512,1024]{1,0:T(8,128)(2,1)} %copy-done.47), channel_id=1, source_target_pairs={{0,4},{1,5},{2,6},{3,7},{4,0},{5,1},{6,2},{7,3},{8,12},{9,13},{10,... | collective-permute-start | bytes 3145736 | tf_op jit(solution)/shard_map/ppermute | solution.py:70
  556.7 5.5 collective-permute-start.12
  562.2 149.4 %collective-permute-start.9 = (bf16[512,2816]{1,0:T(8,128)(2,1)}, bf16[512,2816]{1,0:T(8,128)(2,1)}, u32[]{:S(2)}, u32[]{:S(2)}) collective-permute-start(bf16[512,2816]{1,0:T(8,128)(2,1)} %get-tuple-element.112), channel_id=1, source_target_pairs={{0,4},{1,5},{2,6},{3,7},{4,0},{5,1},{6,2},{7,3},{8,12},{9,13},{10,... | collective-permute-start | bytes 8650760 | tf_op jit(solution)/shard_map/ppermute | solution.py:70
  706.9 5.2 collective-permute-start.10
  707.8 11.5 %collective-permute-start.14 = (bf16[512,1536]{1,0:T(8,128)(2,1)S(1)}, bf16[512,1536]{1,0:T(8,128)(2,1)S(1)}, u32[]{:S(2)}, u32[]{:S(2)}) collective-permute-start(bf16[512,1536]{1,0:T(8,128)(2,1)S(1)} %get-tuple-element.162), channel_id=1, source_target_pairs={{0,4},{1,5},{2,6},{3,7},{4,0},{5,1},{6,2},{7,3},{8,12},{9,13},{10,... | collective-permute-start | bytes 4718600 | tf_op jit(solution)/shard_map/ppermute | solution.py:70
  711.4 91.5 %collective-permute-start.19 = (bf16[512,1024]{1,0:T(8,128)(2,1)S(1)}, bf16[512,1024]{1,0:T(8,128)(2,1)}, u32[]{:S(2)}, u32[]{:S(2)}) collective-permute-start(bf16[512,1024]{1,0:T(8,128)(2,1)S(1)} %copy-done.33), channel_id=1, source_target_pairs={{0,4},{1,5},{2,6},{3,7},{4,0},{5,1},{6,2},{7,3},{8,12},{9,13},{10,... | collective-permute-start | bytes 3145736 | tf_op jit(solution)/shard_map/ppermute | solution.py:70
  711.7 95.1 %collective-permute-start.15 = (bf16[512,1024]{1,0:T(8,128)(2,1)}, bf16[512,1024]{1,0:T(8,128)(2,1)}, u32[]{:S(2)}, u32[]{:S(2)}) collective-permute-start(bf16[512,1024]{1,0:T(8,128)(2,1)} %get-tuple-element.116), channel_id=1, source_target_pairs={{0,4},{1,5},{2,6},{3,7},{4,0},{5,1},{6,2},{7,3},{8,12},{9,13},{10,... | collective-permute-start | bytes 3145736 | tf_op jit(solution)/shard_map/ppermute | solution.py:70
  795.9 10.9 %collective-permute-start.16 = (bf16[512,2816]{1,0:T(8,128)(2,1)}, bf16[512,2816]{1,0:T(8,128)(2,1)}, u32[]{:S(2)}, u32[]{:S(2)}) collective-permute-start(bf16[512,2816]{1,0:T(8,128)(2,1)} %get-tuple-element.148), channel_id=1, source_target_pairs={{0,4},{1,5},{2,6},{3,7},{4,0},{5,1},{6,2},{7,3},{8,12},{9,13},{10,... | collective-permute-start | bytes 8650760 | tf_op jit(solution)/shard_map/ppermute | solution.py:70
  796.1 6.8 collective-permute-start.20
  796.8 5.2 collective-permute-start.26
  908.2 31.8 %collective-permute-start.17 = (bf16[256,1024]{1,0:T(8,128)(2,1)S(1)}, bf16[256,1024]{1,0:T(8,128)(2,1)S(1)}, u32[]{:S(2)}, u32[]{:S(2)}) collective-permute-start(bf16[256,1024]{1,0:T(8,128)(2,1)S(1)} %get-tuple-element.172), channel_id=1, source_target_pairs={{0,0},{1,4},{2,3},{3,7},{4,1},{5,5},{6,2},{7,6},{8,8},{9,12},{10,1... | collective-permute-start | bytes 1572872 | tf_op jit(solution)/shard_map/ppermute | solution.py:70
  909.0 31.0 %collective-permute-start.18 = (bf16[256,1024]{1,0:T(8,128)(2,1)S(1)}, bf16[256,1024]{1,0:T(8,128)(2,1)S(1)}, u32[]{:S(2)}, u32[]{:S(2)}) collective-permute-start(bf16[256,1024]{1,0:T(8,128)(2,1)S(1)} %get-tuple-element.173), channel_id=1, source_target_pairs={{0,3},{1,7},{2,0},{3,4},{4,2},{5,6},{6,1},{7,5},{8,11},{9,15},{10,... | collective-permute-start | bytes 1572872 | tf_op jit(solution)/shard_map/ppermute | solution.py:70
  916.0 23.8 %collective-permute-start.24 = (bf16[32,2048]{1,0:T(8,128)(2,1)S(1)}, bf16[32,2048]{1,0:T(8,128)(2,1)S(1)}, u32[]{:S(2)}, u32[]{:S(2)}) collective-permute-start(bf16[32,2048]{1,0:T(8,128)(2,1)S(1)} %fusion.91), channel_id=1, source_target_pairs={{0,4},{1,5},{2,6},{3,7},{4,0},{5,1},{6,2},{7,3},{8,12},{9,13},{10,... | collective-permute-start | bytes 393224 | tf_op jit(solution)/shard_map/ppermute | solution.py:70
  916.0 25.5 %collective-permute-start.22 = (bf16[512,1536]{1,0:T(8,128)(2,1)S(1)}, bf16[512,1536]{1,0:T(8,128)(2,1)S(1)}, u32[]{:S(2)}, u32[]{:S(2)}) collective-permute-start(bf16[512,1536]{1,0:T(8,128)(2,1)S(1)} %get-tuple-element.160), channel_id=1, source_target_pairs={{0,4},{1,5},{2,6},{3,7},{4,0},{5,1},{6,2},{7,3},{8,12},{9,13},{10,... | collective-permute-start | bytes 4718600 | tf_op jit(solution)/shard_map/ppermute | solution.py:70
  922.1 4.7 collective-permute-start.32
  926.8 10.5 %collective-permute-start.33 = (f32[2,2,1024]{2,1,0:T(2,128)S(1)}, f32[2,2,1024]{2,1,0:T(2,128)S(1)}, u32[]{:S(2)}, u32[]{:S(2)}) collective-permute-start(f32[2,2,1024]{2,1,0:T(2,128)S(1)} %add.411), channel_id=1, source_target_pairs={{0,2},{1,3},{2,0},{3,1},{4,6},{5,7},{6,4},{7,5},{8,10},{9,11},{10,... | collective-permute-start | bytes 49160 | tf_op jit(solution)/shard_map/ppermute | solution.py:70
  (98 other events, 674.6 us)

commit v4 on v3

--- a/solution.py
+++ b/solution.py
@@ -233,11 +233,17 @@
         other = 1 - c if split else c
         self.pre = remote(part(shard, other), part(whole.at[j, c, f], other), sems, 0, here.swap)
         at = 1
-        self.line = []
-        for t in range(1, grid.F):
-            block = mine.at[j, :, f]
-            self.line.append(remote(block, block, sems, at, here.ring(t)))
-            at += 1
+        self.hops = []
+        for h in range(1, grid.F):
+            hop = []
+            for way in (1, -1):
+                origin = f - way * (h - 1)
+                inside = lambda place: (place >= 0) & (place < grid.F)
+                block = mine.at[j, :, jnp.clip(origin, 0, grid.F - 1)]
+                copy = remote(block, block, sems, at, here.device(j, c, (f + way + grid.F) % grid.F))
+                hop.append((copy, inside(origin) & inside(f + way), inside(f - way * h)))
+                at += 1
+            self.hops.append(hop)
         self.flips = []
         for phase in range(grid.bits):
             sent = []
@@ -254,7 +260,7 @@
 
     @staticmethod
     def count(grid):
-        return 1 + (grid.F - 1) + (grid.J - 1) + grid.J
+        return 1 + 2 * (grid.F - 1) + (grid.J - 1) + grid.J
 
     def begin(self):
         self.own.start()
@@ -263,8 +269,11 @@
     def to_line(self):
         self.own.wait()
         self.pre.wait()
-        for copy in self.line:
-            copy.start()
+        self._hop(0)
+
+    def _hop(self, h):
+        for copy, sends, _ in self.hops[h]:
+            pl.when(sends)(copy.start)
 
     def _send(self, keys):
         for key in keys:
@@ -275,11 +284,18 @@
                 if key < 1 << phase:
                     sent[key].start()
 
-    def steps(self):
-        def first():
-            for copy in self.line:
-                copy.wait()
-            self._send([0])
+    def steps(self, whole):
+        def along(h):
+            for copy, _, comes in self.hops[h]:
+                pl.when(comes)(copy.wait_recv)
+            if h + 1 < len(self.hops):
+                self._hop(h + 1)
+                return
+            for hop in self.hops:
+                for copy, sends, _ in hop:
+                    pl.when(sends)(copy.wait_send)
+            if whole:
+                self._send([0])
 
         def later(phase):
             for copy in self.flips[phase]:
@@ -290,7 +306,10 @@
             for copy in self.swaps:
                 copy.wait()
 
-        return [first] + [functools.partial(later, p) for p in range(len(self.flips))] + [last]
+        line = [functools.partial(along, h) for h in range(len(self.hops))]
+        if not whole:
+            return line
+        return line + [functools.partial(later, p) for p in range(len(self.flips))] + [last]
 
 
 class Regroup:
@@ -341,78 +360,95 @@
 
 
 def gather_body(grid, layers, kinds, *refs):
-    tokens, cotangent, gains = refs[:3]
-    shards = refs[3 : 3 + kinds]
-    outs = refs[3 + kinds :]
-    tokens_out, cotangent_out, gains_out = outs[:3]
-    wholes = outs[3 : 3 + layers * kinds]
-    sems, own_sems, regroup_sems = outs[3 + layers * kinds :]
+    tokens, gains = refs[:2]
+    shards = refs[2 : 2 + kinds]
+    outs = refs[2 + kinds :]
+    tokens_out, gains_out = outs[:2]
+    wholes = outs[2 : 2 + layers * kinds]
+    sems, own_sems, regroup_sems = outs[2 + layers * kinds :]
     here = Here(grid)
     here.greet()
-    rows = Regroup(here, tokens, tokens_out, regroup_sems.at[0], own_sems.at[0])
-    rows_back = Regroup(here, cotangent, cotangent_out, regroup_sems.at[1], own_sems.at[1])
-    moves = [Spread(here, gains, gains_out, sems.at[0], own_sems.at[2], False)]
+    rows = Regroup(here, tokens, tokens_out, regroup_sems, own_sems.at[0])
+    moves = [(Spread(here, gains, gains_out, sems.at[0], own_sems.at[1], False), True)]
     for l in range(layers):
         for i in range(kinds):
             n = l * kinds + i
-            moves.append(
-                Spread(here, shards[i].at[l], wholes[n], sems.at[n + 1], own_sems.at[n + 3], True)
-            )
-    for move in moves:
+            move = Spread(here, shards[i].at[l], wholes[n], sems.at[n + 1], own_sems.at[n + 2], True)
+            moves.append((move, not later_here(l, i)))
+    for move, _ in moves:
         move.begin()
     rows.start()
-    steps = [move.steps() for move in moves]
+    steps = [move.steps(whole) for move, whole in moves]
     count = len(steps[0])
-    moves[0].to_line()
-    moves[1].to_line()
+    moves[0][0].to_line()
+    moves[1][0].to_line()
     for at in range(len(moves) + count - 1):
         if at + 2 < len(moves):
-            moves[at + 2].to_line()
-        if at == len(moves) - 3:
-            rows_back.start()
-        for back in range(count):
-            if 0 <= at - back < len(moves):
+            moves[at + 2][0].to_line()
+        for back in reversed(range(count)):
+            if 0 <= at - back < len(moves) and back < len(steps[at - back]):
                 steps[at - back][back]()
     rows.wait()
-    rows_back.wait()
-
-
-def gather_all(grid, tokens, cotangent, gains, shards):
+
+
+def later_here(l, i):
+    return l > 0 and i >= 2
+
+
+def gather_all(grid, tokens, gains, shards):
     layers, kinds = shards[0].shape[0], len(shards)
     packed = jnp.zeros((8, 128), F32).at[: layers * 2, : gains.shape[2]].set(
         gains.astype(F32).reshape(layers * 2, -1)
     )
     whole = lambda shard: jax.ShapeDtypeStruct((grid.J, 2, grid.F) + shard.shape[-2:], shard.dtype)
-    out_shape = [jax.ShapeDtypeStruct(tokens.shape, BF), jax.ShapeDtypeStruct(tokens.shape, BF), whole(packed)]
+    out_shape = [jax.ShapeDtypeStruct(tokens.shape, BF), whole(packed)]
     out_shape += [whole(shard) for _ in range(layers) for shard in shards]
     moves = 1 + layers * kinds
     outs = pl.pallas_call(
         functools.partial(gather_body, grid, layers, kinds),
-        in_specs=[any_spec()] * (3 + kinds),
+        in_specs=[any_spec()] * (2 + kinds),
         out_specs=[any_spec()] * len(out_shape),
         out_shape=out_shape,
         scratch_shapes=[
             pltpu.SemaphoreType.DMA((moves, 2, Spread.count(grid))),
-            pltpu.SemaphoreType.DMA((moves + 2,)),
-            pltpu.SemaphoreType.DMA((2, 2, 2)),
+            pltpu.SemaphoreType.DMA((moves + 1,)),
+            pltpu.SemaphoreType.DMA((2, 2)),
         ],
         compiler_params=pltpu.CompilerParams(
             collective_id=0, has_side_effects=True, vmem_limit_bytes=VMEM_LIMIT
         ),
-    )(tokens, cotangent, packed, *shards)
-    width = tokens.shape[2]
-    gains_all = outs[2][..., : layers * 2, : gains.shape[2]]
+    )(tokens, packed, *shards)
+    gains_all = outs[1][..., : layers * 2, : gains.shape[2]]
     gains_all = jnp.moveaxis(gains_all, 3, 0).reshape(layers, 2, -1)
-    weights = [
-        [outs[3 + l * kinds + i].reshape(-1, shards[i].shape[2]) for i in range(kinds)]
-        for l in range(layers)
-    ]
-    return outs[0].reshape(-1, width), outs[1].reshape(-1, width), gains_all, weights
+    weights = [list(outs[2 + l * kinds : 2 + (l + 1) * kinds]) for l in range(layers)]
+    return outs[0].reshape(-1, tokens.shape[2]), gains_all, weights
+
+
+def unless(condition, act):
+    if condition is None:
+        act()
+    else:
+        pl.when(jnp.logical_not(condition))(act)
 
 
 class Move:
-    def __init__(self, array, shape, count, copies):
+    def __init__(self, array, shape, count, copies, plan=None, in_place=False):
         self.array, self.shape, self.count, self.copies = array, shape, count, copies
+        self.plan, self.in_place = plan or self._plain, in_place
+
+    def _plain(self, here, source, target, sends, recvs, base):
+        found = []
+        for i, (what, where, peer, giver) in enumerate(self.copies(here, source, target)):
+            copy = pltpu.make_async_remote_copy(
+                src_ref=what,
+                dst_ref=where,
+                send_sem=sends.at[base + i],
+                recv_sem=recvs.at[base + i],
+                device_id=peer,
+                device_id_type=MESH,
+            )
+            found.append((copy, None, None, giver, copy, None))
+        return found
 
 
 def flip_move(grid, parts, phase):
@@ -476,10 +512,104 @@
     return Move(array, (grid.U - 1,) + shape, grid.U - 1, copies)
 
 
+def spread_move(grid, whole, stage):
+    half = whole.shape[-1] // 2
+    keys = [0] if stage == 0 else range(1 << (stage - 1), 1 << stage)
+
+    def copies(here, source, target):
+        mine = target.at[:, :, :, :, pl.ds(pl.multiple_of(here.c * half, 128), half)]
+        found = []
+        for key in keys:
+            block = mine.at[here.place(key)]
+            found.append((block, block, here.swap, here.swap))
+            for phase in range(stage, grid.bits):
+                found.append((block, block, here.flip(phase), here.flip(phase)))
+        return found
+
+    count = len(keys) * (1 + grid.bits - stage)
+    return Move(whole, whole.shape, count, copies, in_place=True)
+
+
+def peer_move(array, peer):
+    return Move(array, array.shape, 1, lambda here, source, target: [(source, target, peer(here), peer(here))])
+
+
+def line_move(grid, array):
+    def copies(here, source, target):
+        return [(source, target.at[t - 1], here.ring(t), here.ring(grid.F - t)) for t in range(1, grid.F)]
+
+    return Move(array, (grid.F - 1,) + array.shape, grid.F - 1, copies)
+
+
+def regroup_move(grid, array):
+    def plan(here, source, target, sends, recvs, base):
+        found = []
+        k = jnp.minimum(here.f, grid.F - 1 - here.f)
+        side = here.f // (grid.F // 2)
+        for m in range(2):
+            c2, f2 = k // grid.Q, (2 * m + here.c) * grid.Q + k % grid.Q
+            same = (c2 == here.c) & (f2 == here.f)
+            away = pltpu.make_async_remote_copy(
+                src_ref=source.at[m],
+                dst_ref=target.at[side],
+                send_sem=sends.at[base + m],
+                recv_sem=recvs.at[base + side],
+                device_id=here.device(here.j, c2, f2),
+                device_id_type=MESH,
+            )
+            own = pltpu.make_async_copy(source.at[m], target.at[side], sends.at[base + m])
+            from_f = here.k if m == 0 else grid.F - 1 - here.k
+            same_in = (here.r == here.c) & (from_f == here.f)
+            came = pltpu.make_async_remote_copy(
+                src_ref=source.at[0],
+                dst_ref=target.at[m],
+                send_sem=sends.at[base],
+                recv_sem=recvs.at[base + m],
+                device_id=here.swap,
+                device_id_type=MESH,
+            )
+            found.append((away, same, own, here.device(here.j, here.r, from_f), came, same_in))
+        return found
+
+    return Move(array, array.shape, 2, None, plan)
+
+
+def regroup_back_move(grid, array):
+    def plan(here, source, target, sends, recvs, base):
+        found = []
+        for piece in range(2):
+            f = here.k if piece == 0 else grid.F - 1 - here.k
+            same = (here.r == here.c) & (f == here.f)
+            away = pltpu.make_async_remote_copy(
+                src_ref=source.at[piece],
+                dst_ref=target.at[here.m],
+                send_sem=sends.at[base + piece],
+                recv_sem=recvs.at[base + here.m],
+                device_id=here.device(here.j, here.r, f),
+                device_id_type=MESH,
+            )
+            own = pltpu.make_async_copy(source.at[piece], target.at[here.m], sends.at[base + piece])
+            k = jnp.minimum(here.f, grid.F - 1 - here.f)
+            c2, f2 = k // grid.Q, (2 * piece + here.c) * grid.Q + k % grid.Q
+            same_in = (c2 == here.c) & (f2 == here.f)
+            came = pltpu.make_async_remote_copy(
+                src_ref=source.at[0],
+                dst_ref=target.at[piece],
+                send_sem=sends.at[base],
+                recv_sem=recvs.at[base + piece],
+                device_id=here.swap,
+                device_id_type=MESH,
+            )
+            found.append((away, same, own, here.device(here.j, c2, f2), came, same_in))
+        return found
+
+    return Move(array, array.shape, 2, None, plan)
+
+
 IDS = [1]
 
 
-def host(grid, body, steps, in_specs, operands, out_specs, out_shape, moves=(), scratch=(), cost=None, first=None):
+def host(grid, body, steps, in_specs, operands, out_specs, out_shape, moves=(), scratch=(), cost=None, reaches=False):
     counts = [len(operands), len(moves), len(out_shape), len(moves), len(scratch)]
 
     def kernel(*refs):
@@ -490,30 +620,35 @@
         ins, sources, outs, targets, held = parts
         here = Here(grid)
         step = pl.program_id(0)
-        copies = []
+        planned = []
         if moves:
-            send_sems, recv_sems = refs[at:]
-            listed = [c for m, s, t in zip(moves, sources, targets) for c in m.copies(here, s, t)]
-            for i, (source, target, peer, _) in enumerate(listed):
-                copies.append(
-                    pltpu.make_async_remote_copy(
-                        src_ref=source,
-                        dst_ref=target,
-                        send_sem=send_sems.at[i],
-                        recv_sem=recv_sems.at[i],
-                        device_id=peer,
-                        device_id_type=MESH,
-                    )
-                )
+            sends, recvs = refs[at:]
+            base = 0
+            for move, source, target in zip(moves, sources, targets):
+                planned += move.plan(here, source, target, sends, recvs, base)
+                base += move.count
+
+        if moves or reaches:
 
             @pl.when(step == 0)
             def _():
                 barrier = pltpu.get_barrier_semaphore()
-                for _, _, _, peer in listed:
-                    pl.semaphore_signal(barrier, inc=1, device_id=peer, device_id_type=MESH)
-                pl.semaphore_wait(barrier, len(listed))
-                for copy in copies:
-                    copy.start()
+                if reaches:
+                    pl.semaphore_signal(barrier, inc=1, device_id=here.swap, device_id_type=MESH)
+                for _, _, _, giver, _, same_in in planned:
+                    signal = functools.partial(
+                        pl.semaphore_signal, barrier, inc=1, device_id=giver, device_id_type=MESH
+                    )
+                    unless(same_in, signal)
+                due = int(reaches) + sum(same is None for _, same, _, _, _, _ in planned)
+                for _, same, _, _, _, _ in planned:
+                    if same is not None:
+                        due = due + 1 - same.astype(jnp.int32)
+                pl.semaphore_wait(barrier, due)
+                for away, same, own, _, _, _ in planned:
+                    unless(same, away.start)
+                    if same is not None:
+                        pl.when(same)(own.start)
 
         if body is not None:
             body(here, step, ins, outs, held)
@@ -521,15 +656,19 @@
 
             @pl.when(step == steps - 1)
             def _():
-                for copy in copies:
-                    copy.wait()
+                for away, same, own, _, came, same_in in planned:
+                    unless(same, away.wait_send)
+                    if same is not None:
+                        pl.when(same)(own.wait)
+                    unless(same_in, came.wait_recv)
 
     total = sum(move.count for move in moves)
     extra = {}
     sems = []
-    if moves:
+    if moves or reaches:
         extra = {"collective_id": IDS[0], "has_side_effects": True}
         IDS[0] += 1
+    if moves:
         sems = [pltpu.SemaphoreType.DMA((total,)), pltpu.SemaphoreType.DMA((total,))]
     outs = pl.pallas_call(
         kernel,
@@ -538,6 +677,9 @@
         out_specs=list(out_specs) + [any_spec()] * len(moves),
         out_shape=list(out_shape) + [jax.ShapeDtypeStruct(m.shape, m.array.dtype) for m in moves],
         scratch_shapes=list(scratch) + sems,
+        input_output_aliases={
+            len(operands) + i: len(out_shape) + i for i, move in enumerate(moves) if move.in_place
+        },
         compiler_params=pltpu.CompilerParams(vmem_limit_bytes=VMEM_LIMIT, **extra),
         cost_estimate=cost,
     )(*operands, *[move.array for move in moves])
@@ -548,16 +690,28 @@
     return host(grid, None, 1, [], [], [], [], moves)[1]
 
 
-def scatter_gains(grid, total):
-    layers, kinds, width = total.shape
-    devices = grid.n_dp * grid.F
-    total = total + grid.swap(total)
-    for p in range(grid.bits):
-        total = total + grid.permute(total, lambda j, c, f: (j ^ (1 << p), c, f))
-    for step in [1 << p for p in range(grid.F.bit_length() - 1)]:
-        total = total + grid.permute(total, lambda j, c, f: (j, c, f ^ step))
-    here = (grid.j * 2 + grid.c) * grid.F + grid.f
-    return lax.dynamic_slice_in_dim(total, here * (width // devices), width // devices, axis=2)
+class GainSum:
+    def __init__(self, grid, total):
+        self.grid, self.total, self.stage = grid, total, 0
+
+    def move(self):
+        grid, phase = self.grid, self.stage - 1
+        if self.stage == 0:
+            return swap_move(self.total)
+        if phase < grid.bits:
+            return peer_move(self.total, lambda here: here.flip(phase))
+        return line_move(grid, self.total)
+
+    def took(self, got):
+        if self.stage > self.grid.bits:
+            got = sum(got[t] for t in range(self.grid.F - 1))
+        self.total = self.total + got
+        self.stage += 1
+
+    def finish(self):
+        while self.stage <= self.grid.bits + 1:
+            self.took(send(self.grid, [self.move()])[0])
+        return self.total
 
 
 def rope_tables():
@@ -1002,6 +1156,72 @@
     return pulled, grad_gain
 
 
+PRODUCT_TILE = 256
+
+
+def product(grid, left, left_other, right, moves=()):
+    rows, height = left.shape
+    stacked = right.ndim == 3
+    half = right.shape[-1] if stacked else right.shape[-1] // 2
+    tiles = height // PRODUCT_TILE
+
+    def part(ref, c):
+        return ref.at[c] if stacked else ref.at[:, pl.ds(pl.multiple_of(c * half, 128), half)]
+
+    def body(here, step, ins, outs, held):
+        own_ref, other_ref, right_ref = ins
+        own_right, other_right, total, own_sem, sems = held
+        own = pltpu.make_async_copy(part(right_ref, here.c), own_right, own_sem)
+        swap = pltpu.make_async_remote_copy(
+            src_ref=part(right_ref, 1 - here.c),
+            dst_ref=other_right,
+            send_sem=sems.at[0],
+            recv_sem=sems.at[1],
+            device_id=here.swap,
+            device_id_type=MESH,
+        )
+
+        @pl.when(step == 0)
+        def _():
+            own.start()
+            swap.start()
+            own.wait()
+
+        @pl.when(step < tiles)
+        def _():
+            total[step] = dot(own_ref[...], own_right[...], (0, 0))
+
+        @pl.when(step == tiles)
+        def _():
+            swap.wait()
+
+        @pl.when(step >= tiles)
+        def _():
+            outs[0][...] = (total[step - tiles] + dot(other_ref[...], other_right[...], (0, 0))).astype(BF)
+
+    early = lambda i: jnp.minimum(i, tiles - 1)
+    late = lambda i: jnp.maximum(i - tiles, 0)
+    outs, got = host(
+        grid, body, 2 * tiles,
+        [pl.BlockSpec((rows, PRODUCT_TILE), lambda i: (0, early(i))),
+         pl.BlockSpec((rows, PRODUCT_TILE), lambda i: (0, late(i))), any_spec()],
+        [left, left_other, right],
+        [pl.BlockSpec((PRODUCT_TILE, half), lambda i: (late(i), 0))],
+        [kind(height, half)],
+        moves,
+        scratch=[
+            pltpu.VMEM((rows, half), BF),
+            pltpu.VMEM((rows, half), BF),
+            pltpu.VMEM((tiles, PRODUCT_TILE, half), F32),
+            pltpu.SemaphoreType.DMA,
+            pltpu.SemaphoreType.DMA((2,)),
+        ],
+        cost=pl.CostEstimate(flops=4 * rows * height * half, bytes_accessed=2 * height * half, transcendentals=0),
+        reaches=True,
+    )
+    return outs[0], got
+
+
 class Reduce:
     def __init__(self, grid, total):
         self.grid = grid
@@ -1088,20 +1308,23 @@
         size = value.shape[-1] // 2
         return lax.dynamic_slice_in_dim(value, c * size, size, axis=value.ndim - 1)
 
-    def chip(value):
-        return jnp.concatenate([value, grid.swap(value)])
-
-    hidden, cotangent_rows, gains, weights = gather_all(
-        grid, tokens, cotangent, norm_gains, [attention_in, attention_out, feed_in, feed_out]
+    hidden, gains, weights = gather_all(
+        grid, tokens, norm_gains, [attention_in, attention_out, feed_in, feed_out]
     )
     hidden = hidden.astype(F32)
     gain = lambda l, i: gains[l, i][None]
+    flat = lambda w: w.reshape(-1, w.shape[-1])
     saved = []
+    cotangent_rows = None
     for l in range(layers):
-        w_qkv, w_out, w_up, w_down = weights[l]
+        w_qkv, w_out = flat(weights[l][0]), flat(weights[l][1])
         memory = l == layers - 1
         normed = norm(hidden, gain(l, 0)).astype(BF)
-        split, _ = split_heads(grid, memory, tables, mm(normed, w_qkv))
+        coming = weights[l + 1] if l + 1 < layers else None
+        moves = [spread_move(grid, weights[l][3], 1)] if later_here(l, 3) else []
+        split, got = split_heads(grid, memory, tables, mm(normed, w_qkv), moves)
+        if moves:
+            weights[l][3] = got[0]
         (others,) = send(grid, [member_move(grid, split[1], False)])
         pairs = [split[1]] + [others[t] for t in range(grid.U - 1)]
         extra = None
@@ -1112,44 +1335,78 @@
             slots = jnp.swapaxes(slots, 0, 1).reshape(2, n_dp * topk, -1)
             slots = both_halves(slots, grid.swap(slots))
             extra = {"query": split[2], "keys": slots[0], "values": slots[1], "bias": bias}
-        attended, _ = attend(grid, valid, split[0], pairs, extra)
+        moves = []
+        if later_here(l, 2):
+            moves += [spread_move(grid, weights[l][2], 1), spread_move(grid, weights[l][3], 2)]
+        if coming is not None:
+            moves.append(spread_move(grid, coming[3], 0))
+        attended, got = attend(grid, valid, split[0], pairs, extra, moves)
+        if later_here(l, 2):
+            weights[l][2], weights[l][3] = got[:2]
+            (weights[l][2],) = send(grid, [spread_move(grid, weights[l][2], 2)])
+            for stage in range(3, grid.bits + 1):
+                weights[l][2:] = send(grid, [spread_move(grid, w, stage) for w in weights[l][2:]])
+        if coming is not None:
+            coming[3] = got[-1]
         middle = hidden + mm(attended, w_out)
-        (out, normed_feed, both, inner), _ = feed(grid, middle, gain(l, 1), w_up, w_down)
+        moves = []
+        if coming is not None:
+            moves = [spread_move(grid, coming[2], 0), regroup_move(grid, cotangent)]
+        w_up, w_down = flat(weights[l][2]), flat(weights[l][3])
+        (out, normed_feed, both, inner), got = feed(grid, middle, gain(l, 1), w_up, w_down, moves)
+        if coming is not None:
+            coming[2], cotangent_rows = got
         saved.append((hidden, normed, split[0], pairs, extra, attended, middle, normed_feed, both, inner))
         hidden = out
-    layer_output = grid.from_units(hidden.astype(BF))
-
+    weights = [[flat(w) for w in kinds] for kinds in weights]
+    cotangent_rows = cotangent_rows.reshape(-1, width)
+    out_rows = hidden.astype(BF).reshape(2, grid.R, width)
     grad = cotangent_rows.astype(F32)
     found = [[None] * 4 for _ in range(layers)]
     grad_gains = [[None, None] for _ in range(layers)]
-    before = None
+    layer_output = None
+    above = None
     for l in reversed(range(layers)):
         w_qkv, w_out, w_up, w_down = weights[l]
         hidden, normed, query, pairs, extra, attended, middle, normed_feed, both, inner = saved[l]
         low = grad.astype(BF)
-        right = jnp.concatenate([half(low, grid.c), grid.swap(half(low, 1 - grid.c))])
-        down = Reduce(grid, mm(chip(inner), right, (0, 0)).astype(BF))
-
-        moves = [down.flip()] + ([up_before.ring(), last_before.flip()] if before else [])
+
+        moves = [swap_move(inner), swap_move(normed_feed), swap_move(normed), swap_move(attended)]
+        if above is None:
+            moves.append(regroup_back_move(grid, out_rows))
+        else:
+            moves += [above[1].flip(), above[2].flip(), above[0].ring()]
         (grad, grad_low, grads, gain_feed), got = feed_back(
             grid, grad, middle, gain(l, 1), both, w_up, w_down, moves
         )
+        inner_other, normed_feed_other, normed_other, attended_other = got[:4]
+        if above is None:
+            layer_output = got[4]
+            moves = []
+        else:
+            above[1].flipped(got[4])
+            above[2].flipped(got[5])
+            above[0].arrived(got[6])
+            moves = [above[1].flip(), above[2].flip()]
+        total, got = product(grid, inner, inner_other, low, moves)
+        down = Reduce(grid, total)
+        if above is not None:
+            above[1].flipped(got[0])
+            above[2].flipped(got[1])
+        total, got = product(grid, normed_feed, normed_feed_other, grads, [down.flip()])
+        up = Reduce(grid, total)
         down.flipped(got[0])
-        if before:
-            up_before.arrived(got[1])
-            last_before.flipped(got[2])
-        grads_mine = lax.dynamic_index_in_dim(grads, grid.c, 0, keepdims=False)
-        grads_give = lax.dynamic_index_in_dim(grads, 1 - grid.c, 0, keepdims=False)
-        right = jnp.concatenate([grads_mine, grid.swap(grads_give)])
-        up = Reduce(grid, mm(chip(normed_feed), right, (0, 0)).astype(BF))
         grad_heads = mm(grad_low, w_out, (1, 1)).astype(BF)
 
-        moves = [up.flip(), down.flip()] + ([last_before.ring()] if before else [])
+        moves = [up.flip(), down.flip()]
+        if above is not None:
+            moves += [above[1].ring(), above[2].ring()]
         outs, got = attend_back(grid, valid, tables, query, grad_heads, pairs, extra, moves)
         up.flipped(got[0])
         down.flipped(got[1])
-        if before:
-            last_before.arrived(got[2])
+        if above is not None:
+            above[1].arrived(got[2])
+            above[2].arrived(got[3])
         grad_query, own, others = outs[:3]
         memory_grad = None
         moves = [member_move(grid, others, True)]
@@ -1157,11 +1414,15 @@
             moves.append(swap_move(half(outs[3], 1 - grid.c)))
         got = send(grid, moves)
         others = got[0]
+        moves = []
         if extra is not None:
             joined = half(outs[3], grid.c).astype(F32) + got[1].astype(F32)
             joined = joined.astype(BF).reshape(2, n_dp, topk, -1)
-            (came,) = send(grid, [slots_move(grid, joined, True)])
-            total = joined[:, 0].astype(F32) + sum(came[t].astype(F32) for t in range(n_dp - 1))
+            moves = [slots_move(grid, joined, True)]
+        total, got = product(grid, attended, attended_other, grad_low, moves)
+        across = Reduce(grid, total)
+        if extra is not None:
+            total = joined[:, 0].astype(F32) + sum(got[0][t].astype(F32) for t in range(n_dp - 1))
             for t in range(1, grid.Q):
                 total = total + grid.within(total.astype(BF), t).astype(F32)
             total = total.astype(BF)
@@ -1171,45 +1432,47 @@
         )
         up.flipped(got[0])
         down.arrived(got[1])
-        grads_mine, grads_give = half(grad_projected, grid.c), half(grad_projected, 1 - grid.c)
-        right = jnp.concatenate([grads_mine, grid.swap(grads_give)])
-        w_qkv_sum = mm(chip(normed), right, (0, 0)).astype(BF)
-        right = jnp.concatenate([half(grad_low, grid.c), grid.swap(half(grad_low, 1 - grid.c))])
-        w_out_sum = mm(chip(attended), right, (0, 0)).astype(BF)
-        last = Reduce(grid, jnp.concatenate([w_out_sum, w_qkv_sum], axis=1))
         pulled, gain_attention = norm_back(hidden, gain(l, 0), mm(grad_projected, w_qkv, (1, 1)))
         grad = grad + pulled
         grad_gains[l] = [gain_attention[0], gain_feed[0]]
+        moves = []
+        if l == 0:
+            small = GainSum(grid, jnp.stack([jnp.stack(pair) for pair in grad_gains]).reshape(-1, HEAD_DIM))
+            moves = [up.ring(), across.flip(), small.move()]
+        total, got = product(grid, normed, normed_other, grad_projected, moves)
+        last = Reduce(grid, total)
+        if l == 0:
+            up.arrived(got[0])
+            across.flipped(got[1])
+            small.took(got[2])
         found[l][3] = down.done(grid.swap(down.give))
-        if before:
-            found[l + 1][2] = up_before.done(grid.swap(up_before.give))
-            both_last = last_before.done(grid.swap(last_before.give))
-            found[l + 1][0], found[l + 1][1] = last_parts(both_last, width)
-        if l > 0:
-            (came,) = send(grid, [last.flip()])
-            last.flipped(came)
-        before, up_before, last_before = True, up, last
-    came = send(grid, [last.flip(), up.ring()])
-    last.flipped(came[0])
-    up.arrived(came[1])
-    last.arrived(send(grid, [last.ring()])[0])
-    found[0][2] = up.done(grid.swap(up.give))
-    found[0][0], found[0][1] = last_parts(last.done(grid.swap(last.give)), width)
-    input_grad = grid.from_units(grad.astype(BF)).astype(F32)
+        if above is not None:
+            for i, reduced in zip((2, 1, 0), above):
+                found[l + 1][i] = reduced.done(grid.swap(reduced.give))
+        above = (up, across, last)
+    up, across, last = above
+    in_rows = grad.astype(BF).reshape(2, grid.R, width)
+    got = send(grid, [last.flip(), across.flip(), regroup_back_move(grid, in_rows), small.move()])
+    last.flipped(got[0])
+    across.flipped(got[1])
+    input_grad = got[2].astype(F32)
+    small.took(got[3])
+    got = send(grid, [last.flip(), across.ring(), small.move()])
+    last.flipped(got[0])
+    across.arrived(got[1])
+    small.took(got[2])
+    got = send(grid, [last.ring(), small.move()])
+    last.arrived(got[0])
+    small.took(got[1])
+    total_gains = small.finish().reshape(layers, 2, n_dp * pieces, -1)
+    device = (grid.j * 2 + grid.c) * grid.F + grid.f
+    for i, reduced in zip((2, 1, 0), above):
+        found[0][i] = reduced.done(grid.swap(reduced.give))
     return (
         layer_output,
         input_grad,
         *(jnp.stack([found[l][i] for l in range(layers)]) for i in range(4)),
-        scatter_gains(grid, jnp.stack([jnp.stack(pair) for pair in grad_gains])),
-    )
-
-
-def last_parts(value, width):
-    size = value.shape[1] // 2
-    halves = [value[:, :size], value[:, size:]]
-    return (
-        jnp.concatenate([h[:, width // 2 :] for h in halves], axis=1),
-        jnp.concatenate([h[:, : width // 2] for h in halves], axis=1),
+        lax.dynamic_index_in_dim(total_gains, device, 2, keepdims=False),
     )
 
 

time: 1030 us -> 962 us (0.934)
  Pallas kernels: 752 us -> 797 us
  matrix products: 80.9 us -> 40 us
  waiting for transfers between devices: 38 us -> 0.89 us
  starting transfers between devices: 31.2 us -> 2.87 us
  local copies, waits for them, and re-layouts: 67.5 us -> 55.7 us
    pallas_call x22 -> x29, Pallas kernels: 474 us -> 596 us  [host(): pl.pallas_call(kernel, grid=(steps,), in_specs=list(in_specs) + [any_spec...]
    pallas_call x1, Pallas kernels: 274 us -> 198 us  [gather_all(): pl.pallas_call(functools.partial(gather_body, grid, layers, kinds), in_sp...]
    dot_general x16 -> x8, matrix products: 80.9 us -> 40 us  [dot(): lax.dot_general(left, right, (((contract[0],), (contract[1],)), ((), ()))...]
    ppermute x34 -> x11, waiting for transfers between devices: 38 us -> 0.89 us  [permute(): return lax.ppermute(value, ('dp', 'fsdp'), pairs)]
    ppermute x34 -> x11, starting transfers between devices: 31.2 us -> 2.87 us  [permute(): return lax.ppermute(value, ('dp', 'fsdp'), pairs)]
    squeeze x2 -> x0, local copies, waits for them, and re-layouts: 12.3 us -> none  [local(): grads_mine = lax.dynamic_index_in_dim(grads, grid.c, 0, keepdims=False)]
    unnamed x177 -> x206, local copies, waits for them, and re-layouts: 34.8 us -> 36.6 us
  transfers between devices with their start and end apart: 34 -> 11, of which waited for: 11 -> 1; matrix products, arithmetic and copies ran while one was open for 11% -> 4% of each run, Pallas kernels for 49% -> 30%
where the time goes in v4:
time: 962 us; the launch traced here: 955 us
  Pallas kernels  797 us (83%)
  other arithmetic  55.8 us (6%)
  local copies, waits for them, and re-layouts  55.7 us (6%)
  matrix products  40 us (4%)
    pallas_call x29, Pallas kernels, host(): pl.pallas_call(kernel, grid=(steps,), in_specs=list(in_specs) + [any_spec...  596 us
    pallas_call x1, Pallas kernels, gather_all(): pl.pallas_call(functools.partial(gather_body, grid, layers, kinds), in_sp...  198 us
    dot_general x8, matrix products, dot(): lax.dot_general(left, right, (((contract[0],), (contract[1],)), ((), ()))...  40 us
    unnamed x206, local copies, waits for them, and re-layouts  36.6 us
  transfers between devices with their start and end apart: 11, of which 1 were waited for; matrix products, arithmetic and copies ran while one was open for 4% of the time, Pallas kernels for 30%

profile of v4, /device:TPU:0, one launch (start us, length us, event | category | flops | bytes accessed | tf_op | source)
XLA Modules:
  0.0 955.0 jit_solution(17134341712561929402)
XLA Ops:
  9.0 197.8 %shard_map.153 = (bf16[2,256,1024]{2,1,0:T(8,128)(2,1)S(1)}, f32[4,2,4,8,128]{4,3,2,1,0:T(8,128)S(1)}, bf16[4,2,4,32,3072]{4,3,2,1,0:T(8,128)(2,1)}, bf16[4,2,4,...) custom-call(bf16[2,256,1024]{2,1,0:T(8,128)(2,1)S(1)} %copy-done.52,, ...), custom_call_target="tpu_custom_call" | custom-call | tf_op jit(solution)/shard_map/pallas_call | solution.py:407
  209.0 8.4 fusion.30.refs_2_.refs_3_.refs_4_
  234.6 20.8 %shard_map.156 = (bf16[512,1024]{1,0:T(8,128)(2,1)S(1)}, bf16[4,2,4,88,1024]{4,3,2,1,0:T(8,128)(2,1)}) custom-call(s32[1]{0:T(128)} %bitcast.2.refs_0_, bf16[512,1024]{1,0:T(8,128)(2,1)S(1)} %copy-done.24, bf16[2,512,1024]{2,1,0:T(8,128)(2,1)S(1)} %get-tuple-element.117.refs_0_.refs_2_.refs_5_, ...), custom_call_target="tpu_custom_call", output_to_operand_aliasing={{1}: (4, {})} | custom-call | flops 1610612736 | bytes 8388608 | tf_op jit(solution)/shard_map/pallas_call | solution.py:673
  258.0 37.8 %shard_map.157 = (f32[512,1024]{1,0:T(8,128)S(1)}, bf16[512,1024]{1,0:T(8,128)(2,1)S(1)}, bf16[2,512,2816]{2,1,0:T(8,128)(2,1)}, bf16[512,2816]{1,0:T(8,128)(2,1...) custom-call(f32[512,1024]{1,0:T(8,128)} %bitcast_add_fusion.refs_0_.re, ...), custom_call_target="tpu_custom_call", output_to_operand_aliasing={{4}: (5, {})} | custom-call | flops 8858370048 | bytes 17301504 | tf_op jit(solution)/shard_map/pallas_call | solution.py:673
  304.2 13.6 %shard_map.158 = (bf16[512,1024]{1,0:T(8,128)(2,1)S(1)}, bf16[3,512,1024]{2,1,0:T(8,128)(2,1)}, bf16[512,1024]{1,0:T(8,128)(2,1)S(1)}, bf16[4,2,4,88,1024]{4,3,2,1,0:T(8,128)(2,1)}) custom-call(f32[1024,128]{1,0:T(8,128)S(1)} %copy-done.9, f32[1024,128]{1,0:T(8,128)S(1)} %copy-done.12, ...), custom_call_target="tpu_custom_call", output_to_operand_aliasing={{3}: (5, {})} | custom-call | flops 15728640 | bytes 12582912 | tf_op jit(solution)/shard_map/pallas_call | solution.py:673
  333.5 30.0 %shard_map.161 = bf16[7,2,128,512]{3,2,1,0:T(8,128)(2,1)S(1)} custom-call(bf16[2,128,512]{2,1,0:T(8,128)(2,1)S(1)} %shard_map.160.refs_0_), custom_call_target="tpu_custom_call" | custom-call | tf_op jit(solution)/shard_map/pallas_call | solution.py:673
  378.9 24.8 %shard_map.162 = (bf16[512,1024]{1,0:T(8,128)(2,1)S(1)}, bf16[4,2,4,32,5632]{4,3,2,1,0:T(8,128)(2,1)}, bf16[4,2,4,88,1024]{4,3,2,1,0:T(8,128)(2,1)}) custom-call(s32[1]{0:T(128)} %bitcast.2.refs_0_, bf16[512,1024]{1,0:T(8,128)(2,1)S(1)} %copy-done.42, ...), custom_call_target="tpu_custom_call", output_to_operand_aliasing={{1}: (8, {}), {2}: (9, {})} | custom-call | flops 3758096384 | bytes 16777216 | tf_op jit(solution)/shard_map/pallas_call | solution.py:673
  410.8 18.4 %shard_map.164 = (f32[512,1024]{1,0:T(8,128)S(1)}, bf16[512,1024]{1,0:T(8,128)(2,1)S(1)}, bf16[2,512,2816]{2,1,0:T(8,128)(2,1)}, bf16[512,2816]{1,0:T(8,128)(2,1)}) custom-call(f32[512,1024]{1,0:T(8,128)S(1)} %convolution_add_fusion.refs_0_.refs_1_, f32[1,1024]{1,0:T(1,128)S(1)} %get-tuple-element.251.refs_1_.refs_2_, bf16[1024,5632]{1,0:T(8,128)(2,1)} %bitcast.260, ...), custom_call_target="tpu_custom_call" | custom-call | flops 8858370048 | bytes 17301504 | tf_op jit(solution)/shard_map/pallas_call | solution.py:673
  430.5 32.0 %shard_map.165 = (f32[512,1024]{1,0:T(8,128)}, bf16[512,1024]{1,0:T(8,128)(2,1)S(1)}, bf16[2,512,2816]{2,1,0:T(8,128)(2,1)}, f32[1,1024]{1,0:T(1,128)S(1)}, bf16...) custom-call(f32[512,1024]{1,0:T(8,128)} %bitcast_convert_fusion.refs, ...), custom_call_target="tpu_custom_call" | custom-call | flops 8858370048 | bytes 17301504 | tf_op jit(solution)/shard_map/pallas_call | solution.py:673
  464.8 15.0 %shard_map.166 = bf16[2816,512]{1,0:T(8,128)(2,1)S(1)} custom-call(bf16[512,2816]{1,0:T(8,128)(2,1)} %get-tuple-element.138.refs_7_.refs_0_, bf16[512,2816]{1,0:T(8,128)(2,1)} %get-tuple-element.146.refs_1_, bf16[512,1024]{1,0:T(8,128)(2,1)S(1)} %bitcast.253), custom_call_target="tpu_custom_call" | custom-call | flops 2952790016 | bytes 2883584 | tf_op jit(solution)/shard_map/pallas_call | solution.py:673
  481.5 20.7 %shard_map.167 = (bf16[1024,2816]{1,0:T(8,128)(2,1)}, bf16[2,704,512]{2,1,0:T(8,128)(2,1)S(1)}) custom-call(bf16[512,1024]{1,0:T(8,128)(2,1)S(1)} %copy-done.51, bf16[512,1024]{1,0:T(8,128)(2,1)S(1)} %get-tuple-element.144.refs_1_, bf16[2,512,2816]{2,1,0:T(8,128)(2,1)} %get-tuple-element.145.refs_2_, bf16[4,704,512]{2,1,0:T(8,128)(2,1)} %bitcast.254), custom_call_target="tpu_custom_call" | custom-call | flops 5905580032 | bytes 5767168 | tf_op jit(solution)/shard_map/pallas_call | solution.py:673
  507.9 44.4 %shard_map.168 = (bf16[512,1024]{1,0:T(8,128)(2,1)S(1)}, f32[2,512,1024]{2,1,0:T(8,128)}, bf16[1,2,512,1024]{3,2,1,0:T(8,128)(2,1)}, bf16[2,1024,1024]{2,1,0:T(8...) custom-call(s32[1]{0:T(128)} %bitcast.2.refs_0_, f32[1024,128]{1,0:T(8,128)S(1)} %copy-done.10, ...), custom_call_target="tpu_custom_call" | custom-call | flops 9395240960 | bytes 16777216 | tf_op jit(solution)/shard_map/pallas_call | solution.py:673
  567.7 31.3 %shard_map.170 = (bf16[1024,512]{1,0:T(8,128)(2,1)S(1)}, bf16[7,2,128,512]{3,2,1,0:T(8,128)(2,1)S(1)}) custom-call(bf16[512,1024]{1,0:T(8,128)(2,1)S(1)} %copy-done.17, bf16[512,1024]{1,0:T(8,128)(2,1)S(1)} %get-tuple-element.155.refs_1_, bf16[512,1024]{1,0:T(8,128)(2,1)S(1)} %get-tuple-element.143.refs_2_, bf16[2,8,128,512]{3,2,1,0:T(8,128)(2,1)} %bitcast.274), custom_call_target="tpu_custom_call" | custom-call | flops 1073741824 | bytes 1048576 | tf_op jit(solution)/shard_map/pallas_call | solution.py:673
  605.8 21.4 %shard_map.171 = (bf16[512,3072]{1,0:T(8,128)(2,1)}, bf16[1,256,2816]{2,1,0:T(8,128)(2,1)S(1)}, bf16[3,2,88,512]{3,2,1,0:T(8,128)(2,1)S(1)}) custom-call(bf16[512,1024]{1,0:T(8,128)(2,1)S(1)} %get-tuple-element.149.refs_0_, f32[2,512,1024]{2,1,0:T(8,128)} %get-tuple-element.150.refs_1_, bf16[1,2,512,1024]{3,2,1,0:T(8,128)(2,1)} %copy-done.32, ...), custom_call_target="tpu_custom_call" | custom-call | flops 1048576 | bytes 8388608 | tf_op jit(solution)/shard_map/pallas_call | solution.py:673
  651.0 33.3 %shard_map.173 = (f32[512,1024]{1,0:T(8,128)}, bf16[512,1024]{1,0:T(8,128)(2,1)S(1)}, bf16[2,512,2816]{2,1,0:T(8,128)(2,1)}, f32[1,1024]{1,0:T(1,128)S(1)}, bf16...) custom-call(f32[512,1024]{1,0:T(8,128)} %get-tuple-element.214.refs_, ...), custom_call_target="tpu_custom_call" | custom-call | flops 8858370048 | bytes 17301504 | tf_op jit(solution)/shard_map/pallas_call | solution.py:673
  688.1 17.3 %shard_map.174 = (bf16[2816,512]{1,0:T(8,128)(2,1)}, bf16[1,256,512]{2,1,0:T(8,128)(2,1)S(1)}, bf16[1,256,1536]{2,1,0:T(8,128)(2,1)S(1)}) custom-call(bf16[512,2816]{1,0:T(8,128)(2,1)} %get-tuple-element.161.refs_7_.refs_0_, bf16[512,2816]{1,0:T(8,128)(2,1)} %get-tuple-element.170.refs_1_, bf16[512,1024]{1,0:T(8,128)(2,1)S(1)} %get-tuple-element.213.refs_2_, ...), custom_call_target="tpu_custom_call" | custom-call | flops 2952790016 | bytes 2883584 | tf_op jit(solution)/shard_map/pallas_call | solution.py:673
  710.2 21.1 %shard_map.175 = (bf16[1024,2816]{1,0:T(8,128)(2,1)}, bf16[2,704,512]{2,1,0:T(8,128)(2,1)S(1)}) custom-call(bf16[512,1024]{1,0:T(8,128)(2,1)S(1)} %copy-done.40, bf16[512,1024]{1,0:T(8,128)(2,1)S(1)} %get-tuple-element.168.refs_1_, bf16[2,512,2816]{2,1,0:T(8,128)(2,1)} %get-tuple-element.169.refs_2_, bf16[4,704,512]{2,1,0:T(8,128)(2,1)} %bitcast.284), custom_call_target="tpu_custom_call" | custom-call | flops 5905580032 | bytes 5767168 | tf_op jit(solution)/shard_map/pallas_call | solution.py:673
  734.8 52.1 %shard_map.176 = (bf16[512,1024]{1,0:T(8,128)(2,1)S(1)}, f32[2,512,1024]{2,1,0:T(8,128)}, bf16[1,2,512,1024]{3,2,1,0:T(8,128)(2,1)}, bf16[2,256,2816]{2,1,0:T(8,...) custom-call(s32[1]{0:T(128)} %bitcast.2.refs_0_, ...), custom_call_target="tpu_custom_call" | custom-call | flops 4026531840 | bytes 8388608 | tf_op jit(solution)/shard_map/pallas_call | solution.py:673
  797.0 21.1 %shard_map.178 = (bf16[512,3072]{1,0:T(8,128)(2,1)}, bf16[1,256,2816]{2,1,0:T(8,128)(2,1)S(1)}, bf16[3,2,88,512]{3,2,1,0:T(8,128)(2,1)S(1)}) custom-call(bf16[512,1024]{1,0:T(8,128)(2,1)S(1)} %get-tuple-element.178.refs_0_, f32[2,512,1024]{2,1,0:T(8,128)} %get-tuple-element.179.refs_1_, bf16[1,2,512,1024]{3,2,1,0:T(8,128)(2,1)S(1)} %shard_map.177.refs_2_, ...), custom_call_target="tpu_custom_call" | custom-call | flops 1048576 | bytes 8388608 | tf_op jit(solution)/shard_map/pallas_call | solution.py:673
  818.2 10.0 %fusion.6 = (f32[512]{0:T(512)}, f32[1024]{0:T(1024)S(1)}, f32[512,1024]{1,0:T(8,128)}) fusion(bf16[2,256,1024]{2,1,0:T(8,128)(2,1)S(1)} %copy-done.7, f32[1024]{0:T(1024)S(1)} %bitcast.288, f32[512]{0:T(512)S(1)} %bitcast.294, bf16[512,3072]{1,0:T(8,128)(2,1)} %get-tuple-element.183.refs_2_, bf16[1024,3072]{1,0:T(8,128)(2,1)} %bitcast.302), kind=kOutput, calls=%fused_computation.24 | convolution fusion | flops 3224893952 | bytes 12595200 | tf_op jit(solution)/shard_map/dot_general | solution.py:761
  836.4 29.2 %shard_map.180 = (bf16[1024,1536]{1,0:T(8,128)(2,1)}, bf16[3,2,32,2816]{3,2,1,0:T(8,128)(2,1)S(1)}, bf16[2,256,512]{2,1,0:T(8,128)(2,1)S(1)}, f32[32,128]{1,0:T(8,128)S(1)}) custom-call(bf16[512,1024]{1,0:T(8,128)(2,1)S(1)} %copy-done.18, bf16[512,1024]{1,0:T(8,128)(2,1)S(1)} %copy-done.79, bf16[512,3072]{1,0:T(8,128)(2,1)} %get-tuple-element.183.refs_2_, ...), custom_call_target="tpu_custom_call" | custom-call | flops 3221225472 | bytes 3145728 | tf_op jit(solution)/shard_map/pallas_call | solution.py:673
  868.8 32.7 %shard_map.181 = (bf16[2,256,1536]{2,1,0:T(8,128)(2,1)S(1)}, bf16[1,256,512]{2,1,0:T(8,128)(2,1)S(1)}, bf16[2,256,1024]{2,1,0:T(8,128)(2,1)S(1)}, f32[32,128]{1,0:T(8,128)S(1)}) custom-call(bf16[4,256,1536]{2,1,0:T(8,128)(2,1)} %bitcast.279, bf16[2,256,512]{2,1,0:T(8,128)(2,1)S(1)} %add_convert_fusion.13.refs_1_, bf16[2,256,1024]{2,1,0:T(8,128)(2,1)S(1)} %bitcast.233, ...), custom_call_target="tpu_custom_call" | custom-call | tf_op jit(solution)/shard_map/pallas_call | solution.py:673
  903.2 12.3 %shard_map.182 = (bf16[1,256,1536]{2,1,0:T(8,128)(2,1)S(1)}, bf16[3,2,32,512]{3,2,1,0:T(8,128)(2,1)S(1)}, f32[32,128]{1,0:T(8,128)S(1)}) custom-call(bf16[2,256,1536]{2,1,0:T(8,128)(2,1)S(1)} %add_convert_fusion.3.refs_0_, bf16[2,4,32,512]{3,2,1,0:T(8,128)(2,1)S(1)} %bitcast.251, f32[32,128]{1,0:T(8,128)S(1)} %add.420.refs_2_), custom_call_target="tpu_custom_call" | custom-call | tf_op jit(solution)/shard_map/pallas_call | solution.py:673
  915.8 21.5 %shard_map.183 = (bf16[3,2,32,1536]{3,2,1,0:T(8,128)(2,1)S(1)}, f32[3,32,128]{2,1,0:T(8,128)S(1)}) custom-call(bf16[2,4,32,1536]{3,2,1,0:T(8,128)(2,1)S(1)} %bitcast.236, f32[32,128]{1,0:T(8,128)S(1)} %add.423.refs_1_), custom_call_target="tpu_custom_call" | custom-call | tf_op jit(solution)/shard_map/pallas_call | solution.py:673
  (367 shorter events, 185.6 us)
Async XLA Ops:
  0.6 326.8 %collective-permute-start = (s32[2,1,8,128]{3,2,1,0:T(8,128)}, s32[2,1,8,128]{3,2,1,0:T(8,128)S(1)}, u32[]{:S(2)}, u32[]{:S(2)}) collective-permute-start(s32[2,1,8,128]{3,2,1,0:T(8,128)} %param.16), channel_id=1, source_target_pairs={{0,4},{1,5},{2,6},{3,7},{4,0},{5,1},{6,2},{7,3},{8,12},{9,13},{10,... | collective-permute-start | bytes 24584 | tf_op jit(solution)/shard_map/ppermute | solution.py:70
  208.2 47.2 %copy-start.6 = (bf16[2,256,1024]{2,1,0:T(8,128)(2,1)}, bf16[2,256,1024]{2,1,0:T(8,128)(2,1)S(1)}, u32[]{:S(2)}) copy-start(bf16[2,256,1024]{2,1,0:T(8,128)(2,1)S(1)} %get-tuple-element.113) | copy-start | bytes 3145732
  208.4 609.8 %copy-start.91 = (f32[1,1,1024]{2,1,0:T(1,128)}, f32[1,1,1024]{2,1,0:T(1,128)S(1)}, u32[]{:S(2)}) copy-start(f32[1,1,1024]{2,1,0:T(1,128)S(1)} %get-tuple-element.254) | copy-start | bytes 12292
  255.4 43.4 %slice-start = ((s8[6291456]{0:T(1024)(128)(4,1)}), s8[4194304]{0:T(1024)(128)(4,1)S(1)}, s32[]{:S(2)}) async-start(s8[6291456]{0:T(1024)(128)(4,1)} %bitcast.304), calls=%async_computation | async-start | bytes 8388608
  258.0 40.8 %slice-start.1 = ((s8[6291456]{0:T(1024)(128)(4,1)}), s8[2097152]{0:T(1024)(128)(4,1)S(1)}, s32[]{:S(2)}) async-start(s8[6291456]{0:T(1024)(128)(4,1)} %bitcast.304), calls=%async_computation.1 | async-start | bytes 4194304
  365.3 6.5 collective-permute-start.1
  368.8 449.3 %copy-start.93 = (f32[1,2,2,128]{3,1,2,0:T(2,128)}, f32[1,2,2,128]{3,1,2,0:T(2,128)S(1)}, u32[]{:S(2)}) copy-start(f32[1,2,2,128]{3,1,2,0:T(2,128)S(1)} %copy.48) | copy-start | bytes 6148
  378.8 24.9 %copy-start.14 = (bf16[1024,1024]{1,0:T(8,128)(2,1)}, bf16[1024,1024]{1,0:T(8,128)(2,1)S(1)}, u32[]{:S(2)}) copy-start(bf16[1024,1024]{1,0:T(8,128)(2,1)S(1)} %get-tuple-element.222.refs_5_.refs_8_) | copy-start | bytes 6291460
  600.7 5.0 collective-permute-start.2
  605.7 21.6 %copy-start.26 = (bf16[1,704,512]{2,1,0:T(8,128)(2,1)}, bf16[1,704,512]{2,1,0:T(8,128)(2,1)S(1)}, u32[]{:S(2)}) copy-start(bf16[1,704,512]{2,1,0:T(8,128)(2,1)S(1)} %add_convert_fusion.12) | copy-start | bytes 2162692
  605.8 21.5 %copy-start.81 = (bf16[2,256,2816]{2,1,0:T(8,128)(2,1)S(1)}, bf16[2,256,2816]{2,1,0:T(8,128)(2,1)}, u32[]{:S(2)}) copy-start(bf16[2,256,2816]{2,1,0:T(8,128)(2,1)} %add_convert_fusion.1.refs_5_) | copy-start | bytes 8650756
  685.4 21.9 %copy-start.55 = (bf16[512,1024]{1,0:T(8,128)(2,1)}, bf16[512,1024]{1,0:T(8,128)(2,1)S(1)}, u32[]{:S(2)}) copy-start(bf16[512,1024]{1,0:T(8,128)(2,1)S(1)} %get-tuple-element.167.refs_2_) | copy-start | bytes 3145732
  734.8 52.1 %copy-start.82 = (bf16[2,704,512]{2,1,0:T(8,128)(2,1)S(1)}, bf16[2,704,512]{2,1,0:T(8,128)(2,1)}, u32[]{:S(2)}) copy-start(bf16[2,704,512]{2,1,0:T(8,128)(2,1)} %add_convert_fusion.6.refs_8_) | copy-start | bytes 4325380
  836.4 29.3 %copy-start.96 = (f32[512]{0:T(512)S(1)}, f32[512]{0:T(512)}, u32[]{:S(2)}) copy-start(f32[512]{0:T(512)} %get-tuple-element.209) | copy-start | bytes 6148
  836.4 31.2 %copy-start.87 = (f32[512,1024]{1,0:T(8,128)S(1)}, f32[512,1024]{1,0:T(8,128)}, u32[]{:S(2)}) copy-start(f32[512,1024]{1,0:T(8,128)} %get-tuple-element.261) | copy-start | bytes 6291460
  915.5 21.7 %copy-start.72 = (bf16[3,2,32,512]{3,2,1,0:T(8,128)(2,1)}, bf16[3,2,32,512]{3,2,1,0:T(8,128)(2,1)S(1)}, u32[]{:S(2)}) copy-start(bf16[3,2,32,512]{3,2,1,0:T(8,128)(2,1)S(1)} %get-tuple-element.200) | copy-start | bytes 589828
  939.6 10.0 %collective-permute-start.9 = (bf16[88,512]{1,0:T(8,128)(2,1)S(1)}, bf16[88,512]{1,0:T(8,128)(2,1)S(1)}, u32[]{:S(2)}, u32[]{:S(2)}) collective-permute-start(bf16[88,512]{1,0:T(8,128)(2,1)S(1)} %fusion.20), channel_id=1, source_target_pairs={{0,4},{1,5},{2,6},{3,7},{4,0},{5,1},{6,2},{7,3},{8,12},{9,13},{10,... | collective-permute-start | bytes 270344 | tf_op jit(solution)/shard_map/ppermute | solution.py:70
  941.1 8.9 collective-permute-start.10
  941.8 10.2 %collective-permute-start.7 = (bf16[32,2816]{1,0:T(8,128)(2,1)S(1)}, bf16[32,2816]{1,0:T(8,128)(2,1)S(1)}, u32[]{:S(2)}, u32[]{:S(2)}) collective-permute-start(bf16[32,2816]{1,0:T(8,128)(2,1)S(1)} %fusion.15), channel_id=1, source_target_pairs={{0,4},{1,5},{2,6},{3,7},{4,0},{5,1},{6,2},{7,3},{8,12},{9,13},{10,... | collective-permute-start | bytes 540680 | tf_op jit(solution)/shard_map/ppermute | solution.py:70
  943.2 8.9 collective-permute-start.8
  944.6 2.8 collective-permute-start.5
  947.4 1.2 collective-permute-start.6
  948.6 2.4 collective-permute-start.3
  949.6 1.4 collective-permute-start.4
  (89 other events, 335.8 us)

commit v5 on v4

--- a/solution.py
+++ b/solution.py
@@ -369,26 +369,31 @@
     here = Here(grid)
     here.greet()
     rows = Regroup(here, tokens, tokens_out, regroup_sems, own_sems.at[0])
-    moves = [(Spread(here, gains, gains_out, sems.at[0], own_sems.at[1], False), True)]
-    for l in range(layers):
-        for i in range(kinds):
-            n = l * kinds + i
-            move = Spread(here, shards[i].at[l], wholes[n], sems.at[n + 1], own_sems.at[n + 2], True)
-            moves.append((move, not later_here(l, i)))
+    moves = []
+    for l, i in ORDER:
+        n = l * kinds + i
+        move = Spread(here, shards[i].at[l], wholes[n], sems.at[n + 1], own_sems.at[n + 2], True)
+        moves.append((move, not later_here(l, i)))
+    moves.insert(GAINS_AT, (Spread(here, gains, gains_out, sems.at[0], own_sems.at[1], False), True))
     for move, _ in moves:
         move.begin()
-    rows.start()
     steps = [move.steps(whole) for move, whole in moves]
     count = len(steps[0])
-    moves[0][0].to_line()
-    moves[1][0].to_line()
+    for at in range(AHEAD):
+        moves[at][0].to_line()
     for at in range(len(moves) + count - 1):
-        if at + 2 < len(moves):
-            moves[at + 2][0].to_line()
+        if at == ROWS_AT:
+            rows.start()
+        if at + AHEAD < len(moves):
+            moves[at + AHEAD][0].to_line()
         for back in reversed(range(count)):
             if 0 <= at - back < len(moves) and back < len(steps[at - back]):
                 steps[at - back][back]()
     rows.wait()
+
+
+ORDER = [(0, 1), (0, 3), (0, 2), (0, 0), (1, 0), (1, 1), (1, 3), (1, 2)]
+GAINS_AT, ROWS_AT, AHEAD = 3, 6, 1
 
 
 def later_here(l, i):
@@ -482,6 +487,16 @@
     return Move(array, array.shape if give is None else array.shape[1:], 1, copies)
 
 
+def swap_half_move(array):
+    half = array.shape[-1] // 2
+
+    def copies(here, source, target):
+        start = pl.multiple_of((1 - here.c) * half, 128)
+        return [(source.at[:, :, pl.ds(start, half)], target, here.swap, here.swap)]
+
+    return Move(array, array.shape[:-1] + (half,), 1, copies)
+
+
 def slots_move(grid, array, back):
     def copies(here, source, target):
         found = []
@@ -512,21 +527,26 @@
     return Move(array, (grid.U - 1,) + shape, grid.U - 1, copies)
 
 
-def spread_move(grid, whole, stage):
+def spread_move(grid, whole, stages):
     half = whole.shape[-1] // 2
-    keys = [0] if stage == 0 else range(1 << (stage - 1), 1 << stage)
+
+    def keys_of(stage):
+        return [0] if stage == 0 else range(1 << (stage - 1), 1 << stage)
 
     def copies(here, source, target):
-        mine = target.at[:, :, :, :, pl.ds(pl.multiple_of(here.c * half, 128), half)]
         found = []
-        for key in keys:
-            block = mine.at[here.place(key)]
-            found.append((block, block, here.swap, here.swap))
-            for phase in range(stage, grid.bits):
-                found.append((block, block, here.flip(phase), here.flip(phase)))
+        for stage, part, parts in stages:
+            size = half // parts
+            columns = pl.ds(pl.multiple_of(here.c * half + part * size, 128), size)
+            mine = target.at[:, :, :, :, columns]
+            for key in keys_of(stage):
+                block = mine.at[here.place(key)]
+                found.append((block, block, here.swap, here.swap))
+                for phase in range(stage, grid.bits):
+                    found.append((block, block, here.flip(phase), here.flip(phase)))
         return found
 
-    count = len(keys) * (1 + grid.bits - stage)
+    count = sum(len(keys_of(stage)) * (1 + grid.bits - stage) for stage, _, _ in stages)
     return Move(whole, whole.shape, count, copies, in_place=True)
 
 
@@ -767,38 +787,53 @@
     return dot(left, right, contract)
 
 
-def split_heads(grid, memory, tables, projected, moves=()):
-    rows, width = projected.shape
-    heads = width // (3 * HEAD_DIM)
+def project(grid, memory, tables, hidden, gain, weight, moves=()):
+    rows, width = hidden.shape
+    heads = weight.shape[1] // (3 * HEAD_DIM)
+    together = 2
+    size = together * HEAD_DIM
+    steps = heads // together
     count = 3 if memory else 2
 
     def body(here, step, ins, outs, held):
-        cos_ref, sin_ref, q_ref, k_ref, v_ref = ins
+        cos_ref, sin_ref, hidden_ref, gain_ref = ins[:4]
+        normed_ref, q_out, kv_out = outs[:3]
+
+        @pl.when(step == 0)
+        def _():
+            normed_ref[...] = norm(hidden_ref[...].astype(F32), gain_ref[...]).astype(BF)
+
         for part in range(2):
             at = pl.ds(part * grid.R, grid.R)
             cos = table_rows(grid, cos_ref, here.k, part)
             sin = table_rows(grid, sin_ref, here.k, part)
-            query, key = q_ref[at, :], k_ref[at, :]
-            outs[0][at, :] = turn(query, cos, sin).astype(BF)
-            outs[1][0, at, :] = turn(key, cos, sin).astype(BF)
-            outs[1][1, at, :] = v_ref[at, :].astype(BF)
+            normed = normed_ref[at, :]
+            query, key, value = (dot(normed, w[...], (1, 0)) for w in ins[4:])
+            kv_out[1, at, :] = value.astype(BF)
+            for h in range(together):
+                columns = slice(h * HEAD_DIM, (h + 1) * HEAD_DIM)
+                q_out[at, columns] = turn(query[:, columns], cos, sin).astype(BF)
+                kv_out[0, at, columns] = turn(key[:, columns], cos, sin).astype(BF)
             if memory:
-                outs[1][2, at, :] = key.astype(BF)
-                outs[2][at, :] = query.astype(BF)
-
-    piece = lambda at: columns_spec(rows, HEAD_DIM, first=at * heads)
+                kv_out[2, at, :] = key.astype(BF)
+                outs[3][at, :] = query.astype(BF)
+
+    piece = columns_spec(rows, size)
+    table = whole_spec(SEG, HEAD_DIM)
     flat = kind(rows, heads * HEAD_DIM)
-    table = whole_spec(SEG, HEAD_DIM)
     return host(
         grid,
         body,
-        heads,
-        [table, table, piece(0), piece(1), piece(2)],
-        [*tables, projected, projected, projected],
-        [piece(0), columns_spec(count, rows, HEAD_DIM)] + [piece(0)] * memory,
-        [flat, kind(count, rows, heads * HEAD_DIM)] + [flat] * memory,
+        steps,
+        [table, table, whole_spec(rows, width), whole_spec(1, width)]
+        + [columns_spec(width, size, first=i * steps) for i in range(3)],
+        [*tables, hidden, gain, weight, weight, weight],
+        [whole_spec(rows, width), piece, columns_spec(count, rows, size)] + [piece] * memory,
+        [kind(rows, width), flat, kind(count, rows, heads * HEAD_DIM)] + [flat] * memory,
         moves,
-        cost=pl.CostEstimate(flops=10 * rows * width, bytes_accessed=8 * rows * width, transcendentals=0),
+        cost=pl.CostEstimate(
+            flops=2 * rows * width * weight.shape[1], bytes_accessed=2 * width * weight.shape[1], transcendentals=0
+        ),
     )
 
 
@@ -1013,40 +1048,42 @@
         dq_ref, own_ref, others_ref = ins[:3]
         out_ref = outs[0]
 
-        @pl.when(step < heads)
+        @pl.when(step == 0)
         def _():
             out_ref[...] = dq_ref[...]
 
-        @pl.when(step >= heads)
+        @pl.when(step > 0)
         def _():
-            total = own_ref[0] + sum(others_ref[t, 0].astype(F32) for t in range(U - 1))
             for side in range(2):
-                at = slice(side * R, (side + 1) * R)
-                value = total[at]
-                if memory is not None:
-                    picked = ins[3][0]
-                    down = lax.broadcasted_iota(jnp.int32, (R, picked.shape[1]), 0)
-                    chosen = (down + piece_start(grid, here.k, side) == picked).astype(BF)
-                    value = value + dot(chosen, ins[4][0], (1, 0))
-                out_ref[at, :] = value.astype(BF)
-
-    which = lambda b: jnp.maximum(b // heads - 1, 0)
-    head = lambda b: jnp.where(b < heads, 0, b % heads)
+                at = pl.ds(side * R, R)
+                for h in range(heads):
+                    columns = pl.ds(h * HEAD_DIM, HEAD_DIM)
+                    value = own_ref[0, at, columns]
+                    for t in range(U - 1):
+                        value = value + others_ref[t, 0, at, columns].astype(F32)
+                    if memory is not None:
+                        picked = ins[3][h]
+                        down = lax.broadcasted_iota(jnp.int32, (R, picked.shape[1]), 0)
+                        chosen = (down + piece_start(grid, here.k, side) == picked).astype(BF)
+                        value = value + dot(chosen, ins[4][0, :, columns], (1, 0))
+                    out_ref[at, columns] = value.astype(BF)
+
+    which = lambda b: jnp.maximum(b - 1, 0)
     operands = [grad_query, own, others]
     specs = [
-        pl.BlockSpec((rows, HEAD_DIM), lambda b: (0, jnp.minimum(b, heads - 1))),
-        pl.BlockSpec((1, rows, HEAD_DIM), lambda b: (which(b), 0, head(b))),
-        pl.BlockSpec((U - 1, 1, rows, HEAD_DIM), lambda b: (0, which(b), 0, head(b))),
+        whole_spec(rows, width),
+        pl.BlockSpec((1, rows, width), lambda b: (which(b), 0, 0)),
+        pl.BlockSpec((U - 1, 1, rows, width), lambda b: (0, which(b), 0, 0)),
     ]
     if memory is not None:
         topk = picks.shape[1]
         operands += [picks[:, None, :], memory]
         specs += [
-            pl.BlockSpec((1, 1, topk), lambda b: (b % heads, 0, 0)),
-            pl.BlockSpec((1, topk, HEAD_DIM), lambda b: (which(b), 0, head(b))),
+            whole_spec(heads, 1, topk),
+            pl.BlockSpec((1, topk, width), lambda b: (which(b), 0, 0)),
         ]
     outs, got = host(
-        grid, body, 3 * heads, specs, operands, [columns_spec(rows, HEAD_DIM)], [kind(rows, 3 * width)], moves,
+        grid, body, 3, specs, operands, [columns_spec(rows, width)], [kind(rows, 3 * width)], moves,
         cost=pl.CostEstimate(flops=2 * rows * width, bytes_accessed=16 * rows * width, transcendentals=0),
     )
     return outs[0], got
@@ -1156,35 +1193,33 @@
     return pulled, grad_gain
 
 
-PRODUCT_TILE = 256
-
-
-def product(grid, left, left_other, right, moves=()):
+def product(grid, left, left_other, right, moves=(), piece=(0, 1)):
     rows, height = left.shape
     stacked = right.ndim == 3
-    half = right.shape[-1] if stacked else right.shape[-1] // 2
-    tiles = height // PRODUCT_TILE
+    full = right.shape[-1] if stacked else right.shape[-1] // 2
+    half = full // piece[1]
+    tile = 512 if height % 512 == 0 else height // 2
+    tiles = height // tile
+    fetch = left_other is None
 
     def part(ref, c):
-        return ref.at[c] if stacked else ref.at[:, pl.ds(pl.multiple_of(c * half, 128), half)]
+        ref = ref.at[c] if stacked else ref
+        start = piece[0] * half if stacked else c * full + piece[0] * half
+        return ref.at[:, pl.ds(pl.multiple_of(start, 128), half)]
 
     def body(here, step, ins, outs, held):
         own_ref, other_ref, right_ref = ins
-        own_right, other_right, total, own_sem, sems = held
+        own_right, other_right, total, own_sem, sems = held[:5]
         own = pltpu.make_async_copy(part(right_ref, here.c), own_right, own_sem)
-        swap = pltpu.make_async_remote_copy(
-            src_ref=part(right_ref, 1 - here.c),
-            dst_ref=other_right,
-            send_sem=sems.at[0],
-            recv_sem=sems.at[1],
-            device_id=here.swap,
-            device_id_type=MESH,
-        )
+        swaps = [remote(part(right_ref, 1 - here.c), other_right, sems, 0, here.swap)]
+        if fetch:
+            swaps.append(remote(other_ref, held[5], sems, 1, here.swap))
 
         @pl.when(step == 0)
         def _():
             own.start()
-            swap.start()
+            for swap in swaps:
+                swap.start()
             own.wait()
 
         @pl.when(step < tiles)
@@ -1193,29 +1228,33 @@
 
         @pl.when(step == tiles)
         def _():
-            swap.wait()
+            for swap in swaps:
+                swap.wait()
 
         @pl.when(step >= tiles)
         def _():
-            outs[0][...] = (total[step - tiles] + dot(other_ref[...], other_right[...], (0, 0))).astype(BF)
+            other = other_ref
+            if fetch:
+                other = held[5].at[:, pl.ds(pl.multiple_of((step - tiles) * tile, 128), tile)]
+            outs[0][...] = (total[step - tiles] + dot(other[...], other_right[...], (0, 0))).astype(BF)
 
     early = lambda i: jnp.minimum(i, tiles - 1)
     late = lambda i: jnp.maximum(i - tiles, 0)
+    other_spec = any_spec() if fetch else pl.BlockSpec((rows, tile), lambda i: (0, late(i)))
     outs, got = host(
         grid, body, 2 * tiles,
-        [pl.BlockSpec((rows, PRODUCT_TILE), lambda i: (0, early(i))),
-         pl.BlockSpec((rows, PRODUCT_TILE), lambda i: (0, late(i))), any_spec()],
-        [left, left_other, right],
-        [pl.BlockSpec((PRODUCT_TILE, half), lambda i: (late(i), 0))],
+        [pl.BlockSpec((rows, tile), lambda i: (0, early(i))), other_spec, any_spec()],
+        [left, left if fetch else left_other, right],
+        [pl.BlockSpec((tile, half), lambda i: (late(i), 0))],
         [kind(height, half)],
         moves,
         scratch=[
             pltpu.VMEM((rows, half), BF),
             pltpu.VMEM((rows, half), BF),
-            pltpu.VMEM((tiles, PRODUCT_TILE, half), F32),
+            pltpu.VMEM((tiles, tile, half), F32),
             pltpu.SemaphoreType.DMA,
-            pltpu.SemaphoreType.DMA((2,)),
-        ],
+            pltpu.SemaphoreType.DMA((2, 2)),
+        ] + [pltpu.VMEM((rows, height), BF)] * fetch,
         cost=pl.CostEstimate(flops=4 * rows * height * half, bytes_accessed=2 * height * half, transcendentals=0),
         reaches=True,
     )
@@ -1311,7 +1350,6 @@
     hidden, gains, weights = gather_all(
         grid, tokens, norm_gains, [attention_in, attention_out, feed_in, feed_out]
     )
-    hidden = hidden.astype(F32)
     gain = lambda l, i: gains[l, i][None]
     flat = lambda w: w.reshape(-1, w.shape[-1])
     saved = []
@@ -1319,14 +1357,23 @@
     for l in range(layers):
         w_qkv, w_out = flat(weights[l][0]), flat(weights[l][1])
         memory = l == layers - 1
-        normed = norm(hidden, gain(l, 0)).astype(BF)
         coming = weights[l + 1] if l + 1 < layers else None
-        moves = [spread_move(grid, weights[l][3], 1)] if later_here(l, 3) else []
-        split, got = split_heads(grid, memory, tables, mm(normed, w_qkv), moves)
-        if moves:
-            weights[l][3] = got[0]
-        (others,) = send(grid, [member_move(grid, split[1], False)])
-        pairs = [split[1]] + [others[t] for t in range(grid.U - 1)]
+        moves = []
+        if coming is not None:
+            moves.append(spread_move(grid, coming[3], [(0, 0, 1)]))
+        if later_here(l, 2):
+            moves += [
+                spread_move(grid, weights[l][2], [(1, 0, 2), (1, 1, 2)]),
+                spread_move(grid, weights[l][3], [(2, 0, 1)]),
+            ]
+        split, got = project(grid, memory, tables, hidden, gain(l, 0), w_qkv, moves)
+        if coming is not None:
+            coming[3] = got[0]
+        if later_here(l, 2):
+            weights[l][2:] = got[-2:]
+        normed, query = split[:2]
+        (others,) = send(grid, [member_move(grid, split[2], False)])
+        pairs = [split[2]] + [others[t] for t in range(grid.U - 1)]
         extra = None
         if memory:
             chosen = pick_memory(grid, picks, pairs, grid.c)
@@ -1334,84 +1381,102 @@
             slots = jnp.concatenate([chosen[None], came])
             slots = jnp.swapaxes(slots, 0, 1).reshape(2, n_dp * topk, -1)
             slots = both_halves(slots, grid.swap(slots))
-            extra = {"query": split[2], "keys": slots[0], "values": slots[1], "bias": bias}
-        moves = []
-        if later_here(l, 2):
-            moves += [spread_move(grid, weights[l][2], 1), spread_move(grid, weights[l][3], 2)]
-        if coming is not None:
-            moves.append(spread_move(grid, coming[3], 0))
-        attended, got = attend(grid, valid, split[0], pairs, extra, moves)
-        if later_here(l, 2):
-            weights[l][2], weights[l][3] = got[:2]
-            (weights[l][2],) = send(grid, [spread_move(grid, weights[l][2], 2)])
-            for stage in range(3, grid.bits + 1):
-                weights[l][2:] = send(grid, [spread_move(grid, w, stage) for w in weights[l][2:]])
-        if coming is not None:
-            coming[3] = got[-1]
-        middle = hidden + mm(attended, w_out)
+            extra = {"query": split[3], "keys": slots[0], "values": slots[1], "bias": bias}
         moves = []
         if coming is not None:
-            moves = [spread_move(grid, coming[2], 0), regroup_move(grid, cotangent)]
+            moves.append(spread_move(grid, coming[2], [(0, 0, 2)]))
+        if later_here(l, 2):
+            moves.append(spread_move(grid, weights[l][2], [(2, 0, 1)]))
+        if memory:
+            moves.append(regroup_move(grid, cotangent))
+        attended, got = attend(grid, valid, query, pairs, extra, moves)
+        if coming is not None:
+            coming[2] = got[0]
+        if later_here(l, 2):
+            weights[l][2] = got[-2]
+            for stage in range(3, grid.bits + 1):
+                weights[l][2:] = send(grid, [spread_move(grid, w, [(stage, 0, 1)]) for w in weights[l][2:]])
+        if memory:
+            cotangent_rows = got[-1]
+        middle = hidden.astype(F32) + mm(attended, w_out)
+        moves = []
+        if coming is not None:
+            moves = [spread_move(grid, coming[2], [(0, 1, 2)]), spread_move(grid, coming[3], [(1, 0, 1)])]
         w_up, w_down = flat(weights[l][2]), flat(weights[l][3])
         (out, normed_feed, both, inner), got = feed(grid, middle, gain(l, 1), w_up, w_down, moves)
         if coming is not None:
-            coming[2], cotangent_rows = got
-        saved.append((hidden, normed, split[0], pairs, extra, attended, middle, normed_feed, both, inner))
+            coming[2:] = got
+        saved.append((hidden, normed, query, pairs, extra, attended, middle, normed_feed, both, inner))
         hidden = out
     weights = [[flat(w) for w in kinds] for kinds in weights]
     cotangent_rows = cotangent_rows.reshape(-1, width)
-    out_rows = hidden.astype(BF).reshape(2, grid.R, width)
+    def row_halves(value):
+        value = value.astype(BF).reshape(2, grid.R, width)
+        return value[:, : grid.R // 2], value[:, grid.R // 2 :]
+
+    out_rows = row_halves(hidden)
     grad = cotangent_rows.astype(F32)
     found = [[None] * 4 for _ in range(layers)]
     grad_gains = [[None, None] for _ in range(layers)]
-    layer_output = None
-    above = None
+    layer_output, above, inner_other = [], None, None
+
+    def took(got, reduces):
+        for result, (reduce, what) in zip(got, reduces):
+            (reduce.flipped if what == "flip" else reduce.arrived)(result)
+
+    def moves_of(reduces):
+        return [reduce.flip() if what == "flip" else reduce.ring() for reduce, what in reduces]
+
     for l in reversed(range(layers)):
         w_qkv, w_out, w_up, w_down = weights[l]
         hidden, normed, query, pairs, extra, attended, middle, normed_feed, both, inner = saved[l]
         low = grad.astype(BF)
-
-        moves = [swap_move(inner), swap_move(normed_feed), swap_move(normed), swap_move(attended)]
-        if above is None:
-            moves.append(regroup_back_move(grid, out_rows))
-        else:
-            moves += [above[1].flip(), above[2].flip(), above[0].ring()]
+        last_layer = above is None
+
+        reduces = [] if last_layer else [(above[1], "flip")]
+        total, got = product(grid, inner, inner_other, low, moves_of(reduces))
+        took(got, reduces)
+        down = Reduce(grid, total)
+
+        reduces = [(down, "flip")]
+        if not last_layer:
+            reduces += [(above[0], "flip"), (above[1], "flip")] + [(up, "ring") for up in above[2]]
+        moves = moves_of(reduces) + [swap_move(normed_feed), swap_move(normed), swap_move(attended)]
+        if last_layer:
+            moves += [swap_move(saved[l - 1][9]), regroup_back_move(grid, out_rows[0])]
         (grad, grad_low, grads, gain_feed), got = feed_back(
             grid, grad, middle, gain(l, 1), both, w_up, w_down, moves
         )
-        inner_other, normed_feed_other, normed_other, attended_other = got[:4]
-        if above is None:
-            layer_output = got[4]
-            moves = []
-        else:
-            above[1].flipped(got[4])
-            above[2].flipped(got[5])
-            above[0].arrived(got[6])
-            moves = [above[1].flip(), above[2].flip()]
-        total, got = product(grid, inner, inner_other, low, moves)
-        down = Reduce(grid, total)
-        if above is not None:
-            above[1].flipped(got[0])
-            above[2].flipped(got[1])
-        total, got = product(grid, normed_feed, normed_feed_other, grads, [down.flip()])
-        up = Reduce(grid, total)
-        down.flipped(got[0])
+        took(got, reduces)
+        normed_feed_other, normed_other, attended_other = got[len(reduces) : len(reduces) + 3]
+        if last_layer:
+            inner_other = got[-2]
+            layer_output.append(got[-1])
+
+        ups = []
+        pieces_of_up = 1 if last_layer else 2
+        for piece in range(pieces_of_up):
+            if piece == 0:
+                reduces = [(down, "flip")]
+            else:
+                reduces = [(ups[0], "flip"), (above[0], "ring"), (above[1], "ring")]
+            total, got = product(
+                grid, normed_feed, normed_feed_other, grads, moves_of(reduces), (piece, pieces_of_up)
+            )
+            took(got, reduces)
+            ups.append(Reduce(grid, total))
         grad_heads = mm(grad_low, w_out, (1, 1)).astype(BF)
 
-        moves = [up.flip(), down.flip()]
-        if above is not None:
-            moves += [above[1].ring(), above[2].ring()]
-        outs, got = attend_back(grid, valid, tables, query, grad_heads, pairs, extra, moves)
-        up.flipped(got[0])
-        down.flipped(got[1])
-        if above is not None:
-            above[1].arrived(got[2])
-            above[2].arrived(got[3])
+        reduces = [(ups[-1], "flip"), (down, "ring")]
+        if not last_layer:
+            reduces.append((ups[0], "flip"))
+        outs, got = attend_back(grid, valid, tables, query, grad_heads, pairs, extra, moves_of(reduces))
+        took(got, reduces)
         grad_query, own, others = outs[:3]
         memory_grad = None
         moves = [member_move(grid, others, True)]
         if extra is not None:
-            moves.append(swap_move(half(outs[3], 1 - grid.c)))
+            moves.append(swap_half_move(outs[3]))
         got = send(grid, moves)
         others = got[0]
         moves = []
@@ -1427,47 +1492,56 @@
                 total = total + grid.within(total.astype(BF), t).astype(F32)
             total = total.astype(BF)
             memory_grad = both_halves(total, grid.swap(total))
-        grad_projected, got = finish_gradient(
-            grid, grad_query, own, others, picks, memory_grad, [up.flip(), down.ring()]
+        reduces = [(ups[-1], "flip"), (across, "flip")]
+        if not last_layer:
+            reduces.append((ups[0], "ring"))
+        moves = moves_of(reduces)
+        if last_layer:
+            moves.append(regroup_back_move(grid, out_rows[1]))
+        grad_projected, got = finish_gradient(grid, grad_query, own, others, picks, memory_grad, moves)
+        took(got, reduces)
+        if last_layer:
+            layer_output.append(got[-1])
+        pulled, gain_attention = norm_back(
+            hidden.astype(F32), gain(l, 0), mm(grad_projected, w_qkv, (1, 1))
         )
-        up.flipped(got[0])
-        down.arrived(got[1])
-        pulled, gain_attention = norm_back(hidden, gain(l, 0), mm(grad_projected, w_qkv, (1, 1)))
         grad = grad + pulled
         grad_gains[l] = [gain_attention[0], gain_feed[0]]
-        moves = []
+        reduces, moves = [], []
         if l == 0:
             small = GainSum(grid, jnp.stack([jnp.stack(pair) for pair in grad_gains]).reshape(-1, HEAD_DIM))
-            moves = [up.ring(), across.flip(), small.move()]
-        total, got = product(grid, normed, normed_other, grad_projected, moves)
+            reduces = [(ups[-1], "ring"), (across, "flip")]
+            moves = [small.move()]
+        total, got = product(grid, normed, normed_other, grad_projected, moves_of(reduces) + moves)
+        took(got, reduces)
+        if l == 0:
+            small.took(got[-1])
         last = Reduce(grid, total)
-        if l == 0:
-            up.arrived(got[0])
-            across.flipped(got[1])
-            small.took(got[2])
         found[l][3] = down.done(grid.swap(down.give))
-        if above is not None:
-            for i, reduced in zip((2, 1, 0), above):
-                found[l + 1][i] = reduced.done(grid.swap(reduced.give))
-        above = (up, across, last)
-    up, across, last = above
-    in_rows = grad.astype(BF).reshape(2, grid.R, width)
-    got = send(grid, [last.flip(), across.flip(), regroup_back_move(grid, in_rows), small.move()])
-    last.flipped(got[0])
-    across.flipped(got[1])
-    input_grad = got[2].astype(F32)
-    small.took(got[3])
-    got = send(grid, [last.flip(), across.ring(), small.move()])
-    last.flipped(got[0])
-    across.arrived(got[1])
-    small.took(got[2])
-    got = send(grid, [last.ring(), small.move()])
-    last.arrived(got[0])
-    small.took(got[1])
+        if not last_layer:
+            found[l + 1] = [r.done(grid.swap(r.give)) for r in (above[1], above[0])] + [
+                feed_parts([r.done(grid.swap(r.give)) for r in above[2]]), found[l + 1][3]
+            ]
+        above = (across, last, ups)
+    across, last, ups = above
+    in_rows = row_halves(grad)
+    input_grad = []
+    for i, reduces in enumerate([[(last, "flip"), (across, "ring")], [(last, "flip")], [(last, "ring")]]):
+        moves = moves_of(reduces)
+        if i < 2:
+            moves.append(regroup_back_move(grid, in_rows[i]))
+        got = send(grid, moves + [small.move()])
+        took(got, reduces)
+        small.took(got[-1])
+        if i < 2:
+            input_grad.append(got[-2])
+    layer_output = jnp.concatenate(layer_output, axis=1)
+    input_grad = jnp.concatenate(input_grad, axis=1).astype(F32)
+    found[0] = [r.done(grid.swap(r.give)) for r in (last, across)] + [
+        feed_parts([r.done(grid.swap(r.give)) for r in ups]), found[0][3]
+    ]
     total_gains = small.finish().reshape(layers, 2, n_dp * pieces, -1)
     device = (grid.j * 2 + grid.c) * grid.F + grid.f
-    for i, reduced in zip((2, 1, 0), above):
-        found[0][i] = reduced.done(grid.swap(reduced.give))
     return (
         layer_output,
         input_grad,
@@ -1476,6 +1550,11 @@
     )
 
 
+def feed_parts(parts):
+    sides = [[part[:, : part.shape[1] // 2] for part in parts], [part[:, part.shape[1] // 2 :] for part in parts]]
+    return jnp.concatenate(sides[0] + sides[1], axis=1)
+
+
 def solution(mesh):
     rows = P(None, ("dp", "fsdp"), None)
     in_specs = (rows, rows, P(), P(), P(None, "dp", None, None), rows, rows, rows, rows, P(None, None, ("dp", "fsdp")))

time: 962 us -> 896 us (0.931)
  Pallas kernels: 797 us -> 753 us
  matrix products: 40 us -> 22.1 us
    pallas_call x1, Pallas kernels: 198 us -> 172 us  [gather_all(): pl.pallas_call(functools.partial(gather_body, grid, layers, kinds), in_sp...]
    dot_general x8 -> x6, matrix products: 40 us -> 22.1 us  [dot(): lax.dot_general(left, right, (((contract[0],), (contract[1],)), ((), ()))...]
    pallas_call x29, Pallas kernels: 596 us -> 578 us  [host(): pl.pallas_call(kernel, grid=(steps,), in_specs=list(in_specs) + [any_spec...]
    unnamed x206 -> x213, local copies, waits for them, and re-layouts: 36.6 us -> 40.7 us
  transfers between devices with their start and end apart: 11 -> 12, of which waited for: 1 -> 1; matrix products, arithmetic and copies ran while one was open for 4% -> 3% of each run, Pallas kernels for 30% -> 31%
where the time goes in v5:
time: 896 us; the launch traced here: 889 us
  Pallas kernels  753 us (84%)
  local copies, waits for them, and re-layouts  57.6 us (6%)
  other arithmetic  49.2 us (5%)
  matrix products  22.1 us (2%)
    pallas_call x29, Pallas kernels, host(): pl.pallas_call(kernel, grid=(steps,), in_specs=list(in_specs) + [any_spec...  578 us
    pallas_call x1, Pallas kernels, gather_all(): pl.pallas_call(functools.partial(gather_body, grid, layers, kinds), in_sp...  172 us
    unnamed x213, local copies, waits for them, and re-layouts  40.7 us
    dot_general x6, matrix products, dot(): lax.dot_general(left, right, (((contract[0],), (contract[1],)), ((), ()))...  22.1 us
  transfers between devices with their start and end apart: 12, of which 1 were waited for; matrix products, arithmetic and copies ran while one was open for 3% of the time, Pallas kernels for 31%

profile of v5, /device:TPU:0, one launch (start us, length us, event | category | flops | bytes accessed | tf_op | source)
XLA Modules:
  0.0 889.1 jit_solution(11486589332932237160)
XLA Ops:
  9.0 171.6 %shard_map.153 = (bf16[2,256,1024]{2,1,0:T(8,128)(2,1)S(1)}, f32[4,2,4,8,128]{4,3,2,1,0:T(8,128)S(1)}, bf16[4,2,4,32,3072]{4,3,2,1,0:T(8,128)(2,1)}, bf16[4,2,4,...) custom-call(bf16[2,256,1024]{2,1,0:T(8,128)(2,1)S(1)} %copy-done.54,, ...), custom_call_target="tpu_custom_call" | custom-call | tf_op jit(solution)/shard_map/pallas_call | solution.py:412
  185.1 22.1 %shard_map.154 = (bf16[512,1024]{1,0:T(8,128)(2,1)S(1)}, bf16[512,1024]{1,0:T(8,128)(2,1)S(1)}, bf16[2,512,1024]{2,1,0:T(8,128)(2,1)}, bf16[4,2,4,88,1024]{4,3,2,1,0:T(8,128)(2,1)}) custom-call(f32[1024,128]{1,0:T(8,128)S(1)} %get-tuple-element.288.refs_0_.refs_1_, ...), custom_call_target="tpu_custom_call", output_to_operand_aliasing={{3}: (7, {})} | custom-call | flops 3221225472 | bytes 6291456 | tf_op jit(solution)/shard_map/pallas_call | solution.py:693
  218.1 20.5 %shard_map.156 = (bf16[512,1024]{1,0:T(8,128)(2,1)S(1)}, bf16[4,2,4,32,5632]{4,3,2,1,0:T(8,128)(2,1)}) custom-call(s32[1]{0:T(128)} %bitcast.refs_0_, bf16[512,1024]{1,0:T(8,128)(2,1)S(1)} %copy-done.39, bf16[2,512,1024]{2,1,0:T(8,128)(2,1)S(1)} %copy-done.8, bf16[2,512,1024]{2,1,0:T(8,128)(2,1)} %bitcast.223, ...), custom_call_target="tpu_custom_call", output_to_operand_aliasing={{1}: (4, {})} | custom-call | flops 1610612736 | bytes 8388608 | tf_op jit(solution)/shard_map/pallas_call | solution.py:693
  240.0 29.0 %shard_map.157 = (f32[512,1024]{1,0:T(8,128)S(1)}, bf16[512,1024]{1,0:T(8,128)(2,1)S(1)}, bf16[2,512,2816]{2,1,0:T(8,128)(2,1)}, bf16[512,2816]{1,0:T(8,128)(2,1...) custom-call(f32[512,1024]{1,0:T(8,128)S(1)} %convert_add_fusion.refs, ...), custom_call_target="tpu_custom_call", output_to_operand_aliasing={{4}: (5, {}), {5}: (6, {})} | custom-call | flops 8858370048 | bytes 17301504 | tf_op jit(solution)/shard_map/pallas_call | solution.py:693
  271.3 22.8 %shard_map.158 = (bf16[512,1024]{1,0:T(8,128)(2,1)S(1)}, bf16[512,1024]{1,0:T(8,128)(2,1)S(1)}, bf16[3,512,1024]{2,1,0:T(8,128)(2,1)}, bf16[512,1024]{1,0:T(8,12...) custom-call(f32[1024,128]{1,0:T(8,128)S(1)} %copy-done.14, ...), custom_call_target="tpu_custom_call", output_to_operand_aliasing={{4}: (7, {}), {5}: (8, {})} | custom-call | flops 3221225472 | bytes 6291456 | tf_op jit(solution)/shard_map/pallas_call | solution.py:693
  310.3 30.0 %shard_map.161 = bf16[7,2,128,512]{3,2,1,0:T(8,128)(2,1)S(1)} custom-call(bf16[2,128,512]{2,1,0:T(8,128)(2,1)S(1)} %shard_map.160.refs_0_), custom_call_target="tpu_custom_call" | custom-call | tf_op jit(solution)/shard_map/pallas_call | solution.py:693
  355.8 25.4 %shard_map.162 = (bf16[512,1024]{1,0:T(8,128)(2,1)S(1)}, bf16[4,2,4,32,5632]{4,3,2,1,0:T(8,128)(2,1)}, bf16[2,256,1024]{2,1,0:T(8,128)(2,1)S(1)}) custom-call(s32[1]{0:T(128)} %bitcast.refs_0_, bf16[512,1024]{1,0:T(8,128)(2,1)S(1)} %copy-done.44, bf16[3,512,1024]{2,1,0:T(8,128)(2,1)} %get-tuple-element.140.refs_0_.refs_2_.refs_5_, ...), custom_call_target="tpu_custom_call", output_to_operand_aliasing={{1}: (8, {})} | custom-call | flops 3758096384 | bytes 16777216 | tf_op jit(solution)/shard_map/pallas_call | solution.py:693
  382.5 18.4 %shard_map.163 = (f32[512,1024]{1,0:T(8,128)S(1)}, bf16[512,1024]{1,0:T(8,128)(2,1)S(1)}, bf16[2,512,2816]{2,1,0:T(8,128)(2,1)}, bf16[512,2816]{1,0:T(8,128)(2,1)}) custom-call(f32[512,1024]{1,0:T(8,128)S(1)} %convolution_add_fusion.refs_0_.refs_1_, f32[1,1024]{1,0:T(1,128)S(1)} %get-tuple-element.280.refs_1_.refs_2_, bf16[1024,5632]{1,0:T(8,128)(2,1)} %bitcast.257, ...), custom_call_target="tpu_custom_call" | custom-call | flops 8858370048 | bytes 17301504 | tf_op jit(solution)/shard_map/pallas_call | solution.py:693
  403.6 12.4 %shard_map.164 = bf16[2816,512]{1,0:T(8,128)(2,1)S(1)} custom-call(bf16[512,2816]{1,0:T(8,128)(2,1)} %get-tuple-element.149.refs_0_.refs_1_, bf16[512,2816]{1,0:T(8,128)(2,1)} %get-tuple-element.149.refs_0_.refs_1_, bf16[512,1024]{1,0:T(8,128)(2,1)S(1)} %bitcast.250), custom_call_target="tpu_custom_call" | custom-call | flops 2952790016 | bytes 2883584 | tf_op jit(solution)/shard_map/pallas_call | solution.py:693
  417.7 27.4 %shard_map.165 = (f32[512,1024]{1,0:T(8,128)}, bf16[512,1024]{1,0:T(8,128)(2,1)S(1)}, bf16[2,512,2816]{2,1,0:T(8,128)(2,1)}, f32[1,1024]{1,0:T(1,128)S(1)}, bf16...) custom-call(f32[512,1024]{1,0:T(8,128)} %bitcast_convert_fusion.refs, ...), custom_call_target="tpu_custom_call" | custom-call | flops 8858370048 | bytes 17301504 | tf_op jit(solution)/shard_map/pallas_call | solution.py:693
  447.9 13.6 %shard_map.166 = (bf16[1024,2816]{1,0:T(8,128)(2,1)}, bf16[1,704,512]{2,1,0:T(8,128)(2,1)S(1)}) custom-call(bf16[512,1024]{1,0:T(8,128)(2,1)S(1)} %copy-done.53, bf16[512,1024]{1,0:T(8,128)(2,1)S(1)} %get-tuple-element.156.refs_1_, bf16[2,512,2816]{2,1,0:T(8,128)(2,1)} %get-tuple-element.157.refs_2_, bf16[2,704,512]{2,1,0:T(8,128)(2,1)S(1)} %add_convert_fusion.8.refs_3_), custom_call_target="tpu_custom_call" | custom-call | flops 5905580032 | bytes 5767168 | tf_op jit(solution)/shard_map/pallas_call | solution.py:693
  466.7 38.7 %shard_map.167 = (bf16[512,1024]{1,0:T(8,128)(2,1)S(1)}, f32[2,512,1024]{2,1,0:T(8,128)}, bf16[1,2,512,1024]{3,2,1,0:T(8,128)(2,1)}, bf16[2,1024,1024]{2,1,0:T(8...) custom-call(s32[1]{0:T(128)} %bitcast.refs_0_, f32[1024,128]{1,0:T(8,128)S(1)} %copy-done.15, ...), custom_call_target="tpu_custom_call" | custom-call | flops 9395240960 | bytes 16777216 | tf_op jit(solution)/shard_map/pallas_call | solution.py:693
  519.0 31.5 %shard_map.169 = (bf16[1024,512]{1,0:T(8,128)(2,1)S(1)}, bf16[7,2,128,512]{3,2,1,0:T(8,128)(2,1)S(1)}) custom-call(bf16[512,1024]{1,0:T(8,128)(2,1)S(1)} %copy-done.22, bf16[512,1024]{1,0:T(8,128)(2,1)S(1)} %copy-done.51, bf16[512,1024]{1,0:T(8,128)(2,1)S(1)} %copy-done.49, bf16[2,8,128,512]{3,2,1,0:T(8,128)(2,1)} %bitcast.277), custom_call_target="tpu_custom_call" | custom-call | flops 1073741824 | bytes 1048576 | tf_op jit(solution)/shard_map/pallas_call | solution.py:693
  556.3 27.9 %shard_map.170 = (bf16[512,3072]{1,0:T(8,128)(2,1)}, bf16[1,256,2816]{2,1,0:T(8,128)(2,1)S(1)}, bf16[2,256,512]{2,1,0:T(8,128)(2,1)S(1)}, bf16[2,128,1024]{2,1,0:T(8,128)(2,1)S(1)}) custom-call(bf16[512,1024]{1,0:T(8,128)(2,1)S(1)} %copy-done.56, f32[2,512,1024]{2,1,0:T(8,128)} %get-tuple-element.162.refs_1_, bf16[1,2,512,1024]{3,2,1,0:T(8,128)(2,1)} %copy-done.32, ...), custom_call_target="tpu_custom_call" | custom-call | flops 1048576 | bytes 8388608 | tf_op jit(solution)/shard_map/pallas_call | solution.py:693
  604.2 22.5 %shard_map.172 = (bf16[2816,512]{1,0:T(8,128)(2,1)S(1)}, bf16[2,256,1536]{2,1,0:T(8,128)(2,1)S(1)}) custom-call(bf16[512,2816]{1,0:T(8,128)(2,1)} %get-tuple-element.152.refs_11_.refs_0_, bf16[512,2816]{1,0:T(8,128)(2,1)} %get-tuple-element.176.refs_1_, bf16[512,1024]{1,0:T(8,128)(2,1)S(1)} %get-tuple-element.231.refs_2_, bf16[4,256,1536]{2,1,0:T(8,128)(2,1)} %bitcast.252), custom_call_target="tpu_custom_call" | custom-call | flops 2952790016 | bytes 2883584 | tf_op jit(solution)/shard_map/pallas_call | solution.py:693
  628.9 34.3 %shard_map.173 = (f32[512,1024]{1,0:T(8,128)}, bf16[512,1024]{1,0:T(8,128)(2,1)S(1)}, bf16[2,512,2816]{2,1,0:T(8,128)(2,1)}, f32[1,1024]{1,0:T(1,128)S(1)}, bf16...) custom-call(f32[512,1024]{1,0:T(8,128)} %get-tuple-element.232.refs_, ...), custom_call_target="tpu_custom_call" | custom-call | flops 8858370048 | bytes 17301504 | tf_op jit(solution)/shard_map/pallas_call | solution.py:693
  666.5 12.7 %shard_map.174 = (bf16[1024,1408]{1,0:T(8,128)(2,1)}, bf16[1,704,512]{2,1,0:T(8,128)(2,1)S(1)}) custom-call(bf16[512,1024]{1,0:T(8,128)(2,1)S(1)} %copy-done.20, bf16[512,1024]{1,0:T(8,128)(2,1)S(1)} %get-tuple-element.185.refs_1_, bf16[2,512,2816]{2,1,0:T(8,128)(2,1)} %get-tuple-element.186.refs_2_, bf16[2,704,512]{2,1,0:T(8,128)(2,1)S(1)} %add_convert_fusion.6.refs_3_), custom_call_target="tpu_custom_call" | custom-call | flops 2952790016 | bytes 2883584 | tf_op jit(solution)/shard_map/pallas_call | solution.py:693
  682.5 28.3 %shard_map.175 = (bf16[1024,1408]{1,0:T(8,128)(2,1)}, bf16[2,256,1408]{2,1,0:T(8,128)(2,1)S(1)}, bf16[3,2,32,512]{3,2,1,0:T(8,128)(2,1)S(1)}, bf16[3,2,32,1536]{3,2,1,0:T(8,128)(2,1)S(1)}) custom-call(bf16[512,1024]{1,0:T(8,128)(2,1)S(1)} %copy-done.20, bf16[512,1024]{1,0:T(8,128)(2,1)S(1)} %get-tuple-element.185.refs_1_, ...), custom_call_target="tpu_custom_call" | custom-call | flops 2952790016 | bytes 2883584 | tf_op jit(solution)/shard_map/pallas_call | solution.py:693
  714.0 31.6 %shard_map.176 = (bf16[512,1024]{1,0:T(8,128)(2,1)S(1)}, f32[2,512,1024]{2,1,0:T(8,128)}, bf16[1,2,512,1024]{3,2,1,0:T(8,128)(2,1)}, bf16[2,256,1408]{2,1,0:T(8,...) custom-call(s32[1]{0:T(128)} %bitcast.refs_0_, f32[1024,128]{1,0:T(8,128)S(1)} %copy-done.15, ...), custom_call_target="tpu_custom_call" | custom-call | flops 4026531840 | bytes 8388608 | tf_op jit(solution)/shard_map/pallas_call | solution.py:693
  756.5 19.9 %shard_map.179 = (bf16[512,3072]{1,0:T(8,128)(2,1)}, bf16[1,256,1408]{2,1,0:T(8,128)(2,1)S(1)}, bf16[2,256,512]{2,1,0:T(8,128)(2,1)S(1)}, bf16[3,2,32,1408]{3,2,1,0:T(8,128)(2,1)S(1)}) custom-call(bf16[512,1024]{1,0:T(8,128)(2,1)S(1)} %get-tuple-element.194.refs_0_, f32[2,512,1024]{2,1,0:T(8,128)} %get-tuple-element.195.refs_1_, ...), custom_call_target="tpu_custom_call" | custom-call | flops 1048576 | bytes 8388608 | tf_op jit(solution)/shard_map/pallas_call | solution.py:693
  787.9 19.1 %shard_map.180 = (bf16[1024,1536]{1,0:T(8,128)(2,1)}, bf16[3,2,32,1408]{3,2,1,0:T(8,128)(2,1)S(1)}, bf16[1,256,512]{2,1,0:T(8,128)(2,1)S(1)}, f32[32,128]{1,0:T(8,128)S(1)}) custom-call(bf16[512,1024]{1,0:T(8,128)(2,1)S(1)} %copy-done.37, bf16[512,1024]{1,0:T(8,128)(2,1)S(1)} %copy-done.86, bf16[512,3072]{1,0:T(8,128)(2,1)} %get-tuple-element.200.refs_2_, ...), custom_call_target="tpu_custom_call" | custom-call | flops 3221225472 | bytes 3145728 | tf_op jit(solution)/shard_map/pallas_call | solution.py:693
  809.0 25.2 %shard_map.181 = (bf16[2,256,1536]{2,1,0:T(8,128)(2,1)S(1)}, bf16[3,2,32,512]{3,2,1,0:T(8,128)(2,1)S(1)}, bf16[2,128,1024]{2,1,0:T(8,128)(2,1)S(1)}, f32[32,128]{1,0:T(8,128)S(1)}) custom-call(bf16[4,256,1536]{2,1,0:T(8,128)(2,1)} %bitcast.281, bf16[2,4,32,512]{3,2,1,0:T(8,128)(2,1)S(1)} %bitcast.242, bf16[2,128,1024]{2,1,0:T(8,128)(2,1)S(1)} %get-tuple-element.252.refs_2_, ...), custom_call_target="tpu_custom_call" | custom-call | tf_op jit(solution)/shard_map/pallas_call | solution.py:693
  835.7 12.5 %shard_map.182 = (bf16[1,256,1536]{2,1,0:T(8,128)(2,1)S(1)}, bf16[2,128,1024]{2,1,0:T(8,128)(2,1)S(1)}, f32[32,128]{1,0:T(8,128)S(1)}) custom-call(bf16[2,256,1536]{2,1,0:T(8,128)(2,1)S(1)} %add_convert_fusion.2.refs_0_, bf16[2,128,1024]{2,1,0:T(8,128)(2,1)S(1)} %get-tuple-element.251.refs_1_, f32[32,128]{1,0:T(8,128)S(1)} %add.442.refs_2_), custom_call_target="tpu_custom_call" | custom-call | tf_op jit(solution)/shard_map/pallas_call | solution.py:693
  849.0 20.9 %shard_map.183 = (bf16[3,2,32,1536]{3,2,1,0:T(8,128)(2,1)S(1)}, f32[3,32,128]{2,1,0:T(8,128)S(1)}) custom-call(bf16[2,4,32,1536]{3,2,1,0:T(8,128)(2,1)S(1)} %bitcast.233, f32[32,128]{1,0:T(8,128)S(1)} %add.445.refs_1_), custom_call_target="tpu_custom_call" | custom-call | tf_op jit(solution)/shard_map/pallas_call | solution.py:693
  (379 shorter events, 167.9 us)
Async XLA Ops:
  0.6 304.1 %collective-permute-start = (s32[2,1,8,128]{3,2,1,0:T(8,128)}, s32[2,1,8,128]{3,2,1,0:T(8,128)S(1)}, u32[]{:S(2)}, u32[]{:S(2)}) collective-permute-start(s32[2,1,8,128]{3,2,1,0:T(8,128)} %param.16), channel_id=1, source_target_pairs={{0,4},{1,5},{2,6},{3,7},{4,0},{5,1},{6,2},{7,3},{8,12},{9,13},{10,... | collective-permute-start | bytes 24584 | tf_op jit(solution)/shard_map/ppermute | solution.py:70
  182.0 56.7 %copy-start.4 = (bf16[2,256,1024]{2,1,0:T(8,128)(2,1)}, bf16[2,256,1024]{2,1,0:T(8,128)(2,1)S(1)}, u32[]{:S(2)}) copy-start(bf16[2,256,1024]{2,1,0:T(8,128)(2,1)S(1)} %get-tuple-element.122) | copy-start | bytes 3145732
  185.1 22.1 %copy-start.13 = (f32[1024,128]{1,0:T(8,128)}, f32[1024,128]{1,0:T(8,128)S(1)}, u32[]{:S(2)}) copy-start(f32[1024,128]{1,0:T(8,128)S(1)} %get-tuple-element.288.refs_0_.refs_1_) | copy-start | bytes 1572868
  239.9 29.1 %copy-start.6 = (f32[512,1024]{1,0:T(8,128)}, f32[512,1024]{1,0:T(8,128)S(1)}, u32[]{:S(2)}) copy-start(f32[512,1024]{1,0:T(8,128)S(1)} %convert_add_fusion.refs_0_.refs_1_) | copy-start | bytes 6291460
  240.0 31.3 %copy-start.14 = (f32[1024,128]{1,0:T(8,128)S(1)}, f32[1024,128]{1,0:T(8,128)}, u32[]{:S(2)}) copy-start(f32[1024,128]{1,0:T(8,128)} %copy-done.13) | copy-start | bytes 1572868
  240.0 31.3 %copy-start.17 = (f32[1024,128]{1,0:T(8,128)S(1)}, f32[1024,128]{1,0:T(8,128)}, u32[]{:S(2)}) copy-start(f32[1024,128]{1,0:T(8,128)} %copy-done.16) | copy-start | bytes 1572868
  342.0 5.0 collective-permute-start.1
  355.8 25.4 %copy-start.102 = (bf16[4,2,4,32,1024]{4,3,2,1,0:T(8,128)(2,1)S(1)}, bf16[4,2,4,32,1024]{4,3,2,1,0:T(8,128)(2,1)}, u32[]{:S(2)}) copy-start(bf16[4,2,4,32,1024]{4,3,2,1,0:T(8,128)(2,1)} %get-tuple-element.145) | copy-start | bytes 6291460
  551.9 4.0 collective-permute-start.2
  552.1 2.9 collective-permute-start.11
  556.3 28.8 %copy-start.87 = (bf16[2,256,2816]{2,1,0:T(8,128)(2,1)S(1)}, bf16[2,256,2816]{2,1,0:T(8,128)(2,1)}, u32[]{:S(2)}) copy-start(bf16[2,256,2816]{2,1,0:T(8,128)(2,1)} %add_convert_fusion.refs_5_) | copy-start | bytes 8650756
  628.9 34.4 %copy-start.88 = (bf16[2,256,1536]{2,1,0:T(8,128)(2,1)S(1)}, bf16[2,256,1536]{2,1,0:T(8,128)(2,1)}, u32[]{:S(2)}) copy-start(bf16[2,256,1536]{2,1,0:T(8,128)(2,1)} %add_convert_fusion.3.refs_9_) | copy-start | bytes 4718596
  681.0 33.1 %copy-start.33 = (bf16[1,704,512]{2,1,0:T(8,128)(2,1)}, bf16[1,704,512]{2,1,0:T(8,128)(2,1)S(1)}, u32[]{:S(2)}) copy-start(bf16[1,704,512]{2,1,0:T(8,128)(2,1)S(1)} %add_convert_fusion.13) | copy-start | bytes 2162692
  714.0 31.6 %copy-start.90 = (bf16[2,256,1408]{2,1,0:T(8,128)(2,1)S(1)}, bf16[2,256,1408]{2,1,0:T(8,128)(2,1)}, u32[]{:S(2)}) copy-start(bf16[2,256,1408]{2,1,0:T(8,128)(2,1)} %add_convert_fusion.5.refs_9_) | copy-start | bytes 4325380
  848.2 22.4 %copy-start.62 = (bf16[3,2,88,512]{3,2,1,0:T(8,128)(2,1)S(1)}, bf16[3,2,88,512]{3,2,1,0:T(8,128)(2,1)}, u32[]{:S(2)}) copy-start(bf16[3,2,88,512]{3,2,1,0:T(8,128)(2,1)} %copy-done.61) | copy-start | bytes 1622020
  848.2 23.6 %copy-start.64 = (bf16[3,2,32,1408]{3,2,1,0:T(8,128)(2,1)S(1)}, bf16[3,2,32,1408]{3,2,1,0:T(8,128)(2,1)}, u32[]{:S(2)}) copy-start(bf16[3,2,32,1408]{3,2,1,0:T(8,128)(2,1)} %copy-done.63) | copy-start | bytes 1622020
  871.7 12.6 %collective-permute-start.10 = (bf16[88,512]{1,0:T(8,128)(2,1)S(1)}, bf16[88,512]{1,0:T(8,128)(2,1)S(1)}, u32[]{:S(2)}, u32[]{:S(2)}) collective-permute-start(bf16[88,512]{1,0:T(8,128)(2,1)S(1)} %fusion.16), channel_id=1, source_target_pairs={{0,4},{1,5},{2,6},{3,7},{4,0},{5,1},{6,2},{7,3},{8,12},{9,13},{10,... | collective-permute-start | bytes 270344 | tf_op jit(solution)/shard_map/ppermute | solution.py:70
  872.9 11.7 %collective-permute-start.7 = (bf16[32,1408]{1,0:T(8,128)(2,1)S(1)}, bf16[32,1408]{1,0:T(8,128)(2,1)S(1)}, u32[]{:S(2)}, u32[]{:S(2)}) collective-permute-start(bf16[32,1408]{1,0:T(8,128)(2,1)S(1)} %fusion.14), channel_id=1, source_target_pairs={{0,4},{1,5},{2,6},{3,7},{4,0},{5,1},{6,2},{7,3},{8,12},{9,13},{10,... | collective-permute-start | bytes 270344 | tf_op jit(solution)/shard_map/ppermute | solution.py:70
  874.5 10.1 %collective-permute-start.8 = (bf16[32,1408]{1,0:T(8,128)(2,1)S(1)}, bf16[32,1408]{1,0:T(8,128)(2,1)S(1)}, u32[]{:S(2)}, u32[]{:S(2)}) collective-permute-start(bf16[32,1408]{1,0:T(8,128)(2,1)S(1)} %fusion.15), channel_id=1, source_target_pairs={{0,4},{1,5},{2,6},{3,7},{4,0},{5,1},{6,2},{7,3},{8,12},{9,13},{10,... | collective-permute-start | bytes 270344 | tf_op jit(solution)/shard_map/ppermute | solution.py:70
  875.9 11.4 %collective-permute-start.9 = (bf16[32,2816]{1,0:T(8,128)(2,1)S(1)}, bf16[32,2816]{1,0:T(8,128)(2,1)S(1)}, u32[]{:S(2)}, u32[]{:S(2)}) collective-permute-start(bf16[32,2816]{1,0:T(8,128)(2,1)S(1)} %fusion.10), channel_id=1, source_target_pairs={{0,4},{1,5},{2,6},{3,7},{4,0},{5,1},{6,2},{7,3},{8,12},{9,13},{10,... | collective-permute-start | bytes 540680 | tf_op jit(solution)/shard_map/ppermute | solution.py:70
  876.5 5.4 collective-permute-start.5
  881.9 1.3 collective-permute-start.6
  883.2 3.0 collective-permute-start.3
  884.4 2.0 collective-permute-start.4
  (94 other events, 388.5 us)

commit v6 on v5

--- a/solution.py
+++ b/solution.py
@@ -470,14 +470,14 @@
     return Move(parts, (count,) + parts.shape[1:], count, copies)
 
 
-def ring_move(grid, line):
+def ring_move(grid, line, distances):
     def copies(here, source, target):
         return [
-            (source.at[:, (here.f + t) % grid.F], target.at[t - 1], here.ring(t), here.ring(grid.F - t))
-            for t in range(1, grid.F)
+            (source.at[:, (here.f + t) % grid.F], target.at[i], here.ring(t), here.ring(grid.F - t))
+            for i, t in enumerate(distances)
         ]
 
-    return Move(line, (grid.F - 1, 2) + line.shape[2:], grid.F - 1, copies)
+    return Move(line, (len(distances), 2) + line.shape[2:], len(distances), copies)
 
 
 def swap_move(array, give=None):
@@ -629,7 +629,7 @@
 IDS = [1]
 
 
-def host(grid, body, steps, in_specs, operands, out_specs, out_shape, moves=(), scratch=(), cost=None, reaches=False):
+def host(grid, body, steps, in_specs, operands, out_specs, out_shape, moves=(), scratch=(), cost=None, reaches=None):
     counts = [len(operands), len(moves), len(out_shape), len(moves), len(scratch)]
 
     def kernel(*refs):
@@ -653,14 +653,15 @@
             @pl.when(step == 0)
             def _():
                 barrier = pltpu.get_barrier_semaphore()
-                if reaches:
-                    pl.semaphore_signal(barrier, inc=1, device_id=here.swap, device_id_type=MESH)
+                givers = reaches(here) if reaches else []
+                for giver in givers:
+                    pl.semaphore_signal(barrier, inc=1, device_id=giver, device_id_type=MESH)
                 for _, _, _, giver, _, same_in in planned:
                     signal = functools.partial(
                         pl.semaphore_signal, barrier, inc=1, device_id=giver, device_id_type=MESH
                     )
                     unless(same_in, signal)
-                due = int(reaches) + sum(same is None for _, same, _, _, _, _ in planned)
+                due = len(givers) + sum(same is None for _, same, _, _, _, _ in planned)
                 for _, same, _, _, _, _ in planned:
                     if same is not None:
                         due = due + 1 - same.astype(jnp.int32)
@@ -795,9 +796,25 @@
     steps = heads // together
     count = 3 if memory else 2
 
+    width_out = heads * HEAD_DIM
+
+    def sends(here, held, target, step):
+        columns = pl.ds(pl.multiple_of(step * size, 128), size)
+        return [
+            pltpu.make_async_remote_copy(
+                src_ref=held[0].at[:, :, columns],
+                dst_ref=target.at[t - 1, :, :, columns],
+                send_sem=held[1].at[0, t - 1, step],
+                recv_sem=held[1].at[1, t - 1, step],
+                device_id=here.member(t),
+                device_id_type=MESH,
+            )
+            for t in range(1, grid.U)
+        ]
+
     def body(here, step, ins, outs, held):
         cos_ref, sin_ref, hidden_ref, gain_ref = ins[:4]
-        normed_ref, q_out, kv_out = outs[:3]
+        normed_ref, q_out, kv_out, others = outs[:4]
 
         @pl.when(step == 0)
         def _():
@@ -816,11 +833,20 @@
                 kv_out[0, at, columns] = turn(key[:, columns], cos, sin).astype(BF)
             if memory:
                 kv_out[2, at, :] = key.astype(BF)
-                outs[3][at, :] = query.astype(BF)
+                outs[4][at, :] = query.astype(BF)
+        held[0][:, :, pl.ds(pl.multiple_of(step * size, 128), size)] = kv_out[...]
+        for copy in sends(here, held, others, step):
+            copy.start()
+
+        @pl.when(step == steps - 1)
+        def _():
+            for i in range(steps):
+                for copy in sends(here, held, others, i):
+                    copy.wait()
 
     piece = columns_spec(rows, size)
     table = whole_spec(SEG, HEAD_DIM)
-    flat = kind(rows, heads * HEAD_DIM)
+    flat = kind(rows, width_out)
     return host(
         grid,
         body,
@@ -828,12 +854,18 @@
         [table, table, whole_spec(rows, width), whole_spec(1, width)]
         + [columns_spec(width, size, first=i * steps) for i in range(3)],
         [*tables, hidden, gain, weight, weight, weight],
-        [whole_spec(rows, width), piece, columns_spec(count, rows, size)] + [piece] * memory,
-        [kind(rows, width), flat, kind(count, rows, heads * HEAD_DIM)] + [flat] * memory,
+        [whole_spec(rows, width), piece, columns_spec(count, rows, size), any_spec()] + [piece] * memory,
+        [kind(rows, width), flat, kind(count, rows, width_out), kind(grid.U - 1, count, rows, width_out)]
+        + [flat] * memory,
         moves,
+        scratch=[
+            pltpu.VMEM((count, rows, width_out), BF),
+            pltpu.SemaphoreType.DMA((2, grid.U - 1, steps)),
+        ],
         cost=pl.CostEstimate(
             flops=2 * rows * width * weight.shape[1], bytes_accessed=2 * width * weight.shape[1], transcendentals=0
         ),
+        reaches=lambda here: [here.member(grid.U - t) for t in range(1, grid.U)],
     )
 
 
@@ -873,11 +905,9 @@
 
 
 def memory_operands(grid, extra):
-    rows = extra["keys"].shape[0]
-    piece = columns_spec(grid.T, HEAD_DIM)
-    column = columns_spec(rows, HEAD_DIM)
-    return [extra["query"], extra["keys"], extra["values"], extra["bias"]], [
-        piece, column, column, whole_spec(rows, 1)
+    rows = extra["memory"].shape[1]
+    return [extra["query"], extra["memory"], extra["bias"]], [
+        columns_spec(grid.T, HEAD_DIM), columns_spec(2, rows, HEAD_DIM), whole_spec(rows, 1)
     ], rows
 
 
@@ -895,8 +925,8 @@
             scores = [s for _, _, s in found]
             mixed = [values[t][side * R : (side + 1) * R] for t, side, _ in found]
             if extra is not None:
-                scores.append(dot(refs[1][...], refs[0][at, :], (1, 1)) + refs[3][...])
-                mixed.append(refs[2][...])
+                scores.append(dot(refs[1][0], refs[0][at, :], (1, 1)) + refs[2][...])
+                mixed.append(refs[1][1])
             total = sum(
                 dot(value, p.astype(BF), (0, 0)) for value, p in zip(mixed, softmax_parts(scores))
             )
@@ -920,6 +950,32 @@
     rows, width = query.shape
     heads = width // HEAD_DIM
     R, U = grid.R, grid.U
+    per = heads // 2
+
+    def sends(here, held, target, h):
+        columns = pl.ds(pl.multiple_of(h * HEAD_DIM, HEAD_DIM), HEAD_DIM)
+        return [
+            pltpu.make_async_remote_copy(
+                src_ref=held[0].at[h, t - 1],
+                dst_ref=target.at[t - 1, :, :, columns],
+                send_sem=held[1].at[0, t - 1, h],
+                recv_sem=held[1].at[1, t - 1, h],
+                device_id=here.member(U - t),
+                device_id_type=MESH,
+            )
+            for t in range(1, U)
+        ]
+
+    def memory_send(here, held, target, h):
+        columns = pl.ds(pl.multiple_of(h * HEAD_DIM, HEAD_DIM), HEAD_DIM)
+        return pltpu.make_async_remote_copy(
+            src_ref=held[2].at[h],
+            dst_ref=target.at[:, :, columns],
+            send_sem=held[3].at[0, h],
+            recv_sem=held[3].at[1, h],
+            device_id=here.swap,
+            device_id_type=MESH,
+        )
 
     def body(here, step, ins, outs, held):
         valid_ref, cos_ref, sin_ref, q_ref, g_ref = ins[:5]
@@ -942,9 +998,9 @@
             if extra is not None:
                 places.append("memory")
                 queries.append(refs[0][at_rows, :])
-                scores.append(dot(refs[1][...], queries[-1], (1, 1)) + refs[3][...])
-                part_keys.append(refs[1][...])
-                part_values.append(refs[2][...])
+                scores.append(dot(refs[1][0], queries[-1], (1, 1)) + refs[2][...])
+                part_keys.append(refs[1][0])
+                part_values.append(refs[1][1])
             probs = softmax_parts(scores)
             grads = [dot(value, grads_in, (1, 1)) for value in part_values]
             inner = sum(jnp.sum(p * d, axis=0, keepdims=True) for p, d in zip(probs, grads))
@@ -975,11 +1031,30 @@
                     outs[1][0, at_rows, :] = key
                     outs[1][1, at_rows, :] = grad_values[(t, side)]
                 else:
-                    outs[2][t - 1, 0, at_rows, :] = key.astype(BF)
-                    outs[2][t - 1, 1, at_rows, :] = grad_values[(t, side)].astype(BF)
+                    held[0][step, t - 1, 0, at_rows, :] = key.astype(BF)
+                    held[0][step, t - 1, 1, at_rows, :] = grad_values[(t, side)].astype(BF)
+        for copy in sends(here, held, outs[2], step):
+            copy.start()
         if extra is not None:
-            outs[3][0] = (grad_keys["memory"] * SCALE).astype(BF)
-            outs[3][1] = grad_values["memory"].astype(BF)
+            memory_key = (grad_keys["memory"] * SCALE).astype(BF)
+            memory_value = grad_values["memory"].astype(BF)
+            outs[3][0] = memory_key
+            outs[3][1] = memory_value
+
+            @pl.when(step // per == 1 - here.c)
+            def _():
+                held[2][step % per, 0] = memory_key
+                held[2][step % per, 1] = memory_value
+                memory_send(here, held, outs[4], step % per).start()
+
+        @pl.when(step == heads - 1)
+        def _():
+            for h in range(heads):
+                for copy in sends(here, held, outs[2], h):
+                    copy.wait()
+            if extra is not None:
+                for h in range(per):
+                    memory_send(here, held, outs[4], h).wait()
 
     piece = columns_spec(rows, HEAD_DIM)
     pair = columns_spec(2, rows, HEAD_DIM)
@@ -987,16 +1062,24 @@
     operands = [valid, *tables, query, grad, *pairs]
     specs = [smem(), table, table, piece, piece] + [pair] * U
     out_shape = [kind(rows, width), kind(2, rows, width, dtype=F32), kind(U - 1, 2, rows, width)]
-    out_specs = [piece, pair, columns_spec(U - 1, 2, rows, HEAD_DIM)]
+    out_specs = [piece, pair, any_spec()]
+    scratch = [pltpu.VMEM((heads, U - 1, 2, rows, HEAD_DIM), BF), pltpu.SemaphoreType.DMA((2, U - 1, heads))]
     memory_rows = 0
     if extra is not None:
         more, more_specs, memory_rows = memory_operands(grid, extra)
         operands, specs = operands + more, specs + more_specs
-        out_shape.append(kind(2, memory_rows, width))
-        out_specs.append(columns_spec(2, memory_rows, HEAD_DIM))
+        out_shape += [kind(2, memory_rows, width), kind(2, memory_rows, width // 2)]
+        out_specs += [columns_spec(2, memory_rows, HEAD_DIM), any_spec()]
+        scratch += [pltpu.VMEM((per, 2, memory_rows, HEAD_DIM), BF), pltpu.SemaphoreType.DMA((2, per))]
+
+    def reaches(here):
+        return [here.member(t) for t in range(1, U)] + [here.swap] * (extra is not None)
+
     return host(
         grid, body, heads, specs, operands, out_specs, out_shape, moves,
+        scratch=scratch,
         cost=attention_cost(grid, heads, memory_rows, 5),
+        reaches=reaches,
     )
 
 
@@ -1037,6 +1120,37 @@
             flops=4 * topk * SEG * HEAD_DIM * per, bytes_accessed=4 * SEG * HEAD_DIM * per, transcendentals=0
         ),
     )(c.reshape(1).astype(jnp.int32), picks[:, :, None], *stacked)
+
+
+def gather_memory(grid, chosen):
+    n = grid.n_dp
+    half = chosen.shape[2]
+
+    def body(here, step, ins, outs, held):
+        source, target = ins[0], outs[0]
+        own_sem, sems = held
+        mine = target.at[:, :, :, pl.ds(pl.multiple_of(here.c * half, 128), half)]
+        own = pltpu.make_async_copy(source, mine.at[:, 0], own_sem)
+        across = [remote(source, mine.at[:, t], sems, t, here.slots(t)) for t in range(1, n)]
+        swaps = [remote(source, mine.at[:, 0], sems, n, here.swap)]
+        swaps += [remote(mine.at[:, t], mine.at[:, t], sems, n + t, here.swap) for t in range(1, n)]
+        for copy in across + [swaps[0], own]:
+            copy.start()
+        for t in range(1, n):
+            across[t - 1].wait_recv()
+            swaps[t].start()
+        own.wait()
+        for copy in across:
+            copy.wait_send()
+        for copy in swaps:
+            copy.wait()
+
+    outs, _ = host(
+        grid, body, 1, [any_spec()], [chosen], [any_spec()], [kind(2, n, chosen.shape[1], 2 * half)],
+        scratch=[pltpu.SemaphoreType.DMA, pltpu.SemaphoreType.DMA((2, 2 * n))],
+        reaches=lambda here: [here.slots(n - t) for t in range(1, n)] + [here.swap],
+    )
+    return outs[0]
 
 
 def finish_gradient(grid, grad_query, own, others, picks, memory, moves=()):
@@ -1256,7 +1370,7 @@
             pltpu.SemaphoreType.DMA((2, 2)),
         ] + [pltpu.VMEM((rows, height), BF)] * fetch,
         cost=pl.CostEstimate(flops=4 * rows * height * half, bytes_accessed=2 * height * half, transcendentals=0),
-        reaches=True,
+        reaches=lambda here: [here.swap],
     )
     return outs[0], got
 
@@ -1265,7 +1379,7 @@
     def __init__(self, grid, total):
         self.grid = grid
         self.parts = total.reshape(grid.J, total.shape[0] // grid.J, total.shape[1])
-        self.phase = 0
+        self.phase, self.came = 0, []
 
     def flip(self):
         return flip_move(self.grid, self.parts, self.phase)
@@ -1286,15 +1400,27 @@
         if self.phase == grid.bits:
             self.line = self.parts.reshape(2, grid.F, -1, self.parts.shape[2])
 
-    def ring(self):
-        while self.phase < self.grid.bits:
-            self.flipped(send(self.grid, [self.flip()])[0])
-        return ring_move(self.grid, self.line)
+    def ring(self, distances=None):
+        grid = self.grid
+        while self.phase < grid.bits:
+            self.flipped(send(grid, [self.flip()])[0])
+        return ring_move(grid, self.line, distances or list(range(1, grid.F)))
+
+    def far(self):
+        return self.ring([self.grid.F // 2])
+
+    def near(self):
+        return self.ring([t for t in range(1, self.grid.F) if t != self.grid.F // 2])
 
     def arrived(self, got):
         grid = self.grid
+        self.came.append(got)
+        if sum(part.shape[0] for part in self.came) < grid.F - 1:
+            return
         here = lax.dynamic_index_in_dim(self.line, grid.f, 1, keepdims=False)
-        self.summed = here.astype(F32) + sum(got[t].astype(F32) for t in range(grid.F - 1))
+        self.summed = here.astype(F32) + sum(
+            part[i].astype(F32) for part in self.came for i in range(part.shape[0])
+        )
         give = lax.dynamic_index_in_dim(self.summed, 1 - grid.c, 0, keepdims=False)
         self.give = give.astype(BF)
 
@@ -1372,16 +1498,12 @@
         if later_here(l, 2):
             weights[l][2:] = got[-2:]
         normed, query = split[:2]
-        (others,) = send(grid, [member_move(grid, split[2], False)])
-        pairs = [split[2]] + [others[t] for t in range(grid.U - 1)]
+        pairs = [split[2]] + [split[3][t] for t in range(grid.U - 1)]
         extra = None
         if memory:
             chosen = pick_memory(grid, picks, pairs, grid.c)
-            (came,) = send(grid, [slots_move(grid, chosen, False)])
-            slots = jnp.concatenate([chosen[None], came])
-            slots = jnp.swapaxes(slots, 0, 1).reshape(2, n_dp * topk, -1)
-            slots = both_halves(slots, grid.swap(slots))
-            extra = {"query": split[3], "keys": slots[0], "values": slots[1], "bias": bias}
+            slots = gather_memory(grid, chosen).reshape(2, n_dp * topk, -1)
+            extra = {"query": split[4], "memory": slots, "bias": bias}
         moves = []
         if coming is not None:
             moves.append(spread_move(grid, coming[2], [(0, 0, 2)]))
@@ -1425,7 +1547,7 @@
             (reduce.flipped if what == "flip" else reduce.arrived)(result)
 
     def moves_of(reduces):
-        return [reduce.flip() if what == "flip" else reduce.ring() for reduce, what in reduces]
+        return [getattr(reduce, what)() for reduce, what in reduces]
 
     for l in reversed(range(layers)):
         w_qkv, w_out, w_up, w_down = weights[l]
@@ -1433,14 +1555,14 @@
         low = grad.astype(BF)
         last_layer = above is None
 
-        reduces = [] if last_layer else [(above[1], "flip")]
+        reduces = [] if last_layer else [(above[1], "flip"), (above[2][0], "far")]
         total, got = product(grid, inner, inner_other, low, moves_of(reduces))
         took(got, reduces)
         down = Reduce(grid, total)
 
         reduces = [(down, "flip")]
         if not last_layer:
-            reduces += [(above[0], "flip"), (above[1], "flip")] + [(up, "ring") for up in above[2]]
+            reduces += [(above[0], "flip"), (above[1], "flip"), (above[2][0], "near")]
         moves = moves_of(reduces) + [swap_move(normed_feed), swap_move(normed), swap_move(attended)]
         if last_layer:
             moves += [swap_move(saved[l - 1][9]), regroup_back_move(grid, out_rows[0])]
@@ -1457,9 +1579,9 @@
         pieces_of_up = 1 if last_layer else 2
         for piece in range(pieces_of_up):
             if piece == 0:
-                reduces = [(down, "flip")]
+                reduces = [(down, "flip")] if last_layer else [(down, "flip"), (above[1], "far")]
             else:
-                reduces = [(ups[0], "flip"), (above[0], "ring"), (above[1], "ring")]
+                reduces = [(ups[0], "flip"), (above[1], "near")]
             total, got = product(
                 grid, normed_feed, normed_feed_other, grads, moves_of(reduces), (piece, pieces_of_up)
             )
@@ -1469,19 +1591,14 @@
 
         reduces = [(ups[-1], "flip"), (down, "ring")]
         if not last_layer:
-            reduces.append((ups[0], "flip"))
+            reduces += [(ups[0], "flip"), (above[0], "ring")]
         outs, got = attend_back(grid, valid, tables, query, grad_heads, pairs, extra, moves_of(reduces))
         took(got, reduces)
         grad_query, own, others = outs[:3]
         memory_grad = None
-        moves = [member_move(grid, others, True)]
-        if extra is not None:
-            moves.append(swap_half_move(outs[3]))
-        got = send(grid, moves)
-        others = got[0]
         moves = []
         if extra is not None:
-            joined = half(outs[3], grid.c).astype(F32) + got[1].astype(F32)
+            joined = half(outs[3], grid.c).astype(F32) + outs[4].astype(F32)
             joined = joined.astype(BF).reshape(2, n_dp, topk, -1)
             moves = [slots_move(grid, joined, True)]
         total, got = product(grid, attended, attended_other, grad_low, moves)

time: 896 us -> 855 us (0.954)
  Pallas kernels: 753 us -> 727 us
  local copies, waits for them, and re-layouts: 57.6 us -> 45.5 us
    pallas_call x29 -> x25, Pallas kernels: 578 us -> 552 us  [host(): pl.pallas_call(kernel, grid=(steps,), in_specs=list(in_specs) + [any_spec...]
    unnamed x213 -> x189, local copies, waits for them, and re-layouts: 40.7 us -> 34.5 us
  transfers between devices with their start and end apart: 12 -> 11, of which waited for: 1 -> 1; matrix products, arithmetic and copies ran while one was open for 3% -> 3% of each run, Pallas kernels for 31% -> 31%
where the time goes in v6:
time: 855 us; the launch traced here: 848 us
  Pallas kernels  727 us (85%)
  other arithmetic  46.7 us (5%)
  local copies, waits for them, and re-layouts  45.5 us (5%)
  matrix products  21.7 us (3%)
    pallas_call x25, Pallas kernels, host(): pl.pallas_call(kernel, grid=(steps,), in_specs=list(in_specs) + [any_spec...  552 us
    pallas_call x1, Pallas kernels, gather_all(): pl.pallas_call(functools.partial(gather_body, grid, layers, kinds), in_sp...  172 us
    unnamed x189, local copies, waits for them, and re-layouts  34.5 us
    dot_general x6, matrix products, dot(): lax.dot_general(left, right, (((contract[0],), (contract[1],)), ((), ()))...  21.7 us
  transfers between devices with their start and end apart: 11, of which 1 were waited for; matrix products, arithmetic and copies ran while one was open for 3% of the time, Pallas kernels for 31%

profile of v6, /device:TPU:0, one launch (start us, length us, event | category | flops | bytes accessed | tf_op | source)
XLA Modules:
  0.0 847.6 jit_solution(16395143547590813659)
XLA Ops:
  10.3 171.6 %shard_map.153 = (bf16[2,256,1024]{2,1,0:T(8,128)(2,1)S(1)}, f32[4,2,4,8,128]{4,3,2,1,0:T(8,128)S(1)}, bf16[4,2,4,32,3072]{4,3,2,1,0:T(8,128)(2,1)}, bf16[4,2,4,...) custom-call(bf16[2,256,1024]{2,1,0:T(8,128)(2,1)S(1)} %copy-done.35,, ...), custom_call_target="tpu_custom_call" | custom-call | tf_op jit(solution)/shard_map/pallas_call | solution.py:412
  187.3 22.1 %shard_map.154 = (bf16[512,1024]{1,0:T(8,128)(2,1)S(1)}, bf16[512,1024]{1,0:T(8,128)(2,1)S(1)}, bf16[2,512,1024]{2,1,0:T(8,128)(2,1)}, bf16[1,2,512,1024]{3,2,1,0:T(8,128)(2,1)}, bf16[4,2,4,88,1024]{4,3,2,1,0:T(8,128)(2,1)}) custom-call(f32[1024,128]{1,0:T(8,128)S(1)} %get-tuple-element.292.refs_0_.refs_1_, ...), custom_call_target="tpu_custom_call", output_to_operand_aliasing={{4}: (7, {})} | custom-call | flops 3221225472 | bytes 6291456 | tf_op jit(solution)/shard_map/pallas_call | solution.py:694
  212.4 19.9 %shard_map.155 = (bf16[512,1024]{1,0:T(8,128)(2,1)S(1)}, bf16[4,2,4,32,5632]{4,3,2,1,0:T(8,128)(2,1)}) custom-call(s32[1]{0:T(128)} %bitcast.refs_0_, bf16[512,1024]{1,0:T(8,128)(2,1)S(1)} %get-tuple-element.129.refs_1_.refs_3_, bf16[2,512,1024]{2,1,0:T(8,128)(2,1)S(1)} %copy-done.17, ...), custom_call_target="tpu_custom_call", output_to_operand_aliasing={{1}: (4, {})} | custom-call | flops 1610612736 | bytes 8388608 | tf_op jit(solution)/shard_map/pallas_call | solution.py:694
  233.6 29.3 %shard_map.156 = (f32[512,1024]{1,0:T(8,128)S(1)}, bf16[512,1024]{1,0:T(8,128)(2,1)S(1)}, bf16[2,512,2816]{2,1,0:T(8,128)(2,1)}, bf16[512,2816]{1,0:T(8,128)(2,1...) custom-call(f32[512,1024]{1,0:T(8,128)S(1)} %convert_add_fusion.refs, ...), custom_call_target="tpu_custom_call", output_to_operand_aliasing={{4}: (5, {}), {5}: (6, {})} | custom-call | flops 8858370048 | bytes 17301504 | tf_op jit(solution)/shard_map/pallas_call | solution.py:694
  266.2 22.9 %shard_map.157 = (bf16[512,1024]{1,0:T(8,128)(2,1)S(1)}, bf16[512,1024]{1,0:T(8,128)(2,1)S(1)}, bf16[3,512,1024]{2,1,0:T(8,128)(2,1)}, bf16[1,3,512,1024]{3,2,1,...) custom-call(f32[1024,128]{1,0:T(8,128)S(1)} %get-tuple-element.292.r, ...), custom_call_target="tpu_custom_call", output_to_operand_aliasing={{5}: (7, {}), {6}: (8, {})} | custom-call | flops 3221225472 | bytes 6291456 | tf_op jit(solution)/shard_map/pallas_call | solution.py:694
  298.0 28.8 %shard_map.159 = bf16[2,8,128,1024]{3,2,1,0:T(8,128)(2,1)S(1)} custom-call(bf16[2,128,512]{2,1,0:T(8,128)(2,1)S(1)} %shard_map.158.refs_0_), custom_call_target="tpu_custom_call" | custom-call | tf_op jit(solution)/shard_map/pallas_call | solution.py:694
  328.9 26.5 %shard_map.160 = (bf16[512,1024]{1,0:T(8,128)(2,1)S(1)}, bf16[4,2,4,32,5632]{4,3,2,1,0:T(8,128)(2,1)}, bf16[2,256,1024]{2,1,0:T(8,128)(2,1)S(1)}) custom-call(s32[1]{0:T(128)} %bitcast.refs_0_, bf16[512,1024]{1,0:T(8,128)(2,1)S(1)} %copy-done.29, bf16[3,512,1024]{2,1,0:T(8,128)(2,1)} %get-tuple-element.144.refs_0_.refs_2_.refs_5_, ...), custom_call_target="tpu_custom_call", output_to_operand_aliasing={{1}: (7, {})} | custom-call | flops 3758096384 | bytes 16777216 | tf_op jit(solution)/shard_map/pallas_call | solution.py:694
  356.7 18.3 %shard_map.161 = (f32[512,1024]{1,0:T(8,128)S(1)}, bf16[512,1024]{1,0:T(8,128)(2,1)S(1)}, bf16[2,512,2816]{2,1,0:T(8,128)(2,1)}, bf16[512,2816]{1,0:T(8,128)(2,1)}) custom-call(f32[512,1024]{1,0:T(8,128)S(1)} %convolution_add_fusion.refs_0_.refs_1_, f32[1,1024]{1,0:T(1,128)S(1)} %get-tuple-element.284.refs_1_.refs_2_, bf16[1024,5632]{1,0:T(8,128)(2,1)} %bitcast.248, ...), custom_call_target="tpu_custom_call" | custom-call | flops 8858370048 | bytes 17301504 | tf_op jit(solution)/shard_map/pallas_call | solution.py:694
  377.6 11.0 %shard_map.162 = bf16[2816,512]{1,0:T(8,128)(2,1)S(1)} custom-call(bf16[512,2816]{1,0:T(8,128)(2,1)} %get-tuple-element.154.refs_0_.refs_1_, bf16[512,2816]{1,0:T(8,128)(2,1)} %get-tuple-element.154.refs_0_.refs_1_, bf16[512,1024]{1,0:T(8,128)(2,1)S(1)} %bitcast.241), custom_call_target="tpu_custom_call" | custom-call | flops 2952790016 | bytes 2883584 | tf_op jit(solution)/shard_map/pallas_call | solution.py:694
  390.3 26.4 %shard_map.163 = (f32[512,1024]{1,0:T(8,128)}, bf16[512,1024]{1,0:T(8,128)(2,1)S(1)}, bf16[2,512,2816]{2,1,0:T(8,128)(2,1)}, f32[1,1024]{1,0:T(1,128)S(1)}, bf16...) custom-call(f32[512,1024]{1,0:T(8,128)} %bitcast_convert_fusion.refs, ...), custom_call_target="tpu_custom_call" | custom-call | flops 8858370048 | bytes 17301504 | tf_op jit(solution)/shard_map/pallas_call | solution.py:694
  418.8 13.2 %shard_map.164 = (bf16[1024,2816]{1,0:T(8,128)(2,1)}, bf16[1,704,512]{2,1,0:T(8,128)(2,1)S(1)}) custom-call(bf16[512,1024]{1,0:T(8,128)(2,1)S(1)} %copy-done.34, bf16[512,1024]{1,0:T(8,128)(2,1)S(1)} %get-tuple-element.161.refs_1_, bf16[2,512,2816]{2,1,0:T(8,128)(2,1)} %get-tuple-element.162.refs_2_, bf16[2,704,512]{2,1,0:T(8,128)(2,1)S(1)} %add_convert_fusion.8.refs_3_), custom_call_target="tpu_custom_call" | custom-call | flops 5905580032 | bytes 5767168 | tf_op jit(solution)/shard_map/pallas_call | solution.py:694
  437.2 43.2 %shard_map.165 = (bf16[512,1024]{1,0:T(8,128)(2,1)S(1)}, f32[2,512,1024]{2,1,0:T(8,128)}, bf16[1,2,512,1024]{3,2,1,0:T(8,128)(2,1)}, bf16[2,1024,1024]{2,1,0:T(8...) custom-call(s32[1]{0:T(128)} %bitcast.refs_0_, ...), custom_call_target="tpu_custom_call" | custom-call | flops 9395240960 | bytes 16777216 | tf_op jit(solution)/shard_map/pallas_call | solution.py:694
  484.6 31.6 %shard_map.166 = (bf16[1024,512]{1,0:T(8,128)(2,1)S(1)}, bf16[7,2,128,512]{3,2,1,0:T(8,128)(2,1)S(1)}) custom-call(bf16[512,1024]{1,0:T(8,128)(2,1)S(1)} %copy-done.11, bf16[512,1024]{1,0:T(8,128)(2,1)S(1)} %get-tuple-element.171.refs_1_, bf16[512,1024]{1,0:T(8,128)(2,1)S(1)} %get-tuple-element.160.refs_2_, bf16[2,8,128,512]{3,2,1,0:T(8,128)(2,1)} %bitcast.273), custom_call_target="tpu_custom_call" | custom-call | flops 1073741824 | bytes 1048576 | tf_op jit(solution)/shard_map/pallas_call | solution.py:694
  523.5 27.9 %shard_map.167 = (bf16[512,3072]{1,0:T(8,128)(2,1)}, bf16[1,256,2816]{2,1,0:T(8,128)(2,1)S(1)}, bf16[2,256,512]{2,1,0:T(8,128)(2,1)S(1)}, bf16[2,128,1024]{2,1,0:T(8,128)(2,1)S(1)}) custom-call(bf16[512,1024]{1,0:T(8,128)(2,1)S(1)} %get-tuple-element.166.refs_0_, f32[2,512,1024]{2,1,0:T(8,128)} %get-tuple-element.167.refs_1_, ...), custom_call_target="tpu_custom_call" | custom-call | flops 1048576 | bytes 8388608 | tf_op jit(solution)/shard_map/pallas_call | solution.py:694
  571.2 24.2 %shard_map.169 = (bf16[2816,512]{1,0:T(8,128)(2,1)}, bf16[2,256,1536]{2,1,0:T(8,128)(2,1)S(1)}, bf16[1,2,32,2816]{3,2,1,0:T(8,128)(2,1)S(1)}) custom-call(bf16[512,2816]{1,0:T(8,128)(2,1)} %get-tuple-element.157.refs_11_.refs_0_, bf16[512,2816]{1,0:T(8,128)(2,1)} %get-tuple-element.180.refs_1_, bf16[512,1024]{1,0:T(8,128)(2,1)S(1)} %get-tuple-element.237.refs_2_, ...), custom_call_target="tpu_custom_call" | custom-call | flops 2952790016 | bytes 2883584 | tf_op jit(solution)/shard_map/pallas_call | solution.py:694
  598.7 34.2 %shard_map.170 = (f32[512,1024]{1,0:T(8,128)}, bf16[512,1024]{1,0:T(8,128)(2,1)S(1)}, bf16[2,512,2816]{2,1,0:T(8,128)(2,1)}, f32[1,1024]{1,0:T(1,128)S(1)}, bf16...) custom-call(f32[512,1024]{1,0:T(8,128)} %get-tuple-element.238.refs_, ...), custom_call_target="tpu_custom_call" | custom-call | flops 8858370048 | bytes 17301504 | tf_op jit(solution)/shard_map/pallas_call | solution.py:694
  636.4 13.4 %shard_map.171 = (bf16[1024,1408]{1,0:T(8,128)(2,1)}, bf16[1,704,512]{2,1,0:T(8,128)(2,1)S(1)}, bf16[1,2,32,1536]{3,2,1,0:T(8,128)(2,1)S(1)}) custom-call(bf16[512,1024]{1,0:T(8,128)(2,1)S(1)} %copy-done.15, bf16[512,1024]{1,0:T(8,128)(2,1)S(1)} %get-tuple-element.189.refs_1_, bf16[2,512,2816]{2,1,0:T(8,128)(2,1)} %get-tuple-element.190.refs_2_, ...), custom_call_target="tpu_custom_call" | custom-call | flops 2952790016 | bytes 2883584 | tf_op jit(solution)/shard_map/pallas_call | solution.py:694
  650.6 22.2 %shard_map.172 = (bf16[1024,1408]{1,0:T(8,128)(2,1)}, bf16[2,256,1408]{2,1,0:T(8,128)(2,1)S(1)}, bf16[2,2,32,1536]{3,2,1,0:T(8,128)(2,1)S(1)}) custom-call(bf16[512,1024]{1,0:T(8,128)(2,1)S(1)} %copy-done.15, bf16[512,1024]{1,0:T(8,128)(2,1)S(1)} %get-tuple-element.189.refs_1_, bf16[2,512,2816]{2,1,0:T(8,128)(2,1)} %get-tuple-element.190.refs_2_, ...), custom_call_target="tpu_custom_call" | custom-call | flops 2952790016 | bytes 2883584 | tf_op jit(solution)/shard_map/pallas_call | solution.py:694
  680.1 29.0 %shard_map.173 = (bf16[512,1024]{1,0:T(8,128)(2,1)S(1)}, f32[2,512,1024]{2,1,0:T(8,128)}, bf16[1,2,512,1024]{3,2,1,0:T(8,128)(2,1)}, bf16[2,256,1408]{2,1,0:T(8,...) custom-call(s32[1]{0:T(128)} %bitcast.refs_0_, ...), custom_call_target="tpu_custom_call" | custom-call | flops 4026531840 | bytes 8388608 | tf_op jit(solution)/shard_map/pallas_call | solution.py:694
  716.0 20.6 %shard_map.175 = (bf16[512,3072]{1,0:T(8,128)(2,1)}, bf16[1,256,1408]{2,1,0:T(8,128)(2,1)S(1)}, bf16[2,256,512]{2,1,0:T(8,128)(2,1)S(1)}, bf16[3,2,32,1408]{3,2,1,0:T(8,128)(2,1)S(1)}) custom-call(bf16[512,1024]{1,0:T(8,128)(2,1)S(1)} %get-tuple-element.198.refs_0_, f32[2,512,1024]{2,1,0:T(8,128)} %get-tuple-element.199.refs_1_, ...), custom_call_target="tpu_custom_call" | custom-call | flops 1048576 | bytes 8388608 | tf_op jit(solution)/shard_map/pallas_call | solution.py:694
  747.2 18.9 %shard_map.176 = (bf16[1024,1536]{1,0:T(8,128)(2,1)}, bf16[3,2,32,1408]{3,2,1,0:T(8,128)(2,1)S(1)}, bf16[1,256,512]{2,1,0:T(8,128)(2,1)S(1)}, f32[32,128]{1,0:T(8,128)S(1)}) custom-call(bf16[512,1024]{1,0:T(8,128)(2,1)S(1)} %copy-done.23, bf16[512,1024]{1,0:T(8,128)(2,1)S(1)} %copy-done.72, bf16[512,3072]{1,0:T(8,128)(2,1)} %get-tuple-element.204.refs_2_, ...), custom_call_target="tpu_custom_call" | custom-call | flops 3221225472 | bytes 3145728 | tf_op jit(solution)/shard_map/pallas_call | solution.py:694
  768.3 25.2 %shard_map.177 = (bf16[2,256,1536]{2,1,0:T(8,128)(2,1)S(1)}, bf16[3,2,32,512]{3,2,1,0:T(8,128)(2,1)S(1)}, bf16[2,128,1024]{2,1,0:T(8,128)(2,1)S(1)}, f32[32,128]{1,0:T(8,128)S(1)}) custom-call(bf16[4,256,1536]{2,1,0:T(8,128)(2,1)} %bitcast.275, bf16[2,4,32,512]{3,2,1,0:T(8,128)(2,1)S(1)} %bitcast.233, bf16[2,128,1024]{2,1,0:T(8,128)(2,1)S(1)} %get-tuple-element.256.refs_2_, ...), custom_call_target="tpu_custom_call" | custom-call | tf_op jit(solution)/shard_map/pallas_call | solution.py:694
  795.4 12.6 %shard_map.178 = (bf16[1,256,1536]{2,1,0:T(8,128)(2,1)S(1)}, bf16[2,128,1024]{2,1,0:T(8,128)(2,1)S(1)}, f32[32,128]{1,0:T(8,128)S(1)}) custom-call(bf16[2,256,1536]{2,1,0:T(8,128)(2,1)S(1)} %add_convert_fusion.2.refs_0_, bf16[2,128,1024]{2,1,0:T(8,128)(2,1)S(1)} %get-tuple-element.255.refs_1_, f32[32,128]{1,0:T(8,128)S(1)} %add.442.refs_2_), custom_call_target="tpu_custom_call" | custom-call | tf_op jit(solution)/shard_map/pallas_call | solution.py:694
  808.8 20.8 %shard_map.179 = (bf16[3,2,32,1536]{3,2,1,0:T(8,128)(2,1)S(1)}, f32[3,32,128]{2,1,0:T(8,128)S(1)}) custom-call(bf16[2,4,32,1536]{3,2,1,0:T(8,128)(2,1)S(1)} %bitcast.227, f32[32,128]{1,0:T(8,128)S(1)} %add.445.refs_1_), custom_call_target="tpu_custom_call" | custom-call | tf_op jit(solution)/shard_map/pallas_call | solution.py:694
  (346 shorter events, 131.1 us)
Async XLA Ops:
  0.6 183.5 %copy-start.87 = (s32[2,8]{1,0:T(2,128)S(1)}, s32[2,8]{1,0:T(2,128)}, u32[]{:S(2)}) copy-start(s32[2,8]{1,0:T(2,128)} %param.15) | copy-start | bytes 196
  0.6 291.7 %collective-permute-start = (s32[2,1,8,128]{3,2,1,0:T(8,128)}, s32[2,1,8,128]{3,2,1,0:T(8,128)S(1)}, u32[]{:S(2)}, u32[]{:S(2)}) collective-permute-start(s32[2,1,8,128]{3,2,1,0:T(8,128)} %param.16), channel_id=1, source_target_pairs={{0,4},{1,5},{2,6},{3,7},{4,0},{5,1},{6,2},{7,3},{8,12},{9,13},{10,... | collective-permute-start | bytes 24584 | tf_op jit(solution)/shard_map/ppermute | solution.py:70
  183.2 49.1 %copy-start.5 = (bf16[2,256,1024]{2,1,0:T(8,128)(2,1)}, bf16[2,256,1024]{2,1,0:T(8,128)(2,1)S(1)}, u32[]{:S(2)}) copy-start(bf16[2,256,1024]{2,1,0:T(8,128)(2,1)S(1)} %get-tuple-element.125) | copy-start | bytes 3145732
  210.4 21.9 %copy-start.24 = (bf16[512,1024]{1,0:T(8,128)(2,1)}, bf16[512,1024]{1,0:T(8,128)(2,1)S(1)}, u32[]{:S(2)}) copy-start(bf16[512,1024]{1,0:T(8,128)(2,1)S(1)} %get-tuple-element.129.refs_1_.refs_3_) | copy-start | bytes 3145732
  233.6 29.3 %copy-start.7 = (f32[512,1024]{1,0:T(8,128)}, f32[512,1024]{1,0:T(8,128)S(1)}, u32[]{:S(2)}) copy-start(f32[512,1024]{1,0:T(8,128)S(1)} %convert_add_fusion.refs_0_.refs_1_) | copy-start | bytes 6291460
  266.2 26.2 %copy-start.86 = (s32[2,1,8,128]{3,2,1,0:T(8,128)S(1)}, s32[2,1,8,128]{3,2,1,0:T(8,128)}, u32[]{:S(2)}) copy-start(s32[2,1,8,128]{3,2,1,0:T(8,128)} %param.16) | copy-start | bytes 24580
  298.0 30.8 %copy-start.21 = (bf16[2,256,1024]{2,1,0:T(8,128)(2,1)S(1)}, bf16[2,256,1024]{2,1,0:T(8,128)(2,1)}, u32[]{:S(2)}) copy-start(bf16[2,256,1024]{2,1,0:T(8,128)(2,1)} %refs_8_.1) | copy-start | bytes 3145732
  298.0 30.8 %copy-start.29 = (bf16[512,1024]{1,0:T(8,128)(2,1)S(1)}, bf16[512,1024]{1,0:T(8,128)(2,1)}, u32[]{:S(2)}) copy-start(bf16[512,1024]{1,0:T(8,128)(2,1)} %copy-done.28) | copy-start | bytes 3145732
  298.0 30.8 %copy-start.32 = (bf16[512,1024]{1,0:T(8,128)(2,1)S(1)}, bf16[512,1024]{1,0:T(8,128)(2,1)}, u32[]{:S(2)}) copy-start(bf16[512,1024]{1,0:T(8,128)(2,1)} %copy-done.31) | copy-start | bytes 3145732
  328.9 26.5 %copy-start.1 = (f32[512,1024]{1,0:T(8,128)S(1)}, f32[512,1024]{1,0:T(8,128)}, u32[]{:S(2)}) copy-start(f32[512,1024]{1,0:T(8,128)} %copy-done) | copy-start | bytes 6291460
  328.9 26.5 %copy-start.88 = (bf16[4,2,4,32,1024]{4,3,2,1,0:T(8,128)(2,1)S(1)}, bf16[4,2,4,32,1024]{4,3,2,1,0:T(8,128)(2,1)}, u32[]{:S(2)}) copy-start(bf16[4,2,4,32,1024]{4,3,2,1,0:T(8,128)(2,1)} %get-tuple-element.150) | copy-start | bytes 6291460
  517.6 5.7 collective-permute-start.1
  517.8 4.7 collective-permute-start.10
  598.7 34.3 %copy-start.73 = (bf16[2,256,1536]{2,1,0:T(8,128)(2,1)S(1)}, bf16[2,256,1536]{2,1,0:T(8,128)(2,1)}, u32[]{:S(2)}) copy-start(bf16[2,256,1536]{2,1,0:T(8,128)(2,1)} %add_convert_fusion.3.refs_9_) | copy-start | bytes 4718596
  680.1 29.9 %copy-start.77 = (bf16[2,256,1408]{2,1,0:T(8,128)(2,1)S(1)}, bf16[2,256,1408]{2,1,0:T(8,128)(2,1)}, u32[]{:S(2)}) copy-start(bf16[2,256,1408]{2,1,0:T(8,128)(2,1)} %add_convert_fusion.5.refs_9_) | copy-start | bytes 4325380
  714.8 21.9 %slice-start = ((s8[6291456]{0:T(1024)(128)(4,1)}), s8[4194304]{0:T(1024)(128)(4,1)S(1)}, s32[]{:S(2)}) async-start(s8[6291456]{0:T(1024)(128)(4,1)} %bitcast.265), calls=%async_computation | async-start | bytes 8388608
  831.1 12.1 %collective-permute-start.9 = (bf16[88,512]{1,0:T(8,128)(2,1)S(1)}, bf16[88,512]{1,0:T(8,128)(2,1)S(1)}, u32[]{:S(2)}, u32[]{:S(2)}) collective-permute-start(bf16[88,512]{1,0:T(8,128)(2,1)S(1)} %fusion.16), channel_id=1, source_target_pairs={{0,4},{1,5},{2,6},{3,7},{4,0},{5,1},{6,2},{7,3},{8,12},{9,13},{10,... | collective-permute-start | bytes 270344 | tf_op jit(solution)/shard_map/ppermute | solution.py:70
  832.4 11.0 %collective-permute-start.6 = (bf16[32,1408]{1,0:T(8,128)(2,1)S(1)}, bf16[32,1408]{1,0:T(8,128)(2,1)S(1)}, u32[]{:S(2)}, u32[]{:S(2)}) collective-permute-start(bf16[32,1408]{1,0:T(8,128)(2,1)S(1)} %fusion.14), channel_id=1, source_target_pairs={{0,4},{1,5},{2,6},{3,7},{4,0},{5,1},{6,2},{7,3},{8,12},{9,13},{10,... | collective-permute-start | bytes 270344 | tf_op jit(solution)/shard_map/ppermute | solution.py:70
  834.0 9.4 %collective-permute-start.7 = (bf16[32,1408]{1,0:T(8,128)(2,1)S(1)}, bf16[32,1408]{1,0:T(8,128)(2,1)S(1)}, u32[]{:S(2)}, u32[]{:S(2)}) collective-permute-start(bf16[32,1408]{1,0:T(8,128)(2,1)S(1)} %fusion.15), channel_id=1, source_target_pairs={{0,4},{1,5},{2,6},{3,7},{4,0},{5,1},{6,2},{7,3},{8,12},{9,13},{10,... | collective-permute-start | bytes 270344 | tf_op jit(solution)/shard_map/ppermute | solution.py:70
  835.4 10.7 %collective-permute-start.8 = (bf16[32,2816]{1,0:T(8,128)(2,1)S(1)}, bf16[32,2816]{1,0:T(8,128)(2,1)S(1)}, u32[]{:S(2)}, u32[]{:S(2)}) collective-permute-start(bf16[32,2816]{1,0:T(8,128)(2,1)S(1)} %fusion.10), channel_id=1, source_target_pairs={{0,4},{1,5},{2,6},{3,7},{4,0},{5,1},{6,2},{7,3},{8,12},{9,13},{10,... | collective-permute-start | bytes 540680 | tf_op jit(solution)/shard_map/ppermute | solution.py:70
  836.0 4.7 collective-permute-start.4
  840.7 1.3 collective-permute-start.5
  842.0 3.0 collective-permute-start.2
  843.2 2.0 collective-permute-start.3
  (81 other events, 354.5 us)

commit v7 on v6

--- a/solution.py
+++ b/solution.py
@@ -17,7 +17,7 @@
 LOG2E = 1.0 / math.log(2.0)
 BF = jnp.bfloat16
 F32 = jnp.float32
-VMEM_LIMIT = 48 * 1024 * 1024
+VMEM_LIMIT = 44 * 1024 * 1024
 
 
 def slot_layout(lengths):
@@ -888,10 +888,13 @@
     return found
 
 
-def softmax_parts(scores):
+def softmax_parts(scores, stat=None):
     top = functools.reduce(jnp.maximum, [jnp.max(s, axis=0, keepdims=True) for s in scores])
     powers = [jnp.exp2((s - top) * (SCALE * LOG2E)) for s in scores]
-    inverse = 1.0 / sum(jnp.sum(p, axis=0, keepdims=True) for p in powers)
+    total = sum(jnp.sum(p, axis=0, keepdims=True) for p in powers)
+    if stat is not None:
+        stat(top * (SCALE * LOG2E) + jnp.log(total) * LOG2E)
+    inverse = 1.0 / total
     return [p * inverse for p in powers]
 
 
@@ -927,9 +930,12 @@
             if extra is not None:
                 scores.append(dot(refs[1][0], refs[0][at, :], (1, 1)) + refs[2][...])
                 mixed.append(refs[1][1])
-            total = sum(
-                dot(value, p.astype(BF), (0, 0)) for value, p in zip(mixed, softmax_parts(scores))
-            )
+
+            def stat(row):
+                outs[1][0, :, at] = row
+
+            probs = softmax_parts(scores, stat)
+            total = sum(dot(value, p.astype(BF), (0, 0)) for value, p in zip(mixed, probs))
             outs[0][at, :] = total.T.astype(BF)
 
     piece = columns_spec(rows, HEAD_DIM)
@@ -940,17 +946,85 @@
         more, more_specs, memory_rows = memory_operands(grid, extra)
         operands, specs = operands + more, specs + more_specs
     outs, got = host(
-        grid, body, heads, specs, operands, [piece], [kind(rows, width)], moves,
+        grid, body, heads, specs, operands,
+        [piece, rows_spec(1, 1, rows)], [kind(rows, width), kind(heads, 1, rows, dtype=F32)], moves,
         cost=attention_cost(grid, heads, memory_rows, 2),
     )
-    return outs[0], got
-
-
-def attend_back(grid, valid, tables, query, grad, pairs, extra, moves=()):
+    return outs[0], outs[1], got
+
+
+def inner_row(grads, mixed):
+    return jnp.sum((grads.astype(F32) * mixed.astype(F32)).T, axis=0, keepdims=True)
+
+
+def memory_back(grid, grad_heads, attended, extra, moves=()):
+    rows, width = grad_heads.shape
+    heads = width // HEAD_DIM
+    per = heads // 2
+    memory_rows = extra["memory"].shape[1]
+
+    def memory_send(here, held, target, h):
+        columns = pl.ds(pl.multiple_of(h * HEAD_DIM, HEAD_DIM), HEAD_DIM)
+        return pltpu.make_async_remote_copy(
+            src_ref=held[0].at[h],
+            dst_ref=target.at[:, :, columns],
+            send_sem=held[1].at[0, h],
+            recv_sem=held[1].at[1, h],
+            device_id=here.swap,
+            device_id_type=MESH,
+        )
+
+    def body(here, step, ins, outs, held):
+        g_ref, mixed_ref, stat_ref, q_ref, memory_ref, bias_ref = ins
+        grad_key, grad_value = 0.0, 0.0
+        for part in range(2):
+            at = pl.ds(part * grid.R, grid.R)
+            grads, query = g_ref[at, :], q_ref[at, :]
+            inner = inner_row(grads, mixed_ref[at, :])
+            score = dot(memory_ref[0], query, (1, 1)) + bias_ref[...]
+            prob = jnp.exp2(score * (SCALE * LOG2E) - stat_ref[0, :, at])
+            moved = (prob * (dot(memory_ref[1], grads, (1, 1)) - inner)).astype(BF)
+            grad_key = grad_key + dot(moved, query, (1, 0))
+            grad_value = grad_value + dot(prob.astype(BF), grads, (1, 0))
+            outs[0][at, :] = dot(memory_ref[0], moved, (0, 0)).T
+        grad_key, grad_value = (grad_key * SCALE).astype(BF), grad_value.astype(BF)
+        outs[1][0] = grad_key
+        outs[1][1] = grad_value
+
+        @pl.when(step // per == 1 - here.c)
+        def _():
+            held[0][step % per, 0] = grad_key
+            held[0][step % per, 1] = grad_value
+            memory_send(here, held, outs[2], step % per).start()
+
+        @pl.when(step == heads - 1)
+        def _():
+            for h in range(per):
+                memory_send(here, held, outs[2], h).wait()
+
+    piece = columns_spec(rows, HEAD_DIM)
+    column = columns_spec(2, memory_rows, HEAD_DIM)
+    return host(
+        grid, body, heads,
+        [piece, piece, rows_spec(1, 1, rows), piece, column, whole_spec(memory_rows, 1)],
+        [grad_heads, attended, extra["logsum"], extra["query"], extra["memory"], extra["bias"]],
+        [piece, column, any_spec()],
+        [kind(rows, width, dtype=F32), kind(2, memory_rows, width), kind(2, memory_rows, width // 2)],
+        moves,
+        scratch=[pltpu.VMEM((per, 2, memory_rows, HEAD_DIM), BF), pltpu.SemaphoreType.DMA((2, per))],
+        cost=pl.CostEstimate(
+            flops=10 * HEAD_DIM * rows * memory_rows * heads,
+            bytes_accessed=12 * memory_rows * width,
+            transcendentals=rows * memory_rows * heads,
+        ),
+        reaches=lambda here: [here.swap],
+    )
+
+
+def attend_back(grid, valid, tables, query, grad, w_out, pairs, moves=(), memory=None):
     rows, width = query.shape
     heads = width // HEAD_DIM
     R, U = grid.R, grid.U
-    per = heads // 2
 
     def sends(here, held, target, h):
         columns = pl.ds(pl.multiple_of(h * HEAD_DIM, HEAD_DIM), HEAD_DIM)
@@ -966,17 +1040,6 @@
             for t in range(1, U)
         ]
 
-    def memory_send(here, held, target, h):
-        columns = pl.ds(pl.multiple_of(h * HEAD_DIM, HEAD_DIM), HEAD_DIM)
-        return pltpu.make_async_remote_copy(
-            src_ref=held[2].at[h],
-            dst_ref=target.at[:, :, columns],
-            send_sem=held[3].at[0, h],
-            recv_sem=held[3].at[1, h],
-            device_id=here.swap,
-            device_id_type=MESH,
-        )
-
     def body(here, step, ins, outs, held):
         valid_ref, cos_ref, sin_ref, q_ref, g_ref = ins[:5]
         kv_refs, refs = ins[5 : 5 + U], ins[5 + U :]
@@ -986,39 +1049,43 @@
         def add(store, at, value):
             store[at] = store[at] + value if at in store else value
 
+        if memory is None:
+
+            @pl.when(step == 0)
+            def _():
+                held[2][...] = dot(g_ref[...], refs[0][...], (1, 1)).astype(BF)
+
         for part in range(2):
             at_rows = pl.ds(part * R, R)
-            asked, grads_in = q_ref[at_rows, :], g_ref[at_rows, :]
+            asked = q_ref[at_rows, :]
+            if memory is None:
+                grads_in = held[2][at_rows, pl.ds(pl.multiple_of(step * HEAD_DIM, HEAD_DIM), HEAD_DIM)]
+            else:
+                grads_in = g_ref[at_rows, :]
             found = part_scores(grid, here, valid_ref[0], part, asked, keys)
             places = [(t, side) for t, side, _ in found]
             scores = [s for _, _, s in found]
             part_keys = [keys[t][side * R : (side + 1) * R] for t, side in places]
             part_values = [values[t][side * R : (side + 1) * R] for t, side in places]
-            queries = [asked] * len(places)
-            if extra is not None:
-                places.append("memory")
-                queries.append(refs[0][at_rows, :])
-                scores.append(dot(refs[1][0], queries[-1], (1, 1)) + refs[2][...])
-                part_keys.append(refs[1][0])
-                part_values.append(refs[1][1])
-            probs = softmax_parts(scores)
             grads = [dot(value, grads_in, (1, 1)) for value in part_values]
-            inner = sum(jnp.sum(p * d, axis=0, keepdims=True) for p, d in zip(probs, grads))
-            local_query, raw_query = None, None
-            for at, p, d, key, by in zip(places, probs, grads, part_keys, queries):
+            if memory is None:
+                probs = softmax_parts(scores)
+                inner = sum(jnp.sum(p * d, axis=0, keepdims=True) for p, d in zip(probs, grads))
+            else:
+                probs = [jnp.exp2(s * (SCALE * LOG2E) - refs[1][0, :, at_rows]) for s in scores]
+                inner = inner_row(grads_in, refs[0][at_rows, :])
+            back = None
+            for at, p, d, key in zip(places, probs, grads, part_keys):
                 moved = (p * (d - inner)).astype(BF)
-                add(grad_keys, at, dot(moved, by, (1, 0)))
+                add(grad_keys, at, dot(moved, asked, (1, 0)))
                 add(grad_values, at, dot(p.astype(BF), grads_in, (1, 0)))
-                back = dot(key, moved, (0, 0))
-                if at == "memory":
-                    raw_query = back
-                else:
-                    local_query = back if local_query is None else local_query + back
+                share = dot(key, moved, (0, 0))
+                back = share if back is None else back + share
             cos = table_rows(grid, cos_ref, here.k, part)
             sin = table_rows(grid, sin_ref, here.k, part)
-            result = turn(local_query.T, cos, -sin)
-            if extra is not None:
-                result = result + raw_query.T
+            result = turn(back.T, cos, -sin)
+            if memory is not None:
+                result = result + refs[2][at_rows, :]
             outs[0][at_rows, :] = (result * SCALE).astype(BF)
         for t in range(U):
             member = (here.k - t + U) % U
@@ -1035,104 +1102,72 @@
                     held[0][step, t - 1, 1, at_rows, :] = grad_values[(t, side)].astype(BF)
         for copy in sends(here, held, outs[2], step):
             copy.start()
-        if extra is not None:
-            memory_key = (grad_keys["memory"] * SCALE).astype(BF)
-            memory_value = grad_values["memory"].astype(BF)
-            outs[3][0] = memory_key
-            outs[3][1] = memory_value
-
-            @pl.when(step // per == 1 - here.c)
-            def _():
-                held[2][step % per, 0] = memory_key
-                held[2][step % per, 1] = memory_value
-                memory_send(here, held, outs[4], step % per).start()
 
         @pl.when(step == heads - 1)
         def _():
             for h in range(heads):
                 for copy in sends(here, held, outs[2], h):
                     copy.wait()
-            if extra is not None:
-                for h in range(per):
-                    memory_send(here, held, outs[4], h).wait()
 
     piece = columns_spec(rows, HEAD_DIM)
     pair = columns_spec(2, rows, HEAD_DIM)
     table = whole_spec(SEG, HEAD_DIM)
     operands = [valid, *tables, query, grad, *pairs]
-    specs = [smem(), table, table, piece, piece] + [pair] * U
-    out_shape = [kind(rows, width), kind(2, rows, width, dtype=F32), kind(U - 1, 2, rows, width)]
-    out_specs = [piece, pair, any_spec()]
     scratch = [pltpu.VMEM((heads, U - 1, 2, rows, HEAD_DIM), BF), pltpu.SemaphoreType.DMA((2, U - 1, heads))]
-    memory_rows = 0
-    if extra is not None:
-        more, more_specs, memory_rows = memory_operands(grid, extra)
-        operands, specs = operands + more, specs + more_specs
-        out_shape += [kind(2, memory_rows, width), kind(2, memory_rows, width // 2)]
-        out_specs += [columns_spec(2, memory_rows, HEAD_DIM), any_spec()]
-        scratch += [pltpu.VMEM((per, 2, memory_rows, HEAD_DIM), BF), pltpu.SemaphoreType.DMA((2, per))]
-
-    def reaches(here):
-        return [here.member(t) for t in range(1, U)] + [here.swap] * (extra is not None)
-
+    if memory is None:
+        specs = [smem(), table, table, piece, whole_spec(rows, width)] + [pair] * U + [whole_spec(width, width)]
+        operands.append(w_out)
+        scratch.append(pltpu.VMEM((rows, width), BF))
+    else:
+        specs = [smem(), table, table, piece, piece] + [pair] * U + [piece, rows_spec(1, 1, rows), piece]
+        operands += memory
     return host(
-        grid, body, heads, specs, operands, out_specs, out_shape, moves,
+        grid, body, heads, specs, operands,
+        [piece, pair, any_spec()],
+        [kind(rows, width), kind(2, rows, width, dtype=F32), kind(U - 1, 2, rows, width)],
+        moves,
         scratch=scratch,
-        cost=attention_cost(grid, heads, memory_rows, 5),
-        reaches=reaches,
+        cost=attention_cost(grid, heads, 0, 5),
+        reaches=lambda here: [here.member(t) for t in range(1, U)],
     )
 
 
-def pick_memory(grid, picks, stacked, c):
+def gather_memory(grid, picks, pairs):
+    n, U, R = grid.n_dp, grid.U, grid.R
     heads, topk = picks.shape
     per = heads // 2
-    R, U = grid.R, grid.U
-
-    def body(info_ref, picks_ref, *refs):
-        chosen_from, out_ref = refs[:U], refs[U]
-        here = Here(grid)
-        picked = picks_ref[0]
-        key, value = 0.0, 0.0
-        for t in range(U):
-            member = (here.k - t + U) % U
-            for side in range(2):
-                across = lax.broadcasted_iota(jnp.int32, (picked.shape[0], R), 1)
-                chosen = (picked == across + piece_start(grid, member, side)).astype(BF)
-                at = pl.ds(side * R, R)
-                key = key + dot(chosen, chosen_from[t][2, at, :], (1, 0))
-                value = value + dot(chosen, chosen_from[t][1, at, :], (1, 0))
-        out_ref[0] = key.astype(BF)
-        out_ref[1] = value.astype(BF)
-
-    at = lambda h, info: info[0] * per + h
-    piece = pl.BlockSpec((3, grid.T, HEAD_DIM), lambda h, info: (0, 0, at(h, info)))
-    return pl.pallas_call(
-        body,
-        grid_spec=pltpu.PrefetchScalarGridSpec(
-            num_scalar_prefetch=1,
-            grid=(per,),
-            in_specs=[pl.BlockSpec((1, topk, 1), lambda h, info: (at(h, info), 0, 0))] + [piece] * U,
-            out_specs=pl.BlockSpec((2, topk, HEAD_DIM), lambda h, info: (0, 0, h)),
-        ),
-        out_shape=kind(2, topk, per * HEAD_DIM),
-        compiler_params=pltpu.CompilerParams(vmem_limit_bytes=VMEM_LIMIT),
-        cost_estimate=pl.CostEstimate(
-            flops=4 * topk * SEG * HEAD_DIM * per, bytes_accessed=4 * SEG * HEAD_DIM * per, transcendentals=0
-        ),
-    )(c.reshape(1).astype(jnp.int32), picks[:, :, None], *stacked)
-
-
-def gather_memory(grid, chosen):
-    n = grid.n_dp
-    half = chosen.shape[2]
+    half = per * HEAD_DIM
 
     def body(here, step, ins, outs, held):
-        source, target = ins[0], outs[0]
-        own_sem, sems = held
-        mine = target.at[:, :, :, pl.ds(pl.multiple_of(here.c * half, 128), half)]
-        own = pltpu.make_async_copy(source, mine.at[:, 0], own_sem)
-        across = [remote(source, mine.at[:, t], sems, t, here.slots(t)) for t in range(1, n)]
-        swaps = [remote(source, mine.at[:, 0], sems, n, here.swap)]
+        picks_ref, sources, target = ins[0], ins[1:], outs[0]
+        rows, chosen, load_sems, own_sem, sems = held
+        columns = pl.ds(pl.multiple_of(here.c * half, 128), half)
+        loads = [
+            pltpu.make_async_copy(source.at[1:3, :, columns], rows.at[t], load_sems.at[t])
+            for t, source in enumerate(sources)
+        ]
+        for load in loads:
+            load.start()
+        for load in loads:
+            load.wait()
+        for h in range(per):
+            picked = picks_ref[here.c * per + h]
+            at_columns = slice(h * HEAD_DIM, (h + 1) * HEAD_DIM)
+            totals = [0.0, 0.0]
+            for t in range(U):
+                member = (here.k - t + U) % U
+                for side in range(2):
+                    across = lax.broadcasted_iota(jnp.int32, (topk, R), 1)
+                    mask = (picked == across + piece_start(grid, member, side)).astype(BF)
+                    for i in range(2):
+                        block = rows[t, i, side * R : (side + 1) * R, at_columns]
+                        totals[i] = totals[i] + dot(mask, block, (1, 0))
+            chosen[0, :, at_columns] = totals[1].astype(BF)
+            chosen[1, :, at_columns] = totals[0].astype(BF)
+        mine = target.at[:, :, :, columns]
+        own = pltpu.make_async_copy(chosen, mine.at[:, 0], own_sem)
+        across = [remote(chosen, mine.at[:, t], sems, t, here.slots(t)) for t in range(1, n)]
+        swaps = [remote(chosen, mine.at[:, 0], sems, n, here.swap)]
         swaps += [remote(mine.at[:, t], mine.at[:, t], sems, n + t, here.swap) for t in range(1, n)]
         for copy in across + [swaps[0], own]:
             copy.start()
@@ -1146,8 +1181,17 @@
             copy.wait()
 
     outs, _ = host(
-        grid, body, 1, [any_spec()], [chosen], [any_spec()], [kind(2, n, chosen.shape[1], 2 * half)],
-        scratch=[pltpu.SemaphoreType.DMA, pltpu.SemaphoreType.DMA((2, 2 * n))],
+        grid, body, 1,
+        [whole_spec(heads, topk, 1)] + [any_spec()] * U,
+        [picks[:, :, None], *pairs],
+        [any_spec()], [kind(2, n, topk, 2 * half)],
+        scratch=[
+            pltpu.VMEM((U, 2, grid.T, half), BF),
+            pltpu.VMEM((2, topk, half), BF),
+            pltpu.SemaphoreType.DMA((U,)),
+            pltpu.SemaphoreType.DMA,
+            pltpu.SemaphoreType.DMA((2, 2 * n)),
+        ],
         reaches=lambda here: [here.slots(n - t) for t in range(1, n)] + [here.swap],
     )
     return outs[0]
@@ -1206,18 +1250,19 @@
 FEED_TILE = 256
 
 
-def feed(grid, middle, gain, w_up, w_down, moves=()):
-    rows, width = middle.shape
+def feed(grid, hidden_rows, attended, gain, w_out, w_up, w_down, moves=()):
+    rows, width = hidden_rows.shape
     hidden = w_down.shape[0]
     steps = hidden // FEED_TILE
 
     def body(here, step, ins, outs, held):
-        middle_ref, gain_ref, gate_w, up_w, down_w = ins
-        out_ref, normed_ref, both_ref, inner_ref = outs
+        hidden_ref, attended_ref, gain_ref, out_w, gate_w, up_w, down_w = ins
+        out_ref, middle_ref, normed_ref, both_ref, inner_ref = outs
 
         @pl.when(step == 0)
         def _():
-            value = middle_ref[...]
+            value = hidden_ref[...].astype(F32) + dot(attended_ref[...], out_w[...], (1, 0))
+            middle_ref[...] = value
             normed_ref[...] = norm(value, gain_ref[...]).astype(BF)
             held[0][...] = value
 
@@ -1236,10 +1281,11 @@
     tile = columns_spec(width, FEED_TILE)
     return host(
         grid, body, steps,
-        [whole_spec(rows, width), whole_spec(1, width), tile, columns_spec(width, FEED_TILE, first=steps), rows_spec(FEED_TILE, width)],
-        [middle, gain, w_up, w_up, w_down],
-        [whole_spec(rows, width), whole_spec(rows, width), columns_spec(2, rows, FEED_TILE), columns_spec(rows, FEED_TILE)],
-        [kind(rows, width, dtype=F32), kind(rows, width), kind(2, rows, hidden), kind(rows, hidden)],
+        [whole_spec(rows, width), whole_spec(rows, width), whole_spec(1, width), whole_spec(width, width), tile,
+         columns_spec(width, FEED_TILE, first=steps), rows_spec(FEED_TILE, width)],
+        [hidden_rows, attended, gain, w_out, w_up, w_up, w_down],
+        [whole_spec(rows, width)] * 3 + [columns_spec(2, rows, FEED_TILE), columns_spec(rows, FEED_TILE)],
+        [kind(rows, width, dtype=F32), kind(rows, width, dtype=F32), kind(rows, width), kind(2, rows, hidden), kind(rows, hidden)],
         moves,
         scratch=[pltpu.VMEM((rows, width), F32)],
         cost=pl.CostEstimate(flops=6 * rows * width * hidden, bytes_accessed=6 * width * hidden, transcendentals=rows * hidden),
@@ -1473,6 +1519,7 @@
         size = value.shape[-1] // 2
         return lax.dynamic_slice_in_dim(value, c * size, size, axis=value.ndim - 1)
 
+    tokens, *tables = lax.optimization_barrier((tokens, *tables))
     hidden, gains, weights = gather_all(
         grid, tokens, norm_gains, [attention_in, attention_out, feed_in, feed_out]
     )
@@ -1501,8 +1548,7 @@
         pairs = [split[2]] + [split[3][t] for t in range(grid.U - 1)]
         extra = None
         if memory:
-            chosen = pick_memory(grid, picks, pairs, grid.c)
-            slots = gather_memory(grid, chosen).reshape(2, n_dp * topk, -1)
+            slots = gather_memory(grid, picks, pairs).reshape(2, n_dp * topk, -1)
             extra = {"query": split[4], "memory": slots, "bias": bias}
         moves = []
         if coming is not None:
@@ -1511,7 +1557,7 @@
             moves.append(spread_move(grid, weights[l][2], [(2, 0, 1)]))
         if memory:
             moves.append(regroup_move(grid, cotangent))
-        attended, got = attend(grid, valid, query, pairs, extra, moves)
+        attended, logsum, got = attend(grid, valid, query, pairs, extra, moves)
         if coming is not None:
             coming[2] = got[0]
         if later_here(l, 2):
@@ -1520,12 +1566,14 @@
                 weights[l][2:] = send(grid, [spread_move(grid, w, [(stage, 0, 1)]) for w in weights[l][2:]])
         if memory:
             cotangent_rows = got[-1]
-        middle = hidden.astype(F32) + mm(attended, w_out)
+            extra["logsum"] = logsum
         moves = []
         if coming is not None:
             moves = [spread_move(grid, coming[2], [(0, 1, 2)]), spread_move(grid, coming[3], [(1, 0, 1)])]
         w_up, w_down = flat(weights[l][2]), flat(weights[l][3])
-        (out, normed_feed, both, inner), got = feed(grid, middle, gain(l, 1), w_up, w_down, moves)
+        (out, middle, normed_feed, both, inner), got = feed(
+            grid, hidden, attended, gain(l, 1), w_out, w_up, w_down, moves
+        )
         if coming is not None:
             coming[2:] = got
         saved.append((hidden, normed, query, pairs, extra, attended, middle, normed_feed, both, inner))
@@ -1587,44 +1635,50 @@
             )
             took(got, reduces)
             ups.append(Reduce(grid, total))
-        grad_heads = mm(grad_low, w_out, (1, 1)).astype(BF)
 
         reduces = [(ups[-1], "flip"), (down, "ring")]
         if not last_layer:
             reduces += [(ups[0], "flip"), (above[0], "ring")]
-        outs, got = attend_back(grid, valid, tables, query, grad_heads, pairs, extra, moves_of(reduces))
-        took(got, reduces)
-        grad_query, own, others = outs[:3]
         memory_grad = None
-        moves = []
-        if extra is not None:
-            joined = half(outs[3], grid.c).astype(F32) + outs[4].astype(F32)
+        if extra is None:
+            outs, got = attend_back(grid, valid, tables, query, grad_low, w_out, pairs, moves_of(reduces))
+            took(got, reduces)
+        else:
+            grad_heads = mm(grad_low, w_out, (1, 1)).astype(BF)
+            moves = moves_of(reduces)
+            if last_layer:
+                moves.append(regroup_back_move(grid, out_rows[1]))
+            outs, got = memory_back(grid, grad_heads, attended, extra, moves)
+            took(got, reduces)
+            if last_layer:
+                layer_output.append(got[-1])
+            joined = half(outs[1], grid.c).astype(F32) + outs[2].astype(F32)
             joined = joined.astype(BF).reshape(2, n_dp, topk, -1)
-            moves = [slots_move(grid, joined, True)]
-        total, got = product(grid, attended, attended_other, grad_low, moves)
-        across = Reduce(grid, total)
-        if extra is not None:
+            outs, got = attend_back(
+                grid, valid, tables, query, grad_heads, w_out, pairs, [slots_move(grid, joined, True)],
+                [attended, extra["logsum"], outs[0]],
+            )
             total = joined[:, 0].astype(F32) + sum(got[0][t].astype(F32) for t in range(n_dp - 1))
             for t in range(1, grid.Q):
                 total = total + grid.within(total.astype(BF), t).astype(F32)
             total = total.astype(BF)
             memory_grad = both_halves(total, grid.swap(total))
-        reduces = [(ups[-1], "flip"), (across, "flip")]
+        grad_query, own, others = outs[:3]
+        total, got = product(grid, attended, attended_other, grad_low)
+        across = Reduce(grid, total)
+        reduces = [(ups[-1], "flip")]
         if not last_layer:
-            reduces.append((ups[0], "ring"))
-        moves = moves_of(reduces)
-        if last_layer:
-            moves.append(regroup_back_move(grid, out_rows[1]))
-        grad_projected, got = finish_gradient(grid, grad_query, own, others, picks, memory_grad, moves)
+            reduces += [(across, "flip"), (ups[0], "ring")]
+        grad_projected, got = finish_gradient(
+            grid, grad_query, own, others, picks, memory_grad, moves_of(reduces)
+        )
         took(got, reduces)
-        if last_layer:
-            layer_output.append(got[-1])
         pulled, gain_attention = norm_back(
             hidden.astype(F32), gain(l, 0), mm(grad_projected, w_qkv, (1, 1))
         )
         grad = grad + pulled
         grad_gains[l] = [gain_attention[0], gain_feed[0]]
-        reduces, moves = [], []
+        reduces, moves = [(across, "flip")], []
         if l == 0:
             small = GainSum(grid, jnp.stack([jnp.stack(pair) for pair in grad_gains]).reshape(-1, HEAD_DIM))
             reduces = [(ups[-1], "ring"), (across, "flip")]

time: 855 us -> 835 us (0.977)
  Pallas kernels: 727 us -> 711 us
  local copies, waits for them, and re-layouts: 45.5 us -> 57.5 us
  other arithmetic: 46.7 us -> 36 us
    unnamed x189 -> x227, local copies, waits for them, and re-layouts: 34.5 us -> 48.9 us
    pallas_call x25 -> x26, Pallas kernels: 552 us -> 540 us  [host(): pl.pallas_call(kernel, grid=(steps,), in_specs=list(in_specs) + [any_spec...]
    convert_element_type x18, other arithmetic: 16.1 us -> 6.03 us  [flipped(): self.parts = (kept.astype(F32) + got.astype(F32)).astype(BF)]
    dot_general x6 -> x3, matrix products: 21.7 us -> 16.5 us  [dot(): lax.dot_general(left, right, (((contract[0],), (contract[1],)), ((), ()))...]
  transfers between devices with their start and end apart: 11 -> 11, of which waited for: 1 -> 1; matrix products, arithmetic and copies ran while one was open for 3% -> 3% of each run, Pallas kernels for 31% -> 32%
where the time goes in v7:
time: 835 us; the launch traced here: 828 us
  Pallas kernels  711 us (85%)
  local copies, waits for them, and re-layouts  57.5 us (7%)
  other arithmetic  36 us (4%)
  matrix products  16.5 us (2%)
    pallas_call x26, Pallas kernels, host(): pl.pallas_call(kernel, grid=(steps,), in_specs=list(in_specs) + [any_spec...  540 us
    pallas_call x1, Pallas kernels, gather_all(): pl.pallas_call(functools.partial(gather_body, grid, layers, kinds), in_sp...  171 us
    unnamed x227, local copies, waits for them, and re-layouts  48.9 us
  transfers between devices with their start and end apart: 11, of which 1 were waited for; matrix products, arithmetic and copies ran while one was open for 3% of the time, Pallas kernels for 32%

profile of v7, /device:TPU:0, one launch (start us, length us, event | category | flops | bytes accessed | tf_op | source)
XLA Modules:
  0.0 827.9 jit_solution(5086921499188919630)
XLA Ops:
  6.8 171.5 %shard_map.153 = (bf16[2,256,1024]{2,1,0:T(8,128)(2,1)S(1)}, f32[4,2,4,8,128]{4,3,2,1,0:T(8,128)S(1)}, bf16[4,2,4,32,3072]{4,3,2,1,0:T(8,128)(2,1)}, bf16[4,2,4,...) custom-call(bf16[2,256,1024]{2,1,0:T(8,128)(2,1)S(1)} %copy-done.55,, ...), custom_call_target="tpu_custom_call" | custom-call | tf_op jit(solution)/shard_map/pallas_call | solution.py:412
  182.5 21.4 %shard_map.154 = (bf16[512,1024]{1,0:T(8,128)(2,1)S(1)}, bf16[512,1024]{1,0:T(8,128)(2,1)S(1)}, bf16[2,512,1024]{2,1,0:T(8,128)(2,1)S(1)}, bf16[1,2,512,1024]{3,...) custom-call(f32[1024,128]{1,0:T(8,128)S(1)} %get-tuple-element.132.refs_0_.refs_1_, ...), custom_call_target="tpu_custom_call", output_to_operand_aliasing={{4}: (7, {})} | custom-call | flops 3221225472 | bytes 6291456 | tf_op jit(solution)/shard_map/pallas_call | solution.py:694
  204.0 20.0 %shard_map.155 = (bf16[512,1024]{1,0:T(8,128)(2,1)S(1)}, f32[8,1,512]{2,1,0:T(1,128)}, bf16[4,2,4,32,5632]{4,3,2,1,0:T(8,128)(2,1)}) custom-call(s32[1]{0:T(128)} %bitcast.refs_0_, bf16[512,1024]{1,0:T(8,128)(2,1)S(1)} %get-tuple-element.139.refs_1_.refs_3_, ...), custom_call_target="tpu_custom_call", output_to_operand_aliasing={{2}: (4, {})} | custom-call | flops 1610612736 | bytes 8388608 | tf_op jit(solution)/shard_map/pallas_call | solution.py:694
  224.1 28.8 %shard_map.156 = (f32[512,1024]{1,0:T(8,128)S(1)}, f32[512,1024]{1,0:T(8,128)S(1)}, bf16[512,1024]{1,0:T(8,128)(2,1)S(1)}, bf16[2,512,2816]{2,1,0:T(8,128)(2,1)}...) custom-call(bf16[512,1024]{1,0:T(8,128)(2,1)S(1)} %bitcast.205, ...), custom_call_target="tpu_custom_call", output_to_operand_aliasing={{5}: (7, {}), {6}: (8, {})} | custom-call | flops 8858370048 | bytes 17301504 | tf_op jit(solution)/shard_map/pallas_call | solution.py:694
  259.5 21.1 %shard_map.157 = (bf16[512,1024]{1,0:T(8,128)(2,1)S(1)}, bf16[512,1024]{1,0:T(8,128)(2,1)S(1)}, bf16[3,512,1024]{2,1,0:T(8,128)(2,1)S(1)}, bf16[1,3,512,1024]{3,...) custom-call(f32[1024,128]{1,0:T(8,128)S(1)} %copy-done.14, ...), custom_call_target="tpu_custom_call", output_to_operand_aliasing={{5}: (7, {}), {6}: (8, {})} | custom-call | flops 3221225472 | bytes 6291456 | tf_op jit(solution)/shard_map/pallas_call | solution.py:694
  292.3 30.5 %shard_map.158 = bf16[2,8,128,1024]{3,2,1,0:T(8,128)(2,1)} custom-call(s32[8,128,1]{2,1,0:T(8,128)S(1)} %copy-done.34, bf16[3,512,1024]{2,1,0:T(8,128)(2,1)S(1)} %copy-done.2, bf16[3,512,1024]{2,1,0:T(8,128)(2,1)S(1)} %bitcast.211), custom_call_target="tpu_custom_call" | custom-call | tf_op jit(solution)/shard_map/pallas_call | solution.py:694
  322.8 26.0 %shard_map.159 = (bf16[512,1024]{1,0:T(8,128)(2,1)S(1)}, f32[8,1,512]{2,1,0:T(1,128)S(1)}, bf16[4,2,4,32,5632]{4,3,2,1,0:T(8,128)(2,1)}, bf16[2,256,1024]{2,1,0:T(8,128)(2,1)S(1)}) custom-call(s32[1]{0:T(128)} %bitcast.refs_0_, bf16[512,1024]{1,0:T(8,128)(2,1)S(1)} %copy-done.48, ...), custom_call_target="tpu_custom_call", output_to_operand_aliasing={{2}: (7, {})} | custom-call | flops 3758096384 | bytes 16777216 | tf_op jit(solution)/shard_map/pallas_call | solution.py:694
  348.8 20.2 %shard_map.160 = (f32[512,1024]{1,0:T(8,128)S(1)}, f32[512,1024]{1,0:T(8,128)S(1)}, bf16[512,1024]{1,0:T(8,128)(2,1)S(1)}, bf16[2,512,2816]{2,1,0:T(8,128)(2,1)}, bf16[512,2816]{1,0:T(8,128)(2,1)}) custom-call(f32[512,1024]{1,0:T(8,128)S(1)} %get-tuple-element.149.refs_2_.refs_0_, bf16[512,1024]{1,0:T(8,128)(2,1)S(1)} %get-tuple-element.159.refs_1_.refs_10_.refs_7_.refs_0_, ...), custom_call_target="tpu_custom_call" | custom-call | flops 8858370048 | bytes 17301504 | tf_op jit(solution)/shard_map/pallas_call | solution.py:694
  372.9 9.6 %shard_map.161 = bf16[2816,512]{1,0:T(8,128)(2,1)S(1)} custom-call(bf16[512,2816]{1,0:T(8,128)(2,1)S(1)} %copy-done.93, bf16[512,2816]{1,0:T(8,128)(2,1)S(1)} %copy-done.93, bf16[512,1024]{1,0:T(8,128)(2,1)S(1)} %bitcast.249), custom_call_target="tpu_custom_call" | custom-call | flops 2952790016 | bytes 2883584 | tf_op jit(solution)/shard_map/pallas_call | solution.py:694
  384.5 26.4 %shard_map.162 = (f32[512,1024]{1,0:T(8,128)}, bf16[512,1024]{1,0:T(8,128)(2,1)S(1)}, bf16[2,512,2816]{2,1,0:T(8,128)(2,1)}, f32[1,1024]{1,0:T(1,128)S(1)}, bf16...) custom-call(f32[512,1024]{1,0:T(8,128)} %bitcast_convert_fusion.refs, ...), custom_call_target="tpu_custom_call" | custom-call | flops 8858370048 | bytes 17301504 | tf_op jit(solution)/shard_map/pallas_call | solution.py:694
  411.9 11.7 %shard_map.163 = (bf16[1024,2816]{1,0:T(8,128)(2,1)S(1)}, bf16[1,704,512]{2,1,0:T(8,128)(2,1)S(1)}) custom-call(bf16[512,1024]{1,0:T(8,128)(2,1)S(1)} %get-tuple-element.166.refs_8_.refs_0_, bf16[512,1024]{1,0:T(8,128)(2,1)S(1)} %get-tuple-element.173.refs_1_, bf16[2,512,2816]{2,1,0:T(8,128)(2,1)} %get-tuple-element.174.refs_2_, ...), custom_call_target="tpu_custom_call" | custom-call | flops 5905580032 | bytes 5767168 | tf_op jit(solution)/shard_map/pallas_call | solution.py:694
  430.8 38.8 %shard_map.164 = (f32[512,1024]{1,0:T(8,128)S(1)}, bf16[2,1024,1024]{2,1,0:T(8,128)(2,1)}, bf16[2,1024,512]{2,1,0:T(8,128)(2,1)S(1)}, bf16[2,256,2816]{2,1,0:T(8...) custom-call(bf16[512,1024]{1,0:T(8,128)(2,1)S(1)} %copy-done.97, ...), custom_call_target="tpu_custom_call" | custom-call | flops 5368709120 | bytes 12582912 | tf_op jit(solution)/shard_map/pallas_call | solution.py:694
  474.6 32.0 %shard_map.165 = (bf16[512,1024]{1,0:T(8,128)(2,1)S(1)}, f32[2,512,1024]{2,1,0:T(8,128)}, bf16[1,2,512,1024]{3,2,1,0:T(8,128)(2,1)S(1)}, bf16[7,2,128,512]{3,2,1,0:T(8,128)(2,1)S(1)}) custom-call(s32[1]{0:T(128)} %bitcast.refs_0_, f32[1024,128]{1,0:T(8,128)S(1)} %copy-done.15, f32[1024,128]{1,0:T(8,128)S(1)} %copy-done.18, bf16[512,1024]{1,0:T(8,128)(2,1)S(1)} %copy-done.49, ...), custom_call_target="tpu_custom_call" | custom-call | flops 4026531840 | bytes 8388608 | tf_op jit(solution)/shard_map/pallas_call | solution.py:694
  516.5 21.6 %shard_map.166 = (bf16[512,3072]{1,0:T(8,128)(2,1)}, bf16[1,256,2816]{2,1,0:T(8,128)(2,1)S(1)}) custom-call(bf16[512,1024]{1,0:T(8,128)(2,1)S(1)} %copy-done.54, f32[2,512,1024]{2,1,0:T(8,128)} %get-tuple-element.185.refs_1_, bf16[1,2,512,1024]{3,2,1,0:T(8,128)(2,1)S(1)} %get-tuple-element.186.refs_2_, s32[8,1,128]{2,1,0:T(1,128)S(1)} %bitcast.255, ...), custom_call_target="tpu_custom_call" | custom-call | flops 1048576 | bytes 8388608 | tf_op jit(solution)/shard_map/pallas_call | solution.py:694
  561.4 22.8 %shard_map.169 = (bf16[2816,512]{1,0:T(8,128)(2,1)S(1)}, bf16[2,256,1536]{2,1,0:T(8,128)(2,1)S(1)}, bf16[1,2,32,2816]{3,2,1,0:T(8,128)(2,1)S(1)}) custom-call(bf16[512,2816]{1,0:T(8,128)(2,1)S(1)} %copy-done.5, bf16[512,2816]{1,0:T(8,128)(2,1)} %get-tuple-element.192.refs_1_, bf16[512,1024]{1,0:T(8,128)(2,1)S(1)} %get-tuple-element.251.refs_2_, ...), custom_call_target="tpu_custom_call" | custom-call | flops 2952790016 | bytes 2883584 | tf_op jit(solution)/shard_map/pallas_call | solution.py:694
  588.5 34.4 %shard_map.170 = (f32[512,1024]{1,0:T(8,128)}, bf16[512,1024]{1,0:T(8,128)(2,1)S(1)}, bf16[2,512,2816]{2,1,0:T(8,128)(2,1)}, f32[1,1024]{1,0:T(1,128)S(1)}, bf16...) custom-call(f32[512,1024]{1,0:T(8,128)} %get-tuple-element.252.refs_, ...), custom_call_target="tpu_custom_call" | custom-call | flops 8858370048 | bytes 17301504 | tf_op jit(solution)/shard_map/pallas_call | solution.py:694
  626.6 12.1 %shard_map.171 = (bf16[1024,1408]{1,0:T(8,128)(2,1)S(1)}, bf16[1,704,512]{2,1,0:T(8,128)(2,1)S(1)}, bf16[1,2,32,1536]{3,2,1,0:T(8,128)(2,1)S(1)}) custom-call(bf16[512,1024]{1,0:T(8,128)(2,1)S(1)} %copy-done.20, bf16[512,1024]{1,0:T(8,128)(2,1)S(1)} %get-tuple-element.203.refs_1_, bf16[2,512,2816]{2,1,0:T(8,128)(2,1)} %get-tuple-element.204.refs_2_, ...), custom_call_target="tpu_custom_call" | custom-call | flops 2952790016 | bytes 2883584 | tf_op jit(solution)/shard_map/pallas_call | solution.py:694
  642.2 20.2 %shard_map.172 = (bf16[1024,1408]{1,0:T(8,128)(2,1)S(1)}, bf16[2,256,1408]{2,1,0:T(8,128)(2,1)S(1)}, bf16[2,2,32,1536]{3,2,1,0:T(8,128)(2,1)S(1)}) custom-call(bf16[512,1024]{1,0:T(8,128)(2,1)S(1)} %copy-done.20, bf16[512,1024]{1,0:T(8,128)(2,1)S(1)} %copy-done.61, bf16[2,512,2816]{2,1,0:T(8,128)(2,1)} %get-tuple-element.204.refs_2_, ...), custom_call_target="tpu_custom_call" | custom-call | flops 2952790016 | bytes 2883584 | tf_op jit(solution)/shard_map/pallas_call | solution.py:694
  665.6 29.6 %shard_map.173 = (bf16[512,1024]{1,0:T(8,128)(2,1)S(1)}, f32[2,512,1024]{2,1,0:T(8,128)}, bf16[1,2,512,1024]{3,2,1,0:T(8,128)(2,1)}, bf16[2,256,1408]{2,1,0:T(8,...) custom-call(s32[1]{0:T(128)} %bitcast.refs_0_, ...), custom_call_target="tpu_custom_call" | custom-call | flops 4026531840 | bytes 8388608 | tf_op jit(solution)/shard_map/pallas_call | solution.py:694
  701.3 20.1 %shard_map.175 = (bf16[512,3072]{1,0:T(8,128)(2,1)}, bf16[1,256,1408]{2,1,0:T(8,128)(2,1)S(1)}, bf16[2,256,512]{2,1,0:T(8,128)(2,1)S(1)}, bf16[3,2,32,1408]{3,2,1,0:T(8,128)(2,1)S(1)}) custom-call(bf16[512,1024]{1,0:T(8,128)(2,1)S(1)} %get-tuple-element.212.refs_0_, f32[2,512,1024]{2,1,0:T(8,128)} %get-tuple-element.213.refs_1_, ...), custom_call_target="tpu_custom_call" | custom-call | flops 1048576 | bytes 8388608 | tf_op jit(solution)/shard_map/pallas_call | solution.py:694
  731.7 17.6 %shard_map.176 = (bf16[1024,1536]{1,0:T(8,128)(2,1)S(1)}, bf16[3,2,32,1408]{3,2,1,0:T(8,128)(2,1)S(1)}, bf16[1,256,512]{2,1,0:T(8,128)(2,1)S(1)}, f32[32,128]{1,0:T(8,128)S(1)}) custom-call(bf16[512,1024]{1,0:T(8,128)(2,1)S(1)} %copy-done.41, bf16[512,1024]{1,0:T(8,128)(2,1)S(1)} %copy-done.95, bf16[512,3072]{1,0:T(8,128)(2,1)} %get-tuple-element.218.refs_2_, ...), custom_call_target="tpu_custom_call" | custom-call | flops 3221225472 | bytes 3145728 | tf_op jit(solution)/shard_map/pallas_call | solution.py:694
  750.5 24.9 %shard_map.177 = (bf16[2,256,1536]{2,1,0:T(8,128)(2,1)S(1)}, bf16[3,2,32,512]{3,2,1,0:T(8,128)(2,1)S(1)}, bf16[2,128,1024]{2,1,0:T(8,128)(2,1)S(1)}, f32[32,128]{1,0:T(8,128)S(1)}) custom-call(bf16[4,256,1536]{2,1,0:T(8,128)(2,1)S(1)} %bitcast.213, bf16[2,4,32,512]{3,2,1,0:T(8,128)(2,1)S(1)} %bitcast.241, ...), custom_call_target="tpu_custom_call" | custom-call | tf_op jit(solution)/shard_map/pallas_call | solution.py:694
  776.3 12.7 %shard_map.178 = (bf16[1,256,1536]{2,1,0:T(8,128)(2,1)S(1)}, bf16[2,128,1024]{2,1,0:T(8,128)(2,1)S(1)}, f32[32,128]{1,0:T(8,128)S(1)}) custom-call(bf16[2,256,1536]{2,1,0:T(8,128)(2,1)S(1)} %add_convert_fusion.2.refs_0_, bf16[2,128,1024]{2,1,0:T(8,128)(2,1)S(1)} %get-tuple-element.269.refs_1_, f32[32,128]{1,0:T(8,128)S(1)} %add.434.refs_2_), custom_call_target="tpu_custom_call" | custom-call | tf_op jit(solution)/shard_map/pallas_call | solution.py:694
  789.7 20.8 %shard_map.179 = (bf16[3,2,32,1536]{3,2,1,0:T(8,128)(2,1)S(1)}, f32[3,32,128]{2,1,0:T(8,128)S(1)}) custom-call(bf16[2,4,32,1536]{3,2,1,0:T(8,128)(2,1)S(1)} %bitcast.227, f32[32,128]{1,0:T(8,128)S(1)} %add.437.refs_1_), custom_call_target="tpu_custom_call" | custom-call | tf_op jit(solution)/shard_map/pallas_call | solution.py:694
  (380 shorter events, 130.4 us)
Async XLA Ops:
  0.6 285.7 %collective-permute-start = (s32[2,1,8,128]{3,2,1,0:T(8,128)}, s32[2,1,8,128]{3,2,1,0:T(8,128)S(1)}, u32[]{:S(2)}, u32[]{:S(2)}) collective-permute-start(s32[2,1,8,128]{3,2,1,0:T(8,128)} %param.16), channel_id=1, source_target_pairs={{0,4},{1,5},{2,6},{3,7},{4,0},{5,1},{6,2},{7,3},{8,12},{9,13},{10,... | collective-permute-start | bytes 24584 | tf_op jit(solution)/shard_map/ppermute | solution.py:70
  6.6 197.3 %copy-start.13 = (f32[1024,128]{1,0:T(8,128)}, f32[1024,128]{1,0:T(8,128)S(1)}, u32[]{:S(2)}) copy-start(f32[1024,128]{1,0:T(8,128)S(1)} %get-tuple-element.132.refs_0_.refs_1_) | copy-start | bytes 1572868
  6.7 197.3 %copy-start.16 = (f32[1024,128]{1,0:T(8,128)}, f32[1024,128]{1,0:T(8,128)S(1)}, u32[]{:S(2)}) copy-start(f32[1024,128]{1,0:T(8,128)S(1)} %get-tuple-element.133.refs_1_.refs_2_) | copy-start | bytes 1572868
  6.7 175.0 %copy-start.110 = (s32[2,8]{1,0:T(2,128)S(1)}, s32[2,8]{1,0:T(2,128)}, u32[]{:S(2)}) copy-start(s32[2,8]{1,0:T(2,128)} %param.15) | copy-start | bytes 196
  224.1 28.8 %copy-start.6 = (bf16[512,1024]{1,0:T(8,128)(2,1)}, bf16[512,1024]{1,0:T(8,128)(2,1)S(1)}, u32[]{:S(2)}) copy-start(bf16[512,1024]{1,0:T(8,128)(2,1)S(1)} %get-tuple-element.143.refs_1_.refs_13_.refs_0_) | copy-start | bytes 3145732
  259.5 26.9 %copy-start.108 = (s32[2,1,8,128]{3,2,1,0:T(8,128)S(1)}, s32[2,1,8,128]{3,2,1,0:T(8,128)}, u32[]{:S(2)}) copy-start(s32[2,1,8,128]{3,2,1,0:T(8,128)} %param.16) | copy-start | bytes 24580
  292.2 30.5 %copy-start.3 = (bf16[3,512,1024]{2,1,0:T(8,128)(2,1)S(1)}, bf16[3,512,1024]{2,1,0:T(8,128)(2,1)}, u32[]{:S(2)}) copy-start(bf16[3,512,1024]{2,1,0:T(8,128)(2,1)} %copy-done.1) | copy-start | bytes 9437188
  292.2 30.5 %copy-start.32 = (f32[1024,1]{1,0:T(8,128)S(1)}, f32[1024,1]{1,0:T(8,128)}, u32[]{:S(2)}) copy-start(f32[1024,1]{1,0:T(8,128)} %copy.36.refs_6_.refs_5_) | copy-start | bytes 12292
  292.2 30.5 %copy-start.38 = (bf16[2,256,1024]{2,1,0:T(8,128)(2,1)S(1)}, bf16[2,256,1024]{2,1,0:T(8,128)(2,1)}, u32[]{:S(2)}) copy-start(bf16[2,256,1024]{2,1,0:T(8,128)(2,1)} %refs_8_.1) | copy-start | bytes 3145732
  292.2 30.5 %copy-start.48 = (bf16[512,1024]{1,0:T(8,128)(2,1)S(1)}, bf16[512,1024]{1,0:T(8,128)(2,1)}, u32[]{:S(2)}) copy-start(bf16[512,1024]{1,0:T(8,128)(2,1)} %copy-done.47) | copy-start | bytes 3145732
  292.2 30.5 %copy-start.51 = (bf16[512,1024]{1,0:T(8,128)(2,1)S(1)}, bf16[512,1024]{1,0:T(8,128)(2,1)}, u32[]{:S(2)}) copy-start(bf16[512,1024]{1,0:T(8,128)(2,1)} %copy-done.50) | copy-start | bytes 3145732
  508.2 8.1 collective-permute-start.1
  512.0 3.5 collective-permute-start.10
  588.5 35.5 %copy-start.98 = (bf16[2,256,1536]{2,1,0:T(8,128)(2,1)S(1)}, bf16[2,256,1536]{2,1,0:T(8,128)(2,1)}, u32[]{:S(2)}) copy-start(bf16[2,256,1536]{2,1,0:T(8,128)(2,1)} %add_convert_fusion.3.refs_9_) | copy-start | bytes 4718596
  695.2 26.3 %slice-start = ((s8[6291456]{0:T(1024)(128)(4,1)}), s8[2097152]{0:T(1024)(128)(4,1)S(1)}, s32[]{:S(2)}) async-start(s8[6291456]{0:T(1024)(128)(4,1)} %bitcast.273), calls=%async_computation | async-start | bytes 4194304
  789.0 22.9 %copy-start.69 = (bf16[3,2,32,1408]{3,2,1,0:T(8,128)(2,1)S(1)}, bf16[3,2,32,1408]{3,2,1,0:T(8,128)(2,1)}, u32[]{:S(2)}) copy-start(bf16[3,2,32,1408]{3,2,1,0:T(8,128)(2,1)} %copy-done.68) | copy-start | bytes 1622020
  811.8 11.6 %collective-permute-start.9 = (bf16[88,512]{1,0:T(8,128)(2,1)S(1)}, bf16[88,512]{1,0:T(8,128)(2,1)S(1)}, u32[]{:S(2)}, u32[]{:S(2)}) collective-permute-start(bf16[88,512]{1,0:T(8,128)(2,1)S(1)} %fusion.7), channel_id=1, source_target_pairs={{0,4},{1,5},{2,6},{3,7},{4,0},{5,1},{6,2},{7,3},{8,12},{9,13},{10,... | collective-permute-start | bytes 270344 | tf_op jit(solution)/shard_map/ppermute | solution.py:70
  812.9 10.7 %collective-permute-start.6 = (bf16[32,1408]{1,0:T(8,128)(2,1)S(1)}, bf16[32,1408]{1,0:T(8,128)(2,1)S(1)}, u32[]{:S(2)}, u32[]{:S(2)}) collective-permute-start(bf16[32,1408]{1,0:T(8,128)(2,1)S(1)} %fusion.5), channel_id=1, source_target_pairs={{0,4},{1,5},{2,6},{3,7},{4,0},{5,1},{6,2},{7,3},{8,12},{9,13},{10,... | collective-permute-start | bytes 270344 | tf_op jit(solution)/shard_map/ppermute | solution.py:70
  814.6 9.1 %collective-permute-start.7 = (bf16[32,1408]{1,0:T(8,128)(2,1)S(1)}, bf16[32,1408]{1,0:T(8,128)(2,1)S(1)}, u32[]{:S(2)}, u32[]{:S(2)}) collective-permute-start(bf16[32,1408]{1,0:T(8,128)(2,1)S(1)} %fusion.6), channel_id=1, source_target_pairs={{0,4},{1,5},{2,6},{3,7},{4,0},{5,1},{6,2},{7,3},{8,12},{9,13},{10,... | collective-permute-start | bytes 270344 | tf_op jit(solution)/shard_map/ppermute | solution.py:70
  816.0 10.4 %collective-permute-start.8 = (bf16[32,2816]{1,0:T(8,128)(2,1)S(1)}, bf16[32,2816]{1,0:T(8,128)(2,1)S(1)}, u32[]{:S(2)}, u32[]{:S(2)}) collective-permute-start(bf16[32,2816]{1,0:T(8,128)(2,1)S(1)} %fusion.1), channel_id=1, source_target_pairs={{0,4},{1,5},{2,6},{3,7},{4,0},{5,1},{6,2},{7,3},{8,12},{9,13},{10,... | collective-permute-start | bytes 540680 | tf_op jit(solution)/shard_map/ppermute | solution.py:70
  816.6 4.4 collective-permute-start.4
  820.9 1.3 collective-permute-start.5
  822.3 3.0 collective-permute-start.2
  823.4 2.0 collective-permute-start.3
  (100 other events, 479.6 us)

commit v8 on v7

--- a/solution.py
+++ b/solution.py
@@ -1461,22 +1461,97 @@
     def arrived(self, got):
         grid = self.grid
         self.came.append(got)
-        if sum(part.shape[0] for part in self.came) < grid.F - 1:
-            return
+
+    def done(self):
+        grid = self.grid
         here = lax.dynamic_index_in_dim(self.line, grid.f, 1, keepdims=False)
-        self.summed = here.astype(F32) + sum(
+        summed = here.astype(F32) + sum(
             part[i].astype(F32) for part in self.came for i in range(part.shape[0])
         )
-        give = lax.dynamic_index_in_dim(self.summed, 1 - grid.c, 0, keepdims=False)
-        self.give = give.astype(BF)
-
-    def done(self, got):
-        grid = self.grid
-        mine = lax.dynamic_index_in_dim(self.summed, grid.c, 0, keepdims=False)
-        got = got.astype(F32)
+        mine = lax.dynamic_index_in_dim(summed, grid.c, 0, keepdims=False)
+        give = lax.dynamic_index_in_dim(summed, 1 - grid.c, 0, keepdims=False)
+        got = grid.swap(give.astype(BF)).astype(F32)
         return jnp.concatenate(
             [jnp.where(grid.c == 0, mine, got), jnp.where(grid.c == 0, got, mine)], axis=1
         )
+
+
+def settle(grid, wanted, row_halves, moves):
+    flat, ins, specs, scratch, out_shape = [], [], [], [], []
+    for o, by_layer in enumerate(wanted):
+        for layer, parts in enumerate(by_layer):
+            for piece, reduce in enumerate(parts):
+                flat.append((o, layer, piece, len(parts), reduce))
+        rows, size = wanted[o][0][0].line.shape[2:]
+        out_shape.append(kind(len(by_layer), rows, 2 * size * len(by_layer[0]), dtype=F32))
+    for _, _, _, _, reduce in flat:
+        _, F, rows, size = reduce.line.shape
+        ins += [reduce.line, *reduce.came]
+        scratch += [
+            pltpu.VMEM((F, 2, rows, size), BF),
+            pltpu.VMEM((2, rows, size), F32),
+            pltpu.VMEM((rows, size), BF),
+            pltpu.VMEM((rows, size), BF),
+        ]
+    count = len(flat)
+    ins += row_halves
+    high, width = row_halves[0].shape[1:]
+    scratch += [pltpu.VMEM((2, 2, high, width), BF)]
+    scratch += [pltpu.SemaphoreType.DMA((len(ins),)), pltpu.SemaphoreType.DMA((2, count))]
+    out_shape.append(kind(2, 2 * high, width, dtype=F32))
+
+    def body(here, step, refs, outs, held):
+        rows_held, load_sems, sems = held[4 * count :]
+        loads, swaps, at = [], [], 0
+        for i, (_, _, _, _, reduce) in enumerate(flat):
+            blocks, _, give, got = held[4 * i : 4 * i + 4]
+            mine = [pltpu.make_async_copy(refs[at].at[:, here.f], blocks.at[0], load_sems.at[at])]
+            at, filled = at + 1, 1
+            for part in reduce.came:
+                size = part.shape[0]
+                mine.append(
+                    pltpu.make_async_copy(refs[at], blocks.at[pl.ds(filled, size)], load_sems.at[at])
+                )
+                at, filled = at + 1, filled + size
+            loads.append(mine)
+            swaps.append(remote(give, got, sems, i, here.swap))
+        loads.append(
+            [pltpu.make_async_copy(refs[at + i], rows_held.at[i], load_sems.at[at + i]) for i in range(2)]
+        )
+        for mine in loads:
+            for copy in mine:
+                copy.start()
+        for i in range(count):
+            blocks, summed, give, _ = held[4 * i : 4 * i + 4]
+            for copy in loads[i]:
+                copy.wait()
+            total = blocks[0].astype(F32)
+            for t in range(1, blocks.shape[0]):
+                total = total + blocks[t].astype(F32)
+            summed[...] = total
+            give[...] = summed[1 - here.c].astype(BF)
+            swaps[i].start()
+        for copy in loads[count]:
+            copy.wait()
+        for i in range(2):
+            outs[-1][:, i * high : (i + 1) * high, :] = rows_held[i].astype(F32)
+        for i, (o, layer, piece, pieces, _) in enumerate(flat):
+            _, summed, _, got = held[4 * i : 4 * i + 4]
+            swaps[i].wait()
+            size = got.shape[1]
+
+            def columns(c):
+                return pl.ds(pl.multiple_of((c * pieces + piece) * size, 128), size)
+
+            outs[o][layer, :, columns(here.c)] = summed[here.c]
+            outs[o][layer, :, columns(1 - here.c)] = got[...].astype(F32)
+
+    return host(
+        grid, body, 1, [any_spec()] * len(ins), ins,
+        [whole_spec(*o.shape) for o in out_shape], out_shape, moves,
+        scratch=scratch,
+        reaches=lambda here: [here.swap],
+    )
 
 
 def local(
@@ -1688,42 +1763,35 @@
         if l == 0:
             small.took(got[-1])
         last = Reduce(grid, total)
-        found[l][3] = down.done(grid.swap(down.give))
-        if not last_layer:
-            found[l + 1] = [r.done(grid.swap(r.give)) for r in (above[1], above[0])] + [
-                feed_parts([r.done(grid.swap(r.give)) for r in above[2]]), found[l + 1][3]
-            ]
+        found[l] = [[last], [across], ups, [down]]
         above = (across, last, ups)
     across, last, ups = above
     in_rows = row_halves(grad)
     input_grad = []
-    for i, reduces in enumerate([[(last, "flip"), (across, "ring")], [(last, "flip")], [(last, "ring")]]):
-        moves = moves_of(reduces)
-        if i < 2:
-            moves.append(regroup_back_move(grid, in_rows[i]))
-        got = send(grid, moves + [small.move()])
+    for i, reduces in enumerate([[(last, "flip"), (across, "ring")], [(last, "flip")]]):
+        got = send(grid, moves_of(reduces) + [regroup_back_move(grid, in_rows[i]), small.move()])
         took(got, reduces)
         small.took(got[-1])
-        if i < 2:
-            input_grad.append(got[-2])
+        input_grad.append(got[-2])
+    wanted = [[found[l][0] for l in range(1, layers)]]
+    wanted += [[found[l][i] for l in range(layers)] for i in range(1, 4)]
+    outs, got = settle(grid, wanted, input_grad, [last.ring(), small.move()])
+    last.arrived(got[0])
+    small.took(got[1])
+    grad_in, grad_out, grad_up, grad_down, input_grad = outs
+    grad_in = jnp.concatenate([last.done()[None], grad_in])
     layer_output = jnp.concatenate(layer_output, axis=1)
-    input_grad = jnp.concatenate(input_grad, axis=1).astype(F32)
-    found[0] = [r.done(grid.swap(r.give)) for r in (last, across)] + [
-        feed_parts([r.done(grid.swap(r.give)) for r in ups]), found[0][3]
-    ]
     total_gains = small.finish().reshape(layers, 2, n_dp * pieces, -1)
     device = (grid.j * 2 + grid.c) * grid.F + grid.f
     return (
         layer_output,
         input_grad,
-        *(jnp.stack([found[l][i] for l in range(layers)]) for i in range(4)),
+        grad_in,
+        grad_out,
+        grad_up,
+        grad_down,
         lax.dynamic_index_in_dim(total_gains, device, 2, keepdims=False),
     )
-
-
-def feed_parts(parts):
-    sides = [[part[:, : part.shape[1] // 2] for part in parts], [part[:, part.shape[1] // 2 :] for part in parts]]
-    return jnp.concatenate(sides[0] + sides[1], axis=1)
 
 
 def solution(mesh):

time: 835 us -> 824 us (0.987)
    unnamed x227 -> x213, local copies, waits for them, and re-layouts: 48.9 us -> 46 us
  transfers between devices with their start and end apart: 11 -> 3, of which waited for: 1 -> 1; matrix products, arithmetic and copies ran while one was open for 3% -> 2% of each run, Pallas kernels for 32% -> 33%
where the time goes in v8:
time: 824 us; the launch traced here: 817 us
  Pallas kernels  714 us (87%)
  local copies, waits for them, and re-layouts  54.1 us (7%)
  other arithmetic  29.8 us (4%)
  matrix products  15.7 us (2%)
    pallas_call x26, Pallas kernels, host(): pl.pallas_call(kernel, grid=(steps,), in_specs=list(in_specs) + [any_spec...  543 us
    pallas_call x1, Pallas kernels, gather_all(): pl.pallas_call(functools.partial(gather_body, grid, layers, kinds), in_sp...  171 us
    unnamed x213, local copies, waits for them, and re-layouts  46 us
  transfers between devices with their start and end apart: 3, of which 1 were waited for; matrix products, arithmetic and copies ran while one was open for 2% of the time, Pallas kernels for 33%

profile of v8, /device:TPU:0, one launch (start us, length us, event | category | flops | bytes accessed | tf_op | source)
XLA Modules:
  0.0 817.3 jit_solution(13022578498447991763)
XLA Ops:
  6.8 171.5 %shard_map.153 = (bf16[2,256,1024]{2,1,0:T(8,128)(2,1)S(1)}, f32[4,2,4,8,128]{4,3,2,1,0:T(8,128)S(1)}, bf16[4,2,4,32,3072]{4,3,2,1,0:T(8,128)(2,1)}, bf16[4,2,4,...) custom-call(bf16[2,256,1024]{2,1,0:T(8,128)(2,1)S(1)} %copy-done.55,, ...), custom_call_target="tpu_custom_call" | custom-call | tf_op jit(solution)/shard_map/pallas_call | solution.py:412
  182.7 21.4 %shard_map.154 = (bf16[512,1024]{1,0:T(8,128)(2,1)S(1)}, bf16[512,1024]{1,0:T(8,128)(2,1)S(1)}, bf16[2,512,1024]{2,1,0:T(8,128)(2,1)S(1)}, bf16[1,2,512,1024]{3,...) custom-call(f32[1024,128]{1,0:T(8,128)S(1)} %get-tuple-element.137.refs_0_.refs_1_, ...), custom_call_target="tpu_custom_call", output_to_operand_aliasing={{4}: (7, {})} | custom-call | flops 3221225472 | bytes 6291456 | tf_op jit(solution)/shard_map/pallas_call | solution.py:694
  204.2 20.0 %shard_map.155 = (bf16[512,1024]{1,0:T(8,128)(2,1)S(1)}, f32[8,1,512]{2,1,0:T(1,128)}, bf16[4,2,4,32,5632]{4,3,2,1,0:T(8,128)(2,1)}) custom-call(s32[1]{0:T(128)} %bitcast.refs_0_, bf16[512,1024]{1,0:T(8,128)(2,1)S(1)} %get-tuple-element.144.refs_1_.refs_3_, ...), custom_call_target="tpu_custom_call", output_to_operand_aliasing={{2}: (4, {})} | custom-call | flops 1610612736 | bytes 8388608 | tf_op jit(solution)/shard_map/pallas_call | solution.py:694
  224.3 28.7 %shard_map.156 = (f32[512,1024]{1,0:T(8,128)S(1)}, f32[512,1024]{1,0:T(8,128)S(1)}, bf16[512,1024]{1,0:T(8,128)(2,1)S(1)}, bf16[2,512,2816]{2,1,0:T(8,128)(2,1)}...) custom-call(bf16[512,1024]{1,0:T(8,128)(2,1)S(1)} %bitcast.104, ...), custom_call_target="tpu_custom_call", output_to_operand_aliasing={{5}: (7, {}), {6}: (8, {})} | custom-call | flops 8858370048 | bytes 17301504 | tf_op jit(solution)/shard_map/pallas_call | solution.py:694
  257.7 21.2 %shard_map.157 = (bf16[512,1024]{1,0:T(8,128)(2,1)S(1)}, bf16[512,1024]{1,0:T(8,128)(2,1)S(1)}, bf16[3,512,1024]{2,1,0:T(8,128)(2,1)S(1)}, bf16[1,3,512,1024]{3,...) custom-call(f32[1024,128]{1,0:T(8,128)S(1)} %copy-done.17, ...), custom_call_target="tpu_custom_call", output_to_operand_aliasing={{5}: (7, {}), {6}: (8, {})} | custom-call | flops 3221225472 | bytes 6291456 | tf_op jit(solution)/shard_map/pallas_call | solution.py:694
  290.5 30.5 %shard_map.158 = bf16[2,8,128,1024]{3,2,1,0:T(8,128)(2,1)} custom-call(s32[8,128,1]{2,1,0:T(8,128)S(1)} %copy-done.38, bf16[3,512,1024]{2,1,0:T(8,128)(2,1)S(1)} %copy-done.4, bf16[3,512,1024]{2,1,0:T(8,128)(2,1)S(1)} %bitcast.107), custom_call_target="tpu_custom_call" | custom-call | tf_op jit(solution)/shard_map/pallas_call | solution.py:694
  321.1 25.9 %shard_map.159 = (bf16[512,1024]{1,0:T(8,128)(2,1)S(1)}, f32[8,1,512]{2,1,0:T(1,128)S(1)}, bf16[4,2,4,32,5632]{4,3,2,1,0:T(8,128)(2,1)}, bf16[2,256,1024]{2,1,0:T(8,128)(2,1)S(1)}) custom-call(s32[1]{0:T(128)} %bitcast.refs_0_, bf16[512,1024]{1,0:T(8,128)(2,1)S(1)} %copy-done.50, ...), custom_call_target="tpu_custom_call", output_to_operand_aliasing={{2}: (7, {})} | custom-call | flops 3758096384 | bytes 16777216 | tf_op jit(solution)/shard_map/pallas_call | solution.py:694
  347.0 20.1 %shard_map.160 = (f32[512,1024]{1,0:T(8,128)S(1)}, f32[512,1024]{1,0:T(8,128)S(1)}, bf16[512,1024]{1,0:T(8,128)(2,1)S(1)}, bf16[2,512,2816]{2,1,0:T(8,128)(2,1)}, bf16[512,2816]{1,0:T(8,128)(2,1)}) custom-call(f32[512,1024]{1,0:T(8,128)S(1)} %get-tuple-element.154.refs_2_.refs_0_, bf16[512,1024]{1,0:T(8,128)(2,1)S(1)} %get-tuple-element.164.refs_1_.refs_10_.refs_7_.refs_0_, ...), custom_call_target="tpu_custom_call" | custom-call | flops 8858370048 | bytes 17301504 | tf_op jit(solution)/shard_map/pallas_call | solution.py:694
  371.0 9.7 %shard_map.161 = bf16[2816,512]{1,0:T(8,128)(2,1)S(1)} custom-call(bf16[512,2816]{1,0:T(8,128)(2,1)S(1)} %copy-done.83, bf16[512,2816]{1,0:T(8,128)(2,1)S(1)} %copy-done.83, bf16[512,1024]{1,0:T(8,128)(2,1)S(1)} %bitcast.145), custom_call_target="tpu_custom_call" | custom-call | flops 2952790016 | bytes 2883584 | tf_op jit(solution)/shard_map/pallas_call | solution.py:694
  382.8 26.3 %shard_map.162 = (f32[512,1024]{1,0:T(8,128)}, bf16[512,1024]{1,0:T(8,128)(2,1)S(1)}, bf16[2,512,2816]{2,1,0:T(8,128)(2,1)}, f32[1,1024]{1,0:T(1,128)S(1)}, bf16...) custom-call(f32[512,1024]{1,0:T(8,128)} %bitcast_convert_fusion.refs, ...), custom_call_target="tpu_custom_call" | custom-call | flops 8858370048 | bytes 17301504 | tf_op jit(solution)/shard_map/pallas_call | solution.py:694
  410.4 11.7 %shard_map.163 = (bf16[1024,2816]{1,0:T(8,128)(2,1)S(1)}, bf16[1,704,512]{2,1,0:T(8,128)(2,1)S(1)}) custom-call(bf16[512,1024]{1,0:T(8,128)(2,1)S(1)} %get-tuple-element.171.refs_8_.refs_0_, bf16[512,1024]{1,0:T(8,128)(2,1)S(1)} %get-tuple-element.178.refs_1_, bf16[2,512,2816]{2,1,0:T(8,128)(2,1)} %get-tuple-element.179.refs_2_, ...), custom_call_target="tpu_custom_call" | custom-call | flops 5905580032 | bytes 5767168 | tf_op jit(solution)/shard_map/pallas_call | solution.py:694
  429.7 38.7 %shard_map.164 = (f32[512,1024]{1,0:T(8,128)S(1)}, bf16[2,1024,1024]{2,1,0:T(8,128)(2,1)}, bf16[2,1024,512]{2,1,0:T(8,128)(2,1)S(1)}, bf16[2,256,2816]{2,1,0:T(8...) custom-call(bf16[512,1024]{1,0:T(8,128)(2,1)S(1)} %convolution_convert_fusion.refs_0_.refs_4_, ...), custom_call_target="tpu_custom_call" | custom-call | flops 5368709120 | bytes 12582912 | tf_op jit(solution)/shard_map/pallas_call | solution.py:694
  473.6 32.2 %shard_map.165 = (bf16[512,1024]{1,0:T(8,128)(2,1)S(1)}, f32[2,512,1024]{2,1,0:T(8,128)}, bf16[1,2,512,1024]{3,2,1,0:T(8,128)(2,1)S(1)}, bf16[7,2,128,512]{3,2,1,0:T(8,128)(2,1)S(1)}) custom-call(s32[1]{0:T(128)} %bitcast.refs_0_, f32[1024,128]{1,0:T(8,128)S(1)} %copy-done.17, f32[1024,128]{1,0:T(8,128)S(1)} %copy-done.20, bf16[512,1024]{1,0:T(8,128)(2,1)S(1)} %copy-done.51, ...), custom_call_target="tpu_custom_call" | custom-call | flops 4026531840 | bytes 8388608 | tf_op jit(solution)/shard_map/pallas_call | solution.py:694
  514.2 21.8 %shard_map.166 = (bf16[512,3072]{1,0:T(8,128)(2,1)}, bf16[1,256,2816]{2,1,0:T(8,128)(2,1)S(1)}) custom-call(bf16[512,1024]{1,0:T(8,128)(2,1)S(1)} %get-tuple-element.188.refs_0_, f32[2,512,1024]{2,1,0:T(8,128)} %get-tuple-element.189.refs_1_, bf16[1,2,512,1024]{3,2,1,0:T(8,128)(2,1)S(1)} %get-tuple-element.190.refs_2_, s32[8,1,128]{2,1,0:T(1,128)S(1)} %bitcast.151, ...), custom_call_target="tpu_custom_call" | custom-call | flops 1048576 | bytes 8388608 | tf_op jit(solution)/shard_map/pallas_call | solution.py:694
  559.3 22.8 %shard_map.169 = (bf16[2816,512]{1,0:T(8,128)(2,1)S(1)}, bf16[2,256,1536]{2,1,0:T(8,128)(2,1)S(1)}, bf16[1,2,32,2816]{3,2,1,0:T(8,128)(2,1)S(1)}) custom-call(bf16[512,2816]{1,0:T(8,128)(2,1)S(1)} %copy-done.7, bf16[512,2816]{1,0:T(8,128)(2,1)} %get-tuple-element.196.refs_1_, bf16[512,1024]{1,0:T(8,128)(2,1)S(1)} %get-tuple-element.261.refs_2_, ...), custom_call_target="tpu_custom_call" | custom-call | flops 2952790016 | bytes 2883584 | tf_op jit(solution)/shard_map/pallas_call | solution.py:694
  585.7 34.4 %shard_map.170 = (f32[512,1024]{1,0:T(8,128)}, bf16[512,1024]{1,0:T(8,128)(2,1)S(1)}, bf16[2,512,2816]{2,1,0:T(8,128)(2,1)}, f32[1,1024]{1,0:T(1,128)S(1)}, bf16...) custom-call(f32[512,1024]{1,0:T(8,128)} %get-tuple-element.262.refs_, ...), custom_call_target="tpu_custom_call" | custom-call | flops 8858370048 | bytes 17301504 | tf_op jit(solution)/shard_map/pallas_call | solution.py:694
  623.4 12.1 %shard_map.171 = (bf16[1024,1408]{1,0:T(8,128)(2,1)S(1)}, bf16[1,704,512]{2,1,0:T(8,128)(2,1)S(1)}, bf16[1,2,32,1536]{3,2,1,0:T(8,128)(2,1)S(1)}) custom-call(bf16[512,1024]{1,0:T(8,128)(2,1)S(1)} %copy-done.23, bf16[512,1024]{1,0:T(8,128)(2,1)S(1)} %get-tuple-element.207.refs_1_, bf16[2,512,2816]{2,1,0:T(8,128)(2,1)} %get-tuple-element.208.refs_2_, ...), custom_call_target="tpu_custom_call" | custom-call | flops 2952790016 | bytes 2883584 | tf_op jit(solution)/shard_map/pallas_call | solution.py:694
  637.8 20.2 %shard_map.172 = (bf16[1024,1408]{1,0:T(8,128)(2,1)S(1)}, bf16[2,256,1408]{2,1,0:T(8,128)(2,1)S(1)}, bf16[2,2,32,1536]{3,2,1,0:T(8,128)(2,1)S(1)}) custom-call(bf16[512,1024]{1,0:T(8,128)(2,1)S(1)} %copy-done.23, bf16[512,1024]{1,0:T(8,128)(2,1)S(1)} %get-tuple-element.207.refs_1_, bf16[2,512,2816]{2,1,0:T(8,128)(2,1)} %get-tuple-element.208.refs_2_, ...), custom_call_target="tpu_custom_call" | custom-call | flops 2952790016 | bytes 2883584 | tf_op jit(solution)/shard_map/pallas_call | solution.py:694
  661.4 29.5 %shard_map.174 = (bf16[512,1024]{1,0:T(8,128)(2,1)S(1)}, f32[2,512,1024]{2,1,0:T(8,128)}, bf16[1,2,512,1024]{3,2,1,0:T(8,128)(2,1)}, bf16[2,256,1408]{2,1,0:T(8,...) custom-call(s32[1]{0:T(128)} %bitcast.refs_0_, ...), custom_call_target="tpu_custom_call" | custom-call | flops 4026531840 | bytes 8388608 | tf_op jit(solution)/shard_map/pallas_call | solution.py:694
  697.6 20.2 %shard_map.175 = (bf16[512,3072]{1,0:T(8,128)(2,1)}, bf16[1,256,1408]{2,1,0:T(8,128)(2,1)S(1)}, bf16[2,256,512]{2,1,0:T(8,128)(2,1)S(1)}, bf16[3,2,32,1408]{3,2,1,0:T(8,128)(2,1)S(1)}) custom-call(bf16[512,1024]{1,0:T(8,128)(2,1)S(1)} %get-tuple-element.219.refs_0_, f32[2,512,1024]{2,1,0:T(8,128)} %get-tuple-element.220.refs_1_, ...), custom_call_target="tpu_custom_call" | custom-call | flops 1048576 | bytes 8388608 | tf_op jit(solution)/shard_map/pallas_call | solution.py:694
  728.1 17.7 %shard_map.176 = (bf16[1024,1536]{1,0:T(8,128)(2,1)S(1)}, bf16[3,2,32,1408]{3,2,1,0:T(8,128)(2,1)S(1)}, bf16[1,256,512]{2,1,0:T(8,128)(2,1)S(1)}, f32[32,128]{1,0:T(8,128)S(1)}) custom-call(bf16[512,1024]{1,0:T(8,128)(2,1)S(1)} %copy-done.43, bf16[512,1024]{1,0:T(8,128)(2,1)S(1)} %copy-done.85, bf16[512,3072]{1,0:T(8,128)(2,1)} %get-tuple-element.226.refs_2_, ...), custom_call_target="tpu_custom_call" | custom-call | flops 3221225472 | bytes 3145728 | tf_op jit(solution)/shard_map/pallas_call | solution.py:694
  746.7 24.9 %shard_map.177 = (bf16[2,256,1536]{2,1,0:T(8,128)(2,1)S(1)}, bf16[3,2,32,512]{3,2,1,0:T(8,128)(2,1)S(1)}, bf16[2,128,1024]{2,1,0:T(8,128)(2,1)S(1)}, f32[32,128]{1,0:T(8,128)S(1)}) custom-call(bf16[4,256,1536]{2,1,0:T(8,128)(2,1)S(1)} %bitcast.112, bf16[2,4,32,512]{3,2,1,0:T(8,128)(2,1)S(1)} %bitcast.133, ...), custom_call_target="tpu_custom_call" | custom-call | tf_op jit(solution)/shard_map/pallas_call | solution.py:694
  772.1 12.8 %shard_map.178 = (bf16[1,256,1536]{2,1,0:T(8,128)(2,1)S(1)}, bf16[2,128,1024]{2,1,0:T(8,128)(2,1)S(1)}, f32[32,128]{1,0:T(8,128)S(1)}) custom-call(bf16[2,256,1536]{2,1,0:T(8,128)(2,1)S(1)} %add_convert_fusion.2.refs_0_, bf16[2,128,1024]{2,1,0:T(8,128)(2,1)S(1)} %get-tuple-element.279.refs_1_, f32[32,128]{1,0:T(8,128)S(1)} %add.298.refs_2_), custom_call_target="tpu_custom_call" | custom-call | tf_op jit(solution)/shard_map/pallas_call | solution.py:694
  786.0 23.4 %shard_map.179 = (f32[1,32,3072]{2,1,0:T(8,128)S(1)}, f32[2,32,1024]{2,1,0:T(8,128)S(1)}, f32[2,32,5632]{2,1,0:T(8,128)}, f32[2,88,1024]{2,1,0:T(8,128)S(1)}, f3...) custom-call(bf16[2,4,32,1536]{3,2,1,0:T(8,128)(2,1)} %bitcast.110, ...), custom_call_target="tpu_custom_call" | custom-call | tf_op jit(solution)/shard_map/pallas_call | solution.py:694
  (316 shorter events, 117.2 us)
Async XLA Ops:
  0.6 284.0 %collective-permute-start = (s32[2,1,8,128]{3,2,1,0:T(8,128)}, s32[2,1,8,128]{3,2,1,0:T(8,128)S(1)}, u32[]{:S(2)}, u32[]{:S(2)}) collective-permute-start(s32[2,1,8,128]{3,2,1,0:T(8,128)} %param.16), channel_id=1, source_target_pairs={{0,4},{1,5},{2,6},{3,7},{4,0},{5,1},{6,2},{7,3},{8,12},{9,13},{10,... | collective-permute-start | bytes 24584 | tf_op jit(solution)/shard_map/ppermute | solution.py:70
  6.6 197.5 %copy-start.16 = (f32[1024,128]{1,0:T(8,128)}, f32[1024,128]{1,0:T(8,128)S(1)}, u32[]{:S(2)}) copy-start(f32[1024,128]{1,0:T(8,128)S(1)} %get-tuple-element.137.refs_0_.refs_1_) | copy-start | bytes 1572868
  6.7 197.5 %copy-start.19 = (f32[1024,128]{1,0:T(8,128)}, f32[1024,128]{1,0:T(8,128)S(1)}, u32[]{:S(2)}) copy-start(f32[1024,128]{1,0:T(8,128)S(1)} %get-tuple-element.138.refs_1_.refs_2_) | copy-start | bytes 1572868
  6.7 175.2 %copy-start.99 = (s32[2,8]{1,0:T(2,128)S(1)}, s32[2,8]{1,0:T(2,128)}, u32[]{:S(2)}) copy-start(s32[2,8]{1,0:T(2,128)} %param.15) | copy-start | bytes 196
  180.9 43.4 %copy-start.1 = (bf16[2,256,1024]{2,1,0:T(8,128)(2,1)}, bf16[2,256,1024]{2,1,0:T(8,128)(2,1)S(1)}, u32[]{:S(2)}) copy-start(bf16[2,256,1024]{2,1,0:T(8,128)(2,1)S(1)} %get-tuple-element.140) | copy-start | bytes 3145732
  204.2 20.1 %copy-start.29 = (bf16[2,512,1024]{2,1,0:T(8,128)(2,1)}, bf16[2,512,1024]{2,1,0:T(8,128)(2,1)S(1)}, u32[]{:S(2)}) copy-start(bf16[2,512,1024]{2,1,0:T(8,128)(2,1)S(1)} %get-tuple-element.145.refs_2_.refs_5_) | copy-start | bytes 6291460
  204.2 20.1 %copy-start.28 = (bf16[4,2,4,32,1024]{4,3,2,1,0:T(8,128)(2,1)S(1)}, bf16[4,2,4,32,1024]{4,3,2,1,0:T(8,128)(2,1)}, u32[]{:S(2)}) copy-start(bf16[4,2,4,32,1024]{4,3,2,1,0:T(8,128)(2,1)} %copy-done.27) | copy-start | bytes 6291460
  224.3 28.8 %copy-start.8 = (bf16[512,1024]{1,0:T(8,128)(2,1)}, bf16[512,1024]{1,0:T(8,128)(2,1)S(1)}, u32[]{:S(2)}) copy-start(bf16[512,1024]{1,0:T(8,128)(2,1)S(1)} %get-tuple-element.148.refs_1_.refs_13_.refs_0_) | copy-start | bytes 3145732
  257.7 27.0 %copy-start.97 = (s32[2,1,8,128]{3,2,1,0:T(8,128)S(1)}, s32[2,1,8,128]{3,2,1,0:T(8,128)}, u32[]{:S(2)}) copy-start(s32[2,1,8,128]{3,2,1,0:T(8,128)} %param.16) | copy-start | bytes 24580
  290.5 30.5 %copy-start.5 = (bf16[3,512,1024]{2,1,0:T(8,128)(2,1)S(1)}, bf16[3,512,1024]{2,1,0:T(8,128)(2,1)}, u32[]{:S(2)}) copy-start(bf16[3,512,1024]{2,1,0:T(8,128)(2,1)} %copy-done.3) | copy-start | bytes 9437188
  290.5 30.5 %copy-start.36 = (f32[1024,1]{1,0:T(8,128)S(1)}, f32[1024,1]{1,0:T(8,128)}, u32[]{:S(2)}) copy-start(f32[1024,1]{1,0:T(8,128)} %copy.29.refs_6_.refs_5_) | copy-start | bytes 12292
  290.5 30.5 %copy-start.40 = (bf16[2,256,1024]{2,1,0:T(8,128)(2,1)S(1)}, bf16[2,256,1024]{2,1,0:T(8,128)(2,1)}, u32[]{:S(2)}) copy-start(bf16[2,256,1024]{2,1,0:T(8,128)(2,1)} %refs_8_.1) | copy-start | bytes 3145732
  290.5 30.5 %copy-start.50 = (bf16[512,1024]{1,0:T(8,128)(2,1)S(1)}, bf16[512,1024]{1,0:T(8,128)(2,1)}, u32[]{:S(2)}) copy-start(bf16[512,1024]{1,0:T(8,128)(2,1)} %copy-done.49) | copy-start | bytes 3145732
  290.5 30.5 %copy-start.53 = (bf16[512,1024]{1,0:T(8,128)(2,1)S(1)}, bf16[512,1024]{1,0:T(8,128)(2,1)}, u32[]{:S(2)}) copy-start(bf16[512,1024]{1,0:T(8,128)(2,1)} %copy-done.52) | copy-start | bytes 3145732
  507.1 7.0 collective-permute-start.1
  514.2 22.1 %copy-start.87 = (bf16[512,1024]{1,0:T(8,128)(2,1)S(1)}, bf16[512,1024]{1,0:T(8,128)(2,1)}, u32[]{:S(2)}) copy-start(bf16[512,1024]{1,0:T(8,128)(2,1)} %copy-done.86) | copy-start | bytes 3145732
  536.3 22.4 %copy-start = (bf16[1,256,2816]{2,1,0:T(8,128)(2,1)}, bf16[1,256,2816]{2,1,0:T(8,128)(2,1)S(1)}, u32[]{:S(2)}) copy-start(bf16[1,256,2816]{2,1,0:T(8,128)(2,1)S(1)} %add_convert_fusion.7) | copy-start | bytes 4325380
  585.6 35.3 %copy-start.89 = (bf16[2,256,1536]{2,1,0:T(8,128)(2,1)S(1)}, bf16[2,256,1536]{2,1,0:T(8,128)(2,1)}, u32[]{:S(2)}) copy-start(bf16[2,256,1536]{2,1,0:T(8,128)(2,1)} %add_convert_fusion.3.refs_9_) | copy-start | bytes 4718596
  637.8 20.2 %copy-start.15 = (bf16[1024,1408]{1,0:T(8,128)(2,1)S(1)}, bf16[1024,1408]{1,0:T(8,128)(2,1)}, u32[]{:S(2)}) copy-start(bf16[1024,1408]{1,0:T(8,128)(2,1)} %copy-done.14) | copy-start | bytes 8650756
  691.0 26.8 %slice-start.2 = ((s8[6291456]{0:T(1024)(128)(4,1)}), s8[2097152]{0:T(1024)(128)(4,1)S(1)}, s32[]{:S(2)}) async-start(s8[6291456]{0:T(1024)(128)(4,1)} %bitcast.169), calls=%async_computation.2 | async-start | bytes 4194304
  696.0 21.9 %slice-start.3 = ((s8[6291456]{0:T(1024)(128)(4,1)}), s8[4194304]{0:T(1024)(128)(4,1)S(1)}, s32[]{:S(2)}) async-start(s8[6291456]{0:T(1024)(128)(4,1)} %bitcast.169), calls=%async_computation.3 | async-start | bytes 8388608
  697.6 20.3 %copy-start.2 = (bf16[2,256,1024]{2,1,0:T(8,128)(2,1)S(1)}, bf16[2,256,1024]{2,1,0:T(8,128)(2,1)}, u32[]{:S(2)}) copy-start(bf16[2,256,1024]{2,1,0:T(8,128)(2,1)} %copy-done.1) | copy-start | bytes 3145732
  697.6 20.3 %copy-start.96 = (f32[1,1,1024]{2,1,0:T(1,128)S(1)}, f32[1,1,1024]{2,1,0:T(1,128)}, u32[]{:S(2)}) copy-start(f32[1,1,1024]{2,1,0:T(1,128)} %get-tuple-element.289) | copy-start | bytes 12292
  810.7 1.4 collective-permute-start.2
  (83 other events, 391.7 us)

commit v9 on v8

--- a/solution.py
+++ b/solution.py
@@ -17,7 +17,7 @@
 LOG2E = 1.0 / math.log(2.0)
 BF = jnp.bfloat16
 F32 = jnp.float32
-VMEM_LIMIT = 44 * 1024 * 1024
+VMEM_LIMIT = 42 * 1024 * 1024
 
 
 def slot_layout(lengths):
@@ -392,8 +392,8 @@
     rows.wait()
 
 
-ORDER = [(0, 1), (0, 3), (0, 2), (0, 0), (1, 0), (1, 1), (1, 3), (1, 2)]
-GAINS_AT, ROWS_AT, AHEAD = 3, 6, 1
+ORDER = [(0, 1), (0, 3), (0, 0), (0, 2), (1, 0), (1, 1), (1, 3), (1, 2)]
+GAINS_AT, ROWS_AT, AHEAD = 3, 4, 1
 
 
 def later_here(l, i):

time: 824 us -> 817 us (level)
    unnamed x213 -> x231, local copies, waits for them, and re-layouts: 46 us -> 49.6 us
  transfers between devices with their start and end apart: 3 -> 3, of which waited for: 1 -> 1; matrix products, arithmetic and copies ran while one was open for 2% -> 2% of each run, Pallas kernels for 33% -> 32%
where the time goes in v9:
time: 817 us; the launch traced here: 811 us
  Pallas kernels  708 us (87%)
  local copies, waits for them, and re-layouts  58.3 us (7%)
  other arithmetic  26.7 us (3%)
  matrix products  13.9 us (2%)
    pallas_call x26, Pallas kernels, host(): pl.pallas_call(kernel, grid=(steps,), in_specs=list(in_specs) + [any_spec...  539 us
    pallas_call x1, Pallas kernels, gather_all(): pl.pallas_call(functools.partial(gather_body, grid, layers, kinds), in_sp...  168 us
    unnamed x231, local copies, waits for them, and re-layouts  49.6 us
  transfers between devices with their start and end apart: 3, of which 1 were waited for; matrix products, arithmetic and copies ran while one was open for 2% of the time, Pallas kernels for 32%

profile of v9, /device:TPU:0, one launch (start us, length us, event | category | flops | bytes accessed | tf_op | source)
XLA Modules:
  0.0 810.6 jit_solution(11604902927234392285)
XLA Ops:
  6.8 168.5 %shard_map.153 = (bf16[2,256,1024]{2,1,0:T(8,128)(2,1)S(1)}, f32[4,2,4,8,128]{4,3,2,1,0:T(8,128)S(1)}, bf16[4,2,4,32,3072]{4,3,2,1,0:T(8,128)(2,1)}, bf16[4,2,4,...) custom-call(bf16[2,256,1024]{2,1,0:T(8,128)(2,1)S(1)} %copy-done.59,, ...), custom_call_target="tpu_custom_call" | custom-call | tf_op jit(solution)/shard_map/pallas_call | solution.py:412
  179.7 20.7 %shard_map.154 = (bf16[512,1024]{1,0:T(8,128)(2,1)S(1)}, bf16[512,1024]{1,0:T(8,128)(2,1)S(1)}, bf16[2,512,1024]{2,1,0:T(8,128)(2,1)S(1)}, bf16[1,2,512,1024]{3,...) custom-call(f32[1024,128]{1,0:T(8,128)S(1)} %get-tuple-element.137.refs_0_.refs_1_, ...), custom_call_target="tpu_custom_call", output_to_operand_aliasing={{4}: (7, {})} | custom-call | flops 3221225472 | bytes 6291456 | tf_op jit(solution)/shard_map/pallas_call | solution.py:694
  200.6 20.0 %shard_map.155 = (bf16[512,1024]{1,0:T(8,128)(2,1)S(1)}, f32[8,1,512]{2,1,0:T(1,128)}, bf16[4,2,4,32,5632]{4,3,2,1,0:T(8,128)(2,1)}) custom-call(s32[1]{0:T(128)} %bitcast.refs_0_, bf16[512,1024]{1,0:T(8,128)(2,1)S(1)} %get-tuple-element.144.refs_1_.refs_3_, ...), custom_call_target="tpu_custom_call", output_to_operand_aliasing={{2}: (4, {})} | custom-call | flops 1610612736 | bytes 8388608 | tf_op jit(solution)/shard_map/pallas_call | solution.py:694
  220.6 28.7 %shard_map.156 = (f32[512,1024]{1,0:T(8,128)S(1)}, f32[512,1024]{1,0:T(8,128)S(1)}, bf16[512,1024]{1,0:T(8,128)(2,1)S(1)}, bf16[2,512,2816]{2,1,0:T(8,128)(2,1)}...) custom-call(bf16[512,1024]{1,0:T(8,128)(2,1)S(1)} %bitcast.104, ...), custom_call_target="tpu_custom_call", output_to_operand_aliasing={{5}: (7, {}), {6}: (8, {})} | custom-call | flops 8858370048 | bytes 17301504 | tf_op jit(solution)/shard_map/pallas_call | solution.py:694
  255.5 21.2 %shard_map.157 = (bf16[512,1024]{1,0:T(8,128)(2,1)S(1)}, bf16[512,1024]{1,0:T(8,128)(2,1)S(1)}, bf16[3,512,1024]{2,1,0:T(8,128)(2,1)S(1)}, bf16[1,3,512,1024]{3,...) custom-call(f32[1024,128]{1,0:T(8,128)S(1)} %copy-done.18, ...), custom_call_target="tpu_custom_call", output_to_operand_aliasing={{5}: (7, {}), {6}: (8, {})} | custom-call | flops 3221225472 | bytes 6291456 | tf_op jit(solution)/shard_map/pallas_call | solution.py:694
  288.3 29.8 %shard_map.158 = bf16[2,8,128,1024]{3,2,1,0:T(8,128)(2,1)S(1)} custom-call(s32[8,128,1]{2,1,0:T(8,128)S(1)} %copy-done.42, bf16[3,512,1024]{2,1,0:T(8,128)(2,1)S(1)} %copy-done.5, bf16[3,512,1024]{2,1,0:T(8,128)(2,1)S(1)} %bitcast.108), custom_call_target="tpu_custom_call" | custom-call | tf_op jit(solution)/shard_map/pallas_call | solution.py:694
  323.8 29.1 %shard_map.159 = (bf16[512,1024]{1,0:T(8,128)(2,1)S(1)}, f32[8,1,512]{2,1,0:T(1,128)S(1)}, bf16[4,2,4,32,5632]{4,3,2,1,0:T(8,128)(2,1)}, bf16[2,256,1024]{2,1,0:T(8,128)(2,1)S(1)}) custom-call(s32[1]{0:T(128)} %bitcast.refs_0_, bf16[512,1024]{1,0:T(8,128)(2,1)S(1)} %copy-done.54, ...), custom_call_target="tpu_custom_call", output_to_operand_aliasing={{2}: (7, {})} | custom-call | flops 3758096384 | bytes 16777216 | tf_op jit(solution)/shard_map/pallas_call | solution.py:694
  352.9 19.3 %shard_map.160 = (f32[512,1024]{1,0:T(8,128)S(1)}, f32[512,1024]{1,0:T(8,128)S(1)}, bf16[512,1024]{1,0:T(8,128)(2,1)S(1)}, bf16[2,512,2816]{2,1,0:T(8,128)(2,1)}, bf16[512,2816]{1,0:T(8,128)(2,1)}) custom-call(f32[512,1024]{1,0:T(8,128)S(1)} %get-tuple-element.154.refs_2_.refs_0_, bf16[512,1024]{1,0:T(8,128)(2,1)S(1)} %get-tuple-element.164.refs_1_.refs_10_.refs_7_.refs_0_, ...), custom_call_target="tpu_custom_call" | custom-call | flops 8858370048 | bytes 17301504 | tf_op jit(solution)/shard_map/pallas_call | solution.py:694
  386.9 26.5 %shard_map.162 = (f32[512,1024]{1,0:T(8,128)S(1)}, bf16[512,1024]{1,0:T(8,128)(2,1)S(1)}, bf16[2,512,2816]{2,1,0:T(8,128)(2,1)}, f32[1,1024]{1,0:T(1,128)S(1)}, ...) custom-call(f32[512,1024]{1,0:T(8,128)} %bitcast_convert_fusion.refs, ...), custom_call_target="tpu_custom_call" | custom-call | flops 8858370048 | bytes 17301504 | tf_op jit(solution)/shard_map/pallas_call | solution.py:694
  415.7 11.7 %shard_map.163 = (bf16[1024,2816]{1,0:T(8,128)(2,1)S(1)}, bf16[1,704,512]{2,1,0:T(8,128)(2,1)S(1)}) custom-call(bf16[512,1024]{1,0:T(8,128)(2,1)S(1)} %get-tuple-element.171.refs_8_.refs_0_, bf16[512,1024]{1,0:T(8,128)(2,1)S(1)} %get-tuple-element.178.refs_1_, bf16[2,512,2816]{2,1,0:T(8,128)(2,1)} %get-tuple-element.179.refs_2_, ...), custom_call_target="tpu_custom_call" | custom-call | flops 5905580032 | bytes 5767168 | tf_op jit(solution)/shard_map/pallas_call | solution.py:694
  435.0 38.8 %shard_map.164 = (f32[512,1024]{1,0:T(8,128)S(1)}, bf16[2,1024,1024]{2,1,0:T(8,128)(2,1)}, bf16[2,1024,512]{2,1,0:T(8,128)(2,1)S(1)}, bf16[2,256,2816]{2,1,0:T(8...) custom-call(bf16[512,1024]{1,0:T(8,128)(2,1)S(1)} %convolution_convert_fusion.refs_0_.refs_4_, ...), custom_call_target="tpu_custom_call" | custom-call | flops 5368709120 | bytes 12582912 | tf_op jit(solution)/shard_map/pallas_call | solution.py:694
  477.6 30.7 %shard_map.165 = (bf16[512,1024]{1,0:T(8,128)(2,1)S(1)}, f32[2,512,1024]{2,1,0:T(8,128)}, bf16[1,2,512,1024]{3,2,1,0:T(8,128)(2,1)S(1)}, bf16[7,2,128,512]{3,2,1,0:T(8,128)(2,1)S(1)}) custom-call(s32[1]{0:T(128)} %bitcast.refs_0_, f32[1024,128]{1,0:T(8,128)S(1)} %copy-done.18, f32[1024,128]{1,0:T(8,128)S(1)} %copy-done.21, bf16[512,1024]{1,0:T(8,128)(2,1)S(1)} %copy-done.55, ...), custom_call_target="tpu_custom_call" | custom-call | flops 4026531840 | bytes 8388608 | tf_op jit(solution)/shard_map/pallas_call | solution.py:694
  514.9 20.8 %shard_map.166 = (bf16[512,3072]{1,0:T(8,128)(2,1)S(1)}, bf16[1,256,2816]{2,1,0:T(8,128)(2,1)S(1)}) custom-call(bf16[512,1024]{1,0:T(8,128)(2,1)S(1)} %get-tuple-element.188.refs_0_, f32[2,512,1024]{2,1,0:T(8,128)} %get-tuple-element.189.refs_1_, bf16[1,2,512,1024]{3,2,1,0:T(8,128)(2,1)S(1)} %get-tuple-element.190.refs_2_, s32[8,1,128]{2,1,0:T(1,128)S(1)} %bitcast.155, ...), custom_call_target="tpu_custom_call" | custom-call | flops 1048576 | bytes 8388608 | tf_op jit(solution)/shard_map/pallas_call | solution.py:694
  537.8 9.5 %shard_map.168 = (bf16[1024,1536]{1,0:T(8,128)(2,1)S(1)}, bf16[2,256,512]{2,1,0:T(8,128)(2,1)S(1)}) custom-call(bf16[512,1024]{1,0:T(8,128)(2,1)S(1)} %copy-done.52, bf16[512,1024]{1,0:T(8,128)(2,1)S(1)} %copy-done.94, bf16[512,3072]{1,0:T(8,128)(2,1)S(1)} %get-tuple-element.193.refs_2_, bf16[4,256,512]{2,1,0:T(8,128)(2,1)S(1)} %bitcast.136), custom_call_target="tpu_custom_call" | custom-call | flops 3221225472 | bytes 3145728 | tf_op jit(solution)/shard_map/pallas_call | solution.py:694
  558.3 22.2 %shard_map.169 = (bf16[2816,512]{1,0:T(8,128)(2,1)S(1)}, bf16[2,256,1536]{2,1,0:T(8,128)(2,1)S(1)}, bf16[1,2,32,2816]{3,2,1,0:T(8,128)(2,1)S(1)}) custom-call(bf16[512,2816]{1,0:T(8,128)(2,1)S(1)} %copy-done.9, bf16[512,2816]{1,0:T(8,128)(2,1)} %get-tuple-element.196.refs_1_, bf16[512,1024]{1,0:T(8,128)(2,1)S(1)} %get-tuple-element.261.refs_2_, ...), custom_call_target="tpu_custom_call" | custom-call | flops 2952790016 | bytes 2883584 | tf_op jit(solution)/shard_map/pallas_call | solution.py:694
  584.1 34.9 %shard_map.170 = (f32[512,1024]{1,0:T(8,128)}, bf16[512,1024]{1,0:T(8,128)(2,1)S(1)}, bf16[2,512,2816]{2,1,0:T(8,128)(2,1)}, f32[1,1024]{1,0:T(1,128)S(1)}, bf16...) custom-call(f32[512,1024]{1,0:T(8,128)} %get-tuple-element.262.refs_, ...), custom_call_target="tpu_custom_call" | custom-call | flops 8858370048 | bytes 17301504 | tf_op jit(solution)/shard_map/pallas_call | solution.py:694
  620.3 11.6 %shard_map.171 = (bf16[1024,1408]{1,0:T(8,128)(2,1)S(1)}, bf16[1,704,512]{2,1,0:T(8,128)(2,1)S(1)}, bf16[1,2,32,1536]{3,2,1,0:T(8,128)(2,1)S(1)}) custom-call(bf16[512,1024]{1,0:T(8,128)(2,1)S(1)} %copy-done.24, bf16[512,1024]{1,0:T(8,128)(2,1)S(1)} %get-tuple-element.207.refs_1_, bf16[2,512,2816]{2,1,0:T(8,128)(2,1)} %get-tuple-element.208.refs_2_, ...), custom_call_target="tpu_custom_call" | custom-call | flops 2952790016 | bytes 2883584 | tf_op jit(solution)/shard_map/pallas_call | solution.py:694
  631.9 21.5 %shard_map.172 = (bf16[1024,1408]{1,0:T(8,128)(2,1)S(1)}, bf16[2,256,1408]{2,1,0:T(8,128)(2,1)S(1)}, bf16[2,2,32,1536]{3,2,1,0:T(8,128)(2,1)S(1)}) custom-call(bf16[512,1024]{1,0:T(8,128)(2,1)S(1)} %copy-done.24, bf16[512,1024]{1,0:T(8,128)(2,1)S(1)} %get-tuple-element.207.refs_1_, bf16[2,512,2816]{2,1,0:T(8,128)(2,1)} %get-tuple-element.208.refs_2_, ...), custom_call_target="tpu_custom_call" | custom-call | flops 2952790016 | bytes 2883584 | tf_op jit(solution)/shard_map/pallas_call | solution.py:694
  656.9 29.4 %shard_map.174 = (bf16[512,1024]{1,0:T(8,128)(2,1)S(1)}, f32[2,512,1024]{2,1,0:T(8,128)}, bf16[1,2,512,1024]{3,2,1,0:T(8,128)(2,1)S(1)}, bf16[2,256,1408]{2,1,0:...) custom-call(s32[1]{0:T(128)} %bitcast.refs_0_, ...), custom_call_target="tpu_custom_call" | custom-call | flops 4026531840 | bytes 8388608 | tf_op jit(solution)/shard_map/pallas_call | solution.py:694
  691.7 19.0 %shard_map.175 = (bf16[512,3072]{1,0:T(8,128)(2,1)S(1)}, bf16[1,256,1408]{2,1,0:T(8,128)(2,1)S(1)}, bf16[2,256,512]{2,1,0:T(8,128)(2,1)S(1)}, bf16[3,2,32,1408]{3,2,1,0:T(8,128)(2,1)S(1)}) custom-call(bf16[512,1024]{1,0:T(8,128)(2,1)S(1)} %get-tuple-element.219.refs_0_, f32[2,512,1024]{2,1,0:T(8,128)} %get-tuple-element.220.refs_1_, ...), custom_call_target="tpu_custom_call" | custom-call | flops 1048576 | bytes 8388608 | tf_op jit(solution)/shard_map/pallas_call | solution.py:694
  722.4 17.7 %shard_map.176 = (bf16[1024,1536]{1,0:T(8,128)(2,1)S(1)}, bf16[3,2,32,1408]{3,2,1,0:T(8,128)(2,1)S(1)}, bf16[1,256,512]{2,1,0:T(8,128)(2,1)S(1)}, f32[32,128]{1,0:T(8,128)S(1)}) custom-call(bf16[512,1024]{1,0:T(8,128)(2,1)S(1)} %copy-done.47, bf16[512,1024]{1,0:T(8,128)(2,1)S(1)} %copy-done.92, bf16[512,3072]{1,0:T(8,128)(2,1)S(1)} %copy-done.89, ...), custom_call_target="tpu_custom_call" | custom-call | flops 3221225472 | bytes 3145728 | tf_op jit(solution)/shard_map/pallas_call | solution.py:694
  741.0 25.1 %shard_map.177 = (bf16[2,256,1536]{2,1,0:T(8,128)(2,1)S(1)}, bf16[3,2,32,512]{3,2,1,0:T(8,128)(2,1)S(1)}, bf16[2,128,1024]{2,1,0:T(8,128)(2,1)S(1)}, f32[32,128]{1,0:T(8,128)S(1)}) custom-call(bf16[4,256,1536]{2,1,0:T(8,128)(2,1)S(1)} %bitcast.114, bf16[2,4,32,512]{3,2,1,0:T(8,128)(2,1)S(1)} %bitcast.137, ...), custom_call_target="tpu_custom_call" | custom-call | tf_op jit(solution)/shard_map/pallas_call | solution.py:694
  766.6 12.6 %shard_map.178 = (bf16[1,256,1536]{2,1,0:T(8,128)(2,1)S(1)}, bf16[2,128,1024]{2,1,0:T(8,128)(2,1)S(1)}, f32[32,128]{1,0:T(8,128)S(1)}) custom-call(bf16[2,256,1536]{2,1,0:T(8,128)(2,1)S(1)} %add_convert_fusion.2.refs_0_, bf16[2,128,1024]{2,1,0:T(8,128)(2,1)S(1)} %get-tuple-element.279.refs_1_, f32[32,128]{1,0:T(8,128)S(1)} %add.298.refs_2_), custom_call_target="tpu_custom_call" | custom-call | tf_op jit(solution)/shard_map/pallas_call | solution.py:694
  779.5 23.4 %shard_map.179 = (f32[1,32,3072]{2,1,0:T(8,128)S(1)}, f32[2,32,1024]{2,1,0:T(8,128)S(1)}, f32[2,32,5632]{2,1,0:T(8,128)}, f32[2,88,1024]{2,1,0:T(8,128)S(1)}, f3...) custom-call(bf16[2,4,32,1536]{3,2,1,0:T(8,128)(2,1)S(1)} %bitcast.112, ...), custom_call_target="tpu_custom_call" | custom-call | tf_op jit(solution)/shard_map/pallas_call | solution.py:694
  (334 shorter events, 115.6 us)
Async XLA Ops:
  0.6 281.8 %collective-permute-start = (s32[2,1,8,128]{3,2,1,0:T(8,128)}, s32[2,1,8,128]{3,2,1,0:T(8,128)S(1)}, u32[]{:S(2)}, u32[]{:S(2)}) collective-permute-start(s32[2,1,8,128]{3,2,1,0:T(8,128)} %param.16), channel_id=1, source_target_pairs={{0,4},{1,5},{2,6},{3,7},{4,0},{5,1},{6,2},{7,3},{8,12},{9,13},{10,... | collective-permute-start | bytes 24584 | tf_op jit(solution)/shard_map/ppermute | solution.py:70
  6.6 193.8 %copy-start.17 = (f32[1024,128]{1,0:T(8,128)}, f32[1024,128]{1,0:T(8,128)S(1)}, u32[]{:S(2)}) copy-start(f32[1024,128]{1,0:T(8,128)S(1)} %get-tuple-element.137.refs_0_.refs_1_) | copy-start | bytes 1572868
  6.7 193.8 %copy-start.20 = (f32[1024,128]{1,0:T(8,128)}, f32[1024,128]{1,0:T(8,128)S(1)}, u32[]{:S(2)}) copy-start(f32[1024,128]{1,0:T(8,128)S(1)} %get-tuple-element.138.refs_1_.refs_2_) | copy-start | bytes 1572868
  6.7 172.2 %copy-start.108 = (s32[2,8]{1,0:T(2,128)S(1)}, s32[2,8]{1,0:T(2,128)}, u32[]{:S(2)}) copy-start(s32[2,8]{1,0:T(2,128)} %param.15) | copy-start | bytes 196
  177.9 42.7 %copy-start.1 = (bf16[2,256,1024]{2,1,0:T(8,128)(2,1)}, bf16[2,256,1024]{2,1,0:T(8,128)(2,1)S(1)}, u32[]{:S(2)}) copy-start(bf16[2,256,1024]{2,1,0:T(8,128)(2,1)S(1)} %get-tuple-element.140) | copy-start | bytes 3145732
  200.5 20.1 %copy-start.31 = (bf16[2,512,1024]{2,1,0:T(8,128)(2,1)}, bf16[2,512,1024]{2,1,0:T(8,128)(2,1)S(1)}, u32[]{:S(2)}) copy-start(bf16[2,512,1024]{2,1,0:T(8,128)(2,1)S(1)} %get-tuple-element.145.refs_2_.refs_5_) | copy-start | bytes 6291460
  200.5 20.1 %copy-start.32 = (bf16[1,2,512,1024]{3,2,1,0:T(8,128)(2,1)}, bf16[1,2,512,1024]{3,2,1,0:T(8,128)(2,1)S(1)}, u32[]{:S(2)}) copy-start(bf16[1,2,512,1024]{3,2,1,0:T(8,128)(2,1)S(1)} %get-tuple-element.146) | copy-start | bytes 6291460
  200.5 20.1 %copy-start.45 = (bf16[512,1024]{1,0:T(8,128)(2,1)}, bf16[512,1024]{1,0:T(8,128)(2,1)S(1)}, u32[]{:S(2)}) copy-start(bf16[512,1024]{1,0:T(8,128)(2,1)S(1)} %get-tuple-element.205.refs_12_.refs_0_) | copy-start | bytes 3145732
  200.5 20.1 %copy-start.48 = (bf16[512,1024]{1,0:T(8,128)(2,1)}, bf16[512,1024]{1,0:T(8,128)(2,1)S(1)}, u32[]{:S(2)}) copy-start(bf16[512,1024]{1,0:T(8,128)(2,1)S(1)} %get-tuple-element.144.refs_1_.refs_3_) | copy-start | bytes 3145732
  200.5 20.1 %copy-start.30 = (bf16[4,2,4,32,1024]{4,3,2,1,0:T(8,128)(2,1)S(1)}, bf16[4,2,4,32,1024]{4,3,2,1,0:T(8,128)(2,1)}, u32[]{:S(2)}) copy-start(bf16[4,2,4,32,1024]{4,3,2,1,0:T(8,128)(2,1)} %copy-done.29) | copy-start | bytes 6291460
  220.6 28.7 %copy-start.10 = (bf16[512,1024]{1,0:T(8,128)(2,1)}, bf16[512,1024]{1,0:T(8,128)(2,1)S(1)}, u32[]{:S(2)}) copy-start(bf16[512,1024]{1,0:T(8,128)(2,1)S(1)} %get-tuple-element.148.refs_1_.refs_13_.refs_0_) | copy-start | bytes 3145732
  255.5 26.9 %copy-start.105 = (s32[2,1,8,128]{3,2,1,0:T(8,128)S(1)}, s32[2,1,8,128]{3,2,1,0:T(8,128)}, u32[]{:S(2)}) copy-start(s32[2,1,8,128]{3,2,1,0:T(8,128)} %param.16) | copy-start | bytes 24580
  282.4 428.3 %copy-start.103 = (f32[1,2,2,128]{3,1,2,0:T(2,128)}, f32[1,2,2,128]{3,1,2,0:T(2,128)S(1)}, u32[]{:S(2)}) copy-start(f32[1,2,2,128]{3,1,2,0:T(2,128)S(1)} %copy.35) | copy-start | bytes 6148
  288.3 31.8 %copy-start.6 = (bf16[3,512,1024]{2,1,0:T(8,128)(2,1)S(1)}, bf16[3,512,1024]{2,1,0:T(8,128)(2,1)}, u32[]{:S(2)}) copy-start(bf16[3,512,1024]{2,1,0:T(8,128)(2,1)} %copy-done.4) | copy-start | bytes 9437188
  288.3 31.8 %copy-start.38 = (f32[1024,1]{1,0:T(8,128)S(1)}, f32[1024,1]{1,0:T(8,128)}, u32[]{:S(2)}) copy-start(f32[1024,1]{1,0:T(8,128)} %copy.29.refs_6_.refs_5_) | copy-start | bytes 12292
  323.8 29.1 %copy-start.35 = (bf16[4,2,4,32,1024]{4,3,2,1,0:T(8,128)(2,1)S(1)}, bf16[4,2,4,32,1024]{4,3,2,1,0:T(8,128)(2,1)}, u32[]{:S(2)}) copy-start(bf16[4,2,4,32,1024]{4,3,2,1,0:T(8,128)(2,1)} %copy-done.34) | copy-start | bytes 6291460
  509.6 5.2 collective-permute-start.1
  536.1 21.8 %copy-start = (bf16[1,256,2816]{2,1,0:T(8,128)(2,1)}, bf16[1,256,2816]{2,1,0:T(8,128)(2,1)S(1)}, u32[]{:S(2)}) copy-start(bf16[1,256,2816]{2,1,0:T(8,128)(2,1)S(1)} %add_convert_fusion.7) | copy-start | bytes 4325380
  584.1 35.0 %copy-start.95 = (bf16[2,256,1536]{2,1,0:T(8,128)(2,1)S(1)}, bf16[2,256,1536]{2,1,0:T(8,128)(2,1)}, u32[]{:S(2)}) copy-start(bf16[2,256,1536]{2,1,0:T(8,128)(2,1)} %add_convert_fusion.3.refs_9_) | copy-start | bytes 4718596
  631.9 21.6 %copy-start.83 = (bf16[1,2,32,1536]{3,2,1,0:T(8,128)(2,1)}, bf16[1,2,32,1536]{3,2,1,0:T(8,128)(2,1)S(1)}, u32[]{:S(2)}) copy-start(bf16[1,2,32,1536]{3,2,1,0:T(8,128)(2,1)S(1)} %get-tuple-element.210.refs_1_) | copy-start | bytes 589828
  690.5 20.3 %slice-start.2 = ((s8[6291456]{0:T(1024)(128)(4,1)}), s8[2097152]{0:T(1024)(128)(4,1)S(1)}, s32[]{:S(2)}) async-start(s8[6291456]{0:T(1024)(128)(4,1)} %bitcast.173), calls=%async_computation.2 | async-start | bytes 4194304
  691.7 19.1 %copy-start.2 = (bf16[2,256,1024]{2,1,0:T(8,128)(2,1)S(1)}, bf16[2,256,1024]{2,1,0:T(8,128)(2,1)}, u32[]{:S(2)}) copy-start(bf16[2,256,1024]{2,1,0:T(8,128)(2,1)} %copy-done.1) | copy-start | bytes 3145732
  691.7 19.1 %slice-start.3 = ((s8[6291456]{0:T(1024)(128)(4,1)}), s8[4194304]{0:T(1024)(128)(4,1)S(1)}, s32[]{:S(2)}) async-start(s8[6291456]{0:T(1024)(128)(4,1)} %bitcast.173), calls=%async_computation.3 | async-start | bytes 8388608
  803.9 1.4 collective-permute-start.2
  (92 other events, 429.2 us)

commit v10 on v9

--- a/solution.py
+++ b/solution.py
@@ -17,7 +17,7 @@
 LOG2E = 1.0 / math.log(2.0)
 BF = jnp.bfloat16
 F32 = jnp.float32
-VMEM_LIMIT = 42 * 1024 * 1024
+VMEM_LIMIT = 40 * 1024 * 1024
 
 
 def slot_layout(lengths):

time: 817 us -> 828 us (1.013)
  local copies, waits for them, and re-layouts: 58.3 us -> 78.2 us
    unnamed x231 -> x265, local copies, waits for them, and re-layouts: 49.6 us -> 68.7 us
where the time goes in v10:
time: 828 us; the launch traced here: 821 us
  Pallas kernels  705 us (85%)
  local copies, waits for them, and re-layouts  78.2 us (9%)
  other arithmetic  23.3 us (3%)
  matrix products  10.7 us (1%)
    pallas_call x26, Pallas kernels, host(): pl.pallas_call(kernel, grid=(steps,), in_specs=list(in_specs) + [any_spec...  537 us
    pallas_call x1, Pallas kernels, gather_all(): pl.pallas_call(functools.partial(gather_body, grid, layers, kinds), in_sp...  168 us
    unnamed x265, local copies, waits for them, and re-layouts  68.7 us
  transfers between devices with their start and end apart: 3, of which 1 were waited for; matrix products, arithmetic and copies ran while one was open for 2% of the time, Pallas kernels for 32%

profile of v10, /device:TPU:0, one launch (start us, length us, event | category | flops | bytes accessed | tf_op | source)
XLA Modules:
  0.0 821.5 jit_solution(14541487004232069962)
XLA Ops:
  6.8 168.0 %shard_map.153 = (bf16[2,256,1024]{2,1,0:T(8,128)(2,1)S(1)}, f32[4,2,4,8,128]{4,3,2,1,0:T(8,128)S(1)}, bf16[4,2,4,32,3072]{4,3,2,1,0:T(8,128)(2,1)}, bf16[4,2,4,...) custom-call(bf16[2,256,1024]{2,1,0:T(8,128)(2,1)S(1)} %copy-done.70,, ...), custom_call_target="tpu_custom_call" | custom-call | tf_op jit(solution)/shard_map/pallas_call | solution.py:412
  184.3 20.6 %shard_map.154 = (bf16[512,1024]{1,0:T(8,128)(2,1)S(1)}, bf16[512,1024]{1,0:T(8,128)(2,1)S(1)}, bf16[2,512,1024]{2,1,0:T(8,128)(2,1)S(1)}, bf16[1,2,512,1024]{3,...) custom-call(f32[1024,128]{1,0:T(8,128)S(1)} %get-tuple-element.137.refs_0_.refs_1_, ...), custom_call_target="tpu_custom_call", output_to_operand_aliasing={{4}: (7, {})} | custom-call | flops 3221225472 | bytes 6291456 | tf_op jit(solution)/shard_map/pallas_call | solution.py:694
  208.6 19.9 %shard_map.155 = (bf16[512,1024]{1,0:T(8,128)(2,1)S(1)}, f32[8,1,512]{2,1,0:T(1,128)}, bf16[4,2,4,32,5632]{4,3,2,1,0:T(8,128)(2,1)}) custom-call(s32[1]{0:T(128)} %bitcast.refs_0_, bf16[512,1024]{1,0:T(8,128)(2,1)S(1)} %get-tuple-element.144.refs_1_.refs_3_, ...), custom_call_target="tpu_custom_call", output_to_operand_aliasing={{2}: (4, {})} | custom-call | flops 1610612736 | bytes 8388608 | tf_op jit(solution)/shard_map/pallas_call | solution.py:694
  228.6 28.8 %shard_map.156 = (f32[512,1024]{1,0:T(8,128)S(1)}, f32[512,1024]{1,0:T(8,128)S(1)}, bf16[512,1024]{1,0:T(8,128)(2,1)S(1)}, bf16[2,512,2816]{2,1,0:T(8,128)(2,1)}...) custom-call(bf16[512,1024]{1,0:T(8,128)(2,1)S(1)} %bitcast.108, ...), custom_call_target="tpu_custom_call", output_to_operand_aliasing={{5}: (7, {}), {6}: (8, {})} | custom-call | flops 8858370048 | bytes 17301504 | tf_op jit(solution)/shard_map/pallas_call | solution.py:694
  263.7 21.2 %shard_map.157 = (bf16[512,1024]{1,0:T(8,128)(2,1)S(1)}, bf16[512,1024]{1,0:T(8,128)(2,1)S(1)}, bf16[3,512,1024]{2,1,0:T(8,128)(2,1)S(1)}, bf16[1,3,512,1024]{3,...) custom-call(f32[1024,128]{1,0:T(8,128)S(1)} %copy-done.23, ...), custom_call_target="tpu_custom_call", output_to_operand_aliasing={{5}: (7, {}), {6}: (8, {})} | custom-call | flops 3221225472 | bytes 6291456 | tf_op jit(solution)/shard_map/pallas_call | solution.py:694
  298.2 29.8 %shard_map.158 = bf16[2,8,128,1024]{3,2,1,0:T(8,128)(2,1)S(1)} custom-call(s32[8,128,1]{2,1,0:T(8,128)S(1)} %copy-done.49, bf16[3,512,1024]{2,1,0:T(8,128)(2,1)S(1)} %copy-done.8, bf16[3,512,1024]{2,1,0:T(8,128)(2,1)S(1)} %bitcast.112), custom_call_target="tpu_custom_call" | custom-call | tf_op jit(solution)/shard_map/pallas_call | solution.py:694
  332.4 30.3 %shard_map.159 = (bf16[512,1024]{1,0:T(8,128)(2,1)S(1)}, f32[8,1,512]{2,1,0:T(1,128)S(1)}, bf16[4,2,4,32,5632]{4,3,2,1,0:T(8,128)(2,1)}, bf16[2,256,1024]{2,1,0:T(8,128)(2,1)S(1)}) custom-call(s32[1]{0:T(128)} %bitcast.refs_0_, bf16[512,1024]{1,0:T(8,128)(2,1)S(1)} %copy-done.61, ...), custom_call_target="tpu_custom_call", output_to_operand_aliasing={{2}: (7, {})} | custom-call | flops 3758096384 | bytes 16777216 | tf_op jit(solution)/shard_map/pallas_call | solution.py:694
  362.8 18.5 %shard_map.160 = (f32[512,1024]{1,0:T(8,128)S(1)}, f32[512,1024]{1,0:T(8,128)S(1)}, bf16[512,1024]{1,0:T(8,128)(2,1)S(1)}, bf16[2,512,2816]{2,1,0:T(8,128)(2,1)}, bf16[512,2816]{1,0:T(8,128)(2,1)S(1)}) custom-call(f32[512,1024]{1,0:T(8,128)S(1)} %get-tuple-element.154.refs_2_.refs_0_, ...), custom_call_target="tpu_custom_call" | custom-call | flops 8858370048 | bytes 17301504 | tf_op jit(solution)/shard_map/pallas_call | solution.py:694
  395.8 26.0 %shard_map.162 = (f32[512,1024]{1,0:T(8,128)S(1)}, bf16[512,1024]{1,0:T(8,128)(2,1)S(1)}, bf16[2,512,2816]{2,1,0:T(8,128)(2,1)}, f32[1,1024]{1,0:T(1,128)S(1)}, ...) custom-call(f32[512,1024]{1,0:T(8,128)S(1)} %bitcast_convert_fusion., ...), custom_call_target="tpu_custom_call" | custom-call | flops 8858370048 | bytes 17301504 | tf_op jit(solution)/shard_map/pallas_call | solution.py:694
  424.2 11.7 %shard_map.163 = (bf16[1024,2816]{1,0:T(8,128)(2,1)S(1)}, bf16[1,704,512]{2,1,0:T(8,128)(2,1)S(1)}) custom-call(bf16[512,1024]{1,0:T(8,128)(2,1)S(1)} %copy-done.67, bf16[512,1024]{1,0:T(8,128)(2,1)S(1)} %get-tuple-element.178.refs_1_, bf16[2,512,2816]{2,1,0:T(8,128)(2,1)} %get-tuple-element.179.refs_2_, bf16[2,704,512]{2,1,0:T(8,128)(2,1)S(1)} %add_convert_fusion.8.refs_3_), custom_call_target="tpu_custom_call" | custom-call | flops 5905580032 | bytes 5767168 | tf_op jit(solution)/shard_map/pallas_call | solution.py:694
  442.1 38.7 %shard_map.164 = (f32[512,1024]{1,0:T(8,128)S(1)}, bf16[2,1024,1024]{2,1,0:T(8,128)(2,1)}, bf16[2,1024,512]{2,1,0:T(8,128)(2,1)S(1)}, bf16[2,256,2816]{2,1,0:T(8...) custom-call(bf16[512,1024]{1,0:T(8,128)(2,1)S(1)} %convolution_convert_fusion.refs_0_.refs_4_, ...), custom_call_target="tpu_custom_call" | custom-call | flops 5368709120 | bytes 12582912 | tf_op jit(solution)/shard_map/pallas_call | solution.py:694
  483.3 30.4 %shard_map.165 = (bf16[512,1024]{1,0:T(8,128)(2,1)S(1)}, f32[2,512,1024]{2,1,0:T(8,128)}, bf16[1,2,512,1024]{3,2,1,0:T(8,128)(2,1)S(1)}, bf16[7,2,128,512]{3,2,1,0:T(8,128)(2,1)S(1)}) custom-call(s32[1]{0:T(128)} %bitcast.refs_0_, f32[1024,128]{1,0:T(8,128)S(1)} %copy-done.23, f32[1024,128]{1,0:T(8,128)S(1)} %copy-done.26, bf16[512,1024]{1,0:T(8,128)(2,1)S(1)} %copy-done.62, ...), custom_call_target="tpu_custom_call" | custom-call | flops 4026531840 | bytes 8388608 | tf_op jit(solution)/shard_map/pallas_call | solution.py:694
  521.1 20.8 %shard_map.166 = (bf16[512,3072]{1,0:T(8,128)(2,1)S(1)}, bf16[1,256,2816]{2,1,0:T(8,128)(2,1)S(1)}) custom-call(bf16[512,1024]{1,0:T(8,128)(2,1)S(1)} %get-tuple-element.188.refs_0_, f32[2,512,1024]{2,1,0:T(8,128)} %get-tuple-element.189.refs_1_, bf16[1,2,512,1024]{3,2,1,0:T(8,128)(2,1)S(1)} %get-tuple-element.190.refs_2_, s32[8,1,128]{2,1,0:T(1,128)S(1)} %bitcast.159, ...), custom_call_target="tpu_custom_call" | custom-call | flops 1048576 | bytes 8388608 | tf_op jit(solution)/shard_map/pallas_call | solution.py:694
  543.1 9.9 %shard_map.168 = (bf16[1024,1536]{1,0:T(8,128)(2,1)S(1)}, bf16[2,256,512]{2,1,0:T(8,128)(2,1)S(1)}) custom-call(bf16[512,1024]{1,0:T(8,128)(2,1)S(1)} %copy-done.59, bf16[512,1024]{1,0:T(8,128)(2,1)S(1)} %get-tuple-element.184.refs_1_, bf16[512,3072]{1,0:T(8,128)(2,1)S(1)} %get-tuple-element.193.refs_2_, bf16[4,256,512]{2,1,0:T(8,128)(2,1)S(1)} %bitcast.142), custom_call_target="tpu_custom_call" | custom-call | flops 3221225472 | bytes 3145728 | tf_op jit(solution)/shard_map/pallas_call | solution.py:694
  561.8 21.2 %shard_map.169 = (bf16[2816,512]{1,0:T(8,128)(2,1)S(1)}, bf16[2,256,1536]{2,1,0:T(8,128)(2,1)S(1)}, bf16[1,2,32,2816]{3,2,1,0:T(8,128)(2,1)S(1)}) custom-call(bf16[512,2816]{1,0:T(8,128)(2,1)S(1)} %copy-done.13, bf16[512,2816]{1,0:T(8,128)(2,1)S(1)} %copy-done.34, bf16[512,1024]{1,0:T(8,128)(2,1)S(1)} %get-tuple-element.261.refs_2_, ...), custom_call_target="tpu_custom_call" | custom-call | flops 2952790016 | bytes 2883584 | tf_op jit(solution)/shard_map/pallas_call | solution.py:694
  586.8 34.8 %shard_map.170 = (f32[512,1024]{1,0:T(8,128)}, bf16[512,1024]{1,0:T(8,128)(2,1)S(1)}, bf16[2,512,2816]{2,1,0:T(8,128)(2,1)}, f32[1,1024]{1,0:T(1,128)S(1)}, bf16...) custom-call(f32[512,1024]{1,0:T(8,128)} %get-tuple-element.262.refs_, ...), custom_call_target="tpu_custom_call" | custom-call | flops 8858370048 | bytes 17301504 | tf_op jit(solution)/shard_map/pallas_call | solution.py:694
  626.9 11.6 %shard_map.171 = (bf16[1024,1408]{1,0:T(8,128)(2,1)S(1)}, bf16[1,704,512]{2,1,0:T(8,128)(2,1)S(1)}, bf16[1,2,32,1536]{3,2,1,0:T(8,128)(2,1)S(1)}) custom-call(bf16[512,1024]{1,0:T(8,128)(2,1)S(1)} %copy-done.29, bf16[512,1024]{1,0:T(8,128)(2,1)S(1)} %get-tuple-element.207.refs_1_, bf16[2,512,2816]{2,1,0:T(8,128)(2,1)S(1)} %copy-done.21, ...), custom_call_target="tpu_custom_call" | custom-call | flops 2952790016 | bytes 2883584 | tf_op jit(solution)/shard_map/pallas_call | solution.py:694
  639.2 21.2 %shard_map.172 = (bf16[1024,1408]{1,0:T(8,128)(2,1)S(1)}, bf16[2,256,1408]{2,1,0:T(8,128)(2,1)S(1)}, bf16[2,2,32,1536]{3,2,1,0:T(8,128)(2,1)S(1)}) custom-call(bf16[512,1024]{1,0:T(8,128)(2,1)S(1)} %copy-done.29, bf16[512,1024]{1,0:T(8,128)(2,1)S(1)} %get-tuple-element.207.refs_1_, bf16[2,512,2816]{2,1,0:T(8,128)(2,1)} %get-tuple-element.208.refs_2_, ...), custom_call_target="tpu_custom_call" | custom-call | flops 2952790016 | bytes 2883584 | tf_op jit(solution)/shard_map/pallas_call | solution.py:694
  664.7 29.4 %shard_map.174 = (bf16[512,1024]{1,0:T(8,128)(2,1)S(1)}, f32[2,512,1024]{2,1,0:T(8,128)}, bf16[1,2,512,1024]{3,2,1,0:T(8,128)(2,1)S(1)}, bf16[2,256,1408]{2,1,0:...) custom-call(s32[1]{0:T(128)} %bitcast.refs_0_, ...), custom_call_target="tpu_custom_call" | custom-call | flops 4026531840 | bytes 8388608 | tf_op jit(solution)/shard_map/pallas_call | solution.py:694
  700.0 19.3 %shard_map.175 = (bf16[512,3072]{1,0:T(8,128)(2,1)S(1)}, bf16[1,256,1408]{2,1,0:T(8,128)(2,1)S(1)}, bf16[2,256,512]{2,1,0:T(8,128)(2,1)S(1)}, bf16[3,2,32,1408]{3,2,1,0:T(8,128)(2,1)S(1)}) custom-call(bf16[512,1024]{1,0:T(8,128)(2,1)S(1)} %get-tuple-element.219.refs_0_, f32[2,512,1024]{2,1,0:T(8,128)} %get-tuple-element.220.refs_1_, ...), custom_call_target="tpu_custom_call" | custom-call | flops 1048576 | bytes 8388608 | tf_op jit(solution)/shard_map/pallas_call | solution.py:694
  731.0 17.6 %shard_map.176 = (bf16[1024,1536]{1,0:T(8,128)(2,1)S(1)}, bf16[3,2,32,1408]{3,2,1,0:T(8,128)(2,1)S(1)}, bf16[1,256,512]{2,1,0:T(8,128)(2,1)S(1)}, f32[32,128]{1,0:T(8,128)S(1)}) custom-call(bf16[512,1024]{1,0:T(8,128)(2,1)S(1)} %copy-done.54, bf16[512,1024]{1,0:T(8,128)(2,1)S(1)} %copy-done.111, bf16[512,3072]{1,0:T(8,128)(2,1)S(1)} %copy-done.109, ...), custom_call_target="tpu_custom_call" | custom-call | flops 3221225472 | bytes 3145728 | tf_op jit(solution)/shard_map/pallas_call | solution.py:694
  749.6 25.0 %shard_map.177 = (bf16[2,256,1536]{2,1,0:T(8,128)(2,1)S(1)}, bf16[3,2,32,512]{3,2,1,0:T(8,128)(2,1)S(1)}, bf16[2,128,1024]{2,1,0:T(8,128)(2,1)S(1)}, f32[32,128]{1,0:T(8,128)S(1)}) custom-call(bf16[4,256,1536]{2,1,0:T(8,128)(2,1)S(1)} %bitcast.118, bf16[2,4,32,512]{3,2,1,0:T(8,128)(2,1)S(1)} %bitcast.143, ...), custom_call_target="tpu_custom_call" | custom-call | tf_op jit(solution)/shard_map/pallas_call | solution.py:694
  775.1 12.6 %shard_map.178 = (bf16[1,256,1536]{2,1,0:T(8,128)(2,1)S(1)}, bf16[2,128,1024]{2,1,0:T(8,128)(2,1)S(1)}, f32[32,128]{1,0:T(8,128)S(1)}) custom-call(bf16[2,256,1536]{2,1,0:T(8,128)(2,1)S(1)} %add_convert_fusion.2.refs_0_, bf16[2,128,1024]{2,1,0:T(8,128)(2,1)S(1)} %get-tuple-element.279.refs_1_, f32[32,128]{1,0:T(8,128)S(1)} %add.298.refs_2_), custom_call_target="tpu_custom_call" | custom-call | tf_op jit(solution)/shard_map/pallas_call | solution.py:694
  788.1 22.9 %shard_map.179 = (f32[1,32,3072]{2,1,0:T(8,128)S(1)}, f32[2,32,1024]{2,1,0:T(8,128)S(1)}, f32[2,32,5632]{2,1,0:T(8,128)S(1)}, f32[2,88,1024]{2,1,0:T(8,128)S(1)}...) custom-call(bf16[2,4,32,1536]{3,2,1,0:T(8,128)(2,1)S(1)} %bitcast.116, ...), custom_call_target="tpu_custom_call" | custom-call | tf_op jit(solution)/shard_map/pallas_call | solution.py:694
  (368 shorter events, 128.5 us)
Async XLA Ops:
  0.6 291.7 %collective-permute-start = (s32[2,1,8,128]{3,2,1,0:T(8,128)}, s32[2,1,8,128]{3,2,1,0:T(8,128)S(1)}, u32[]{:S(2)}, u32[]{:S(2)}) collective-permute-start(s32[2,1,8,128]{3,2,1,0:T(8,128)} %param.16), channel_id=1, source_target_pairs={{0,4},{1,5},{2,6},{3,7},{4,0},{5,1},{6,2},{7,3},{8,12},{9,13},{10,... | collective-permute-start | bytes 24584 | tf_op jit(solution)/shard_map/ppermute | solution.py:70
  6.6 198.3 %copy-start.22 = (f32[1024,128]{1,0:T(8,128)}, f32[1024,128]{1,0:T(8,128)S(1)}, u32[]{:S(2)}) copy-start(f32[1024,128]{1,0:T(8,128)S(1)} %get-tuple-element.137.refs_0_.refs_1_) | copy-start | bytes 1572868
  6.7 198.3 %copy-start.25 = (f32[1024,128]{1,0:T(8,128)}, f32[1024,128]{1,0:T(8,128)S(1)}, u32[]{:S(2)}) copy-start(f32[1024,128]{1,0:T(8,128)S(1)} %get-tuple-element.138.refs_1_.refs_2_) | copy-start | bytes 1572868
  6.7 174.1 %copy-start.125 = (s32[2,8]{1,0:T(2,128)S(1)}, s32[2,8]{1,0:T(2,128)}, u32[]{:S(2)}) copy-start(s32[2,8]{1,0:T(2,128)} %param.15) | copy-start | bytes 196
  179.8 48.8 %copy-start.4 = (bf16[2,256,1024]{2,1,0:T(8,128)(2,1)}, bf16[2,256,1024]{2,1,0:T(8,128)(2,1)S(1)}, u32[]{:S(2)}) copy-start(bf16[2,256,1024]{2,1,0:T(8,128)(2,1)S(1)} %get-tuple-element.140) | copy-start | bytes 3145732
  208.6 20.0 %copy-start.37 = (bf16[2,512,1024]{2,1,0:T(8,128)(2,1)}, bf16[2,512,1024]{2,1,0:T(8,128)(2,1)S(1)}, u32[]{:S(2)}) copy-start(bf16[2,512,1024]{2,1,0:T(8,128)(2,1)S(1)} %get-tuple-element.145.refs_2_.refs_5_) | copy-start | bytes 6291460
  208.6 20.0 %copy-start.39 = (bf16[1,2,512,1024]{3,2,1,0:T(8,128)(2,1)}, bf16[1,2,512,1024]{3,2,1,0:T(8,128)(2,1)S(1)}, u32[]{:S(2)}) copy-start(bf16[1,2,512,1024]{3,2,1,0:T(8,128)(2,1)S(1)} %get-tuple-element.146) | copy-start | bytes 6291460
  208.6 20.0 %copy-start.55 = (bf16[512,1024]{1,0:T(8,128)(2,1)}, bf16[512,1024]{1,0:T(8,128)(2,1)S(1)}, u32[]{:S(2)}) copy-start(bf16[512,1024]{1,0:T(8,128)(2,1)S(1)} %get-tuple-element.144.refs_1_.refs_3_) | copy-start | bytes 3145732
  208.6 20.0 %copy-start.36 = (bf16[4,2,4,32,1024]{4,3,2,1,0:T(8,128)(2,1)S(1)}, bf16[4,2,4,32,1024]{4,3,2,1,0:T(8,128)(2,1)}, u32[]{:S(2)}) copy-start(bf16[4,2,4,32,1024]{4,3,2,1,0:T(8,128)(2,1)} %copy-done.35) | copy-start | bytes 6291460
  228.6 28.9 %copy-start.14 = (bf16[512,1024]{1,0:T(8,128)(2,1)}, bf16[512,1024]{1,0:T(8,128)(2,1)S(1)}, u32[]{:S(2)}) copy-start(bf16[512,1024]{1,0:T(8,128)(2,1)S(1)} %get-tuple-element.148.refs_1_.refs_13_.refs_0_) | copy-start | bytes 3145732
  263.7 28.6 %copy-start.122 = (s32[2,1,8,128]{3,2,1,0:T(8,128)S(1)}, s32[2,1,8,128]{3,2,1,0:T(8,128)}, u32[]{:S(2)}) copy-start(s32[2,1,8,128]{3,2,1,0:T(8,128)} %param.16) | copy-start | bytes 24580
  292.3 427.1 %copy-start.120 = (f32[1,2,2,128]{3,1,2,0:T(2,128)}, f32[1,2,2,128]{3,1,2,0:T(2,128)S(1)}, u32[]{:S(2)}) copy-start(f32[1,2,2,128]{3,1,2,0:T(2,128)S(1)} %copy.35) | copy-start | bytes 6148
  298.2 31.8 %copy-start.9 = (bf16[3,512,1024]{2,1,0:T(8,128)(2,1)S(1)}, bf16[3,512,1024]{2,1,0:T(8,128)(2,1)}, u32[]{:S(2)}) copy-start(bf16[3,512,1024]{2,1,0:T(8,128)(2,1)} %copy-done.7) | copy-start | bytes 9437188
  298.2 31.8 %copy-start.45 = (f32[1024,1]{1,0:T(8,128)S(1)}, f32[1024,1]{1,0:T(8,128)}, u32[]{:S(2)}) copy-start(f32[1024,1]{1,0:T(8,128)} %copy.29.refs_6_.refs_5_) | copy-start | bytes 12292
  298.2 31.8 %copy-start.51 = (bf16[2,256,1024]{2,1,0:T(8,128)(2,1)S(1)}, bf16[2,256,1024]{2,1,0:T(8,128)(2,1)}, u32[]{:S(2)}) copy-start(bf16[2,256,1024]{2,1,0:T(8,128)(2,1)} %refs_8_.1) | copy-start | bytes 3145732
  332.4 30.3 %copy-start.42 = (bf16[4,2,4,32,1024]{4,3,2,1,0:T(8,128)(2,1)S(1)}, bf16[4,2,4,32,1024]{4,3,2,1,0:T(8,128)(2,1)}, u32[]{:S(2)}) copy-start(bf16[4,2,4,32,1024]{4,3,2,1,0:T(8,128)(2,1)} %copy-done.41) | copy-start | bytes 6291460
  362.7 20.3 %copy-start.68 = (bf16[2,256,1024]{2,1,0:T(8,128)(2,1)}, bf16[2,256,1024]{2,1,0:T(8,128)(2,1)S(1)}, u32[]{:S(2)}) copy-start(bf16[2,256,1024]{2,1,0:T(8,128)(2,1)S(1)} %get-tuple-element.163) | copy-start | bytes 3145732
  514.1 6.9 collective-permute-start.1
  542.2 43.2 %copy-start.3 = (bf16[1,256,2816]{2,1,0:T(8,128)(2,1)}, bf16[1,256,2816]{2,1,0:T(8,128)(2,1)S(1)}, u32[]{:S(2)}) copy-start(bf16[1,256,2816]{2,1,0:T(8,128)(2,1)S(1)} %add_convert_fusion.7) | copy-start | bytes 4325380
  698.8 20.6 %slice-start.2 = ((s8[6291456]{0:T(1024)(128)(4,1)}), s8[4194304]{0:T(1024)(128)(4,1)S(1)}, s32[]{:S(2)}) async-start(s8[6291456]{0:T(1024)(128)(4,1)} %bitcast.177), calls=%async_computation.2 | async-start | bytes 8388608
  700.0 19.4 %copy-start.5 = (bf16[2,256,1024]{2,1,0:T(8,128)(2,1)S(1)}, bf16[2,256,1024]{2,1,0:T(8,128)(2,1)}, u32[]{:S(2)}) copy-start(bf16[2,256,1024]{2,1,0:T(8,128)(2,1)} %copy-done.4) | copy-start | bytes 3145732
  700.0 19.4 %slice-start.3 = ((s8[6291456]{0:T(1024)(128)(4,1)}), s8[2097152]{0:T(1024)(128)(4,1)S(1)}, s32[]{:S(2)}) async-start(s8[6291456]{0:T(1024)(128)(4,1)} %bitcast.177), calls=%async_computation.3 | async-start | bytes 4194304
  700.0 19.4 %copy-start.118 = (f32[1,1,1024]{2,1,0:T(1,128)S(1)}, f32[1,1,1024]{2,1,0:T(1,128)}, u32[]{:S(2)}) copy-start(f32[1,1,1024]{2,1,0:T(1,128)} %get-tuple-element.289) | copy-start | bytes 12292
  814.9 1.4 collective-permute-start.2
  (109 other events, 454.3 us)
